TPU v7x, 32 devices: a whole 2x2x4 slice. The times are simulated.
32 devices in a mesh: section: 2 (over core), wide: 4 (over y, x), rows: 4 (over z).
Axes of the slice: x: 2, y: 2, z: 4, core: 2. Of those that a mesh axis runs over, the one named last changes fastest.
Arguments:
- enc_embed: bfloat16 [2, 16, 256, 1472], P(None, ('wide', 'rows')), may hold values from -6 to 6
- dec_embed: bfloat16 [2, 16, 64, 1472], P(None, ('wide', 'rows')), may hold values from -6 to 6
- out_cot: bfloat16 [2, 16, 64, 1472], P(None, ('wide', 'rows')), may hold values from -6 to 6
- enc_lengths: int32 [2, 16, 8], P(None, ('wide', 'rows')), may hold values from 1 to 128, 256 in all within a row
- dec_lengths: int32 [2, 16, 8], P(None, ('wide', 'rows')), may hold values from 1 to 32, 64 in all within a row
- norm_gains: float32 [2, 3, 1472], P('section'), may hold values from 0.5 to 1.5
- rel_bias: float32 [2, 32, 6], P('section'), may hold values from -3 to 3
- attn_in: bfloat16 [2, 1472, 1152], P('section', 'wide'), may hold values from -0.09375 to 0.09375
- attn_out: bfloat16 [2, 384, 1472], P('section', None, 'wide'), may hold values from -0.875 to 0.875
- ffn_in: bfloat16 [2, 1472, 7168], P('section', 'wide'), may hold values from -0.15625 to 0.15625
- ffn_out: bfloat16 [2, 3584, 1472], P('section', None, 'wide'), may hold values from -0.09375 to 0.09375
- cross_in: bfloat16 [2, 1472, 384], P('section', 'wide'), may hold values from -0.09375 to 0.09375
- cross_out: bfloat16 [2, 1472, 384], P('section', 'wide'), may hold values from -0.21875 to 0.21875
Outputs:
- dec_out: bfloat16 [2, 16, 64, 1472], P(None, ('wide', 'rows'), None, 'section')
- enc_grad: float32 [2, 16, 256, 1472], P(None, ('wide', 'rows'), None, 'section')
- dec_grad: float32 [2, 16, 64, 1472], P(None, ('wide', 'rows'), None, 'section')
- gain_grad: float32 [2, 3, 1472], P('section')
- bias_grad: float32 [2, 32, 6], P('section')
- attn_in_grad: float32 [2, 1472, 1152], P('section', 'wide', 'rows')
- attn_out_grad: float32 [2, 384, 1472], P('section', 'rows', 'wide')
- ffn_in_grad: float32 [2, 1472, 7168], P('section', 'wide', 'rows')
- ffn_out_grad: float32 [2, 3584, 1472], P('section', 'rows', 'wide')
- cross_in_grad: float32 [2, 1472, 384], P('section', 'wide', 'rows')
- cross_out_grad: float32 [2, 1472, 384], P('section', 'wide', 'rows')
Inputs may be any that keep to these rules, and one draw needn't show every extreme that they name: `enc_lengths`: each row's 8 encoder item lengths sum to 256. `dec_lengths`: each row's 8 target item lengths sum to 64.
All inputs are finite; a program needn't handle non-finite values.
Results may differ from a plain program's by a relative error of at most 0.03.
The roundings to bfloat16 on the way count: a program that leaves them out, or rounds other values in their place, can miss the bound.
Values may be sent and summed in bfloat16 or wider, within the bound.
A program may use at most 960 MiB of HBM per device.

v0:
```python
import jax
import jax.numpy as jnp
import numpy as np
from jax import lax
from jax.sharding import PartitionSpec as P

D = 1472
H = 6
DH = 64
FF = 3584
NB = 32
MAXDIST = 128
MB = 2
LE = 256
LD = 64
HD = 384


EPSILON = 1e-06
NEGATIVE = -1000000000.0
HIGHEST = lax.Precision.HIGHEST


def shifted_2(value, axis, by):
    count = lax.axis_size(axis)
    pairs = [(i, i + by) for i in range(count) if 0 <= i + by < count]
    return lax.ppermute(value, axis, pairs)


def swapped(block, axis, distance):
    count = lax.axis_size(axis)
    route = []
    for low in range(count):
        high = low | 1 << distance
        if high != low and high < count:
            route += [(low, high), (high, low)]
    return lax.ppermute(block, axis, route)


def bucket_table(length, both_ways):
    positions = np.arange(length)
    offsets = positions[None, :] - positions[:, None]
    buckets = NB
    result = np.zeros(offsets.shape, np.int64)
    if both_ways:
        buckets = buckets // 2
        result = result + (offsets > 0) * buckets
        distance = np.abs(offsets)
    else:
        distance = np.maximum(-offsets, 0)
    exact_count = buckets // 2
    log_ratio = np.log(np.maximum(distance, 1) / exact_count) / np.log(MAXDIST / exact_count)
    far_bucket = np.minimum(
        exact_count + np.floor(log_ratio * (buckets - exact_count)).astype(np.int64), buckets - 1
    )
    return result + np.where(distance < exact_count, distance, far_bucket)


def one_hot(length, both_ways):
    bucket_ids = jnp.asarray(bucket_table(length, both_ways), jnp.int32)
    return (bucket_ids[:, :, None] == jnp.arange(NB, dtype=jnp.int32)[None, None, :]).astype(
        jnp.float32
    )


def item_ids(lengths, length):
    item_ends = jnp.cumsum(lengths)
    positions = jnp.arange(length, dtype=jnp.int32)
    return jnp.sum((positions[:, None] >= item_ends[None, :-1]).astype(jnp.int32), axis=1)


def rms_norm(residual, gain_row):
    return (
        residual
        * lax.rsqrt(jnp.mean(residual * residual, axis=-1, keepdims=True) + EPSILON)
        * gain_row
    )


def matmul(left_side, right_side):
    return jnp.dot(left_side, right_side, preferred_element_type=jnp.float32)


def to_low(tensor):
    return tensor.astype(jnp.bfloat16)


def gated(gate_part, up_part):
    return jax.nn.gelu(gate_part, approximate=True) * up_part


def attend_forward(queries, key_rows, value_rows, bias_full, allowed):
    query_count = queries.shape[0]
    heads_q = queries.reshape(query_count, H, DH)
    heads_k = key_rows.reshape(key_rows.shape[0], H, DH)
    heads_v = value_rows.reshape(value_rows.shape[0], H, DH)
    scores = (
        jnp.einsum("qhd,khd->hqk", heads_q, heads_k, preferred_element_type=jnp.float32) + bias_full
    )
    scores = jnp.where(allowed[None], scores, NEGATIVE)
    shifted = jnp.exp(scores - jnp.max(scores, axis=-1, keepdims=True))
    weights = shifted / jnp.sum(shifted, axis=-1, keepdims=True)
    low_weights = to_low(weights)
    context = jnp.einsum("hqk,khd->qhd", low_weights, heads_v, preferred_element_type=jnp.float32)
    return (to_low(context.reshape(query_count, H * DH)), weights, low_weights)


def attend_backward(queries, key_rows, value_rows, weights, low_weights, grad_context):
    query_count = queries.shape[0]
    key_count = key_rows.shape[0]
    heads_q = queries.reshape(query_count, H, DH)
    heads_k = key_rows.reshape(key_count, H, DH)
    heads_v = value_rows.reshape(key_count, H, DH)
    grad_heads = grad_context.reshape(query_count, H, DH)
    grad_weights = jnp.einsum(
        "qhd,khd->hqk", grad_heads, heads_v, preferred_element_type=jnp.float32
    )
    grad_values = jnp.einsum(
        "hqk,qhd->khd", low_weights, grad_heads, preferred_element_type=jnp.float32
    )
    grad_scores = weights * (grad_weights - jnp.sum(grad_weights * weights, axis=-1, keepdims=True))
    low_scores = to_low(grad_scores)
    grad_queries = jnp.einsum(
        "hqk,khd->qhd", low_scores, heads_k, preferred_element_type=jnp.float32
    )
    grad_keys = jnp.einsum("hqk,qhd->khd", low_scores, heads_q, preferred_element_type=jnp.float32)
    return (
        grad_queries.reshape(query_count, H * DH),
        grad_keys.reshape(key_count, H * DH),
        grad_values.reshape(key_count, H * DH),
        low_scores,
    )


def self_forward(residual, gain_row, weight_in, weight_out, bias_full, allowed):
    normed = to_low(rms_norm(residual, gain_row))
    projected = to_low(matmul(normed, weight_in))
    context, weights, low_weights = attend_forward(
        projected[:, :HD], projected[:, HD : 2 * HD], projected[:, 2 * HD :], bias_full, allowed
    )
    return (
        residual + matmul(context, weight_out),
        (residual, normed, projected, context, weights, low_weights),
    )


def self_backward(kept_state, gain_row, weight_in, weight_out, bucket_hot, grad_out):
    residual, normed, projected, context, weights, low_weights = kept_state
    grad_low = to_low(grad_out)
    grad_wout = matmul(context.T, grad_low)
    grad_context = to_low(matmul(grad_low, weight_out.T))
    grad_queries, grad_keys, grad_values, low_scores = attend_backward(
        projected[:, :HD],
        projected[:, HD : 2 * HD],
        projected[:, 2 * HD :],
        weights,
        low_weights,
        grad_context,
    )
    grad_projected = to_low(jnp.concatenate([grad_queries, grad_keys, grad_values], axis=1))
    grad_win = matmul(normed.T, grad_projected)
    _, norm_pull = jax.vjp(rms_norm, residual, gain_row)
    grad_residual, grad_gain = norm_pull(matmul(grad_projected, weight_in.T))
    grad_bias = jnp.einsum(
        "hqk,qkb->bh", low_scores.astype(jnp.float32), bucket_hot, precision=HIGHEST
    )
    return (grad_out + grad_residual, grad_gain, grad_win, grad_wout, grad_bias)


def ffn_forward(residual, gain_row, weight_in, weight_out):
    normed = to_low(rms_norm(residual, gain_row))
    both_parts = matmul(normed, weight_in)
    hidden = to_low(gated(both_parts[:, :FF], both_parts[:, FF:]))
    return (residual + matmul(hidden, weight_out), (residual, normed, both_parts, hidden))


def ffn_backward(kept_state, gain_row, weight_in, weight_out, grad_out):
    residual, normed, both_parts, hidden = kept_state
    grad_low = to_low(grad_out)
    grad_wout = matmul(hidden.T, grad_low)
    _, gate_pull = jax.vjp(gated, both_parts[:, :FF], both_parts[:, FF:])
    grad_gate, grad_up = gate_pull(matmul(grad_low, weight_out.T))
    grad_both = to_low(jnp.concatenate([grad_gate, grad_up], axis=1))
    grad_win = matmul(normed.T, grad_both)
    _, norm_pull = jax.vjp(rms_norm, residual, gain_row)
    grad_residual, grad_gain = norm_pull(matmul(grad_both, weight_in.T))
    return (grad_out + grad_residual, grad_gain, grad_win, grad_wout)


def shards(
    enc_embed,
    dec_embed,
    out_cot,
    enc_lengths,
    dec_lengths,
    norm_gains,
    rel_bias,
    attn_in,
    attn_out,
    ffn_in,
    ffn_out,
    cross_in,
    cross_out,
):
    gathered = (
        lax.all_gather(attn_in[0], "wide", axis=0, tiled=True),
        lax.all_gather(ffn_in[0], "wide", axis=0, tiled=True),
        lax.all_gather(cross_in[0], "wide", axis=0, tiled=True),
        lax.all_gather(cross_out[0], "wide", axis=0, tiled=True),
        lax.all_gather(attn_out[0], "wide", axis=1, tiled=True),
        lax.all_gather(ffn_out[0], "wide", axis=1, tiled=True),
    )
    attn_w_in, ffn_w_in, cross_w_in, cross_w_out, attn_w_out, ffn_w_out = gathered
    memory_weight = jnp.concatenate([cross_w_in, cross_w_out], axis=1)
    gain_rows = norm_gains[0]
    biases = rel_bias[0]
    section_is_dec = lax.axis_index("section") == 1
    enc_hot = one_hot(LE, True)
    dec_hot = one_hot(LD, False)
    enc_bias = jnp.einsum("qkb,bh->hqk", enc_hot, biases, precision=HIGHEST)
    dec_bias = jnp.einsum("qkb,bh->hqk", dec_hot, biases, precision=HIGHEST)
    causal = jnp.arange(LD)[:, None] >= jnp.arange(LD)[None, :]
    zero_kv = jnp.zeros((LE, 2 * HD), jnp.bfloat16)
    zero_target = jnp.zeros((LD, D), jnp.bfloat16)
    zero_enc = jnp.zeros((LE, D), jnp.float32)
    zero_dec = jnp.zeros((LD, D), jnp.float32)
    zero_grads = (
        jnp.zeros((3, D), jnp.float32),
        jnp.zeros((NB, H), jnp.float32),
        jnp.zeros((D, 3 * HD), jnp.float32),
        jnp.zeros((HD, D), jnp.float32),
        jnp.zeros((D, 2 * FF), jnp.float32),
        jnp.zeros((FF, D), jnp.float32),
        jnp.zeros((D, HD), jnp.float32),
        jnp.zeros((D, HD), jnp.float32),
    )

    def encode_states(step_index):
        enc_items = item_ids(enc_lengths[step_index, 0], LE)
        allowed = enc_items[:, None] == enc_items[None, :]
        after_self, self_kept = self_forward(
            enc_embed[step_index, 0].astype(jnp.float32),
            gain_rows[0],
            attn_w_in,
            attn_w_out,
            enc_bias,
            allowed,
        )
        after_ffn, ffn_kept = ffn_forward(after_self, gain_rows[1], ffn_w_in, ffn_w_out)
        memory = to_low(rms_norm(after_ffn, gain_rows[2]))
        return (to_low(matmul(memory, memory_weight)), (self_kept, ffn_kept, after_ffn, memory))

    def encode_backward(step_index, grad_kv):
        _, (self_kept, ffn_kept, after_ffn, memory) = encode_states(step_index)
        grad_memory = matmul(memory.T, grad_kv)
        _, norm_pull = jax.vjp(rms_norm, after_ffn, gain_rows[2])
        grad_after_ffn, grad_final = norm_pull(matmul(grad_kv, memory_weight.T))
        grad_after_self, grad_ffn_gain, grad_fin, grad_fout = ffn_backward(
            ffn_kept, gain_rows[1], ffn_w_in, ffn_w_out, grad_after_ffn
        )
        grad_embed, grad_self_gain, grad_win, grad_wout, grad_bias = self_backward(
            self_kept, gain_rows[0], attn_w_in, attn_w_out, enc_hot, grad_after_self
        )
        grad_parts = (
            jnp.stack([grad_self_gain, grad_ffn_gain, grad_final]),
            grad_bias,
            grad_win,
            grad_wout,
            grad_fin,
            grad_fout,
            grad_memory[:, :HD],
            grad_memory[:, HD:],
        )
        return (grad_embed, grad_parts)

    def decode_states(step_index, memory_kv):
        dec_items = item_ids(dec_lengths[step_index, 0], LD)
        enc_items = item_ids(enc_lengths[step_index, 0], LE)
        allowed = (dec_items[:, None] == dec_items[None, :]) & causal
        after_self, self_kept = self_forward(
            dec_embed[step_index, 0].astype(jnp.float32),
            gain_rows[0],
            attn_w_in,
            attn_w_out,
            dec_bias,
            allowed,
        )
        normed = to_low(rms_norm(after_self, gain_rows[1]))
        queries = to_low(matmul(normed, cross_w_in))
        context, weights, low_weights = attend_forward(
            queries,
            memory_kv[:, :HD],
            memory_kv[:, HD:],
            0.0,
            dec_items[:, None] == enc_items[None, :],
        )
        after_cross = after_self + matmul(context, cross_w_out.T)
        after_ffn, ffn_kept = ffn_forward(after_cross, gain_rows[2], ffn_w_in, ffn_w_out)
        return (
            after_ffn,
            (self_kept, after_self, normed, queries, context, weights, low_weights, ffn_kept),
        )

    def decode_backward(step_index, memory_kv):
        _, kept_state = decode_states(step_index, memory_kv)
        self_kept, after_self, normed, queries, context, weights, low_weights, ffn_kept = kept_state
        grad_out = out_cot[step_index, 0].astype(jnp.float32)
        grad_cross, grad_ffn_gain, grad_fin, grad_fout = ffn_backward(
            ffn_kept, gain_rows[2], ffn_w_in, ffn_w_out, grad_out
        )
        grad_low = to_low(grad_cross)
        grad_cross_out = matmul(grad_low.T, context)
        grad_context = to_low(matmul(grad_low, cross_w_out))
        grad_queries, grad_keys, grad_values, _ = attend_backward(
            queries, memory_kv[:, :HD], memory_kv[:, HD:], weights, low_weights, grad_context
        )
        grad_query_low = to_low(grad_queries)
        grad_cross_in = matmul(normed.T, grad_query_low)
        _, norm_pull = jax.vjp(rms_norm, after_self, gain_rows[1])
        grad_norm_path, grad_cross_gain = norm_pull(matmul(grad_query_low, cross_w_in.T))
        grad_embed, grad_self_gain, grad_win, grad_wout, grad_bias = self_backward(
            self_kept, gain_rows[0], attn_w_in, attn_w_out, dec_hot, grad_cross + grad_norm_path
        )
        grad_kv = to_low(jnp.concatenate([grad_keys, grad_values], axis=1))
        grad_parts = (
            jnp.stack([grad_self_gain, grad_cross_gain, grad_ffn_gain]),
            grad_bias,
            grad_win,
            grad_wout,
            grad_fin,
            grad_fout,
            grad_cross_in,
            grad_cross_out,
        )
        return (grad_kv, grad_embed, grad_parts)

    def forward_pair(enc_step, dec_step, memory_kv):

        def forward_encoder_side():
            if enc_step is None:
                return (zero_kv, zero_target)
            memory_out, _ = encode_states(enc_step)
            return (memory_out, zero_target)

        def forward_decoder_side():
            if dec_step is None:
                return (zero_kv, zero_target)
            output_row, _ = decode_states(dec_step, memory_kv)
            return (zero_kv, output_row.astype(jnp.bfloat16))

        return lax.cond(section_is_dec, forward_decoder_side, forward_encoder_side)

    def backward_pair(enc_step, dec_step, memory_kv, grad_kv_in):

        def backward_encoder_side():
            if enc_step is None:
                return (zero_kv, zero_enc, zero_dec, zero_grads)
            grad_embed, grad_parts = encode_backward(enc_step, grad_kv_in)
            return (zero_kv, grad_embed, zero_dec, grad_parts)

        def backward_decoder_side():
            if dec_step is None:
                return (zero_kv, zero_enc, zero_dec, zero_grads)
            grad_kv, grad_embed, grad_parts = decode_backward(dec_step, memory_kv)
            return (grad_kv, zero_enc, grad_embed, grad_parts)

        return lax.cond(section_is_dec, backward_decoder_side, backward_encoder_side)

    def absorb(totals, grad_parts):
        if totals is None:
            return grad_parts
        return jax.tree.map(jnp.add, totals, grad_parts)

    received = []
    dec_rows = []
    sent = jnp.stack([forward_pair(step_index, None, None)[0] for step_index in range(MB)])
    memory_all = shifted_2(sent, "section", 1)
    received = [memory_all[step_index] for step_index in range(MB)]
    dec_rows = [forward_pair(None, step_index, received[step_index])[1] for step_index in range(MB)]
    totals = None
    enc_grads = []
    dec_grads = []
    sent_grads = []
    dec_parts = []
    for step_index in range(MB):
        grad_kv, _, grad_embed, grad_parts = backward_pair(
            None, step_index, received[step_index], None
        )
        sent_grads.append(grad_kv)
        dec_grads.append(grad_embed)
        dec_parts.append(grad_parts)
    memory_grads = shifted_2(jnp.stack(sent_grads), "section", -1)
    for step_index in range(MB):
        _, grad_embed, _, grad_parts = backward_pair(
            step_index, None, None, memory_grads[step_index]
        )
        enc_grads.append(grad_embed)
        pick_dec_parts = dec_parts[step_index]
        totals = absorb(
            totals,
            jax.tree.map(
                lambda first, second: jnp.where(section_is_dec, first, second),
                pick_dec_parts,
                grad_parts,
            ),
        )
    weight_shards = (
        lax.psum_scatter(
            totals[2].astype(jnp.bfloat16), "wide", scatter_dimension=0, tiled=True
        ).astype(jnp.float32),
        lax.psum_scatter(
            totals[3].astype(jnp.bfloat16), "wide", scatter_dimension=1, tiled=True
        ).astype(jnp.float32),
        lax.psum_scatter(
            totals[4].astype(jnp.bfloat16), "wide", scatter_dimension=0, tiled=True
        ).astype(jnp.float32),
        lax.psum_scatter(
            totals[5].astype(jnp.bfloat16), "wide", scatter_dimension=1, tiled=True
        ).astype(jnp.float32),
        lax.psum_scatter(
            totals[6].astype(jnp.bfloat16), "wide", scatter_dimension=0, tiled=True
        ).astype(jnp.float32),
        lax.psum_scatter(
            totals[7].astype(jnp.bfloat16), "wide", scatter_dimension=0, tiled=True
        ).astype(jnp.float32),
    )
    weight_shards = (
        lax.psum_scatter(
            weight_shards[0].astype(jnp.bfloat16), "rows", scatter_dimension=1, tiled=True
        ).astype(jnp.float32),
        lax.psum_scatter(
            weight_shards[1].astype(jnp.bfloat16), "rows", scatter_dimension=0, tiled=True
        ).astype(jnp.float32),
        lax.psum_scatter(
            weight_shards[2].astype(jnp.bfloat16), "rows", scatter_dimension=1, tiled=True
        ).astype(jnp.float32),
        lax.psum_scatter(
            weight_shards[3].astype(jnp.bfloat16), "rows", scatter_dimension=0, tiled=True
        ).astype(jnp.float32),
        lax.psum_scatter(
            weight_shards[4].astype(jnp.bfloat16), "rows", scatter_dimension=1, tiled=True
        ).astype(jnp.float32),
        lax.psum_scatter(
            weight_shards[5].astype(jnp.bfloat16), "rows", scatter_dimension=1, tiled=True
        ).astype(jnp.float32),
    )
    gain_grad, bias_grad = lax.psum((totals[0], totals[1]), ("wide", "rows"))
    half_width = D // 2
    dec_out_all = jnp.stack(dec_rows)
    dec_grad_all = jnp.stack(dec_grads)
    enc_grad_all = jnp.stack(enc_grads)
    outgoing = jnp.concatenate(
        [
            dec_out_all[:, :, :half_width].astype(jnp.float32),
            dec_grad_all[:, :, :half_width],
            enc_grad_all[:, :, half_width:],
        ],
        axis=1,
    )
    incoming = swapped(outgoing.astype(jnp.bfloat16), "section", 0).astype(outgoing.dtype)
    dec_half = jnp.where(
        section_is_dec, dec_out_all[:, :, half_width:].astype(jnp.float32), incoming[:, :LD]
    ).astype(jnp.bfloat16)
    dec_grad_half = jnp.where(
        section_is_dec, dec_grad_all[:, :, half_width:], incoming[:, LD : 2 * LD]
    )
    enc_grad_half = jnp.where(
        section_is_dec, incoming[:, 2 * LD :], enc_grad_all[:, :, :half_width]
    )
    return (
        dec_half[:, None],
        enc_grad_half[:, None],
        dec_grad_half[:, None],
        gain_grad[None],
        bias_grad[None],
        weight_shards[0][None],
        weight_shards[1][None],
        weight_shards[2][None],
        weight_shards[3][None],
        weight_shards[4][None],
        weight_shards[5][None],
    )


def solution(mesh):
    placed = (
        P(None, ("wide", "rows"), None, None),
        P(None, ("wide", "rows"), None, None),
        P(None, ("wide", "rows"), None, None),
        P(None, ("wide", "rows"), None),
        P(None, ("wide", "rows"), None),
        P("section", None, None),
        P("section", None, None),
        P("section", "wide", None),
        P("section", None, "wide"),
        P("section", "wide", None),
        P("section", None, "wide"),
        P("section", "wide", None),
        P("section", "wide", None),
    )
    return jax.shard_map(
        shards,
        mesh=mesh,
        in_specs=placed,
        out_specs=(
            P(None, ("wide", "rows"), None, "section"),
            P(None, ("wide", "rows"), None, "section"),
            P(None, ("wide", "rows"), None, "section"),
            P("section", None, None),
            P("section", None, None),
            P("section", "wide", "rows"),
            P("section", "rows", "wide"),
            P("section", "wide", "rows"),
            P("section", "rows", "wide"),
            P("section", "wide", "rows"),
            P("section", "wide", "rows"),
        ),
        check_vma=False,
    )
```

profile of v0, /device:TPU:0, one launch (start us, length us, event | category | flops | bytes accessed | tf_op | source)
XLA Modules:
  0.0 1754.5 jit_solution(2119927011094242528)
XLA Ops:
  15.7 11.6 copy.457
  30.8 9.1 all-gather.17.cloned.1.call-done
  39.9 29.2 %all-gather.23.cloned.1.call-done = bf16[1,1472,384]{2,1,0:T(8,128)(2,1)} async-done(((bf16[1,368,384]{2,1,0:T(8,128)(2,1)}), bf16[1,1472,384]{2,1,0:T(8,128)(2,1)}) %all-gather.23.cloned.1.call-update) | async-done | bytes 1130512 | tf_op jit(solution)/shard_map/all_gather | solution.py:209
  72.4 26.0 %all-gather.15.cloned.1.call-done = bf16[1,384,1472]{1,2,0:T(8,128)(2,1)} async-done(((bf16[1,384,368]{1,2,0:T(8,128)(2,1)}), bf16[1,384,1472]{1,2,0:T(8,128)(2,1)}) %all-gather.15.cloned.1.call-update) | async-done | bytes 1130512 | tf_op jit(solution)/shard_map/all_gather | solution.py:210
  98.3 47.8 %all-gather.13.cloned.1.call-done = bf16[1,1472,1152]{2,1,0:T(8,128)(2,1)} async-done(((bf16[1,368,1152]{2,1,0:T(8,128)(2,1)}), bf16[1,1472,1152]{2,1,0:T(8,128)(2,1)}) %all-gather.13.cloned.1.call-update) | async-done | bytes 3391504 | tf_op jit(solution)/shard_map/all_gather | solution.py:206
  146.1 107.3 %all-gather.21.cloned.1.call-done = bf16[1,3584,1472]{1,2,0:T(8,128)(2,1)} async-done(((bf16[1,3584,368]{1,2,0:T(8,128)(2,1)}), bf16[1,3584,1472]{1,2,0:T(8,128)(2,1)}) %all-gather.21.cloned.1.call-update) | async-done | bytes 10551312 | tf_op jit(solution)/shard_map/all_gather | solution.py:211
  253.4 196.0 %all-gather.19.cloned.1.call-done = bf16[1,1472,7168]{2,1,0:T(8,128)(2,1)} async-done(((bf16[1,368,7168]{2,1,0:T(8,128)(2,1)}), bf16[1,1472,7168]{2,1,0:T(8,128)(2,1)}) %all-gather.19.cloned.1.call-update) | async-done | bytes 21102608 | tf_op jit(solution)/shard_map/all_gather | solution.py:207
  449.4 38.3 %conditional.9 = (bf16[1,256,768]{1,2,0:T(8,128)(2,1)S(1)}) conditional(s32[]{:T(128)} %convert_element_type.545, (bf16[2,1,256,1472]{2,3,1,0:T(8,128)(2,1)S(1)}, f32[3,1472]{1,0:T(4,128)S(1)}, bf16[1472,1152]{1,0:T(8,128)(2,1)}, s32[2,1,8]{2,1,0:T(1,128)S(1)}, f32[6,256,256]{2,0,1:T(8,128)}, /*index=5*/bf16[384,1472]{0,1:T(8,128)(2,1)}, ...), branch_computations={%region_9.17_spmd, %region_17.18_spmd} | conditional | flops 9960628224 | bytes 141509056 | solution.py:351
  464.3 15.5 fusion.57
  479.8 6.7 multiply_reduce_fusion.2
  487.7 39.8 %conditional.8 = (bf16[1,256,768]{1,2,0:T(8,128)(2,1)S(1)}) conditional(s32[]{:T(128)} %convert_element_type.545, (bf16[2,1,256,1472]{2,3,1,0:T(8,128)(2,1)}, f32[3,1472]{1,0:T(4,128)S(1)}, bf16[1472,1152]{1,0:T(8,128)(2,1)}, s32[2,1,8]{2,1,0:T(1,128)S(1)}, f32[6,256,256]{2,0,1:T(8,128)}, /*index=5*/bf16[384,1472]{0,1:T(8,128)(2,1)}, ...), branch_computations={%region_0.8_spmd, %region_8.9_spmd} | conditional | flops 9960628224 | bytes 135477408 | solution.py:351
  504.2 15.5 fusion.21
  519.7 6.7 multiply_reduce_fusion
  533.7 43.0 %conditional.12 = (f32[3,1472]{1,0:T(4,128)S(1)}, f32[32,6]{0,1:T(8,128)}, f32[1472,7168]{1,0:T(8,128)}, f32[3584,1472]{0,1:T(8,128)}, f32[1,64,1472]{1,2,0:T(8,...) conditional(s32[]{:T(128)} %convert_element_type.545, () %tuple.91, ...), branch_computations={%region_44.45_spmd, %region_45.65_spmd} | conditional | flops 6856304128 | bytes 258440016 | solution.py:367
  544.8 9.8 broadcast_in_dim.284
  554.6 13.9 broadcast_in_dim.283
  577.3 44.8 %conditional.13 = (f32[3,1472]{1,0:T(4,128)S(1)}, f32[32,6]{0,1:T(8,128)}, f32[1472,7168]{1,0:T(8,128)}, f32[3584,1472]{0,1:T(8,128)}, f32[1,64,1472]{1,2,0:T(8,...) conditional(s32[]{:T(128)} %convert_element_type.545, () %tuple.93, ...), branch_computations={%region_65.66_spmd, %region_66.86_spmd} | conditional | flops 6856304128 | bytes 249570992 | solution.py:367
  588.5 9.7 broadcast_in_dim.314
  598.2 13.9 broadcast_in_dim.313
  625.2 150.2 %collective-permute-done.1 = bf16[2,256,768]{2,1,0:T(8,128)(2,1)S(1)} collective-permute-done((bf16[2,256,768]{2,1,0:T(8,128)(2,1)S(1)}, bf16[2,256,768]{2,1,0:T(8,128)(2,1)S(1)}, u32[]{:S(2)}, u32[]{:S(2)}) %collective-permute-start.1) | collective-permute-done | bytes 786464 | tf_op jit(solution)/shard_map/ppermute | solution.py:27
  775.4 130.5 %conditional.15 = (f32[3,1472]{1,0:T(4,128)S(1)}, f32[32,6]{0,1:T(8,128)S(1)}, f32[1472,7168]{1,0:T(8,128)}, f32[3584,1472]{0,1:T(8,128)}, f32[1,256,1472]{1,2,0...) conditional(s32[]{:T(128)} %convert_element_type.545, ...), branch_computations={%region_102.117_spmd, %region_117.118_spmd} | conditional | flops 29476274176 | bytes 489932608 | solution.py:367
  798.4 11.3 fusion.409
  820.8 6.7 fusion.366
  827.5 12.2 multiply_reduce_fusion.34
  849.9 7.0 convolution_bitcast_fusion.3
  872.6 5.4 fusion.398
  878.0 8.7 fusion.392
  886.7 18.8 %fusion.367 = f32[1472,7168]{1,0:T(8,128)} fusion(bf16[256,3584]{1,0:T(8,128)(2,1)} %get-tuple-element.999, bf16[256,3584]{1,0:T(8,128)(2,1)} %copy-done.99, f32[256,1472]{0,1:T(8,128)} %get-tuple-element.1008, f32[1472]{0:T(1024)S(1)} %get-tuple-element.889, f32[256]{0:T(256)S(1)} %fusion.403), kind=kOutput, calls=%fused_computation.662 | convolution fusion | flops 5410734080 | bytes 47389440 | tf_op jit(solution)/shard_map/cond/branch_0_fun/dot_general | solution.py:81
  906.5 128.6 %conditional.14 = (f32[3,1472]{1,0:T(4,128)S(1)}, f32[32,6]{0,1:T(8,128)S(1)}, f32[1472,7168]{1,0:T(8,128)}, f32[3584,1472]{0,1:T(8,128)}, f32[1,256,1472]{1,2,0...) conditional(s32[]{:T(128)} %convert_element_type.545, ...), branch_computations={%region_86.101_spmd, %region_101.102_spmd} | conditional | flops 29476274176 | bytes 498321344 | solution.py:367
  929.7 11.3 fusion.358
  952.1 6.7 fusion.315
  958.8 12.2 multiply_reduce_fusion.27
  981.2 7.0 convolution_bitcast_fusion.2
  1003.6 4.2 fusion.347
  1007.8 8.6 fusion.341
  1016.5 18.5 %fusion.316 = f32[1472,7168]{1,0:T(8,128)} fusion(bf16[256,3584]{1,0:T(8,128)(2,1)} %get-tuple-element.981, bf16[256,3584]{1,0:T(8,128)(2,1)} %copy-done.100, f32[256,1472]{0,1:T(8,128)S(1)} %copy-done.30, f32[1472]{0:T(1024)S(1)} %get-tuple-element.880, f32[256]{0:T(256)S(1)} %fusion.352), kind=kOutput, calls=%fused_computation.563 | convolution fusion | flops 5410734080 | bytes 47389440 | tf_op jit(solution)/shard_map/cond/branch_0_fun/dot_general | solution.py:81
  1035.2 4.4 add_convert_fusion.5
  1039.6 6.2 add_convert_fusion.2
  1050.1 20.4 %add_convert_fusion.1 = bf16[3584,1472]{0,1:T(8,128)(2,1)} fusion(f32[3584,1472]{0,1:T(8,128)} %get-tuple-element.387, f32[3584,1472]{0,1:T(8,128)} %get-tuple-element.388, f32[3584,1472]{0,1:T(8,128)} %get-tuple-element.385, f32[3584,1472]{0,1:T(8,128)} %get-tuple-element.386, pred[]{:T(512)S(6)} %eq.217), kind=kLoop, calls=%fused_computation.741 | loop fusion | flops 21102592 | bytes 94961664 | tf_op jit(solution)/shard_map/convert_element_type | solution.py:418
  1070.6 35.9 %add_convert_fusion = bf16[1472,7168]{1,0:T(8,128)(2,1)} fusion(f32[1472,7168]{1,0:T(8,128)} %get-tuple-element.383, f32[1472,7168]{1,0:T(8,128)} %get-tuple-element.384, f32[1472,7168]{1,0:T(8,128)} %get-tuple-element.381, f32[1472,7168]{1,0:T(8,128)} %get-tuple-element.382, pred[]{:T(512)S(6)} %eq.217), kind=kLoop, calls=%fused_computation.740 | loop fusion | flops 42205184 | bytes 189923328 | tf_op jit(solution)/shard_map/convert_element_type | solution.py:415
  1108.4 94.4 %all-reduce.9.cloned.1.call-done = (bf16[1472,1152]{0,1:T(8,128)(2,1)}, bf16[384,1472]{1,0:T(8,128)(2,1)}, bf16[1472,384]{0,1:T(8,128)(2,1)}, bf16[1472,384]{0,1:T(8,128)(2,1)}) async-done(((bf16[1472,1152]{0,1:T(8,128)(2,1)}, bf16[384,1472]{1,0:T(8,128)(2,1)}, bf16[1472,384]{0,1:T(8,128)(2,1)}, bf16[1472,384]{0,1:T(8,128)(2,1)}), (bf16[1472,1152]{0,1:T(8,128)(2,1)}, bf16[384,1472]{1,0:T(8,128)(2,1)}, ...) | async-done | bytes 6782992
  1211.2 98.7 %reduce-scatter.23.cloned.1.call-done = bf16[3584,368]{0,1:T(8,128)(2,1)} async-done(((bf16[3584,1472]{0,1:T(8,128)(2,1)}), bf16[3584,368]{0,1:T(8,128)(2,1)}) %reduce-scatter.23.cloned.1.call-update) | async-done | bytes 2637840 | tf_op jit(solution)/shard_map/reduce_scatter | solution.py:417
  1309.9 4.5 copy.550
  1314.5 187.4 %reduce-scatter.31.cloned.1.call-done = bf16[368,7168]{1,0:T(8,128)(2,1)} async-done(((bf16[1472,7168]{1,0:T(8,128)(2,1)}), bf16[368,7168]{1,0:T(8,128)(2,1)}) %reduce-scatter.31.cloned.1.call-update) | async-done | bytes 5275664
  1504.5 7.3 conditional.10
  1522.0 70.5 %collective-permute-start.2 = (bf16[2,384,736]{1,2,0:T(8,128)(2,1)S(1)}, bf16[2,384,736]{1,2,0:T(8,128)(2,1)S(1)}, u32[]{:S(2)}, u32[]{:S(2)}) collective-permute-start(bf16[2,384,736]{1,2,0:T(8,128)(2,1)S(1)} %pad_maximum_fusion.31), channel_id=1, source_target_pairs={{0,16},{16,0},{1,17},{17,1},{2,18},{18,2},{3,19},{19,3},{4,20},{20... | collective-permute-start | bytes 3391496 | tf_op jit(solution)/shard_map/ppermute | solution.py:37
  1592.6 79.1 %all-reduce.5 = (f32[1,3,1472]{2,0,1:T(1,128)}, f32[1,32,6]{1,0,2:T(1,128)}) all-reduce(f32[1,3,1472]{2,0,1:T(1,128)S(1)} %broadcast_in_dim.412, f32[1,32,6]{1,0,2:T(1,128)S(1)} %broadcast_in_dim.413), channel_id=1, replica_groups=mesh['section'=2,'wide'=4,'rows'=4] {'wide','rows'}, use_global_device_ids=true, to_apply=%region_118.119 | all-reduce | flops 4608 | bytes 36864 | tf_op jit(solution)/shard_map/psum | solution.py:447
  1687.9 56.7 %reduce-scatter.21.cloned.1.call-done = bf16[368,1792]{1,0:T(8,128)(2,1)} async-done(((bf16[368,7168]{1,0:T(8,128)(2,1)}), bf16[368,1792]{1,0:T(8,128)(2,1)}) %reduce-scatter.21.cloned.1.call-update) | async-done | bytes 1318928 | tf_op jit(solution)/shard_map/reduce_scatter | solution.py:434
  (466 shorter events, 247.3 us)
Async XLA Ops:
  7.2 32.7 %all-gather.17.cloned.1.call-start = ((), (), s32[]{:S(2)}) async-start(), calls=%async_computation.16 | async-start | bytes 1413120 | tf_op jit(solution)/shard_map/all_gather | solution.py:208
  7.9 61.2 %all-gather.23.cloned.1.call-start = ((), (), s32[]{:S(2)}) async-start(), calls=%async_computation.19 | async-start | bytes 1413120 | tf_op jit(solution)/shard_map/all_gather | solution.py:209
  8.7 89.7 %all-gather.15.cloned.1.call-start = ((), (), s32[]{:S(2)}) async-start(), calls=%async_computation.15 | async-start | bytes 1413120 | tf_op jit(solution)/shard_map/all_gather | solution.py:210
  9.4 136.7 %all-gather.13.cloned.1.call-start = ((), (), s32[]{:S(2)}) async-start(), calls=%async_computation.14 | async-start | bytes 4239360 | tf_op jit(solution)/shard_map/all_gather | solution.py:206
  10.0 243.4 %all-gather.21.cloned.1.call-start = ((), (), s32[]{:S(2)}) async-start(), calls=%async_computation.18 | async-start | bytes 13189120 | tf_op jit(solution)/shard_map/all_gather | solution.py:211
  10.6 438.9 %all-gather.19.cloned.1.call-start = ((), (), s32[]{:S(2)}) async-start(), calls=%async_computation.17 | async-start | bytes 26378240 | tf_op jit(solution)/shard_map/all_gather | solution.py:207
  11.2 1191.6 %all-reduce.9.cloned.1.call-start = ((), (), s32[]{:S(2)}) async-start(), calls=%async_computation.22 | async-start | bytes 14155776
  15.7 11.6 copy-start.170
  69.1 380.3 %copy-start.5 = (bf16[2,1,256,1472]{2,3,1,0:T(8,128)(2,1)S(1)}, bf16[2,1,256,1472]{2,3,1,0:T(8,128)(2,1)}, u32[]{:S(2)}) copy-start(bf16[2,1,256,1472]{2,3,1,0:T(8,128)(2,1)} %param.31) | copy-start | bytes 4521988
  69.1 380.3 %copy-start.189 = (s32[2,1,8]{2,1,0:T(1,128)S(1)}, s32[2,1,8]{2,1,0:T(1,128)}, u32[]{:S(2)}) copy-start(s32[2,1,8]{2,1,0:T(1,128)} %param.34) | copy-start | bytes 196
  462.5 17.3 slice-start
  464.3 15.5 slice-start.1
  464.3 15.5 slice-start.2
  502.3 17.3 slice-start.3
  504.1 15.5 slice-start.4
  504.2 15.5 slice-start.5
  527.7 5.1 collective-permute-start
  531.6 45.1 %copy-start.140 = (pred[64,64]{0,1:T(8,128)(4,1)}, pred[64,64]{0,1:T(8,128)(4,1)S(1)}, u32[]{:S(2)}) copy-start(pred[64,64]{0,1:T(8,128)(4,1)S(1)} %iota_compare_fusion.14) | copy-start | bytes 12292
  622.1 153.3 %copy-start.6 = (bf16[2,1,256,1472]{2,3,1,0:T(8,128)(2,1)S(1)}, bf16[2,1,256,1472]{2,3,1,0:T(8,128)(2,1)}, u32[]{:S(2)}) copy-start(bf16[2,1,256,1472]{2,3,1,0:T(8,128)(2,1)} %param.31) | copy-start | bytes 4521988
  622.1 153.3 %copy-start.190 = (s32[2,1,8]{2,1,0:T(1,128)S(1)}, s32[2,1,8]{2,1,0:T(1,128)}, u32[]{:S(2)}) copy-start(s32[2,1,8]{2,1,0:T(1,128)} %param.34) | copy-start | bytes 196
  623.9 151.5 %collective-permute-start.1 = (bf16[2,256,768]{2,1,0:T(8,128)(2,1)S(1)}, bf16[2,256,768]{2,1,0:T(8,128)(2,1)S(1)}, u32[]{:S(2)}, u32[]{:S(2)}) collective-permute-start(bf16[2,256,768]{2,1,0:T(8,128)(2,1)S(1)} %pad_maximum_fusion.33), channel_id=1, source_target_pairs={{16,0},{17,1},{18,2},{19,3},{20,4},{21,5},{22,6},{23,7},{24,8},{25... | collective-permute-start | bytes 2359304 | tf_op jit(solution)/shard_map/ppermute | solution.py:27
  795.6 18.3 %slice-start.12 = ((s8[10551296]{0:T(1024)(128)(4,1)}), s8[4194304]{0:T(1024)(128)(4,1)S(1)}, s32[]{:S(2)}) async-start(s8[10551296]{0:T(1024)(128)(4,1)} %bitcast.576), calls=%async_computation.35 | async-start | bytes 8388608 | tf_op jit(solution)/shard_map/cond
  798.4 15.5 slice-start.13
  798.4 15.5 slice-start.14
  820.8 18.9 %copy-start.35 = (f32[256,1472]{0,1:T(8,128)}, f32[256,1472]{0,1:T(8,128)S(1)}, u32[]{:S(2)}) copy-start(f32[256,1472]{0,1:T(8,128)S(1)} %add_add_fusion.11) | copy-start | bytes 4521988 | tf_op jit(solution)/shard_map/cond
  827.5 12.2 copy-start.99
  849.9 7.7 copy-start.3
  926.9 18.3 %slice-start.15 = ((s8[10551296]{0:T(1024)(128)(4,1)}), s8[4194304]{0:T(1024)(128)(4,1)S(1)}, s32[]{:S(2)}) async-start(s8[10551296]{0:T(1024)(128)(4,1)} %bitcast.578), calls=%async_computation.38 | async-start | bytes 8388608 | tf_op jit(solution)/shard_map/cond
  929.7 15.5 slice-start.16
  929.7 15.5 slice-start.17
  952.1 18.9 %copy-start.37 = (f32[256,1472]{0,1:T(8,128)}, f32[256,1472]{0,1:T(8,128)S(1)}, u32[]{:S(2)}) copy-start(f32[256,1472]{0,1:T(8,128)S(1)} %add_add_fusion.8) | copy-start | bytes 4521988 | tf_op jit(solution)/shard_map/cond
  958.8 12.2 copy-start.100
  1007.8 8.6 copy-start.30
  1050.1 259.9 %reduce-scatter.23.cloned.1.call-start = ((), (), s32[]{:S(2)}) async-start(), calls=%async_computation.11 | async-start | bytes 13189120 | tf_op jit(solution)/shard_map/reduce_scatter | solution.py:417
  1070.5 431.4 %reduce-scatter.31.cloned.1.call-start = ((), (), s32[]{:S(2)}) async-start(), calls=%async_computation.21 | async-start | bytes 26378240
  1106.5 572.4 %reduce-scatter.19.cloned.1.call-start = ((), (), s32[]{:S(2)}) async-start(), calls=%async_computation.9 | async-start | bytes 368640 | tf_op jit(solution)/shard_map/reduce_scatter | solution.py:431
  1204.6 475.8 %reduce-scatter.25.cloned.1.call-start = ((), (), s32[]{:S(2)}) async-start(), calls=%async_computation.12 | async-start | bytes 368640 | tf_op jit(solution)/shard_map/reduce_scatter | solution.py:440
  1206.6 475.4 %reduce-scatter.27.cloned.1.call-start = ((), (), s32[]{:S(2)}) async-start(), calls=%async_computation.13 | async-start | bytes 368640 | tf_op jit(solution)/shard_map/reduce_scatter | solution.py:443
  1208.6 475.0 %reduce-scatter.17.cloned.1.call-start = ((), (), s32[]{:S(2)}) async-start(), calls=%async_computation.8 | async-start | bytes 1105920 | tf_op jit(solution)/shard_map/reduce_scatter | solution.py:428
  1211.2 474.1 %reduce-scatter.29.cloned.1.call-start = ((), (), s32[]{:S(2)}) async-start(), calls=%async_computation.20 | async-start | bytes 3440640
  1314.5 430.1 %reduce-scatter.21.cloned.1.call-start = ((), (), s32[]{:S(2)}) async-start(), calls=%async_computation.10 | async-start | bytes 6594560 | tf_op jit(solution)/shard_map/reduce_scatter | solution.py:434
  1521.5 71.0 %copy-start.177 = (f32[32,6]{0,1:T(8,128)S(1)}, f32[32,6]{0,1:T(8,128)}, u32[]{:S(2)}) copy-start(f32[32,6]{0,1:T(8,128)} %copy-done.176) | copy-start | bytes 2308
  1521.6 70.9 %copy-start.179 = (f32[32,6]{0,1:T(8,128)S(1)}, f32[32,6]{0,1:T(8,128)}, u32[]{:S(2)}) copy-start(f32[32,6]{0,1:T(8,128)} %copy-done.178) | copy-start | bytes 2308
  1521.6 71.0 %copy-start.154 = (f32[3,1472]{1,0:T(4,128)S(1)}, f32[3,1472]{1,0:T(4,128)}, u32[]{:S(2)}) copy-start(f32[3,1472]{1,0:T(4,128)} %copy-done.153) | copy-start | bytes 52996
  1521.6 71.0 %copy-start.157 = (f32[3,1472]{1,0:T(4,128)S(1)}, f32[3,1472]{1,0:T(4,128)}, u32[]{:S(2)}) copy-start(f32[3,1472]{1,0:T(4,128)} %copy-done.156) | copy-start | bytes 52996
  1521.6 71.0 %copy-start.159 = (f32[3,1472]{1,0:T(4,128)S(1)}, f32[3,1472]{1,0:T(4,128)}, u32[]{:S(2)}) copy-start(f32[3,1472]{1,0:T(4,128)} %copy-done.158) | copy-start | bytes 52996
  1521.6 71.0 %copy-start.161 = (f32[3,1472]{1,0:T(4,128)S(1)}, f32[3,1472]{1,0:T(4,128)}, u32[]{:S(2)}) copy-start(f32[3,1472]{1,0:T(4,128)} %copy-done.160) | copy-start | bytes 52996
  1522.0 149.7 %collective-permute-start.2 = (bf16[2,384,736]{1,2,0:T(8,128)(2,1)S(1)}, bf16[2,384,736]{1,2,0:T(8,128)(2,1)S(1)}, u32[]{:S(2)}, u32[]{:S(2)}) collective-permute-start(bf16[2,384,736]{1,2,0:T(8,128)(2,1)S(1)} %pad_maximum_fusion.31), channel_id=1, source_target_pairs={{0,16},{16,0},{1,17},{17,1},{2,18},{18,2},{3,19},{19,3},{4,20},{20... | collective-permute-start | bytes 3391496 | tf_op jit(solution)/shard_map/ppermute | solution.py:37
  (82 other events, 241.9 us)
Sparse Core Ops, SparseCore 0:
  9.9 30.0 all-gather.16
  41.8 27.3 all-gather.22
  71.0 27.3 all-gather.14
  100.0 46.0 all-gather.12
  147.8 105.5 all-gather.20
  255.1 194.2 all-gather.18
  1050.2 152.4 all-reduce.8
  1205.8 104.0 reduce-scatter.22
  1313.1 188.8 reduce-scatter.30
  1504.2 19.8 reduce-scatter.18
  1526.5 18.1 reduce-scatter.24
  1546.9 18.1 reduce-scatter.26
  1568.0 22.8 reduce-scatter.16
  1593.2 54.6 reduce-scatter.28
  1650.1 94.3 reduce-scatter.20
where the time goes:
time: 1760 us; the launch traced here: 1750 us
  waiting for transfers between devices  1010 us (57%)
  matrix products  261 us (15%)
  local copies, waits for them, and re-layouts  179 us (10%)
  other arithmetic  112 us (6%)
  blocking collectives  79.1 us (4%)
  starting transfers between devices  73.9 us (4%)
  loops' own time  27.2 us (2%)
    unnamed x18, waiting for transfers between devices  286 us
    dot_general x34, matrix products, matmul(): return jnp.dot(left_side, right_side, preferred_element_type=jnp.float32)  199 us
    all_gather x1, waiting for transfers between devices, shards(): lax.all_gather(ffn_in[0], 'wide', axis=0, tiled=True)  196 us
    ppermute x2, waiting for transfers between devices, shifted_2(): return lax.ppermute(value, axis, pairs)  150 us
    all_gather x1, waiting for transfers between devices, shards(): lax.all_gather(ffn_out[0], 'wide', axis=1, tiled=True)  107 us
    reduce_scatter x1, waiting for transfers between devices, shards(): lax.psum_scatter(totals[5].astype(jnp.bfloat16), 'wide', scatter_dimensio...  98.7 us
    psum x1, blocking collectives, shards(): gain_grad, bias_grad = lax.psum((totals[0], totals[1]), ('wide', 'rows'))  79.1 us
    ppermute x1, starting transfers between devices, swapped(): return lax.ppermute(block, axis, route)  70.5 us
  transfers between devices with their start and end apart: 18, of which 11 were waited for; matrix products, arithmetic and copies ran while one was open for 7% of the time, Pallas kernels for 0%

commit v1 on v0

v1 whole, which is shorter than its diff:
```python
import jax
import jax.numpy as jnp
import numpy as np
from jax import lax
from jax.sharding import PartitionSpec as P

D = 1472
H = 6
DH = 64
FF = 3584
NB = 32
MAXDIST = 128
MB = 2
LE = 256
LD = 64
HD = 384


EPSILON = 1e-06
NEGATIVE = -1000000000.0
HIGHEST = lax.Precision.HIGHEST


def bucket_table(length, both_ways):
    positions = np.arange(length)
    offsets = positions[None, :] - positions[:, None]
    buckets = NB
    result = np.zeros(offsets.shape, np.int64)
    if both_ways:
        buckets = buckets // 2
        result = result + (offsets > 0) * buckets
        distance = np.abs(offsets)
    else:
        distance = np.maximum(-offsets, 0)
    exact_count = buckets // 2
    log_ratio = np.log(np.maximum(distance, 1) / exact_count) / np.log(MAXDIST / exact_count)
    far_bucket = np.minimum(
        exact_count + np.floor(log_ratio * (buckets - exact_count)).astype(np.int64), buckets - 1
    )
    return result + np.where(distance < exact_count, distance, far_bucket)


def one_hot(length, both_ways):
    bucket_ids = jnp.asarray(bucket_table(length, both_ways), jnp.int32)
    return (bucket_ids[:, :, None] == jnp.arange(NB, dtype=jnp.int32)[None, None, :]).astype(
        jnp.float32
    )


def item_ids(lengths, length):
    item_ends = jnp.cumsum(lengths)
    positions = jnp.arange(length, dtype=jnp.int32)
    return jnp.sum((positions[:, None] >= item_ends[None, :-1]).astype(jnp.int32), axis=1)


def rms_norm(residual, gain_row):
    return (
        residual
        * lax.rsqrt(jnp.mean(residual * residual, axis=-1, keepdims=True) + EPSILON)
        * gain_row
    )


def matmul(left_side, right_side):
    return jnp.dot(left_side, right_side, preferred_element_type=jnp.float32)


def to_low(tensor):
    return tensor.astype(jnp.bfloat16)


def gated(gate_part, up_part):
    return jax.nn.gelu(gate_part, approximate=True) * up_part


def attend_forward(queries, key_rows, value_rows, bias_full, allowed):
    query_count = queries.shape[0]
    heads_q = queries.reshape(query_count, H, DH)
    heads_k = key_rows.reshape(key_rows.shape[0], H, DH)
    heads_v = value_rows.reshape(value_rows.shape[0], H, DH)
    scores = (
        jnp.einsum("qhd,khd->hqk", heads_q, heads_k, preferred_element_type=jnp.float32) + bias_full
    )
    scores = jnp.where(allowed[None], scores, NEGATIVE)
    shifted = jnp.exp(scores - jnp.max(scores, axis=-1, keepdims=True))
    weights = shifted / jnp.sum(shifted, axis=-1, keepdims=True)
    low_weights = to_low(weights)
    context = jnp.einsum("hqk,khd->qhd", low_weights, heads_v, preferred_element_type=jnp.float32)
    return (to_low(context.reshape(query_count, H * DH)), weights, low_weights)


def attend_backward(queries, key_rows, value_rows, weights, low_weights, grad_context):
    query_count = queries.shape[0]
    key_count = key_rows.shape[0]
    heads_q = queries.reshape(query_count, H, DH)
    heads_k = key_rows.reshape(key_count, H, DH)
    heads_v = value_rows.reshape(key_count, H, DH)
    grad_heads = grad_context.reshape(query_count, H, DH)
    grad_weights = jnp.einsum(
        "qhd,khd->hqk", grad_heads, heads_v, preferred_element_type=jnp.float32
    )
    grad_values = jnp.einsum(
        "hqk,qhd->khd", low_weights, grad_heads, preferred_element_type=jnp.float32
    )
    grad_scores = weights * (grad_weights - jnp.sum(grad_weights * weights, axis=-1, keepdims=True))
    low_scores = to_low(grad_scores)
    grad_queries = jnp.einsum(
        "hqk,khd->qhd", low_scores, heads_k, preferred_element_type=jnp.float32
    )
    grad_keys = jnp.einsum("hqk,qhd->khd", low_scores, heads_q, preferred_element_type=jnp.float32)
    return (
        grad_queries.reshape(query_count, H * DH),
        grad_keys.reshape(key_count, H * DH),
        grad_values.reshape(key_count, H * DH),
        low_scores,
    )


def xor_permute(value, axis, distance):
    count = lax.axis_size(axis)
    return lax.ppermute(value, axis, [(i, i ^ distance) for i in range(count)])


def gather_wide(block):
    count = lax.axis_size("wide")
    if count != 4:
        return [block] + [xor_permute(block, "wide", v) for v in range(1, count)]
    half = block.shape[0] // 2
    first = xor_permute(block, "wide", 1)
    second = xor_permute(block, "wide", 2)
    third = jnp.concatenate(
        [xor_permute(first[:half], "wide", 2), xor_permute(second[half:], "wide", 1)], axis=0
    )
    return [block, first, second, third]


def scatter_wide(parts):
    count = lax.axis_size("wide")
    total = parts[0]
    if count != 4:
        for v in range(1, count):
            total = total + xor_permute(to_low(parts[v]), "wide", v).astype(jnp.float32)
        return total
    half = total.shape[0] // 2
    via_first = xor_permute(to_low(parts[3][:half]), "wide", 1).astype(jnp.float32)
    via_second = xor_permute(to_low(parts[3][half:]), "wide", 2).astype(jnp.float32)
    to_first = jnp.concatenate([parts[1][:half], parts[1][half:] + via_second], axis=0)
    to_second = jnp.concatenate([parts[2][:half] + via_first, parts[2][half:]], axis=0)
    total = total + xor_permute(to_low(to_first), "wide", 1).astype(jnp.float32)
    return total + xor_permute(to_low(to_second), "wide", 2).astype(jnp.float32)


def placed_rows(pieces, place):
    rows = pieces[0].shape[0]
    buffer = jnp.zeros((rows * len(pieces),) + pieces[0].shape[1:], pieces[0].dtype)
    for v, piece in enumerate(pieces):
        start = (place ^ v) * rows
        buffer = lax.dynamic_update_slice(buffer, piece, (start,) + (0,) * (piece.ndim - 1))
    return buffer


def both_sections(own, section):
    other = xor_permute(own, "section", 1)
    is_dec = section == 1
    return jnp.where(is_dec, other, own), jnp.where(is_dec, own, other)


def norm_backward(residual, gain_row, grad_normed):
    _, norm_pull = jax.vjp(rms_norm, residual, gain_row)
    return norm_pull(grad_normed)


def self_forward(residual, gain_row, weight, bias_full, allowed):
    normed = to_low(rms_norm(residual, gain_row))
    projected = to_low(matmul(normed, weight[:, : 3 * HD]))
    context, weights, low_weights = attend_forward(
        projected[:, :HD], projected[:, HD : 2 * HD], projected[:, 2 * HD :], bias_full, allowed
    )
    return (
        residual + matmul(context, weight[:, 3 * HD : 4 * HD].T),
        (residual, normed, projected, context, weights, low_weights),
    )


def self_backward(kept, gain_row, weight, hot, grad_out):
    residual, normed, projected, context, weights, low_weights = kept
    grad_low = to_low(grad_out)
    grad_wout = matmul(grad_low.T, context)
    grad_context = to_low(matmul(grad_low, weight[:, 3 * HD : 4 * HD]))
    grad_queries, grad_keys, grad_values, low_scores = attend_backward(
        projected[:, :HD],
        projected[:, HD : 2 * HD],
        projected[:, 2 * HD :],
        weights,
        low_weights,
        grad_context,
    )
    grad_projected = to_low(jnp.concatenate([grad_queries, grad_keys, grad_values], axis=1))
    grad_win = matmul(normed.T, grad_projected)
    grad_residual, grad_gain = norm_backward(
        residual, gain_row, matmul(grad_projected, weight[:, : 3 * HD].T)
    )
    grad_bias = jnp.einsum(
        "hqk,qkb->bh", low_scores, hot.astype(jnp.bfloat16), preferred_element_type=jnp.float32
    )
    return grad_out + grad_residual, grad_gain, grad_win, grad_wout, grad_bias


def hidden_columns(weight):
    width = weight.shape[1] * 2 // 3
    return weight[:, :width], weight[:, width:]


def ffn_hidden(blocks, weight):
    w_in, _ = hidden_columns(weight)
    both = [matmul(block, w_in) for block in blocks]
    units = w_in.shape[1] // 2
    return both, [to_low(gated(part[:, :units], part[:, units:])) for part in both]


def ffn_forward(residual, gain_row, weight):
    blocks = gather_wide(to_low(rms_norm(residual, gain_row)))
    both, hidden = ffn_hidden(blocks, weight)
    _, w_out = hidden_columns(weight)
    out = residual + scatter_wide([matmul(part, w_out.T) for part in hidden])
    return out, (residual, blocks, both, hidden)


def ffn_backward(kept, gain_row, weight, grad_out, grad_blocks):
    residual, blocks, both, hidden = kept
    w_in, w_out = hidden_columns(weight)
    units = w_out.shape[1]
    parts, grad_both = [], []
    for block, pre in zip(grad_blocks, both):
        _, pull = jax.vjp(gated, pre[:, :units], pre[:, units:])
        grad_gate, grad_up = pull(matmul(block, w_out))
        low = to_low(jnp.concatenate([grad_gate, grad_up], axis=1))
        grad_both.append(low)
        parts.append(matmul(low, w_in.T))
    grad_residual, grad_gain = norm_backward(residual, gain_row, scatter_wide(parts))
    joined = jnp.concatenate(grad_both, axis=0)
    grad_in = matmul(jnp.concatenate(blocks, axis=0).T, joined)
    grad_wout = matmul(jnp.concatenate(grad_blocks, axis=0).T, jnp.concatenate(hidden, axis=0))
    return grad_out + grad_residual, grad_gain, (grad_in, grad_wout)


def core_halves(grad, core, wide):
    depth, columns = grad.shape
    split = to_low(grad).reshape(wide, 2, depth // wide // 2, columns)
    mine = lax.dynamic_index_in_dim(split, core, 1, keepdims=False)
    sent = lax.dynamic_index_in_dim(split, 1 - core, 1, keepdims=False)
    return mine.astype(jnp.float32) + xor_permute(sent, "section", 1).astype(jnp.float32)


def reduce_ffn(grads, core, wide, rows):
    grad_in, grad_wout = grads
    depth = grad_in.shape[0]
    both = jnp.concatenate(
        [grad_in.reshape(depth, rows, -1), grad_wout.reshape(depth, rows, -1)], axis=2
    )
    columns = both.shape[2]
    halves = core_halves(both.reshape(depth, rows * columns), core, wide)
    halves = to_low(halves).reshape(wide * (depth // wide // 2), rows, columns).transpose(1, 0, 2)
    summed = lax.psum_scatter(halves, "rows", scatter_dimension=0, tiled=True)[0]
    blocks = summed.reshape(wide, depth // wide // 2, columns)
    place = lax.axis_index("wide")
    out = [lax.dynamic_index_in_dim(blocks, place, 0, keepdims=False)]
    for v in range(1, wide):
        block = lax.dynamic_index_in_dim(blocks, place ^ v, 0, keepdims=False)
        out.append(xor_permute(block, "wide", v))
    return placed_rows([piece[None] for piece in out], place)


def reduce_attn(grad, core, wide, rows):
    depth, columns = grad.shape
    halves = core_halves(grad, core, wide)
    place = lax.axis_index("wide")
    parts = [
        lax.dynamic_index_in_dim(halves, place ^ v, 0, keepdims=False) for v in range(wide)
    ]
    mine = to_low(scatter_wide(parts))
    pieces, start = [], 0
    for width in (3 * HD, HD, HD, HD):
        pieces.append(mine[:, start : start + width].reshape(mine.shape[0], rows, width // rows))
        start += width
    stacked = jnp.concatenate(pieces, axis=2).transpose(1, 0, 2)
    return lax.psum_scatter(stacked, "rows", scatter_dimension=0, tiled=True)[0]


def to_section(enc_half, dec_half, core):
    is_dec = core == 1
    own = jnp.where(is_dec, dec_half, enc_half)
    got = xor_permute(jnp.where(is_dec, enc_half, dec_half), "section", 1)
    low, high = jnp.where(is_dec, got, own), jnp.where(is_dec, own, got)
    return jnp.concatenate([low, high], axis=-2).astype(jnp.float32)


def shards(
    enc_embed,
    dec_embed,
    out_cot,
    enc_lengths,
    dec_lengths,
    norm_gains,
    rel_bias,
    attn_in,
    attn_out,
    ffn_in,
    ffn_out,
    cross_in,
    cross_out,
):
    core = lax.axis_index("section")
    place = lax.axis_index("wide")
    wide, rows = lax.axis_size("wide"), lax.axis_size("rows")
    depth = attn_in.shape[1]
    unit = FF // (wide * rows)

    small = jnp.concatenate([norm_gains[0].reshape(-1), rel_bias[0].reshape(-1)])
    enc_small, dec_small = both_sections(small, core)
    gains = [each[: 3 * D].reshape(3, D) for each in (enc_small, dec_small)]
    biases = [each[3 * D :].reshape(NB, H) for each in (enc_small, dec_small)]

    attn_shard = jnp.concatenate([attn_in[0], attn_out[0].T, cross_in[0], cross_out[0]], axis=1)
    attn_own = placed_rows(gather_wide(attn_shard), place)
    ffn_blocks = jnp.concatenate(
        [
            ffn_in[0].reshape(depth, 2 * rows, wide, unit).transpose(2, 0, 1, 3).reshape(wide, depth, -1),
            ffn_out[0].T.reshape(depth, rows, wide, unit).transpose(2, 0, 1, 3).reshape(wide, depth, -1),
        ],
        axis=2,
    )
    ffn_got = [lax.dynamic_index_in_dim(ffn_blocks, place, 0, keepdims=False)]
    for v in range(1, wide):
        block = lax.dynamic_index_in_dim(ffn_blocks, place ^ v, 0, keepdims=False)
        ffn_got.append(xor_permute(block, "wide", v))
    ffn_own = placed_rows(ffn_got, place)
    attn_enc, attn_dec = both_sections(attn_own, core)
    ffn_enc, ffn_dec = both_sections(ffn_own, core)
    memory_weight = attn_enc[:, 4 * HD :]
    cross_w_in, cross_w_out = attn_dec[:, 4 * HD : 5 * HD], attn_dec[:, 5 * HD :]

    def own_row(array):
        return lax.dynamic_index_in_dim(array[:, 0], core, 0, keepdims=False)

    enc_row = own_row(enc_embed).astype(jnp.float32)
    dec_row = own_row(dec_embed).astype(jnp.float32)
    cot_row = own_row(out_cot)
    enc_items = item_ids(own_row(enc_lengths), LE)
    dec_items = item_ids(own_row(dec_lengths), LD)
    enc_hot, dec_hot = one_hot(LE, True), one_hot(LD, False)
    enc_bias = jnp.einsum("qkb,bh->hqk", enc_hot, biases[0], precision=HIGHEST)
    dec_bias = jnp.einsum("qkb,bh->hqk", dec_hot, biases[1], precision=HIGHEST)
    causal = jnp.arange(LD)[:, None] >= jnp.arange(LD)[None, :]

    cot_blocks = gather_wide(cot_row)
    x1, enc_self = self_forward(
        enc_row, gains[0][0], attn_enc, enc_bias, enc_items[:, None] == enc_items[None, :]
    )
    y1, dec_self = self_forward(
        dec_row,
        gains[1][0],
        attn_dec,
        dec_bias,
        (dec_items[:, None] == dec_items[None, :]) & causal,
    )
    x2, enc_ffn = ffn_forward(x1, gains[0][1], ffn_enc)
    memory = to_low(rms_norm(x2, gains[0][2]))
    memory_kv = to_low(matmul(memory, memory_weight))
    cross_normed = to_low(rms_norm(y1, gains[1][1]))
    queries = to_low(matmul(cross_normed, cross_w_in))
    context, weights, low_weights = attend_forward(
        queries,
        memory_kv[:, :HD],
        memory_kv[:, HD:],
        0.0,
        dec_items[:, None] == enc_items[None, :],
    )
    y2 = y1 + matmul(context, cross_w_out.T)
    y3, dec_ffn = ffn_forward(y2, gains[1][2], ffn_dec)

    g2, dec_ffn_gain, dec_ffn_grads = ffn_backward(
        dec_ffn, gains[1][2], ffn_dec, cot_row.astype(jnp.float32), cot_blocks
    )
    dec_ffn_share = reduce_ffn(dec_ffn_grads, core, wide, rows)
    g2_low = to_low(g2)
    grad_cross_out = matmul(g2_low.T, context)
    grad_context = to_low(matmul(g2_low, cross_w_out))
    grad_queries, grad_keys, grad_values, _ = attend_backward(
        queries, memory_kv[:, :HD], memory_kv[:, HD:], weights, low_weights, grad_context
    )
    grad_query_low = to_low(grad_queries)
    grad_kv = to_low(jnp.concatenate([grad_keys, grad_values], axis=1))
    grad_x2, enc_final_gain = norm_backward(x2, gains[0][2], matmul(grad_kv, memory_weight.T))
    grad_x1, enc_ffn_gain, enc_ffn_grads = ffn_backward(
        enc_ffn, gains[0][1], ffn_enc, grad_x2, gather_wide(to_low(grad_x2))
    )
    enc_ffn_share = reduce_ffn(enc_ffn_grads, core, wide, rows)

    grad_cross_in = matmul(cross_normed.T, grad_query_low)
    grad_memory = matmul(memory.T, grad_kv)
    from_cross, dec_cross_gain = norm_backward(
        y1, gains[1][1], matmul(grad_query_low, cross_w_in.T)
    )
    grad_y, dec_self_gain, dec_win, dec_wout, dec_bias_grad = self_backward(
        dec_self, gains[1][0], attn_dec, dec_hot, g2 + from_cross
    )
    dec_attn_share = reduce_attn(
        jnp.concatenate([dec_win, dec_wout, grad_cross_in, grad_cross_out], axis=1),
        core,
        wide,
        rows,
    )
    grad_x, enc_self_gain, enc_win, enc_wout, enc_bias_grad = self_backward(
        enc_self, gains[0][0], attn_enc, enc_hot, grad_x1
    )
    enc_attn_share = reduce_attn(
        jnp.concatenate([enc_win, enc_wout, grad_memory], axis=1), core, wide, rows
    )

    small_grads = jnp.stack(
        [
            jnp.concatenate(
                [enc_self_gain, enc_ffn_gain, enc_final_gain, enc_bias_grad.reshape(-1)]
            ),
            jnp.concatenate(
                [dec_self_gain, dec_cross_gain, dec_ffn_gain, dec_bias_grad.reshape(-1)]
            ),
        ]
    )
    small_total = lax.psum(small_grads, ("section", "wide", "rows"))
    small_own = jnp.where(core == 1, small_total[1], small_total[0])

    attn_share = to_section(enc_attn_share, dec_attn_share, core)
    ffn_share = to_section(enc_ffn_share, dec_ffn_share, core)
    in_width = 2 * FF // rows // wide
    ffn_in_grad = (
        ffn_share[:, :, :in_width]
        .reshape(wide, depth, 2, unit)
        .transpose(1, 2, 0, 3)
        .reshape(depth, 2 * FF // rows)
    )
    ffn_out_grad = ffn_share[:, :, in_width:].transpose(0, 2, 1).reshape(FF // rows, depth)
    widths = [3 * HD // rows, HD // rows, HD // rows]
    edges = np.cumsum([0] + widths + [HD // rows])
    win, wout, cin, cout = [attn_share[:, a:b] for a, b in zip(edges[:-1], edges[1:])]

    half = D // 2

    def by_half(own):
        halves = jnp.stack([own[:, :half], own[:, half:]])
        keep = lax.dynamic_index_in_dim(halves, core, 0, keepdims=False)
        send = lax.dynamic_index_in_dim(halves, 1 - core, 0, keepdims=False)
        got = xor_permute(send, "section", 1)
        is_dec = core == 1
        return jnp.stack([jnp.where(is_dec, got, keep), jnp.where(is_dec, keep, got)])[:, None]

    return (
        by_half(to_low(y3)),
        by_half(grad_x),
        by_half(grad_y),
        small_own[: 3 * D].reshape(1, 3, D),
        small_own[3 * D :].reshape(1, NB, H),
        win[None],
        wout.T[None],
        ffn_in_grad[None],
        ffn_out_grad[None],
        cin[None],
        cout[None],
    )


def solution(mesh):
    placed = (
        P(None, ("wide", "rows"), None, None),
        P(None, ("wide", "rows"), None, None),
        P(None, ("wide", "rows"), None, None),
        P(None, ("wide", "rows"), None),
        P(None, ("wide", "rows"), None),
        P("section", None, None),
        P("section", None, None),
        P("section", "wide", None),
        P("section", None, "wide"),
        P("section", "wide", None),
        P("section", None, "wide"),
        P("section", "wide", None),
        P("section", "wide", None),
    )
    return jax.shard_map(
        shards,
        mesh=mesh,
        in_specs=placed,
        out_specs=(
            P(None, ("wide", "rows"), None, "section"),
            P(None, ("wide", "rows"), None, "section"),
            P(None, ("wide", "rows"), None, "section"),
            P("section", None, None),
            P("section", None, None),
            P("section", "wide", "rows"),
            P("section", "rows", "wide"),
            P("section", "wide", "rows"),
            P("section", "rows", "wide"),
            P("section", "wide", "rows"),
            P("section", "wide", "rows"),
        ),
        check_vma=False,
    )
```

time: 1760 us -> 901 us (0.51)
  waiting for transfers between devices: 1010 us -> 180 us
  local copies, waits for them, and re-layouts: 179 us -> 300 us
  matrix products: 261 us -> 166 us
  blocking collectives: 79.1 us -> 42.8 us
  loops' own time: 27.2 us -> 0 us
    all_gather x6 -> x0, waiting for transfers between devices: 415 us -> none  [the longest x1 196 us: shards(): lax.all_gather(ffn_in[0], 'wide', axis=0, tiled=True)]
    unnamed x18 -> x4, waiting for transfers between devices: 286 us -> 0.07 us
    reduce_scatter x6 -> x4, waiting for transfers between devices: 155 us -> 26.8 us  [the longest x2 26.8 us: reduce_ffn(): lax.psum_scatter(halves, 'rows', scatter_dimension=0, tiled=True)[0]]
    convert_element_type x8 -> x2, other arithmetic: 75.6 us -> 0.83 us  [to_section(): return jnp.concatenate([low, high], axis=-2).astype(jnp.float32)]
    dot_general x34 -> x57, matrix products: 199 us -> 137 us  [matmul(): return jnp.dot(left_side, right_side, preferred_element_type=jnp.float32)]
    broadcast_in_dim x14 -> x9, local copies, waits for them, and re-layouts: 59.3 us -> 13.3 us  [the longest x2 6.97 us: placed_rows(): jnp.zeros((rows * len(pieces),) + pieces[0].shape[1:], pieces[0].dtype)]
    psum x1, blocking collectives: 79.1 us -> 42.8 us  [shards(): small_total = lax.psum(small_grads, ('section', 'wide', 'rows'))]
    concatenate x2 -> x19, other arithmetic: 3.63 us -> 38.3 us  [the longest x2 14.5 us: reduce_ffn(): jnp.concatenate([grad_in.reshape(depth, rows, -1), grad_wout.reshape(dept...]
  transfers between devices with their start and end apart: 18 -> 69, of which waited for: 11 -> 27; matrix products, arithmetic and copies ran while one was open for 7% -> 60% of each run, Pallas kernels for 0% -> 0%
where the time goes in v1:
time: 901 us; the launch traced here: 888 us
  local copies, waits for them, and re-layouts  300 us (33%)
  waiting for transfers between devices  180 us (20%)
  matrix products  166 us (18%)
  other arithmetic  121 us (13%)
  starting transfers between devices  61.3 us (7%)
  blocking collectives  42.8 us (5%)
  between operations  17.2 us (2%)
    ppermute x65, waiting for transfers between devices, xor_permute(): return lax.ppermute(value, axis, [(i, i ^ distance) for i in range(count)])  153 us
    dot_general x57, matrix products, matmul(): return jnp.dot(left_side, right_side, preferred_element_type=jnp.float32)  137 us
    ppermute x65, starting transfers between devices, xor_permute(): return lax.ppermute(value, axis, [(i, i ^ distance) for i in range(count)])  61.2 us
    psum x1, blocking collectives, shards(): small_total = lax.psum(small_grads, ('section', 'wide', 'rows'))  42.8 us
    unnamed x399, local copies, waits for them, and re-layouts  42.6 us
    convert_element_type x5, local copies, waits for them, and re-layouts, to_low(): return tensor.astype(jnp.bfloat16)  33.9 us
    concatenate x2, local copies, waits for them, and re-layouts, reduce_ffn(): jnp.concatenate([grad_in.reshape(depth, rows, -1), grad_wout.reshape(dept...  29.9 us
    another operation x8, local copies, waits for them, and re-layouts  27 us
  transfers between devices with their start and end apart: 69, of which 27 were waited for; matrix products, arithmetic and copies ran while one was open for 60% of the time, Pallas kernels for 0%

profile of v1, /device:TPU:0, one launch (start us, length us, event | category | flops | bytes accessed | tf_op | source)
XLA Modules:
  0.0 888.1 jit_solution(14299145407191767688)
XLA Ops:
  17.5 8.1 copy.363
  25.5 5.7 copy.364
  36.4 7.0 fusion.42
  43.3 4.1 copy.368
  48.0 4.2 copy.369
  52.6 4.1 copy.370
  68.3 46.5 %collective-permute-done.4 = bf16[184,2304]{1,0:T(8,128)(2,1)S(1)} collective-permute-done((bf16[184,2304]{1,0:T(8,128)(2,1)S(1)}, bf16[184,2304]{1,0:T(8,128)(2,1)S(1)}, u32[]{:S(2)}, u32[]{:S(2)}) %collective-permute-start.4) | collective-permute-done | bytes 847904 | tf_op jit(solution)/shard_map/ppermute | solution.py:121
  131.6 12.8 %copy.360 = pred[256,256,32]{1,2,0:T(32,128)(4,1)} copy(pred[256,256,32]{0,2,1:T(32,128)(4,1)S(1)} %iota_compare_fusion) | data formatting | bytes 4194304 | tf_op jit(solution)/shard_map/eq | solution.py:45
  154.6 9.2 %collective-permute-done.29 = bf16[64,1472]{1,0:T(8,128)(2,1)S(1)} collective-permute-done((bf16[64,1472]{1,0:T(8,128)(2,1)S(1)}, bf16[64,1472]{1,0:T(8,128)(2,1)S(1)}, u32[]{:S(2)}, u32[]{:S(2)}) %collective-permute-start.29) | collective-permute-done | bytes 188448 | tf_op jit(solution)/shard_map/ppermute | solution.py:121
  165.9 4.8 collective-permute-done.27
  184.4 8.6 broadcast_select_fusion.2
  220.6 9.2 %broadcast_select_fusion = (bf16[1472,2688]{1,0:T(8,128)(2,1)}, bf16[1472,2688]{1,0:T(8,128)(2,1)S(1)}) fusion(bf16[1472,2688]{1,0:T(8,128)(2,1)} %constant_dynamic-update-slice_fusion.28, bf16[1472,2688]{1,0:T(8,128)(2,1)} %collective-permute-done.9, pred[]{:T(512)S(6)} %eq.88), kind=kLoop, calls=%fused_computation.19 | loop fusion | flops 7913472 | bytes 31653888 | tf_op jit(solution)/shard_map/jit(_where)/select_n | solution.py:165
  251.4 6.7 collective-permute-done.16
  267.3 8.8 collective-permute-done.17
  320.7 4.6 copy.425
  328.3 5.3 convolution_convert_fusion
  333.6 8.2 copy.424
  341.9 7.3 pad_maximum_fusion.1
  349.1 15.0 %copy.426 = bf16[1472,4,672]{2,1,0:T(4,128)(2,1)} copy(bf16[1472,4,672]{0,2,1:T(8,128)(2,1)} %pad_maximum_fusion.1) | data formatting | bytes 15826944 | tf_op jit(solution)/shard_map/concatenate | solution.py:258
  364.1 16.1 %convert_element_type.457 = bf16[4,2,184,2688]{3,2,1,0:T(8,128)(2,1)} reshape(bf16[1472,4,672]{2,1,0:T(4,128)(2,1)} %copy.426) | data formatting | bytes 15826944 | tf_op jit(solution)/shard_map/convert_element_type | solution.py:69
  386.4 4.3 dynamic-slice_bitcast_fusion
  391.6 4.8 multiply_reduce_fusion.7
  425.9 4.5 fusion.238
  444.2 4.7 pad_maximum_fusion.3
  482.5 18.9 %convolution_convert_fusion.1 = bf16[1472,1792]{1,0:T(8,128)(2,1)} fusion(bf16[1024,1472]{0,1:T(8,128)(2,1)S(1)} %copy-done.101, bf16[256,896]{1,0:T(8,128)(2,1)S(1)} %get-tuple-element.104, bf16[256,896]{1,0:T(8,128)(2,1)S(1)} %get-tuple-element.103, bf16[256,896]{1,0:T(8,128)(2,1)S(1)} %get-tuple-element.106, ...), kind=kOutput, calls=%fused_computation.22 | convolution fusion | flops 5434261504 | bytes 11960320 | tf_op jit(solution)/shard_map/dot_general | solution.py:65
  505.5 4.5 convolution_convert_fusion.5
  510.1 4.6 copy.416
  514.7 8.3 copy.415
  523.0 7.3 pad_maximum_fusion
  530.2 15.0 %copy.417 = bf16[1472,4,672]{2,1,0:T(4,128)(2,1)} copy(bf16[1472,4,672]{0,2,1:T(8,128)(2,1)} %pad_maximum_fusion) | data formatting | bytes 15826944 | tf_op jit(solution)/shard_map/concatenate | solution.py:258
  545.2 16.1 %convert_element_type.452 = bf16[4,2,184,2688]{3,2,1,0:T(8,128)(2,1)} reshape(bf16[1472,4,672]{2,1,0:T(4,128)(2,1)} %copy.417) | data formatting | bytes 15826944 | tf_op jit(solution)/shard_map/convert_element_type | solution.py:69
  561.4 5.2 multiply_reduce_fusion.2
  595.6 5.0 fusion.3
  600.5 11.1 %reshape.563 = bf16[736,4,672]{2,1,0:T(4,128)(2,1)} reshape(bf16[4,184,2688]{2,1,0:T(8,128)(2,1)} %fusion.3) | data formatting | bytes 7913472 | tf_op jit(solution)/shard_map/reshape | solution.py:263
  611.6 8.2 copy.427
  623.8 4.7 dynamic-slice_bitcast_fusion.1
  628.7 5.3 collective-permute-done.51
  642.9 14.6 %collective-permute-done.54 = bf16[184,2304]{1,0:T(8,128)(2,1)S(1)} collective-permute-done((bf16[184,2304]{1,0:T(8,128)(2,1)S(1)}, bf16[184,2304]{1,0:T(8,128)(2,1)S(1)}, u32[]{:S(2)}, u32[]{:S(2)}) %collective-permute-start.54) | collective-permute-done | bytes 847904 | tf_op jit(solution)/shard_map/ppermute | solution.py:121
  658.6 6.9 collective-permute-done.46
  675.2 11.6 %collective-permute-done.49 = bf16[184,2304]{1,0:T(8,128)(2,1)S(1)} collective-permute-done((bf16[184,2304]{1,0:T(8,128)(2,1)}, bf16[184,2304]{1,0:T(8,128)(2,1)S(1)}, u32[]{:S(2)}, u32[]{:S(2)}) %collective-permute-start.49) | collective-permute-done | bytes 847904 | tf_op jit(solution)/shard_map/ppermute | solution.py:121
  700.0 6.2 fusion.4
  706.2 11.2 %reshape.560 = bf16[736,4,672]{2,1,0:T(4,128)(2,1)} reshape(bf16[4,184,2688]{2,1,0:T(8,128)(2,1)} %fusion.4) | data formatting | bytes 7913472 | tf_op jit(solution)/shard_map/reshape | solution.py:263
  717.3 8.2 copy.418
  748.8 42.8 %psum.7 = f32[2,4608]{1,0:T(2,128)S(1)} all-reduce(f32[2,4608]{1,0:T(2,128)S(1)} %pad_maximum_fusion.26), channel_id=1, replica_groups=mesh['section'=2,'wide'=4,'rows'=4] {'section','wide','rows'}, use_global_device_ids=true, to_apply=%region_31.32 | all-reduce | flops 9216 | bytes 73728 | tf_op jit(solution)/shard_map/psum | solution.py:431
  805.7 4.8 collective-permute-done.62
  810.8 26.8 %reduce-scatter.9.cloned.1.call-done = bf16[1,736,672]{1,2,0:T(8,128)(2,1)} async-done(((bf16[4,736,672]{1,2,0:T(8,128)(2,1)}), bf16[1,736,672]{1,2,0:T(8,128)(2,1)}) %reduce-scatter.9.cloned.1.call-update) | async-done | bytes 989200 | tf_op jit(solution)/shard_map/reduce_scatter | solution.py:264
  845.3 4.9 collective-permute-done.57
  851.3 5.0 collective-permute-done.58
  (835 shorter events, 399.2 us)
Async XLA Ops:
  7.2 786.0 %reduce-scatter.11.cloned.1.call-start = ((), (), s32[]{:S(2)}) async-start(), calls=%async_computation.7 | async-start | bytes 5160960 | tf_op jit(solution)/shard_map/reduce_scatter | solution.py:264
  12.5 44.2 %collective-permute-start.2 = (bf16[368,2304]{1,0:T(8,128)(2,1)}, bf16[368,2304]{1,0:T(8,128)(2,1)}, u32[]{:S(2)}, u32[]{:S(2)}) collective-permute-start(bf16[368,2304]{1,0:T(8,128)(2,1)} %get-tuple-element.109), channel_id=1, source_target_pairs={{0,8},{4,12},{8,0},{12,4},{1,9},{5,13},{9,1},{13,5},{2,10},{6,14},... | collective-permute-start | bytes 5087240 | tf_op jit(solution)/shard_map/ppermute | solution.py:121
  15.6 44.4 %collective-permute-start.1 = (bf16[368,2304]{1,0:T(8,128)(2,1)}, bf16[368,2304]{1,0:T(8,128)(2,1)}, u32[]{:S(2)}, u32[]{:S(2)}) collective-permute-start(bf16[368,2304]{1,0:T(8,128)(2,1)} %get-tuple-element.109), channel_id=1, source_target_pairs={{0,4},{4,0},{8,12},{12,8},{1,5},{5,1},{9,13},{13,9},{2,6},{6,2},{1... | collective-permute-start | bytes 5087240 | tf_op jit(solution)/shard_map/ppermute | solution.py:121
  17.4 127.0 %collective-permute-start = (f32[4608]{0:T(1024)S(1)}, f32[4608]{0:T(1024)S(1)}, u32[]{:S(2)}, u32[]{:S(2)}) collective-permute-start(f32[4608]{0:T(1024)S(1)} %pad_maximum_fusion.27), channel_id=1, source_target_pairs={{0,16},{16,0},{1,17},{17,1},{2,18},{18,2},{3,19},{19,3},{4,20},{20... | collective-permute-start | bytes 55304 | tf_op jit(solution)/shard_map/ppermute | solution.py:121
  47.5 124.7 %collective-permute-start.6 = (bf16[368,2688]{1,0:T(8,128)(2,1)}, bf16[368,2688]{1,0:T(8,128)(2,1)}, u32[]{:S(2)}, u32[]{:S(2)}) collective-permute-start(bf16[368,2688]{1,0:T(8,128)(2,1)} %bitcast.446), channel_id=1, source_target_pairs={{0,4},{4,0},{8,12},{12,8},{1,5},{5,1},{9,13},{13,9},{2,6},{6,2},{1... | collective-permute-start | bytes 5935112 | tf_op jit(solution)/shard_map/ppermute | solution.py:121
  52.2 123.5 %collective-permute-start.7 = (bf16[368,2688]{1,0:T(8,128)(2,1)}, bf16[368,2688]{1,0:T(8,128)(2,1)}, u32[]{:S(2)}, u32[]{:S(2)}) collective-permute-start(bf16[368,2688]{1,0:T(8,128)(2,1)} %bitcast.445), channel_id=1, source_target_pairs={{0,8},{4,12},{8,0},{12,4},{1,9},{5,13},{9,1},{13,5},{2,10},{6,14},... | collective-permute-start | bytes 5935112 | tf_op jit(solution)/shard_map/ppermute | solution.py:121
  57.9 56.9 %collective-permute-start.4 = (bf16[184,2304]{1,0:T(8,128)(2,1)S(1)}, bf16[184,2304]{1,0:T(8,128)(2,1)S(1)}, u32[]{:S(2)}, u32[]{:S(2)}) collective-permute-start(bf16[184,2304]{1,0:T(8,128)(2,1)S(1)} %slice.604), channel_id=1, source_target_pairs={{0,4},{4,0},{8,12},{12,8},{1,5},{5,1},{9,13},{13,9},{2,6},{6,2},{1... | collective-permute-start | bytes 2543624 | tf_op jit(solution)/shard_map/ppermute | solution.py:121
  61.1 55.1 %collective-permute-start.3 = (bf16[184,2304]{1,0:T(8,128)(2,1)S(1)}, bf16[184,2304]{1,0:T(8,128)(2,1)S(1)}, u32[]{:S(2)}, u32[]{:S(2)}) collective-permute-start(bf16[184,2304]{1,0:T(8,128)(2,1)S(1)} %slice.603), channel_id=1, source_target_pairs={{0,8},{4,12},{8,0},{12,4},{1,9},{5,13},{9,1},{13,5},{2,10},{6,14},... | collective-permute-start | bytes 2543624 | tf_op jit(solution)/shard_map/ppermute | solution.py:121
  114.8 63.8 %collective-permute-start.8 = (bf16[368,2688]{1,0:T(8,128)(2,1)}, bf16[368,2688]{1,0:T(8,128)(2,1)}, u32[]{:S(2)}, u32[]{:S(2)}) collective-permute-start(bf16[368,2688]{1,0:T(8,128)(2,1)} %bitcast.33), channel_id=1, source_target_pairs={{0,12},{4,8},{8,4},{12,0},{1,13},{5,9},{9,5},{13,1},{2,14},{6,10},... | collective-permute-start | bytes 5935112 | tf_op jit(solution)/shard_map/ppermute | solution.py:121
  117.5 66.8 %collective-permute-start.5 = (bf16[1472,2304]{1,0:T(8,128)(2,1)}, bf16[1472,2304]{1,0:T(8,128)(2,1)}, u32[]{:S(2)}, u32[]{:S(2)}) collective-permute-start(bf16[1472,2304]{1,0:T(8,128)(2,1)} %maximum_dynamic-update-slice_fusion), channel_id=1, source_target_pairs={{0,16},{16,0},{1,17},{17,1},{2,18},{18,2},{3,19},{19,3},{4,20},{20... | collective-permute-start | bytes 20348936 | tf_op jit(solution)/shard_map/ppermute | solution.py:121
  144.4 19.4 %collective-permute-start.29 = (bf16[64,1472]{1,0:T(8,128)(2,1)S(1)}, bf16[64,1472]{1,0:T(8,128)(2,1)S(1)}, u32[]{:S(2)}, u32[]{:S(2)}) collective-permute-start(bf16[64,1472]{1,0:T(8,128)(2,1)S(1)} %get-tuple-element.70), channel_id=1, source_target_pairs={{0,8},{4,12},{8,0},{12,4},{1,9},{5,13},{9,1},{13,5},{2,10},{6,14},... | collective-permute-start | bytes 565256 | tf_op jit(solution)/shard_map/ppermute | solution.py:121
  170.7 13.0 %collective-permute-start.30 = (bf16[32,1472]{1,0:T(8,128)(2,1)S(1)}, bf16[32,1472]{1,0:T(8,128)(2,1)S(1)}, u32[]{:S(2)}, u32[]{:S(2)}) collective-permute-start(bf16[32,1472]{1,0:T(8,128)(2,1)S(1)} %slice.668), channel_id=1, source_target_pairs={{0,4},{4,0},{8,12},{12,8},{1,5},{5,1},{9,13},{13,9},{2,6},{6,2},{1... | collective-permute-start | bytes 282632 | tf_op jit(solution)/shard_map/ppermute | solution.py:121
  181.6 38.9 %collective-permute-start.9 = (bf16[1472,2688]{1,0:T(8,128)(2,1)}, bf16[1472,2688]{1,0:T(8,128)(2,1)}, u32[]{:S(2)}, u32[]{:S(2)}) collective-permute-start(bf16[1472,2688]{1,0:T(8,128)(2,1)} %constant_dynamic-update-slice_fusion.28), channel_id=1, source_target_pairs={{0,16},{16,0},{1,17},{17,1},{2,18},{18,2},{3,19},{19,3},{4,20},{20... | collective-permute-start | bytes 23740424 | tf_op jit(solution)/shard_map/ppermute | solution.py:121
  205.2 28.3 %collective-permute-start.12 = (bf16[256,1472]{0,1:T(8,128)(2,1)}, bf16[256,1472]{0,1:T(8,128)(2,1)S(1)}, u32[]{:S(2)}, u32[]{:S(2)}) collective-permute-start(bf16[256,1472]{0,1:T(8,128)(2,1)} %get-tuple-element.72), channel_id=1, source_target_pairs={{0,8},{4,12},{8,0},{12,4},{1,9},{5,13},{9,1},{13,5},{2,10},{6,14},... | collective-permute-start | bytes 2261000 | tf_op jit(solution)/shard_map/ppermute | solution.py:121
  206.8 28.3 %collective-permute-start.10 = (bf16[256,1472]{0,1:T(8,128)(2,1)}, bf16[256,1472]{0,1:T(8,128)(2,1)S(1)}, u32[]{:S(2)}, u32[]{:S(2)}) collective-permute-start(bf16[256,1472]{0,1:T(8,128)(2,1)} %get-tuple-element.72), channel_id=1, source_target_pairs={{0,4},{4,0},{8,12},{12,8},{1,5},{5,1},{9,13},{13,9},{2,6},{6,2},{1... | collective-permute-start | bytes 2261000 | tf_op jit(solution)/shard_map/ppermute | solution.py:121
  258.3 17.8 %collective-permute-start.17 = (bf16[256,1472]{0,1:T(8,128)(2,1)S(1)}, bf16[256,1472]{0,1:T(8,128)(2,1)S(1)}, u32[]{:S(2)}, u32[]{:S(2)}) collective-permute-start(bf16[256,1472]{0,1:T(8,128)(2,1)S(1)} %pad_maximum_fusion.10), channel_id=1, source_target_pairs={{0,8},{4,12},{8,0},{12,4},{1,9},{5,13},{9,1},{13,5},{2,10},{6,14},... | collective-permute-start | bytes 2261000 | tf_op jit(solution)/shard_map/ppermute | solution.py:121
  261.2 15.3 %collective-permute-start.15 = (bf16[256,1472]{0,1:T(8,128)(2,1)S(1)}, bf16[256,1472]{0,1:T(8,128)(2,1)S(1)}, u32[]{:S(2)}, u32[]{:S(2)}) collective-permute-start(bf16[256,1472]{0,1:T(8,128)(2,1)S(1)} %pad_maximum_fusion.9), channel_id=1, source_target_pairs={{0,4},{4,0},{8,12},{12,8},{1,5},{5,1},{9,13},{13,9},{2,6},{6,2},{1... | collective-permute-start | bytes 2261000 | tf_op jit(solution)/shard_map/ppermute | solution.py:121
  316.3 63.9 %collective-permute-start.33 = (bf16[32,1472]{1,0:T(8,128)(2,1)}, bf16[32,1472]{1,0:T(8,128)(2,1)}, u32[]{:S(2)}, u32[]{:S(2)}) collective-permute-start(bf16[32,1472]{1,0:T(8,128)(2,1)} %get-tuple-element.167), channel_id=1, source_target_pairs={{0,4},{4,0},{8,12},{12,8},{1,5},{5,1},{9,13},{13,9},{2,6},{6,2},{1... | collective-permute-start | bytes 282632 | tf_op jit(solution)/shard_map/ppermute | solution.py:121
  317.8 66.1 %collective-permute-start.31 = (bf16[32,1472]{1,0:T(8,128)(2,1)}, bf16[32,1472]{1,0:T(8,128)(2,1)}, u32[]{:S(2)}, u32[]{:S(2)}) collective-permute-start(bf16[32,1472]{1,0:T(8,128)(2,1)} %get-tuple-element.166), channel_id=1, source_target_pairs={{0,8},{4,12},{8,0},{12,4},{1,9},{5,13},{9,1},{13,5},{2,10},{6,14},... | collective-permute-start | bytes 282632 | tf_op jit(solution)/shard_map/ppermute | solution.py:121
  390.8 204.8 %collective-permute-start.60 = (bf16[4,184,2688]{2,1,0:T(8,128)(2,1)}, bf16[4,184,2688]{2,1,0:T(8,128)(2,1)}, u32[]{:S(2)}, u32[]{:S(2)}) collective-permute-start(bf16[4,184,2688]{2,1,0:T(8,128)(2,1)} %dynamic-slice_bitcast_fusion), channel_id=1, source_target_pairs={{0,16},{16,0},{1,17},{17,1},{2,18},{18,2},{3,19},{19,3},{4,20},{20... | collective-permute-start | bytes 11870216 | tf_op jit(solution)/shard_map/ppermute | solution.py:121
  412.6 45.1 %collective-permute-start.37 = (bf16[256,1472]{0,1:T(8,128)(2,1)}, bf16[256,1472]{0,1:T(8,128)(2,1)}, u32[]{:S(2)}, u32[]{:S(2)}) collective-permute-start(bf16[256,1472]{0,1:T(8,128)(2,1)} %get-tuple-element.74), channel_id=1, source_target_pairs={{0,8},{4,12},{8,0},{12,4},{1,9},{5,13},{9,1},{13,5},{2,10},{6,14},... | collective-permute-start | bytes 2261000 | tf_op jit(solution)/shard_map/ppermute | solution.py:121
  413.1 51.8 %collective-permute-start.35 = (bf16[256,1472]{0,1:T(8,128)(2,1)}, bf16[256,1472]{0,1:T(8,128)(2,1)}, u32[]{:S(2)}, u32[]{:S(2)}) collective-permute-start(bf16[256,1472]{0,1:T(8,128)(2,1)} %get-tuple-element.74), channel_id=1, source_target_pairs={{0,4},{4,0},{8,12},{12,8},{1,5},{5,1},{9,13},{13,9},{2,6},{6,2},{1... | collective-permute-start | bytes 2261000 | tf_op jit(solution)/shard_map/ppermute | solution.py:121
  452.7 136.2 %collective-permute-start.50 = (bf16[4,184,2304]{2,1,0:T(8,128)(2,1)}, bf16[4,184,2304]{2,1,0:T(8,128)(2,1)}, u32[]{:S(2)}, u32[]{:S(2)}) collective-permute-start(bf16[4,184,2304]{2,1,0:T(8,128)(2,1)} %dynamic-slice_bitcast_fusion.2), channel_id=1, source_target_pairs={{0,16},{16,0},{1,17},{17,1},{2,18},{18,2},{3,19},{19,3},{4,20},{20... | collective-permute-start | bytes 10174472 | tf_op jit(solution)/shard_map/ppermute | solution.py:121
  480.0 21.6 %collective-permute-start.41 = (bf16[128,1472]{0,1:T(8,128)(2,1)S(1)}, bf16[128,1472]{0,1:T(8,128)(2,1)S(1)}, u32[]{:S(2)}, u32[]{:S(2)}) collective-permute-start(bf16[128,1472]{0,1:T(8,128)(2,1)S(1)} %get-tuple-element.134), channel_id=1, source_target_pairs={{0,4},{4,0},{8,12},{12,8},{1,5},{5,1},{9,13},{13,9},{2,6},{6,2},{1... | collective-permute-start | bytes 1130504 | tf_op jit(solution)/shard_map/ppermute | solution.py:121
  480.9 22.3 %collective-permute-start.39 = (bf16[128,1472]{0,1:T(8,128)(2,1)S(1)}, bf16[128,1472]{0,1:T(8,128)(2,1)S(1)}, u32[]{:S(2)}, u32[]{:S(2)}) collective-permute-start(bf16[128,1472]{0,1:T(8,128)(2,1)S(1)} %get-tuple-element.133), channel_id=1, source_target_pairs={{0,8},{4,12},{8,0},{12,4},{1,9},{5,13},{9,1},{13,5},{2,10},{6,14},... | collective-permute-start | bytes 1130504 | tf_op jit(solution)/shard_map/ppermute | solution.py:121
  502.7 58.6 %collective-permute-start.42 = (bf16[256,1472]{0,1:T(8,128)(2,1)}, bf16[256,1472]{0,1:T(8,128)(2,1)}, u32[]{:S(2)}, u32[]{:S(2)}) collective-permute-start(bf16[256,1472]{0,1:T(8,128)(2,1)} %pad_maximum_fusion.12), channel_id=1, source_target_pairs={{0,8},{4,12},{8,0},{12,4},{1,9},{5,13},{9,1},{13,5},{2,10},{6,14},... | collective-permute-start | bytes 2261000 | tf_op jit(solution)/shard_map/ppermute | solution.py:121
  504.3 57.1 %collective-permute-start.40 = (bf16[256,1472]{0,1:T(8,128)(2,1)}, bf16[256,1472]{0,1:T(8,128)(2,1)}, u32[]{:S(2)}, u32[]{:S(2)}) collective-permute-start(bf16[256,1472]{0,1:T(8,128)(2,1)} %pad_maximum_fusion.11), channel_id=1, source_target_pairs={{0,4},{4,0},{8,12},{12,8},{1,5},{5,1},{9,13},{13,9},{2,6},{6,2},{1... | collective-permute-start | bytes 2261000 | tf_op jit(solution)/shard_map/ppermute | solution.py:121
  588.9 48.2 %collective-permute-start.45 = (bf16[4,184,2304]{2,1,0:T(8,128)(2,1)}, bf16[4,184,2304]{2,1,0:T(8,128)(2,1)}, u32[]{:S(2)}, u32[]{:S(2)}) collective-permute-start(bf16[4,184,2304]{2,1,0:T(8,128)(2,1)} %dynamic-slice_bitcast_fusion.3), channel_id=1, source_target_pairs={{0,16},{16,0},{1,17},{17,1},{2,18},{18,2},{3,19},{19,3},{4,20},{20... | collective-permute-start | bytes 10174472 | tf_op jit(solution)/shard_map/ppermute | solution.py:121
  619.9 178.5 %reduce-scatter.7.cloned.1.call-start = ((), (), s32[]{:S(2)}) async-start(), calls=%async_computation.5 | async-start | bytes 1474560 | tf_op jit(solution)/shard_map/reduce_scatter | solution.py:287
  621.4 12.6 %collective-permute-start.51 = (bf16[92,2304]{1,0:T(8,128)(2,1)S(1)}, bf16[92,2304]{1,0:T(8,128)(2,1)S(1)}, u32[]{:S(2)}, u32[]{:S(2)}) collective-permute-start(bf16[92,2304]{1,0:T(8,128)(2,1)S(1)} %get-tuple-element.126), channel_id=1, source_target_pairs={{0,8},{4,12},{8,0},{12,4},{1,9},{5,13},{9,1},{13,5},{2,10},{6,14},... | collective-permute-start | bytes 1271816 | tf_op jit(solution)/shard_map/ppermute | solution.py:121
  623.0 12.3 %collective-permute-start.53 = (bf16[92,2304]{1,0:T(8,128)(2,1)S(1)}, bf16[92,2304]{1,0:T(8,128)(2,1)S(1)}, u32[]{:S(2)}, u32[]{:S(2)}) collective-permute-start(bf16[92,2304]{1,0:T(8,128)(2,1)S(1)} %get-tuple-element.127), channel_id=1, source_target_pairs={{0,4},{4,0},{8,12},{12,8},{1,5},{5,1},{9,13},{13,9},{2,6},{6,2},{1... | collective-permute-start | bytes 1271816 | tf_op jit(solution)/shard_map/ppermute | solution.py:121
  628.6 71.4 %collective-permute-start.56 = (bf16[4,184,2688]{2,1,0:T(8,128)(2,1)}, bf16[4,184,2688]{2,1,0:T(8,128)(2,1)}, u32[]{:S(2)}, u32[]{:S(2)}) collective-permute-start(bf16[4,184,2688]{2,1,0:T(8,128)(2,1)} %dynamic-slice_bitcast_fusion.1), channel_id=1, source_target_pairs={{0,16},{16,0},{1,17},{17,1},{2,18},{18,2},{3,19},{19,3},{4,20},{20... | collective-permute-start | bytes 11870216 | tf_op jit(solution)/shard_map/ppermute | solution.py:121
  635.7 21.9 %collective-permute-start.54 = (bf16[184,2304]{1,0:T(8,128)(2,1)S(1)}, bf16[184,2304]{1,0:T(8,128)(2,1)S(1)}, u32[]{:S(2)}, u32[]{:S(2)}) collective-permute-start(bf16[184,2304]{1,0:T(8,128)(2,1)S(1)} %pad_maximum_fusion.8), channel_id=1, source_target_pairs={{0,8},{4,12},{8,0},{12,4},{1,9},{5,13},{9,1},{13,5},{2,10},{6,14},... | collective-permute-start | bytes 2543624 | tf_op jit(solution)/shard_map/ppermute | solution.py:121
  636.3 21.9 %collective-permute-start.52 = (bf16[184,2304]{1,0:T(8,128)(2,1)S(1)}, bf16[184,2304]{1,0:T(8,128)(2,1)S(1)}, u32[]{:S(2)}, u32[]{:S(2)}) collective-permute-start(bf16[184,2304]{1,0:T(8,128)(2,1)S(1)} %pad_maximum_fusion.7), channel_id=1, source_target_pairs={{0,4},{4,0},{8,12},{12,8},{1,5},{5,1},{9,13},{13,9},{2,6},{6,2},{1... | collective-permute-start | bytes 2543624 | tf_op jit(solution)/shard_map/ppermute | solution.py:121
  640.0 25.5 %collective-permute-start.46 = (bf16[92,2304]{1,0:T(8,128)(2,1)S(1)}, bf16[92,2304]{1,0:T(8,128)(2,1)S(1)}, u32[]{:S(2)}, u32[]{:S(2)}) collective-permute-start(bf16[92,2304]{1,0:T(8,128)(2,1)S(1)} %get-tuple-element.131), channel_id=1, source_target_pairs={{0,8},{4,12},{8,0},{12,4},{1,9},{5,13},{9,1},{13,5},{2,10},{6,14},... | collective-permute-start | bytes 1271816 | tf_op jit(solution)/shard_map/ppermute | solution.py:121
  641.6 24.3 %collective-permute-start.48 = (bf16[92,2304]{1,0:T(8,128)(2,1)S(1)}, bf16[92,2304]{1,0:T(8,128)(2,1)S(1)}, u32[]{:S(2)}, u32[]{:S(2)}) collective-permute-start(bf16[92,2304]{1,0:T(8,128)(2,1)S(1)} %get-tuple-element.132), channel_id=1, source_target_pairs={{0,4},{4,0},{8,12},{12,8},{1,5},{5,1},{9,13},{13,9},{2,6},{6,2},{1... | collective-permute-start | bytes 1271816 | tf_op jit(solution)/shard_map/ppermute | solution.py:121
  667.2 19.5 %collective-permute-start.49 = (bf16[184,2304]{1,0:T(8,128)(2,1)}, bf16[184,2304]{1,0:T(8,128)(2,1)S(1)}, u32[]{:S(2)}, u32[]{:S(2)}) collective-permute-start(bf16[184,2304]{1,0:T(8,128)(2,1)} %pad_maximum_fusion.6), channel_id=1, source_target_pairs={{0,8},{4,12},{8,0},{12,4},{1,9},{5,13},{9,1},{13,5},{2,10},{6,14},... | collective-permute-start | bytes 2543624 | tf_op jit(solution)/shard_map/ppermute | solution.py:121
  669.7 19.2 %collective-permute-start.47 = (bf16[184,2304]{1,0:T(8,128)(2,1)}, bf16[184,2304]{1,0:T(8,128)(2,1)}, u32[]{:S(2)}, u32[]{:S(2)}) collective-permute-start(bf16[184,2304]{1,0:T(8,128)(2,1)} %pad_maximum_fusion.5), channel_id=1, source_target_pairs={{0,4},{4,0},{8,12},{12,8},{1,5},{5,1},{9,13},{13,9},{2,6},{6,2},{1... | collective-permute-start | bytes 2543624 | tf_op jit(solution)/shard_map/ppermute | solution.py:121
  672.4 126.0 %reduce-scatter.5.cloned.1.call-start = ((), (), s32[]{:S(2)}) async-start(), calls=%async_computation.4 | async-start | bytes 1474560 | tf_op jit(solution)/shard_map/reduce_scatter | solution.py:287
  692.9 144.7 %reduce-scatter.9.cloned.1.call-start = ((), (), s32[]{:S(2)}) async-start(), calls=%async_computation.6 | async-start | bytes 5160960 | tf_op jit(solution)/shard_map/reduce_scatter | solution.py:264
  698.5 27.1 %collective-permute-start.24 = (bf16[32,1472]{1,0:T(8,128)(2,1)S(1)}, bf16[32,1472]{1,0:T(8,128)(2,1)S(1)}, u32[]{:S(2)}, u32[]{:S(2)}) collective-permute-start(bf16[32,1472]{1,0:T(8,128)(2,1)S(1)} %get-tuple-element.171), channel_id=1, source_target_pairs={{0,4},{4,0},{8,12},{12,8},{1,5},{5,1},{9,13},{13,9},{2,6},{6,2},{1... | collective-permute-start | bytes 282632 | tf_op jit(solution)/shard_map/ppermute | solution.py:121
  699.2 27.8 %collective-permute-start.22 = (bf16[32,1472]{1,0:T(8,128)(2,1)S(1)}, bf16[32,1472]{1,0:T(8,128)(2,1)S(1)}, u32[]{:S(2)}, u32[]{:S(2)}) collective-permute-start(bf16[32,1472]{1,0:T(8,128)(2,1)S(1)} %get-tuple-element.170), channel_id=1, source_target_pairs={{0,8},{4,12},{8,0},{12,4},{1,9},{5,13},{9,1},{13,5},{2,10},{6,14},... | collective-permute-start | bytes 282632 | tf_op jit(solution)/shard_map/ppermute | solution.py:121
  747.3 116.8 %collective-permute-start.43 = (f32[256,736]{0,1:T(8,128)}, f32[256,736]{0,1:T(8,128)}, u32[]{:S(2)}, u32[]{:S(2)}) collective-permute-start(f32[256,736]{0,1:T(8,128)} %fusion.184), channel_id=1, source_target_pairs={{0,16},{16,0},{1,17},{17,1},{2,18},{18,2},{3,19},{19,3},{4,20},{20... | collective-permute-start | bytes 2261000 | tf_op jit(solution)/shard_map/ppermute | solution.py:121
  797.9 12.6 %collective-permute-start.62 = (bf16[184,672]{1,0:T(8,128)(2,1)S(1)}, bf16[184,672]{1,0:T(8,128)(2,1)S(1)}, u32[]{:S(2)}, u32[]{:S(2)}) collective-permute-start(bf16[184,672]{1,0:T(8,128)(2,1)S(1)} %get-tuple-element.114), channel_id=1, source_target_pairs={{0,8},{4,12},{8,0},{12,4},{1,9},{5,13},{9,1},{13,5},{2,10},{6,14},... | collective-permute-start | bytes 741896 | tf_op jit(solution)/shard_map/ppermute | solution.py:121
  800.3 43.4 %collective-permute-start.63 = (bf16[184,672]{1,0:T(8,128)(2,1)}, bf16[184,672]{1,0:T(8,128)(2,1)}, u32[]{:S(2)}, u32[]{:S(2)}) collective-permute-start(bf16[184,672]{1,0:T(8,128)(2,1)} %get-tuple-element.113), channel_id=1, source_target_pairs={{0,12},{4,8},{8,4},{12,0},{1,13},{5,9},{9,5},{13,1},{2,14},{6,10},... | collective-permute-start | bytes 741896 | tf_op jit(solution)/shard_map/ppermute | solution.py:121
  841.7 14.6 %collective-permute-start.58 = (bf16[184,672]{1,0:T(8,128)(2,1)}, bf16[184,672]{1,0:T(8,128)(2,1)}, u32[]{:S(2)}, u32[]{:S(2)}) collective-permute-start(bf16[184,672]{1,0:T(8,128)(2,1)} %get-tuple-element.118), channel_id=1, source_target_pairs={{0,8},{4,12},{8,0},{12,4},{1,9},{5,13},{9,1},{13,5},{2,10},{6,14},... | collective-permute-start | bytes 741896 | tf_op jit(solution)/shard_map/ppermute | solution.py:121
  843.0 14.4 %collective-permute-start.59 = (bf16[184,672]{1,0:T(8,128)(2,1)}, bf16[184,672]{1,0:T(8,128)(2,1)}, u32[]{:S(2)}, u32[]{:S(2)}) collective-permute-start(bf16[184,672]{1,0:T(8,128)(2,1)} %get-tuple-element.117), channel_id=1, source_target_pairs={{0,12},{4,8},{8,4},{12,0},{1,13},{5,9},{9,5},{13,1},{2,14},{6,10},... | collective-permute-start | bytes 741896 | tf_op jit(solution)/shard_map/ppermute | solution.py:121
  843.7 23.4 %collective-permute-start.55 = (bf16[184,576]{0,1:T(8,128)(2,1)}, bf16[184,576]{0,1:T(8,128)(2,1)}, u32[]{:S(2)}, u32[]{:S(2)}) collective-permute-start(bf16[184,576]{0,1:T(8,128)(2,1)} %select_bitcast_fusion.2), channel_id=1, source_target_pairs={{0,16},{16,0},{1,17},{17,1},{2,18},{18,2},{3,19},{19,3},{4,20},{20... | collective-permute-start | bytes 635912 | tf_op jit(solution)/shard_map/ppermute | solution.py:121
  (211 other events, 1435.9 us)
Sparse Core Ops, SparseCore 0:
  620.0 76.4 reduce-scatter.10
  699.6 29.6 reduce-scatter.6
  732.2 27.8 reduce-scatter.4
  762.4 75.1 reduce-scatter.8

commit v2 on v1

--- a/solution.py
+++ b/solution.py
@@ -2,6 +2,8 @@
 import jax.numpy as jnp
 import numpy as np
 from jax import lax
+from jax.experimental import pallas as pl
+from jax.experimental.pallas import tpu as pltpu
 from jax.sharding import PartitionSpec as P
 
 D = 1472
@@ -206,44 +208,6 @@
     return grad_out + grad_residual, grad_gain, grad_win, grad_wout, grad_bias
 
 
-def hidden_columns(weight):
-    width = weight.shape[1] * 2 // 3
-    return weight[:, :width], weight[:, width:]
-
-
-def ffn_hidden(blocks, weight):
-    w_in, _ = hidden_columns(weight)
-    both = [matmul(block, w_in) for block in blocks]
-    units = w_in.shape[1] // 2
-    return both, [to_low(gated(part[:, :units], part[:, units:])) for part in both]
-
-
-def ffn_forward(residual, gain_row, weight):
-    blocks = gather_wide(to_low(rms_norm(residual, gain_row)))
-    both, hidden = ffn_hidden(blocks, weight)
-    _, w_out = hidden_columns(weight)
-    out = residual + scatter_wide([matmul(part, w_out.T) for part in hidden])
-    return out, (residual, blocks, both, hidden)
-
-
-def ffn_backward(kept, gain_row, weight, grad_out, grad_blocks):
-    residual, blocks, both, hidden = kept
-    w_in, w_out = hidden_columns(weight)
-    units = w_out.shape[1]
-    parts, grad_both = [], []
-    for block, pre in zip(grad_blocks, both):
-        _, pull = jax.vjp(gated, pre[:, :units], pre[:, units:])
-        grad_gate, grad_up = pull(matmul(block, w_out))
-        low = to_low(jnp.concatenate([grad_gate, grad_up], axis=1))
-        grad_both.append(low)
-        parts.append(matmul(low, w_in.T))
-    grad_residual, grad_gain = norm_backward(residual, gain_row, scatter_wide(parts))
-    joined = jnp.concatenate(grad_both, axis=0)
-    grad_in = matmul(jnp.concatenate(blocks, axis=0).T, joined)
-    grad_wout = matmul(jnp.concatenate(grad_blocks, axis=0).T, jnp.concatenate(hidden, axis=0))
-    return grad_out + grad_residual, grad_gain, (grad_in, grad_wout)
-
-
 def core_halves(grad, core, wide):
     depth, columns = grad.shape
     split = to_low(grad).reshape(wide, 2, depth // wide // 2, columns)
@@ -252,23 +216,21 @@
     return mine.astype(jnp.float32) + xor_permute(sent, "section", 1).astype(jnp.float32)
 
 
-def reduce_ffn(grads, core, wide, rows):
-    grad_in, grad_wout = grads
-    depth = grad_in.shape[0]
-    both = jnp.concatenate(
-        [grad_in.reshape(depth, rows, -1), grad_wout.reshape(depth, rows, -1)], axis=2
-    )
-    columns = both.shape[2]
-    halves = core_halves(both.reshape(depth, rows * columns), core, wide)
-    halves = to_low(halves).reshape(wide * (depth // wide // 2), rows, columns).transpose(1, 0, 2)
-    summed = lax.psum_scatter(halves, "rows", scatter_dimension=0, tiled=True)[0]
-    blocks = summed.reshape(wide, depth // wide // 2, columns)
+def to_owners(value, axis, wide):
     place = lax.axis_index("wide")
-    out = [lax.dynamic_index_in_dim(blocks, place, 0, keepdims=False)]
-    for v in range(1, wide):
-        block = lax.dynamic_index_in_dim(blocks, place ^ v, 0, keepdims=False)
-        out.append(xor_permute(block, "wide", v))
-    return placed_rows([piece[None] for piece in out], place)
+    size = value.shape[axis] // wide
+
+    def piece(owner):
+        return lax.dynamic_slice_in_dim(value, owner * size, size, axis)
+
+    got = [piece(place)] + [xor_permute(piece(place ^ v), "wide", v) for v in range(1, wide)]
+    return placed_rows([each[None] for each in got], place)
+
+
+def reduce_ffn(share_in, share_out, wide):
+    summed_in = lax.psum_scatter(share_in, "rows", scatter_dimension=0, tiled=True)[0]
+    summed_out = lax.psum_scatter(share_out, "rows", scatter_dimension=0, tiled=True)[0]
+    return to_owners(summed_in, 0, wide), to_owners(summed_out, 1, wide)
 
 
 def reduce_attn(grad, core, wide, rows):
@@ -291,8 +253,753 @@
     is_dec = core == 1
     own = jnp.where(is_dec, dec_half, enc_half)
     got = xor_permute(jnp.where(is_dec, enc_half, dec_half), "section", 1)
+    return jnp.stack([jnp.where(is_dec, got, own), jnp.where(is_dec, own, got)])
+
+
+MESH = pl.DeviceIdType.MESH
+HBM = pl.BlockSpec(memory_space=pl.ANY)
+VM = pl.BlockSpec(memory_space=pltpu.VMEM)
+TILE = 128
+VMEM_LIMIT = 60 * 1024 * 1024
+
+
+def peers_of(count):
+    place, core = lax.axis_index("wide"), lax.axis_index("section")
+    return [{"wide": place ^ v} for v in range(1, count)] + [{"section": 1 - core}]
+
+
+def greet(peers):
+    barrier = pltpu.get_barrier_semaphore()
+    for peer in peers:
+        pl.semaphore_signal(barrier, inc=1, device_id=peer, device_id_type=MESH)
+    pl.semaphore_wait(barrier, len(peers))
+
+
+def remote(source, target, sems, index, peer):
+    return pltpu.make_async_remote_copy(
+        src_ref=source,
+        dst_ref=target,
+        send_sem=sems[0].at[index],
+        recv_sem=sems[1].at[index],
+        device_id=peer,
+        device_id_type=MESH,
+    )
+
+
+def nt(left, right):
+    return lax.dot_general(left, right, (((1,), (1,)), ((), ())), preferred_element_type=jnp.float32)
+
+
+def tn(left, right):
+    return lax.dot_general(left, right, (((0,), (0,)), ((), ())), preferred_element_type=jnp.float32)
+
+
+class GatherPlane:
+    def __init__(self, blocks, sems, base, peers, rows):
+        half = rows // 2
+        first, second = peers[0], peers[1]
+        self.direct = [
+            remote(blocks.at[0], blocks.at[1], sems, base, first),
+            remote(blocks.at[0], blocks.at[2], sems, base + 1, second),
+        ]
+        self.passed = [
+            remote(
+                blocks.at[1, pl.ds(0, half)], blocks.at[3, pl.ds(0, half)], sems, base + 2, second
+            ),
+            remote(
+                blocks.at[2, pl.ds(half, half)],
+                blocks.at[3, pl.ds(half, half)],
+                sems,
+                base + 3,
+                first,
+            ),
+        ]
+
+    def start(self):
+        for copy in self.direct:
+            copy.start()
+
+    def arrive(self, index):
+        if index < 2:
+            self.direct[index].wait_recv()
+            self.passed[index].start()
+        else:
+            for copy in self.passed:
+                copy.wait_recv()
+
+    def finish(self):
+        for copy in self.direct + self.passed:
+            copy.wait_send()
+
+
+class ScatterPlane:
+    def __init__(self, parts, landing, sems, base, peers, rows):
+        half = rows // 2
+        first, second = peers[0], peers[1]
+        low, high = pl.ds(0, half), pl.ds(half, half)
+        self.parts, self.landing, self.half = parts, landing, half
+        self.far = [
+            remote(parts.at[3, low], landing.at[0, low], sems, base, first),
+            remote(parts.at[3, high], landing.at[0, high], sems, base + 1, second),
+        ]
+        self.early = [
+            remote(parts.at[1, low], landing.at[1, low], sems, base + 2, first),
+            remote(parts.at[2, high], landing.at[2, high], sems, base + 3, second),
+        ]
+        self.late = [
+            remote(parts.at[1, high], landing.at[1, high], sems, base + 4, first),
+            remote(parts.at[2, low], landing.at[2, low], sems, base + 5, second),
+        ]
+
+    def send_early(self, index):
+        self.early[index].start()
+
+    def send_far(self):
+        for copy in self.far:
+            copy.start()
+
+    def pass_on(self):
+        low, high = pl.ds(0, self.half), pl.ds(self.half, self.half)
+        self.far[0].wait_recv()
+        self.parts[2, low] = (
+            self.parts[2, low].astype(jnp.float32) + self.landing[0, low].astype(jnp.float32)
+        ).astype(jnp.bfloat16)
+        self.late[1].start()
+        self.far[1].wait_recv()
+        self.parts[1, high] = (
+            self.parts[1, high].astype(jnp.float32) + self.landing[0, high].astype(jnp.float32)
+        ).astype(jnp.bfloat16)
+        self.late[0].start()
+
+    def total(self):
+        for copy in self.early + self.late:
+            copy.wait_recv()
+        return self.landing[1].astype(jnp.float32) + self.landing[2].astype(jnp.float32)
+
+    def finish(self):
+        for copy in self.far + self.early + self.late:
+            copy.wait_send()
+
+
+def rms_rows(residual):
+    return lax.rsqrt(jnp.mean(residual * residual, axis=-1, keepdims=True) + EPSILON)
+
+
+def norm_pull(residual, gain_row, grad_normed):
+    scale = rms_rows(residual)
+    unit = residual * scale
+    inner = grad_normed * gain_row
+    grad_residual = scale * (inner - unit * jnp.mean(inner * unit, axis=-1, keepdims=True))
+    return grad_residual, jnp.sum(grad_normed * unit, axis=0, keepdims=True)
+
+
+def prepare_weights_kernel(wide, rows, in_ref, out_ref, *refs):
+    enc, dec = refs[:wide], refs[wide : 2 * wide]
+    blocks, send_sem, recv_sem, local_sem = refs[2 * wide :]
+    core, place = lax.axis_index("section"), lax.axis_index("wide")
+    sibling = {"section": 1 - core}
+    greet([sibling])
+    units = FF // (wide * rows * 2)
+    per_row = FF // rows
+    row_ids = lax.broadcasted_iota(jnp.int32, (2 * TILE, TILE), 0)
+    lane_ids = lax.broadcasted_iota(jnp.int32, (2 * TILE, TILE), 1)
+    straight = (
+        lax.broadcasted_iota(jnp.int32, (units, TILE), 0)
+        == lax.broadcasted_iota(jnp.int32, (units, TILE), 1)
+    ).astype(jnp.bfloat16)
+    for index in range(2 * wide):
+        target, half = index // 2, index % 2
+        offset = index * units
+        start, shift = offset // TILE * TILE, offset % TILE
+        picks = ((row_ids == lane_ids + shift) & (lane_ids < units)).astype(jnp.bfloat16)
+        window = min(2 * TILE, per_row - start)
+        picks = picks[:window]
+        for part in range(3):
+            for row in range(rows):
+                column = (part * rows + row) * TILE
+                if part < 2:
+                    source = in_ref[0, :, pl.ds(part * FF + row * per_row + start, window)]
+                    tile = matmul(source, picks)
+                else:
+                    source = out_ref[0, pl.ds(row * per_row + offset, units), :]
+                    tile = tn(source, straight)
+                blocks[half, target ^ place, :, pl.ds(column, TILE)] = tile.astype(jnp.bfloat16)
+    def move(outs):
+        copies = []
+        for v in range(wide):
+            keep = pltpu.make_async_copy(blocks.at[core, v], outs[v], local_sem.at[v])
+            give = remote(blocks.at[1 - core, v], outs[v], (send_sem, recv_sem), v, sibling)
+            keep.start()
+            give.start()
+            copies += [keep]
+            copies += [give]
+        for keep in copies[::2]:
+            keep.wait()
+        for give in copies[1::2]:
+            give.wait_send()
+
+    def receive(outs):
+        for v in range(wide):
+            remote(blocks.at[0, v], outs[v], (send_sem, recv_sem), v, sibling).wait_recv()
+
+    @pl.when(core == 0)
+    def _():
+        move(enc)
+        receive(dec)
+
+    @pl.when(core == 1)
+    def _():
+        move(dec)
+        receive(enc)
+
+
+def prepare_weights(wide, rows, ffn_in, ffn_out):
+    depth = ffn_in.shape[1]
+    block = jax.ShapeDtypeStruct((depth, 3 * rows * TILE), jnp.bfloat16)
+    outs = pl.pallas_call(
+        lambda *refs: prepare_weights_kernel(wide, rows, *refs),
+        out_shape=[block] * (2 * wide),
+        in_specs=[VM, VM],
+        out_specs=[HBM] * (2 * wide),
+        scratch_shapes=[
+            pltpu.VMEM((2, wide) + block.shape, jnp.bfloat16),
+            pltpu.SemaphoreType.DMA((wide,)),
+            pltpu.SemaphoreType.DMA((wide,)),
+            pltpu.SemaphoreType.DMA((wide,)),
+        ],
+        compiler_params=pltpu.CompilerParams(
+            collective_id=1, has_side_effects=True, vmem_limit_bytes=VMEM_LIMIT
+        ),
+        name="prepare_weights",
+    )(ffn_in, ffn_out)
+    return outs[:wide], outs[wide:]
+
+
+def ffn_forward_kernel(wide, x_ref, gain_ref, *refs):
+    pieces = refs[:wide]
+    y_ref, at_out, pre_out, hidden_out, weight_out = refs[wide : wide + 5]
+    blocks, at, pre, hidden, weight, parts, landing, acc, send_sem, recv_sem, local_sem = refs[
+        wide + 5 :
+    ]
+    rows = x_ref.shape[0]
+    depth = pieces[0].shape[0]
+    span = weight.shape[2] // 3
+    core, place = lax.axis_index("section"), lax.axis_index("wide")
+    peers = peers_of(wide)
+    sems = (send_sem, recv_sem)
+    greet(peers)
+    residual = x_ref[...]
+    blocks[0] = (residual * rms_rows(residual) * gain_ref[...]).astype(jnp.bfloat16)
+    gather = GatherPlane(blocks, sems, 0, peers, rows)
+    gather.start()
+    loads, swaps = [], []
+    for v in range(wide):
+        place_rows = pl.ds(pl.multiple_of((place ^ v) * depth, 16), depth)
+        load = pltpu.make_async_copy(pieces[v], weight.at[core, place_rows], local_sem.at[v])
+        swap = remote(pieces[v], weight.at[core, place_rows], sems, 10 + v, peers[-1])
+        load.start()
+        swap.start()
+        loads.append(load)
+        swaps.append(swap)
+    scatter = ScatterPlane(parts, landing, sems, 4, peers, rows)
+    for v in range(wide):
+        if v == 0:
+            for load in loads:
+                load.wait()
+        else:
+            gather.arrive(v - 1)
+        block = blocks[v]
+        for step in range(2):
+            if v == 0 and step == 1:
+                for swap in swaps:
+                    swap.wait_recv()
+            half = core if step == 0 else 1 - core
+            token_rows = pl.ds(v * rows, rows)
+            gate = matmul(block, weight[half, :, pl.ds(0, span)])
+            up = matmul(block, weight[half, :, pl.ds(span, span)])
+            pre[half, token_rows, pl.ds(0, span)] = gate.astype(jnp.bfloat16)
+            pre[half, token_rows, pl.ds(span, span)] = up.astype(jnp.bfloat16)
+            low = gated(gate, up).astype(jnp.bfloat16)
+            hidden[half, token_rows, :] = low
+            out = nt(low, weight[half, :, pl.ds(2 * span, span)])
+            if step == 0:
+                acc[...] = out
+            elif v == 0:
+                y_ref[...] = residual + acc[...] + out
+            else:
+                parts[v] = (acc[...] + out).astype(jnp.bfloat16)
+        if v in (1, 2):
+            scatter.send_early(v - 1)
+        if v == 3:
+            scatter.send_far()
+    copies = [
+        pltpu.make_async_copy(pre, pre_out, local_sem.at[4]),
+        pltpu.make_async_copy(weight, weight_out, local_sem.at[5]),
+    ]
+    for copy in copies:
+        copy.start()
+    scatter.pass_on()
+    at[...] = jnp.concatenate([blocks[v] for v in range(wide)], axis=0).T
+    last = pltpu.make_async_copy(at, at_out, local_sem.at[6])
+    last.start()
+    copies.append(last)
+    for half in range(2):
+        hidden_out[half] = hidden[half].T
+    y_ref[...] += scatter.total()
+    for copy in copies:
+        copy.wait()
+    gather.finish()
+    scatter.finish()
+    for swap in swaps:
+        swap.wait_send()
+
+
+def ffn_forward_call(wide, residual, gain_row, pieces, call_id):
+    rows = residual.shape[0]
+    total = rows * wide
+    columns = pieces[0].shape[1]
+    span = columns // 3
+    low = jnp.bfloat16
+    return pl.pallas_call(
+        lambda *refs: ffn_forward_kernel(wide, *refs),
+        out_shape=[
+            jax.ShapeDtypeStruct((rows, D), jnp.float32),
+            jax.ShapeDtypeStruct((D, total), low),
+            jax.ShapeDtypeStruct((2, total, 2 * span), low),
+            jax.ShapeDtypeStruct((2, span, total), low),
+            jax.ShapeDtypeStruct((2, D, columns), low),
+        ],
+        in_specs=[VM, VM] + [HBM] * wide,
+        out_specs=[VM, HBM, HBM, VM, HBM],
+        scratch_shapes=[
+            pltpu.VMEM((wide, rows, D), low),
+            pltpu.VMEM((D, total), low),
+            pltpu.VMEM((2, total, 2 * span), low),
+            pltpu.VMEM((2, total, span), low),
+            pltpu.VMEM((2, D, columns), low),
+            pltpu.VMEM((wide, rows, D), low),
+            pltpu.VMEM((3, rows, D), low),
+            pltpu.VMEM((rows, D), jnp.float32),
+            pltpu.SemaphoreType.DMA((14,)),
+            pltpu.SemaphoreType.DMA((14,)),
+            pltpu.SemaphoreType.DMA((7,)),
+        ],
+        compiler_params=pltpu.CompilerParams(
+            collective_id=call_id, has_side_effects=True, vmem_limit_bytes=VMEM_LIMIT
+        ),
+        name="ffn_forward_%d" % rows,
+    )(residual, gain_row, *pieces)
+
+
+def ffn_backward_kernel(wide, rows_axis, g_ref, x_ref, gain_ref, at_in, pre_in, hidden_in, weight_in, *refs):
+    gx_ref, gain_out, grad_in, grad_out = refs[:4]
+    (
+        blocks,
+        at,
+        pre,
+        hidden,
+        weight,
+        parts,
+        landing,
+        acc,
+        give_in,
+        give_out,
+        got_in,
+        got_out,
+        send_sem,
+        recv_sem,
+        local_sem,
+    ) = refs[4:]
+    rows = x_ref.shape[0]
+    span = weight.shape[2] // 3
+    units = FF // (wide * rows_axis * 2)
+    core = lax.axis_index("section")
+    peers = peers_of(wide)
+    sems = (send_sem, recv_sem)
+    greet(peers)
+    loads = [
+        pltpu.make_async_copy(weight_in, weight, local_sem.at[0]),
+        pltpu.make_async_copy(pre_in, pre, local_sem.at[1]),
+        pltpu.make_async_copy(hidden_in, hidden, local_sem.at[2]),
+        pltpu.make_async_copy(at_in, at, local_sem.at[3]),
+    ]
+    for load in loads:
+        load.start()
+    blocks[0] = g_ref[...].astype(jnp.bfloat16)
+    gather = GatherPlane(blocks, sems, 0, peers, rows)
+    gather.start()
+    scatter = ScatterPlane(parts, landing, sems, 4, peers, rows)
+    loads[0].wait()
+    loads[1].wait()
+    for v in range(wide):
+        if v > 0:
+            gather.arrive(v - 1)
+        block = blocks[v]
+        token_rows = pl.ds(v * rows, rows)
+        for half in range(2):
+            grad_hidden = matmul(block, weight[half, :, pl.ds(2 * span, span)])
+            gate = pre[half, token_rows, pl.ds(0, span)].astype(jnp.float32)
+            up = pre[half, token_rows, pl.ds(span, span)].astype(jnp.float32)
+            inner = GELU_A * (gate + GELU_B * gate * gate * gate)
+            tanh = jnp.tanh(inner)
+            slope = 0.5 * (1.0 + tanh) + 0.5 * gate * (1.0 - tanh * tanh) * GELU_A * (
+                1.0 + 3.0 * GELU_B * gate * gate
+            )
+            value = 0.5 * gate * (1.0 + tanh)
+            low_gate = (grad_hidden * up * slope).astype(jnp.bfloat16)
+            low_up = (grad_hidden * value).astype(jnp.bfloat16)
+            pre[half, token_rows, pl.ds(0, span)] = low_gate
+            pre[half, token_rows, pl.ds(span, span)] = low_up
+            out = nt(low_gate, weight[half, :, pl.ds(0, span)]) + nt(
+                low_up, weight[half, :, pl.ds(span, span)]
+            )
+            if half == 0:
+                acc[...] = out
+            elif v == 0:
+                acc[...] += out
+                gx_ref[...] = acc[...]
+            else:
+                parts[v] = (acc[...] + out).astype(jnp.bfloat16)
+        if v in (1, 2):
+            scatter.send_early(v - 1)
+        if v == 3:
+            scatter.send_far()
+    scatter.pass_on()
+    loads[2].wait()
+    loads[3].wait()
+    chunk = 2 * TILE
+
+    def input_chunk(half, index):
+        columns = pl.ds(pl.multiple_of(index * chunk, chunk), chunk)
+        return matmul(at[...], pre[half, :, columns])
+
+    def output_rows(half):
+        return matmul(hidden[half], blocks[...].reshape(wide * rows, D))
+
+    @pl.loop(0, rows_axis)
+    def _(index):
+        give_in[index] = input_chunk(1 - core, index).astype(jnp.bfloat16)
+
+    swap_in = remote(give_in, got_in, sems, 10, peers[-1])
+    swap_in.start()
+    out_rows = output_rows(1 - core)
+    for row in range(rows_axis):
+        give_out[row] = out_rows[row * TILE : row * TILE + units].astype(jnp.bfloat16)
+    swap_out = remote(give_out, got_out, sems, 11, peers[-1])
+    swap_out.start()
+    total = gx_ref[...] + scatter.total()
+    grad_residual, grad_gain = norm_pull(x_ref[...], gain_ref[...], total)
+    gx_ref[...] = g_ref[...] + grad_residual
+    gain_out[...] = grad_gain
+    out_rows = output_rows(core)
+    swap_in.wait_recv()
+
+    @pl.loop(0, rows_axis)
+    def _(index):
+        got_in[index] = (
+            input_chunk(core, index) + got_in[index].astype(jnp.float32)
+        ).astype(jnp.bfloat16)
+
+    store_in = pltpu.make_async_copy(got_in, grad_in, local_sem.at[4])
+    store_in.start()
+    swap_out.wait_recv()
+    for row in range(rows_axis):
+        got_out[row] = (
+            out_rows[row * TILE : row * TILE + units] + got_out[row].astype(jnp.float32)
+        ).astype(jnp.bfloat16)
+    store_out = pltpu.make_async_copy(got_out, grad_out, local_sem.at[5])
+    store_out.start()
+    store_in.wait()
+    store_out.wait()
+    swap_in.wait_send()
+    swap_out.wait_send()
+    gather.finish()
+    scatter.finish()
+
+
+GELU_A = float(np.sqrt(2.0 / np.pi))
+GELU_B = 0.044715
+
+
+def ffn_backward_call(wide, rows_axis, grad, residual, gain_row, kept, call_id):
+    at, pre, hidden, weight = kept
+    rows = residual.shape[0]
+    low = jnp.bfloat16
+    units = FF // (wide * rows_axis * 2)
+    share_in = (rows_axis, D, 2 * TILE)
+    share_out = (rows_axis, units, D)
+    return pl.pallas_call(
+        lambda *refs: ffn_backward_kernel(wide, rows_axis, *refs),
+        out_shape=[
+            jax.ShapeDtypeStruct((rows, D), jnp.float32),
+            jax.ShapeDtypeStruct((1, D), jnp.float32),
+            jax.ShapeDtypeStruct(share_in, low),
+            jax.ShapeDtypeStruct(share_out, low),
+        ],
+        in_specs=[VM, VM, VM, HBM, HBM, HBM, HBM],
+        out_specs=[VM, VM, HBM, HBM],
+        scratch_shapes=[
+            pltpu.VMEM((wide, rows, D), low),
+            pltpu.VMEM(at.shape, low),
+            pltpu.VMEM(pre.shape, low),
+            pltpu.VMEM(hidden.shape, low),
+            pltpu.VMEM(weight.shape, low),
+            pltpu.VMEM((wide, rows, D), low),
+            pltpu.VMEM((3, rows, D), low),
+            pltpu.VMEM((rows, D), jnp.float32),
+            pltpu.VMEM(share_in, low),
+            pltpu.VMEM(share_out, low),
+            pltpu.VMEM(share_in, low),
+            pltpu.VMEM(share_out, low),
+            pltpu.SemaphoreType.DMA((12,)),
+            pltpu.SemaphoreType.DMA((12,)),
+            pltpu.SemaphoreType.DMA((6,)),
+        ],
+        compiler_params=pltpu.CompilerParams(
+            collective_id=call_id, has_side_effects=True, vmem_limit_bytes=VMEM_LIMIT
+        ),
+        name="ffn_backward_%d" % rows,
+    )(grad, residual, gain_row, at, pre, hidden, weight)
+
+
+def plain_hidden_columns(weight):
+    width = weight.shape[1] * 2 // 3
+    return weight[:, :width], weight[:, width:]
+
+
+def plain_ffn_hidden(blocks, weight):
+    w_in, _ = plain_hidden_columns(weight)
+    both = [matmul(block, w_in) for block in blocks]
+    units = w_in.shape[1] // 2
+    return both, [to_low(gated(part[:, :units], part[:, units:])) for part in both]
+
+
+def plain_ffn_forward(residual, gain_row, weight):
+    blocks = gather_wide(to_low(rms_norm(residual, gain_row)))
+    both, hidden = plain_ffn_hidden(blocks, weight)
+    _, w_out = plain_hidden_columns(weight)
+    out = residual + scatter_wide([matmul(part, w_out.T) for part in hidden])
+    return out, (residual, blocks, both, hidden)
+
+
+def plain_ffn_backward(kept, gain_row, weight, grad_out, grad_blocks):
+    residual, blocks, both, hidden = kept
+    w_in, w_out = plain_hidden_columns(weight)
+    units = w_out.shape[1]
+    parts, grad_both = [], []
+    for block, pre in zip(grad_blocks, both):
+        _, pull = jax.vjp(gated, pre[:, :units], pre[:, units:])
+        grad_gate, grad_up = pull(matmul(block, w_out))
+        low = to_low(jnp.concatenate([grad_gate, grad_up], axis=1))
+        grad_both.append(low)
+        parts.append(matmul(low, w_in.T))
+    grad_residual, grad_gain = norm_backward(residual, gain_row, scatter_wide(parts))
+    joined = jnp.concatenate(grad_both, axis=0)
+    grad_in = matmul(jnp.concatenate(blocks, axis=0).T, joined)
+    grad_wout = matmul(jnp.concatenate(grad_blocks, axis=0).T, jnp.concatenate(hidden, axis=0))
+    return grad_out + grad_residual, grad_gain, (grad_in, grad_wout)
+
+
+def plain_reduce_ffn(grads, core, wide, rows):
+    grad_in, grad_wout = grads
+    depth = grad_in.shape[0]
+    both = jnp.concatenate(
+        [grad_in.reshape(depth, rows, -1), grad_wout.reshape(depth, rows, -1)], axis=2
+    )
+    columns = both.shape[2]
+    halves = core_halves(both.reshape(depth, rows * columns), core, wide)
+    halves = to_low(halves).reshape(wide * (depth // wide // 2), rows, columns).transpose(1, 0, 2)
+    summed = lax.psum_scatter(halves, "rows", scatter_dimension=0, tiled=True)[0]
+    blocks = summed.reshape(wide, depth // wide // 2, columns)
+    place = lax.axis_index("wide")
+    out = [lax.dynamic_index_in_dim(blocks, place, 0, keepdims=False)]
+    for v in range(1, wide):
+        block = lax.dynamic_index_in_dim(blocks, place ^ v, 0, keepdims=False)
+        out.append(xor_permute(block, "wide", v))
+    return placed_rows([piece[None] for piece in out], place)
+
+
+def plain_to_section(enc_half, dec_half, core):
+    is_dec = core == 1
+    own = jnp.where(is_dec, dec_half, enc_half)
+    got = xor_permute(jnp.where(is_dec, enc_half, dec_half), "section", 1)
     low, high = jnp.where(is_dec, got, own), jnp.where(is_dec, own, got)
     return jnp.concatenate([low, high], axis=-2).astype(jnp.float32)
+
+
+def plain_shards(
+    enc_embed,
+    dec_embed,
+    out_cot,
+    enc_lengths,
+    dec_lengths,
+    norm_gains,
+    rel_bias,
+    attn_in,
+    attn_out,
+    ffn_in,
+    ffn_out,
+    cross_in,
+    cross_out,
+):
+    core = lax.axis_index("section")
+    place = lax.axis_index("wide")
+    wide, rows = lax.axis_size("wide"), lax.axis_size("rows")
+    depth = attn_in.shape[1]
+    unit = FF // (wide * rows)
+
+    small = jnp.concatenate([norm_gains[0].reshape(-1), rel_bias[0].reshape(-1)])
+    enc_small, dec_small = both_sections(small, core)
+    gains = [each[: 3 * D].reshape(3, D) for each in (enc_small, dec_small)]
+    biases = [each[3 * D :].reshape(NB, H) for each in (enc_small, dec_small)]
+
+    attn_shard = jnp.concatenate([attn_in[0], attn_out[0].T, cross_in[0], cross_out[0]], axis=1)
+    attn_own = placed_rows(gather_wide(attn_shard), place)
+    ffn_blocks = jnp.concatenate(
+        [
+            ffn_in[0].reshape(depth, 2 * rows, wide, unit).transpose(2, 0, 1, 3).reshape(wide, depth, -1),
+            ffn_out[0].T.reshape(depth, rows, wide, unit).transpose(2, 0, 1, 3).reshape(wide, depth, -1),
+        ],
+        axis=2,
+    )
+    ffn_got = [lax.dynamic_index_in_dim(ffn_blocks, place, 0, keepdims=False)]
+    for v in range(1, wide):
+        block = lax.dynamic_index_in_dim(ffn_blocks, place ^ v, 0, keepdims=False)
+        ffn_got.append(xor_permute(block, "wide", v))
+    ffn_own = placed_rows(ffn_got, place)
+    attn_enc, attn_dec = both_sections(attn_own, core)
+    ffn_enc, ffn_dec = both_sections(ffn_own, core)
+    memory_weight = attn_enc[:, 4 * HD :]
+    cross_w_in, cross_w_out = attn_dec[:, 4 * HD : 5 * HD], attn_dec[:, 5 * HD :]
+
+    def own_row(array):
+        return lax.dynamic_index_in_dim(array[:, 0], core, 0, keepdims=False)
+
+    enc_row = own_row(enc_embed).astype(jnp.float32)
+    dec_row = own_row(dec_embed).astype(jnp.float32)
+    cot_row = own_row(out_cot)
+    enc_items = item_ids(own_row(enc_lengths), LE)
+    dec_items = item_ids(own_row(dec_lengths), LD)
+    enc_hot, dec_hot = one_hot(LE, True), one_hot(LD, False)
+    enc_bias = jnp.einsum("qkb,bh->hqk", enc_hot, biases[0], precision=HIGHEST)
+    dec_bias = jnp.einsum("qkb,bh->hqk", dec_hot, biases[1], precision=HIGHEST)
+    causal = jnp.arange(LD)[:, None] >= jnp.arange(LD)[None, :]
+
+    cot_blocks = gather_wide(cot_row)
+    x1, enc_self = self_forward(
+        enc_row, gains[0][0], attn_enc, enc_bias, enc_items[:, None] == enc_items[None, :]
+    )
+    y1, dec_self = self_forward(
+        dec_row,
+        gains[1][0],
+        attn_dec,
+        dec_bias,
+        (dec_items[:, None] == dec_items[None, :]) & causal,
+    )
+    x2, enc_ffn = plain_ffn_forward(x1, gains[0][1], ffn_enc)
+    memory = to_low(rms_norm(x2, gains[0][2]))
+    memory_kv = to_low(matmul(memory, memory_weight))
+    cross_normed = to_low(rms_norm(y1, gains[1][1]))
+    queries = to_low(matmul(cross_normed, cross_w_in))
+    context, weights, low_weights = attend_forward(
+        queries,
+        memory_kv[:, :HD],
+        memory_kv[:, HD:],
+        0.0,
+        dec_items[:, None] == enc_items[None, :],
+    )
+    y2 = y1 + matmul(context, cross_w_out.T)
+    y3, dec_ffn = plain_ffn_forward(y2, gains[1][2], ffn_dec)
+
+    g2, dec_ffn_gain, dec_ffn_grads = plain_ffn_backward(
+        dec_ffn, gains[1][2], ffn_dec, cot_row.astype(jnp.float32), cot_blocks
+    )
+    dec_ffn_share = plain_reduce_ffn(dec_ffn_grads, core, wide, rows)
+    g2_low = to_low(g2)
+    grad_cross_out = matmul(g2_low.T, context)
+    grad_context = to_low(matmul(g2_low, cross_w_out))
+    grad_queries, grad_keys, grad_values, _ = attend_backward(
+        queries, memory_kv[:, :HD], memory_kv[:, HD:], weights, low_weights, grad_context
+    )
+    grad_query_low = to_low(grad_queries)
+    grad_kv = to_low(jnp.concatenate([grad_keys, grad_values], axis=1))
+    grad_x2, enc_final_gain = norm_backward(x2, gains[0][2], matmul(grad_kv, memory_weight.T))
+    grad_x1, enc_ffn_gain, enc_ffn_grads = plain_ffn_backward(
+        enc_ffn, gains[0][1], ffn_enc, grad_x2, gather_wide(to_low(grad_x2))
+    )
+    enc_ffn_share = plain_reduce_ffn(enc_ffn_grads, core, wide, rows)
+
+    grad_cross_in = matmul(cross_normed.T, grad_query_low)
+    grad_memory = matmul(memory.T, grad_kv)
+    from_cross, dec_cross_gain = norm_backward(
+        y1, gains[1][1], matmul(grad_query_low, cross_w_in.T)
+    )
+    grad_y, dec_self_gain, dec_win, dec_wout, dec_bias_grad = self_backward(
+        dec_self, gains[1][0], attn_dec, dec_hot, g2 + from_cross
+    )
+    dec_attn_share = reduce_attn(
+        jnp.concatenate([dec_win, dec_wout, grad_cross_in, grad_cross_out], axis=1),
+        core,
+        wide,
+        rows,
+    )
+    grad_x, enc_self_gain, enc_win, enc_wout, enc_bias_grad = self_backward(
+        enc_self, gains[0][0], attn_enc, enc_hot, grad_x1
+    )
+    enc_attn_share = reduce_attn(
+        jnp.concatenate([enc_win, enc_wout, grad_memory], axis=1), core, wide, rows
+    )
+
+    small_grads = jnp.stack(
+        [
+            jnp.concatenate(
+                [enc_self_gain, enc_ffn_gain, enc_final_gain, enc_bias_grad.reshape(-1)]
+            ),
+            jnp.concatenate(
+                [dec_self_gain, dec_cross_gain, dec_ffn_gain, dec_bias_grad.reshape(-1)]
+            ),
+        ]
+    )
+    small_total = lax.psum(small_grads, ("section", "wide", "rows"))
+    small_own = jnp.where(core == 1, small_total[1], small_total[0])
+
+    attn_share = plain_to_section(enc_attn_share, dec_attn_share, core)
+    ffn_share = plain_to_section(enc_ffn_share, dec_ffn_share, core)
+    in_width = 2 * FF // rows // wide
+    ffn_in_grad = (
+        ffn_share[:, :, :in_width]
+        .reshape(wide, depth, 2, unit)
+        .transpose(1, 2, 0, 3)
+        .reshape(depth, 2 * FF // rows)
+    )
+    ffn_out_grad = ffn_share[:, :, in_width:].transpose(0, 2, 1).reshape(FF // rows, depth)
+    widths = [3 * HD // rows, HD // rows, HD // rows]
+    edges = np.cumsum([0] + widths + [HD // rows])
+    win, wout, cin, cout = [attn_share[:, a:b] for a, b in zip(edges[:-1], edges[1:])]
+
+    half = D // 2
+
+    def by_half(own):
+        halves = jnp.stack([own[:, :half], own[:, half:]])
+        keep = lax.dynamic_index_in_dim(halves, core, 0, keepdims=False)
+        send = lax.dynamic_index_in_dim(halves, 1 - core, 0, keepdims=False)
+        got = xor_permute(send, "section", 1)
+        is_dec = core == 1
+        return jnp.stack([jnp.where(is_dec, got, keep), jnp.where(is_dec, keep, got)])[:, None]
+
+    return (
+        by_half(to_low(y3)),
+        by_half(grad_x),
+        by_half(grad_y),
+        small_own[: 3 * D].reshape(1, 3, D),
+        small_own[3 * D :].reshape(1, NB, H),
+        win[None],
+        wout.T[None],
+        ffn_in_grad[None],
+        ffn_out_grad[None],
+        cin[None],
+        cout[None],
+    )
 
 
 def shards(
@@ -323,20 +1030,10 @@
 
     attn_shard = jnp.concatenate([attn_in[0], attn_out[0].T, cross_in[0], cross_out[0]], axis=1)
     attn_own = placed_rows(gather_wide(attn_shard), place)
-    ffn_blocks = jnp.concatenate(
-        [
-            ffn_in[0].reshape(depth, 2 * rows, wide, unit).transpose(2, 0, 1, 3).reshape(wide, depth, -1),
-            ffn_out[0].T.reshape(depth, rows, wide, unit).transpose(2, 0, 1, 3).reshape(wide, depth, -1),
-        ],
-        axis=2,
-    )
-    ffn_got = [lax.dynamic_index_in_dim(ffn_blocks, place, 0, keepdims=False)]
-    for v in range(1, wide):
-        block = lax.dynamic_index_in_dim(ffn_blocks, place ^ v, 0, keepdims=False)
-        ffn_got.append(xor_permute(block, "wide", v))
-    ffn_own = placed_rows(ffn_got, place)
+    enc_blocks, dec_blocks = prepare_weights(wide, rows, ffn_in, ffn_out)
+    enc_pieces = [enc_blocks[0]] + [xor_permute(enc_blocks[v], "wide", v) for v in range(1, wide)]
+    dec_pieces = [dec_blocks[0]] + [xor_permute(dec_blocks[v], "wide", v) for v in range(1, wide)]
     attn_enc, attn_dec = both_sections(attn_own, core)
-    ffn_enc, ffn_dec = both_sections(ffn_own, core)
     memory_weight = attn_enc[:, 4 * HD :]
     cross_w_in, cross_w_out = attn_dec[:, 4 * HD : 5 * HD], attn_dec[:, 5 * HD :]
 
@@ -353,7 +1050,6 @@
     dec_bias = jnp.einsum("qkb,bh->hqk", dec_hot, biases[1], precision=HIGHEST)
     causal = jnp.arange(LD)[:, None] >= jnp.arange(LD)[None, :]
 
-    cot_blocks = gather_wide(cot_row)
     x1, enc_self = self_forward(
         enc_row, gains[0][0], attn_enc, enc_bias, enc_items[:, None] == enc_items[None, :]
     )
@@ -364,7 +1060,7 @@
         dec_bias,
         (dec_items[:, None] == dec_items[None, :]) & causal,
     )
-    x2, enc_ffn = ffn_forward(x1, gains[0][1], ffn_enc)
+    x2, *enc_ffn = ffn_forward_call(wide, x1, gains[0][1:2], enc_pieces, 2)
     memory = to_low(rms_norm(x2, gains[0][2]))
     memory_kv = to_low(matmul(memory, memory_weight))
     cross_normed = to_low(rms_norm(y1, gains[1][1]))
@@ -377,12 +1073,12 @@
         dec_items[:, None] == enc_items[None, :],
     )
     y2 = y1 + matmul(context, cross_w_out.T)
-    y3, dec_ffn = ffn_forward(y2, gains[1][2], ffn_dec)
-
-    g2, dec_ffn_gain, dec_ffn_grads = ffn_backward(
-        dec_ffn, gains[1][2], ffn_dec, cot_row.astype(jnp.float32), cot_blocks
-    )
-    dec_ffn_share = reduce_ffn(dec_ffn_grads, core, wide, rows)
+    y3, *dec_ffn = ffn_forward_call(wide, y2, gains[1][2:3], dec_pieces, 3)
+
+    g2, dec_ffn_gain, *dec_ffn_grads = ffn_backward_call(
+        wide, rows, cot_row.astype(jnp.float32), y2, gains[1][2:3], dec_ffn, 4
+    )
+    dec_ffn_share = reduce_ffn(*dec_ffn_grads, wide)
     g2_low = to_low(g2)
     grad_cross_out = matmul(g2_low.T, context)
     grad_context = to_low(matmul(g2_low, cross_w_out))
@@ -392,11 +1088,10 @@
     grad_query_low = to_low(grad_queries)
     grad_kv = to_low(jnp.concatenate([grad_keys, grad_values], axis=1))
     grad_x2, enc_final_gain = norm_backward(x2, gains[0][2], matmul(grad_kv, memory_weight.T))
-    grad_x1, enc_ffn_gain, enc_ffn_grads = ffn_backward(
-        enc_ffn, gains[0][1], ffn_enc, grad_x2, gather_wide(to_low(grad_x2))
-    )
-    enc_ffn_share = reduce_ffn(enc_ffn_grads, core, wide, rows)
-
+    grad_x1, enc_ffn_gain, *enc_ffn_grads = ffn_backward_call(
+        wide, rows, grad_x2, x1, gains[0][1:2], enc_ffn, 5
+    )
+    enc_ffn_share = reduce_ffn(*enc_ffn_grads, wide)
     grad_cross_in = matmul(cross_normed.T, grad_query_low)
     grad_memory = matmul(memory.T, grad_kv)
     from_cross, dec_cross_gain = norm_backward(
@@ -421,26 +1116,28 @@
     small_grads = jnp.stack(
         [
             jnp.concatenate(
-                [enc_self_gain, enc_ffn_gain, enc_final_gain, enc_bias_grad.reshape(-1)]
+                [enc_self_gain, enc_ffn_gain[0], enc_final_gain, enc_bias_grad.reshape(-1)]
             ),
             jnp.concatenate(
-                [dec_self_gain, dec_cross_gain, dec_ffn_gain, dec_bias_grad.reshape(-1)]
+                [dec_self_gain, dec_cross_gain, dec_ffn_gain[0], dec_bias_grad.reshape(-1)]
             ),
         ]
     )
     small_total = lax.psum(small_grads, ("section", "wide", "rows"))
     small_own = jnp.where(core == 1, small_total[1], small_total[0])
 
-    attn_share = to_section(enc_attn_share, dec_attn_share, core)
-    ffn_share = to_section(enc_ffn_share, dec_ffn_share, core)
-    in_width = 2 * FF // rows // wide
+    attn_share = to_section(enc_attn_share, dec_attn_share, core).astype(jnp.float32)
+    attn_share = attn_share.reshape(depth, attn_share.shape[2])
+    in_share = to_section(enc_ffn_share[0], dec_ffn_share[0], core)
+    out_share = to_section(enc_ffn_share[1], dec_ffn_share[1], core)
+    units = unit // 2
     ffn_in_grad = (
-        ffn_share[:, :, :in_width]
-        .reshape(wide, depth, 2, unit)
-        .transpose(1, 2, 0, 3)
+        in_share.reshape(2, wide, depth, 2, TILE)[..., :units]
+        .transpose(2, 3, 1, 0, 4)
         .reshape(depth, 2 * FF // rows)
-    )
-    ffn_out_grad = ffn_share[:, :, in_width:].transpose(0, 2, 1).reshape(FF // rows, depth)
+        .astype(jnp.float32)
+    )
+    ffn_out_grad = out_share.transpose(1, 0, 2, 3).reshape(FF // rows, depth).astype(jnp.float32)
     widths = [3 * HD // rows, HD // rows, HD // rows]
     edges = np.cumsum([0] + widths + [HD // rows])
     win, wout, cin, cout = [attn_share[:, a:b] for a, b in zip(edges[:-1], edges[1:])]
@@ -486,8 +1183,10 @@
         P("section", "wide", None),
         P("section", "wide", None),
     )
+    wide, rows = mesh.shape["wide"], mesh.shape["rows"]
+    in_tiles = D // wide % 16 == 0 and FF // (wide * rows) % 32 == 0
     return jax.shard_map(
-        shards,
+        shards if wide == 4 and rows == 4 and in_tiles else plain_shards,
         mesh=mesh,
         in_specs=placed,
         out_specs=(

time: 901 us -> 723 us (0.80)
  Pallas kernels: 0 us -> 251 us
  local copies, waits for them, and re-layouts: 300 us -> 88.8 us
  matrix products: 166 us -> 69.7 us
  other arithmetic: 121 us -> 68.9 us
  waiting for transfers between devices: 180 us -> 133 us
  starting transfers between devices: 61.3 us -> 44.3 us
    pallas_call x0 -> x5, Pallas kernels: none -> 251 us  [the longest x2 124 us: ffn_forward_call(): pl.pallas_call(lambda *refs: ffn_forward_kernel(wide, *refs), out_shape=[...]
    dot_general x57 -> x21, matrix products: 137 us -> 43.6 us  [matmul(): return jnp.dot(left_side, right_side, preferred_element_type=jnp.float32)]
    ppermute x65 -> x40, waiting for transfers between devices: 153 us -> 106 us  [xor_permute(): return lax.ppermute(value, axis, [(i, i ^ distance) for i in range(count)])]
    concatenate x8 -> x2, local copies, waits for them, and re-layouts: 33.2 us -> 0.16 us  [the longest x1 0.08 us: shards(): jnp.concatenate([enc_self_gain, enc_ffn_gain[0], enc_final_gain, enc_bias...]
    convert_element_type x5 -> x3, local copies, waits for them, and re-layouts: 33.9 us -> 1.95 us  [to_low(): return tensor.astype(jnp.bfloat16)]
    unnamed x4 -> x8, waiting for transfers between devices: 0.07 us -> 27.3 us
    reduce_scatter x4, waiting for transfers between devices: 26.8 us -> 0.03 us  [the longest x2 0.02 us: reduce_ffn(): lax.psum_scatter(share_in, 'rows', scatter_dimension=0, tiled=True)[0]]
    another operation x10 -> x8, local copies, waits for them, and re-layouts: 27 us -> 0.39 us
  transfers between devices with their start and end apart: 69 -> 46, of which waited for: 27 -> 16; matrix products, arithmetic and copies ran while one was open for 60% -> 25% of each run, Pallas kernels for 0% -> 15%
where the time goes in v2:
time: 723 us; the launch traced here: 713 us
  Pallas kernels  251 us (35%)
  waiting for transfers between devices  133 us (18%)
  local copies, waits for them, and re-layouts  88.8 us (12%)
  matrix products  69.7 us (10%)
  other arithmetic  68.9 us (10%)
  starting transfers between devices  44.3 us (6%)
  blocking collectives  41.3 us (6%)
  between operations  16.1 us (2%)
    pallas_call x2, Pallas kernels, ffn_forward_call(): pl.pallas_call(lambda *refs: ffn_forward_kernel(wide, *refs), out_shape=[...  124 us
    pallas_call x2, Pallas kernels, ffn_backward_call(): pl.pallas_call(lambda *refs: ffn_backward_kernel(wide, rows_axis, *refs),...  111 us
    ppermute x40, waiting for transfers between devices, xor_permute(): return lax.ppermute(value, axis, [(i, i ^ distance) for i in range(count)])  106 us
    ppermute x40, starting transfers between devices, xor_permute(): return lax.ppermute(value, axis, [(i, i ^ distance) for i in range(count)])  43.7 us
    dot_general x21, matrix products, matmul(): return jnp.dot(left_side, right_side, preferred_element_type=jnp.float32)  43.6 us
    psum x1, blocking collectives, shards(): small_total = lax.psum(small_grads, ('section', 'wide', 'rows'))  41.3 us
    unnamed x8, waiting for transfers between devices  27.3 us
    unnamed x156, local copies, waits for them, and re-layouts  23.4 us
  transfers between devices with their start and end apart: 46, of which 16 were waited for; matrix products, arithmetic and copies ran while one was open for 25% of the time, Pallas kernels for 15%

profile of v2, /device:TPU:0, one launch (start us, length us, event | category | flops | bytes accessed | tf_op | source)
XLA Modules:
  0.0 713.3 jit_solution(14767235051146579783)
XLA Ops:
  7.3 3.2 broadcast_in_dim.84
  11.9 3.0 collective-permute-start.2
  16.4 35.5 %collective-permute-done.2 = bf16[368,2304]{1,0:T(8,128)(2,1)S(1)} collective-permute-done((bf16[368,2304]{1,0:T(8,128)(2,1)S(1)}, bf16[368,2304]{1,0:T(8,128)(2,1)S(1)}, u32[]{:S(2)}, u32[]{:S(2)}) %collective-permute-start.2) | collective-permute-done | bytes 1695776 | tf_op jit(solution)/shard_map/ppermute | solution.py:123
  58.3 2.8 constant_dynamic-update-slice_fusion.1
  62.4 10.8 %collective-permute-done.4 = bf16[184,2304]{1,0:T(8,128)(2,1)} collective-permute-done((bf16[184,2304]{1,0:T(8,128)(2,1)}, bf16[184,2304]{1,0:T(8,128)(2,1)}, u32[]{:S(2)}, u32[]{:S(2)}) %collective-permute-start.4) | collective-permute-done | bytes 847904 | tf_op jit(solution)/shard_map/ppermute | solution.py:123
  73.2 3.4 collective-permute-done.3
  76.6 2.7 maximum_dynamic-update-slice_fusion
  80.3 4.5 copy.365.refs_1_
  84.8 16.1 %prepare_weights.1 = (bf16[368,1536]{1,0:T(8,128)(2,1)}, bf16[368,1536]{1,0:T(8,128)(2,1)}, bf16[368,1536]{1,0:T(8,128)(2,1)}, bf16[368,1536]{1,0:T(8,128)(2,1)}...) custom-call(bf16[1,368,7168]{2,1,0:T(8,128)(2,1)} %refs_0_.1, ...), custom_call_target="tpu_custom_call" | custom-call | tf_op jit(solution)/shard_map/prepare_weights/pallas_call | solution.py:459
  107.1 2.5 iota_compare_fusion
  110.8 13.4 %copy.361 = pred[256,256,32]{1,2,0:T(32,128)(4,1)} copy(pred[256,256,32]{0,2,1:T(32,128)(4,1)} %iota_compare_fusion) | data formatting | bytes 4194304 | tf_op jit(solution)/shard_map/eq | solution.py:47
  125.7 4.5 fusion.113
  134.8 8.9 %broadcast_select_fusion = (bf16[1472,2304]{1,0:T(8,128)(2,1)}, bf16[1472,2304]{1,0:T(8,128)(2,1)S(1)}) fusion(bf16[1472,2304]{1,0:T(8,128)(2,1)} %collective-permute-done.5, bf16[1472,2304]{1,0:T(8,128)(2,1)} %maximum_dynamic-update-slice_fusion, pred[]{:T(512)S(6)} %eq.88), kind=kLoop, calls=%fused_computation.9 | loop fusion | flops 6782976 | bytes 27131904 | tf_op jit(solution)/shard_map/jit(_where)/select_n | solution.py:167
  143.7 2.8 copy-done.3
  149.4 3.2 fusion.12
  156.0 3.5 fusion.141
  159.5 2.4 convolution_convert_fusion.13
  163.8 3.0 convert_add_fusion.2.refs_0_.refs_1_
  168.5 93.6 %ffn_forward_256.1 = (f32[256,1472]{1,0:T(8,128)}, bf16[1472,1024]{1,0:T(8,128)(2,1)}, bf16[2,1024,1024]{2,1,0:T(8,128)(2,1)}, bf16[2,512,1024]{2,1,0:T(8,128)(2,1)}, bf16[2,1472,1536]{2,1,0:T(8,128)(2,1)}) custom-call(f32[256,1472]{1,0:T(8,128)} %convert_add_fusion.2.refs_0_.refs_1_, f32[1,1472]{1,0:T(1,128)} %slice.306.refs_1_.refs_2_, ...), custom_call_target="tpu_custom_call" | custom-call | tf_op jit(solution)/shard_map/ffn_forward_256/pallas_call | solution.py:563
  263.6 2.9 fusion.35
  271.3 2.5 convolution_add_fusion.refs_0_.refs_1_
  274.9 30.2 %ffn_forward_64.1 = (f32[64,1472]{1,0:T(8,128)}, bf16[1472,256]{1,0:T(8,128)(2,1)}, bf16[2,256,1024]{2,1,0:T(8,128)(2,1)}, bf16[2,512,256]{2,1,0:T(8,128)(2,1)}, bf16[2,1472,1536]{2,1,0:T(8,128)(2,1)}) custom-call(f32[64,1472]{1,0:T(8,128)} %convolution_add_fusion.refs_0_.refs_1_, f32[1,1472]{1,0:T(1,128)} %slice.315.refs_1_.refs_2_, ...), custom_call_target="tpu_custom_call" | custom-call | tf_op jit(solution)/shard_map/ffn_forward_64/pallas_call | solution.py:563
  305.1 32.7 %ffn_backward_64.1 = (f32[64,1472]{1,0:T(8,128)}, f32[1,1472]{1,0:T(1,128)}, bf16[4,1472,256]{2,1,0:T(8,128)(2,1)}, bf16[4,112,1472]{2,1,0:T(8,128)(2,1)}) custom-call(f32[64,1472]{1,0:T(8,128)} %bitcast_convert_fusion.1.refs_0_, f32[64,1472]{1,0:T(8,128)} %convolution_add_fusion.refs_0_.refs_1_, f32[1,1472]{1,0:T(1,128)} %slice.315.refs_1_.refs_2_, ...), custom_call_target="tpu_custom_call" | custom-call | tf_op jit(solution)/shard_map/ffn_backward_64/pallas_call | solution.py:731
  345.5 2.8 multiply_reduce_fusion
  349.8 78.6 %ffn_backward_256.1 = (f32[256,1472]{1,0:T(8,128)}, f32[1,1472]{1,0:T(1,128)}, bf16[4,1472,256]{2,1,0:T(8,128)(2,1)}, bf16[4,112,1472]{2,1,0:T(8,128)(2,1)}) custom-call(f32[256,1472]{1,0:T(8,128)} %add_add_fusion.1.refs_0_, f32[256,1472]{1,0:T(8,128)} %convert_add_fusion.2.refs_0_.refs_1_, f32[1,1472]{1,0:T(1,128)} %slice.306.refs_1_.refs_2_, ...), custom_call_target="tpu_custom_call" | custom-call | tf_op jit(solution)/shard_map/ffn_backward_256/pallas_call | solution.py:731
  428.4 3.0 convolution_convert_fusion.7
  433.1 3.1 convolution_convert_fusion.10
  446.2 4.6 fusion.30
  451.1 4.3 convert_bitcast_fusion.2
  466.1 3.2 fusion.74
  473.4 2.7 convolution_convert_fusion.6
  483.3 3.8 pad_maximum_fusion
  493.5 41.3 %psum.7 = f32[2,4608]{1,0:T(2,128)S(1)} all-reduce(f32[2,4608]{1,0:T(2,128)S(1)} %pad_maximum_fusion.18), channel_id=1, replica_groups=mesh['section'=2,'wide'=4,'rows'=4] {'section','wide','rows'}, use_global_device_ids=true, to_apply=%region_25.26 | all-reduce | flops 9216 | bytes 73728 | tf_op jit(solution)/shard_map/psum | solution.py:1126
  537.8 3.2 pad_maximum_fusion.1
  542.1 3.9 dynamic-slice_bitcast_fusion
  558.9 2.7 collective-permute-done.36
  564.9 3.2 collective-permute-done.37
  569.9 3.6 collective-permute-done.38
  574.4 4.2 convert_add_fusion.1
  581.1 2.6 convert_add_fusion
  585.6 6.3 collective-permute-done.16
  594.7 6.7 collective-permute-done.21
  606.2 13.4 %collective-permute-done.19 = bf16[184,2304]{1,0:T(8,128)(2,1)S(1)} collective-permute-done((bf16[184,2304]{1,0:T(8,128)(2,1)S(1)}, bf16[184,2304]{1,0:T(8,128)(2,1)S(1)}, u32[]{:S(2)}, u32[]{:S(2)}) %collective-permute-start.19) | collective-permute-done | bytes 847904 | tf_op jit(solution)/shard_map/ppermute | solution.py:123
  629.5 7.3 %collective-permute-done.24 = bf16[184,2304]{1,0:T(8,128)(2,1)} collective-permute-done((bf16[184,2304]{1,0:T(8,128)(2,1)}, bf16[184,2304]{1,0:T(8,128)(2,1)}, u32[]{:S(2)}, u32[]{:S(2)}) %collective-permute-start.24) | collective-permute-done | bytes 847904 | tf_op jit(solution)/shard_map/ppermute | solution.py:123
  655.8 4.6 collective-permute-done.27
  661.7 3.7 collective-permute-done.30
  665.4 27.2 %reduce-scatter.21.cloned.1.call-done = bf16[1,184,576]{2,1,0:T(8,128)(2,1)} async-done(((bf16[4,184,576]{2,1,0:T(8,128)(2,1)}), bf16[1,184,576]{2,1,0:T(8,128)(2,1)}) %reduce-scatter.21.cloned.1.call-update) | async-done | bytes 211984
  702.9 3.4 copy.426
  (449 shorter events, 165.3 us)
Async XLA Ops:
  7.2 97.5 %copy-start = (bf16[2,1,256,1472]{2,3,1,0:T(8,128)(2,1)S(1)}, bf16[2,1,256,1472]{2,3,1,0:T(8,128)(2,1)}, u32[]{:S(2)}) copy-start(bf16[2,1,256,1472]{2,3,1,0:T(8,128)(2,1)} %param.15) | copy-start | bytes 4521988
  7.2 543.2 %reduce-scatter.15.cloned.1.call-start = ((), (), s32[]{:S(2)}) async-start(), calls=%async_computation.8 | async-start | bytes 1720320 | tf_op jit(solution)/shard_map/reduce_scatter | solution.py:232
  11.9 40.0 %collective-permute-start.2 = (bf16[368,2304]{1,0:T(8,128)(2,1)S(1)}, bf16[368,2304]{1,0:T(8,128)(2,1)S(1)}, u32[]{:S(2)}, u32[]{:S(2)}) collective-permute-start(bf16[368,2304]{1,0:T(8,128)(2,1)S(1)} %get-tuple-element.129), channel_id=1, source_target_pairs={{0,8},{4,12},{8,0},{12,4},{1,9},{5,13},{9,1},{13,5},{2,10},{6,14},... | collective-permute-start | bytes 5087240 | tf_op jit(solution)/shard_map/ppermute | solution.py:123
  14.9 39.8 %collective-permute-start.1 = (bf16[368,2304]{1,0:T(8,128)(2,1)S(1)}, bf16[368,2304]{1,0:T(8,128)(2,1)S(1)}, u32[]{:S(2)}, u32[]{:S(2)}) collective-permute-start(bf16[368,2304]{1,0:T(8,128)(2,1)S(1)} %get-tuple-element.129), channel_id=1, source_target_pairs={{0,4},{4,0},{8,12},{12,8},{1,5},{5,1},{9,13},{13,9},{2,6},{6,2},{1... | collective-permute-start | bytes 5087240 | tf_op jit(solution)/shard_map/ppermute | solution.py:123
  52.9 20.4 %collective-permute-start.4 = (bf16[184,2304]{1,0:T(8,128)(2,1)}, bf16[184,2304]{1,0:T(8,128)(2,1)}, u32[]{:S(2)}, u32[]{:S(2)}) collective-permute-start(bf16[184,2304]{1,0:T(8,128)(2,1)} %slice.362), channel_id=1, source_target_pairs={{0,4},{4,0},{8,12},{12,8},{1,5},{5,1},{9,13},{13,9},{2,6},{6,2},{1... | collective-permute-start | bytes 2543624 | tf_op jit(solution)/shard_map/ppermute | solution.py:123
  56.8 19.8 %collective-permute-start.3 = (bf16[184,2304]{1,0:T(8,128)(2,1)}, bf16[184,2304]{1,0:T(8,128)(2,1)}, u32[]{:S(2)}, u32[]{:S(2)}) collective-permute-start(bf16[184,2304]{1,0:T(8,128)(2,1)} %slice.361), channel_id=1, source_target_pairs={{0,8},{4,12},{8,0},{12,4},{1,9},{5,13},{9,1},{13,5},{2,10},{6,14},... | collective-permute-start | bytes 2543624 | tf_op jit(solution)/shard_map/ppermute | solution.py:123
  79.3 54.0 %collective-permute-start.5 = (bf16[1472,2304]{1,0:T(8,128)(2,1)}, bf16[1472,2304]{1,0:T(8,128)(2,1)}, u32[]{:S(2)}, u32[]{:S(2)}) collective-permute-start(bf16[1472,2304]{1,0:T(8,128)(2,1)} %maximum_dynamic-update-slice_fusion), channel_id=1, source_target_pairs={{0,16},{16,0},{1,17},{17,1},{2,18},{18,2},{3,19},{19,3},{4,20},{20... | collective-permute-start | bytes 20348936 | tf_op jit(solution)/shard_map/ppermute | solution.py:123
  79.8 44.5 %collective-permute-start = (f32[4608]{0:T(1024)S(1)}, f32[4608]{0:T(1024)S(1)}, u32[]{:S(2)}, u32[]{:S(2)}) collective-permute-start(f32[4608]{0:T(1024)S(1)} %pad_maximum_fusion.19), channel_id=1, source_target_pairs={{0,16},{16,0},{1,17},{17,1},{2,18},{18,2},{3,19},{19,3},{4,20},{20... | collective-permute-start | bytes 55304 | tf_op jit(solution)/shard_map/ppermute | solution.py:123
  101.0 65.9 %collective-permute-start.6 = (bf16[368,1536]{1,0:T(8,128)(2,1)}, bf16[368,1536]{1,0:T(8,128)(2,1)}, u32[]{:S(2)}, u32[]{:S(2)}) collective-permute-start(bf16[368,1536]{1,0:T(8,128)(2,1)} %get-tuple-element.38), channel_id=1, source_target_pairs={{0,4},{4,0},{8,12},{12,8},{1,5},{5,1},{9,13},{13,9},{2,6},{6,2},{1... | collective-permute-start | bytes 3391496 | tf_op jit(solution)/shard_map/ppermute | solution.py:123
  101.5 67.0 %collective-permute-start.7 = (bf16[368,1536]{1,0:T(8,128)(2,1)}, bf16[368,1536]{1,0:T(8,128)(2,1)}, u32[]{:S(2)}, u32[]{:S(2)}) collective-permute-start(bf16[368,1536]{1,0:T(8,128)(2,1)} %get-tuple-element.39), channel_id=1, source_target_pairs={{0,8},{4,12},{8,0},{12,4},{1,9},{5,13},{9,1},{13,5},{2,10},{6,14},... | collective-permute-start | bytes 3391496 | tf_op jit(solution)/shard_map/ppermute | solution.py:123
  102.9 65.5 %collective-permute-start.8 = (bf16[368,1536]{1,0:T(8,128)(2,1)}, bf16[368,1536]{1,0:T(8,128)(2,1)}, u32[]{:S(2)}, u32[]{:S(2)}) collective-permute-start(bf16[368,1536]{1,0:T(8,128)(2,1)} %get-tuple-element.40), channel_id=1, source_target_pairs={{0,12},{4,8},{8,4},{12,0},{1,13},{5,9},{9,5},{13,1},{2,14},{6,10},... | collective-permute-start | bytes 3391496 | tf_op jit(solution)/shard_map/ppermute | solution.py:123
  124.2 149.6 %collective-permute-start.9 = (bf16[368,1536]{1,0:T(8,128)(2,1)}, bf16[368,1536]{1,0:T(8,128)(2,1)}, u32[]{:S(2)}, u32[]{:S(2)}) collective-permute-start(bf16[368,1536]{1,0:T(8,128)(2,1)} %get-tuple-element.43), channel_id=1, source_target_pairs={{0,4},{4,0},{8,12},{12,8},{1,5},{5,1},{9,13},{13,9},{2,6},{6,2},{1... | collective-permute-start | bytes 3391496 | tf_op jit(solution)/shard_map/ppermute | solution.py:123
  133.4 140.5 %collective-permute-start.10 = (bf16[368,1536]{1,0:T(8,128)(2,1)}, bf16[368,1536]{1,0:T(8,128)(2,1)}, u32[]{:S(2)}, u32[]{:S(2)}) collective-permute-start(bf16[368,1536]{1,0:T(8,128)(2,1)} %get-tuple-element.44), channel_id=1, source_target_pairs={{0,8},{4,12},{8,0},{12,4},{1,9},{5,13},{9,1},{13,5},{2,10},{6,14},... | collective-permute-start | bytes 3391496 | tf_op jit(solution)/shard_map/ppermute | solution.py:123
  166.9 107.0 %collective-permute-start.11 = (bf16[368,1536]{1,0:T(8,128)(2,1)}, bf16[368,1536]{1,0:T(8,128)(2,1)S(1)}, u32[]{:S(2)}, u32[]{:S(2)}) collective-permute-start(bf16[368,1536]{1,0:T(8,128)(2,1)} %get-tuple-element.45), channel_id=1, source_target_pairs={{0,12},{4,8},{8,4},{12,0},{1,13},{5,9},{9,5},{13,1},{2,14},{6,10},... | collective-permute-start | bytes 3391496 | tf_op jit(solution)/shard_map/ppermute | solution.py:123
  441.5 105.4 %collective-permute-start.12 = (bf16[64,736]{1,0:T(8,128)(2,1)}, bf16[64,736]{1,0:T(8,128)(2,1)}, u32[]{:S(2)}, u32[]{:S(2)}) collective-permute-start(bf16[64,736]{1,0:T(8,128)(2,1)} %fusion.99), channel_id=1, source_target_pairs={{0,16},{16,0},{1,17},{17,1},{2,18},{18,2},{3,19},{19,3},{4,20},{20... | collective-permute-start | bytes 282632 | tf_op jit(solution)/shard_map/ppermute | solution.py:123
  450.8 103.9 %reduce-scatter.17.cloned.1.call-start = ((), (), s32[]{:S(2)}) async-start(), calls=%async_computation.9 | async-start | bytes 1720320 | tf_op jit(solution)/shard_map/reduce_scatter | solution.py:232
  458.0 168.0 %collective-permute-start.13 = (f32[256,736]{0,1:T(8,128)}, f32[256,736]{0,1:T(8,128)}, u32[]{:S(2)}, u32[]{:S(2)}) collective-permute-start(f32[256,736]{0,1:T(8,128)} %bitcast.430), channel_id=1, source_target_pairs={{0,16},{16,0},{1,17},{17,1},{2,18},{18,2},{3,19},{19,3},{4,20},{20... | collective-permute-start | bytes 2261000 | tf_op jit(solution)/shard_map/ppermute | solution.py:123
  465.0 178.7 %reduce-scatter.11.cloned.1.call-start = ((), (), s32[]{:S(2)}) async-start(), calls=%async_computation.6 | async-start | bytes 3768320 | tf_op jit(solution)/shard_map/reduce_scatter | solution.py:231
  471.0 77.6 %collective-permute-start.14 = (f32[64,736]{1,0:T(8,128)}, f32[64,736]{1,0:T(8,128)}, u32[]{:S(2)}, u32[]{:S(2)}) collective-permute-start(f32[64,736]{1,0:T(8,128)} %fusion.93), channel_id=1, source_target_pairs={{0,16},{16,0},{1,17},{17,1},{2,18},{18,2},{3,19},{19,3},{4,20},{20... | collective-permute-start | bytes 565256 | tf_op jit(solution)/shard_map/ppermute | solution.py:123
  477.5 173.4 %reduce-scatter.13.cloned.1.call-start = ((), (), s32[]{:S(2)}) async-start(), calls=%async_computation.7 | async-start | bytes 3768320 | tf_op jit(solution)/shard_map/reduce_scatter | solution.py:231
  491.1 43.7 %copy-start.47 = (bf16[6,64,64]{2,1,0:T(8,128)(2,1)S(1)}, bf16[6,64,64]{2,1,0:T(8,128)(2,1)}, u32[]{:S(2)}) copy-start(bf16[6,64,64]{2,1,0:T(8,128)(2,1)} %copy-done.46) | copy-start | bytes 147460
  491.1 83.3 %collective-permute-start.15 = (bf16[4,184,2304]{2,1,0:T(8,128)(2,1)}, bf16[4,184,2304]{2,1,0:T(8,128)(2,1)}, u32[]{:S(2)}, u32[]{:S(2)}) collective-permute-start(bf16[4,184,2304]{2,1,0:T(8,128)(2,1)} %dynamic-slice_bitcast_fusion.1), channel_id=1, source_target_pairs={{0,16},{16,0},{1,17},{17,1},{2,18},{18,2},{3,19},{19,3},{4,20},{20... | collective-permute-start | bytes 10174472 | tf_op jit(solution)/shard_map/ppermute | solution.py:123
  546.9 34.3 %collective-permute-start.20 = (bf16[4,184,2304]{2,1,0:T(8,128)(2,1)}, bf16[4,184,2304]{2,1,0:T(8,128)(2,1)}, u32[]{:S(2)}, u32[]{:S(2)}) collective-permute-start(bf16[4,184,2304]{2,1,0:T(8,128)(2,1)} %dynamic-slice_bitcast_fusion), channel_id=1, source_target_pairs={{0,16},{16,0},{1,17},{17,1},{2,18},{18,2},{3,19},{19,3},{4,20},{20... | collective-permute-start | bytes 10174472 | tf_op jit(solution)/shard_map/ppermute | solution.py:123
  546.9 118.5 %reduce-scatter.19.cloned.1.call-start = ((), (), s32[]{:S(2)}) async-start(), calls=%async_computation.10 | async-start | bytes 1177600
  551.7 5.4 collective-permute-start.33
  553.9 9.7 %collective-permute-start.34 = (bf16[112,368]{1,0:T(8,128)(2,1)S(1)}, bf16[112,368]{1,0:T(8,128)(2,1)S(1)}, u32[]{:S(2)}, u32[]{:S(2)}) collective-permute-start(bf16[112,368]{1,0:T(8,128)(2,1)S(1)} %get-tuple-element.183), channel_id=1, source_target_pairs={{0,8},{4,12},{8,0},{12,4},{1,9},{5,13},{9,1},{13,5},{2,10},{6,14},... | collective-permute-start | bytes 247304 | tf_op jit(solution)/shard_map/ppermute | solution.py:123
  557.1 4.5 collective-permute-start.36
  561.6 8.3 %collective-permute-start.35 = (bf16[112,368]{1,0:T(8,128)(2,1)S(1)}, bf16[112,368]{1,0:T(8,128)(2,1)S(1)}, u32[]{:S(2)}, u32[]{:S(2)}) collective-permute-start(bf16[112,368]{1,0:T(8,128)(2,1)S(1)} %get-tuple-element.182), channel_id=1, source_target_pairs={{0,12},{4,8},{8,4},{12,0},{1,13},{5,9},{9,5},{13,1},{2,14},{6,10},... | collective-permute-start | bytes 247304 | tf_op jit(solution)/shard_map/ppermute | solution.py:123
  563.6 4.6 collective-permute-start.37
  568.1 5.4 collective-permute-start.38
  574.4 54.1 %collective-permute-start.39 = (bf16[4,112,368]{2,1,0:T(8,128)(2,1)}, bf16[4,112,368]{2,1,0:T(8,128)(2,1)}, u32[]{:S(2)}, u32[]{:S(2)}) collective-permute-start(bf16[4,112,368]{2,1,0:T(8,128)(2,1)} %broadcast_select_fusion.7), channel_id=1, source_target_pairs={{0,16},{16,0},{1,17},{17,1},{2,18},{18,2},{3,19},{19,3},{4,20},{20... | collective-permute-start | bytes 989192 | tf_op jit(solution)/shard_map/ppermute | solution.py:123
  578.8 13.1 %collective-permute-start.16 = (bf16[92,2304]{1,0:T(8,128)(2,1)S(1)}, bf16[92,2304]{1,0:T(8,128)(2,1)S(1)}, u32[]{:S(2)}, u32[]{:S(2)}) collective-permute-start(bf16[92,2304]{1,0:T(8,128)(2,1)S(1)} %get-tuple-element.152), channel_id=1, source_target_pairs={{0,8},{4,12},{8,0},{12,4},{1,9},{5,13},{9,1},{13,5},{2,10},{6,14},... | collective-permute-start | bytes 1271816 | tf_op jit(solution)/shard_map/ppermute | solution.py:123
  580.5 13.0 %collective-permute-start.18 = (bf16[92,2304]{1,0:T(8,128)(2,1)S(1)}, bf16[92,2304]{1,0:T(8,128)(2,1)S(1)}, u32[]{:S(2)}, u32[]{:S(2)}) collective-permute-start(bf16[92,2304]{1,0:T(8,128)(2,1)S(1)} %get-tuple-element.153), channel_id=1, source_target_pairs={{0,4},{4,0},{8,12},{12,8},{1,5},{5,1},{9,13},{13,9},{2,6},{6,2},{1... | collective-permute-start | bytes 1271816 | tf_op jit(solution)/shard_map/ppermute | solution.py:123
  584.1 17.3 %collective-permute-start.21 = (bf16[92,2304]{1,0:T(8,128)(2,1)S(1)}, bf16[92,2304]{1,0:T(8,128)(2,1)S(1)}, u32[]{:S(2)}, u32[]{:S(2)}) collective-permute-start(bf16[92,2304]{1,0:T(8,128)(2,1)S(1)} %get-tuple-element.147), channel_id=1, source_target_pairs={{0,8},{4,12},{8,0},{12,4},{1,9},{5,13},{9,1},{13,5},{2,10},{6,14},... | collective-permute-start | bytes 1271816 | tf_op jit(solution)/shard_map/ppermute | solution.py:123
  591.9 11.0 %collective-permute-start.23 = (bf16[92,2304]{1,0:T(8,128)(2,1)S(1)}, bf16[92,2304]{1,0:T(8,128)(2,1)S(1)}, u32[]{:S(2)}, u32[]{:S(2)}) collective-permute-start(bf16[92,2304]{1,0:T(8,128)(2,1)S(1)} %get-tuple-element.148), channel_id=1, source_target_pairs={{0,4},{4,0},{8,12},{12,8},{1,5},{5,1},{9,13},{13,9},{2,6},{6,2},{1... | collective-permute-start | bytes 1271816 | tf_op jit(solution)/shard_map/ppermute | solution.py:123
  593.8 25.8 %collective-permute-start.19 = (bf16[184,2304]{1,0:T(8,128)(2,1)S(1)}, bf16[184,2304]{1,0:T(8,128)(2,1)S(1)}, u32[]{:S(2)}, u32[]{:S(2)}) collective-permute-start(bf16[184,2304]{1,0:T(8,128)(2,1)S(1)} %pad_maximum_fusion.5), channel_id=1, source_target_pairs={{0,8},{4,12},{8,0},{12,4},{1,9},{5,13},{9,1},{13,5},{2,10},{6,14},... | collective-permute-start | bytes 2543624 | tf_op jit(solution)/shard_map/ppermute | solution.py:123
  601.4 19.7 %collective-permute-start.17 = (bf16[184,2304]{1,0:T(8,128)(2,1)S(1)}, bf16[184,2304]{1,0:T(8,128)(2,1)S(1)}, u32[]{:S(2)}, u32[]{:S(2)}) collective-permute-start(bf16[184,2304]{1,0:T(8,128)(2,1)S(1)} %pad_maximum_fusion.4), channel_id=1, source_target_pairs={{0,4},{4,0},{8,12},{12,8},{1,5},{5,1},{9,13},{13,9},{2,6},{6,2},{1... | collective-permute-start | bytes 2543624 | tf_op jit(solution)/shard_map/ppermute | solution.py:123
  604.2 32.7 %collective-permute-start.24 = (bf16[184,2304]{1,0:T(8,128)(2,1)}, bf16[184,2304]{1,0:T(8,128)(2,1)}, u32[]{:S(2)}, u32[]{:S(2)}) collective-permute-start(bf16[184,2304]{1,0:T(8,128)(2,1)} %pad_maximum_fusion.7), channel_id=1, source_target_pairs={{0,8},{4,12},{8,0},{12,4},{1,9},{5,13},{9,1},{13,5},{2,10},{6,14},... | collective-permute-start | bytes 2543624 | tf_op jit(solution)/shard_map/ppermute | solution.py:123
  619.6 19.3 %collective-permute-start.22 = (bf16[184,2304]{1,0:T(8,128)(2,1)}, bf16[184,2304]{1,0:T(8,128)(2,1)}, u32[]{:S(2)}, u32[]{:S(2)}) collective-permute-start(bf16[184,2304]{1,0:T(8,128)(2,1)} %pad_maximum_fusion.6), channel_id=1, source_target_pairs={{0,4},{4,0},{8,12},{12,8},{1,5},{5,1},{9,13},{13,9},{2,6},{6,2},{1... | collective-permute-start | bytes 2543624 | tf_op jit(solution)/shard_map/ppermute | solution.py:123
  625.8 66.8 %reduce-scatter.21.cloned.1.call-start = ((), (), s32[]{:S(2)}) async-start(), calls=%async_computation.11 | async-start | bytes 1177600
  645.7 8.9 %collective-permute-start.26 = (bf16[368,256]{1,0:T(8,128)(2,1)}, bf16[368,256]{1,0:T(8,128)(2,1)S(1)}, u32[]{:S(2)}, u32[]{:S(2)}) collective-permute-start(bf16[368,256]{1,0:T(8,128)(2,1)} %get-tuple-element.161), channel_id=1, source_target_pairs={{0,4},{4,0},{8,12},{12,8},{1,5},{5,1},{9,13},{13,9},{2,6},{6,2},{1... | collective-permute-start | bytes 565256 | tf_op jit(solution)/shard_map/ppermute | solution.py:123
  649.0 11.4 %collective-permute-start.27 = (bf16[368,256]{1,0:T(8,128)(2,1)S(1)}, bf16[368,256]{1,0:T(8,128)(2,1)S(1)}, u32[]{:S(2)}, u32[]{:S(2)}) collective-permute-start(bf16[368,256]{1,0:T(8,128)(2,1)S(1)} %get-tuple-element.160), channel_id=1, source_target_pairs={{0,8},{4,12},{8,0},{12,4},{1,9},{5,13},{9,1},{13,5},{2,10},{6,14},... | collective-permute-start | bytes 565256 | tf_op jit(solution)/shard_map/ppermute | solution.py:123
  649.7 10.7 %collective-permute-start.28 = (bf16[368,256]{1,0:T(8,128)(2,1)S(1)}, bf16[368,256]{1,0:T(8,128)(2,1)S(1)}, u32[]{:S(2)}, u32[]{:S(2)}) collective-permute-start(bf16[368,256]{1,0:T(8,128)(2,1)S(1)} %get-tuple-element.159), channel_id=1, source_target_pairs={{0,12},{4,8},{8,4},{12,0},{1,13},{5,9},{9,5},{13,1},{2,14},{6,10},... | collective-permute-start | bytes 565256 | tf_op jit(solution)/shard_map/ppermute | solution.py:123
  652.3 9.4 %collective-permute-start.29 = (bf16[368,256]{1,0:T(8,128)(2,1)S(1)}, bf16[368,256]{1,0:T(8,128)(2,1)S(1)}, u32[]{:S(2)}, u32[]{:S(2)}) collective-permute-start(bf16[368,256]{1,0:T(8,128)(2,1)S(1)} %get-tuple-element.157), channel_id=1, source_target_pairs={{0,4},{4,0},{8,12},{12,8},{1,5},{5,1},{9,13},{13,9},{2,6},{6,2},{1... | collective-permute-start | bytes 565256 | tf_op jit(solution)/shard_map/ppermute | solution.py:123
  653.8 11.5 %collective-permute-start.30 = (bf16[368,256]{1,0:T(8,128)(2,1)S(1)}, bf16[368,256]{1,0:T(8,128)(2,1)S(1)}, u32[]{:S(2)}, u32[]{:S(2)}) collective-permute-start(bf16[368,256]{1,0:T(8,128)(2,1)S(1)} %get-tuple-element.156), channel_id=1, source_target_pairs={{0,8},{4,12},{8,0},{12,4},{1,9},{5,13},{9,1},{13,5},{2,10},{6,14},... | collective-permute-start | bytes 565256 | tf_op jit(solution)/shard_map/ppermute | solution.py:123
  654.6 10.7 %collective-permute-start.31 = (bf16[368,256]{1,0:T(8,128)(2,1)S(1)}, bf16[368,256]{1,0:T(8,128)(2,1)S(1)}, u32[]{:S(2)}, u32[]{:S(2)}) collective-permute-start(bf16[368,256]{1,0:T(8,128)(2,1)S(1)} %get-tuple-element.155), channel_id=1, source_target_pairs={{0,12},{4,8},{8,4},{12,0},{1,13},{5,9},{9,5},{13,1},{2,14},{6,10},... | collective-permute-start | bytes 565256 | tf_op jit(solution)/shard_map/ppermute | solution.py:123
  693.6 1.6 collective-permute-start.25
  694.6 4.3 collective-permute-start.32
  (71 other events, 402.3 us)
Sparse Core Ops, SparseCore 0:
  451.0 32.6 reduce-scatter.14
  486.1 31.4 reduce-scatter.16
  519.9 57.0 reduce-scatter.10
  579.2 58.1 reduce-scatter.12
  640.1 25.1 reduce-scatter.18
  667.6 24.8 reduce-scatter.20

commit v3 on v2

--- a/solution.py
+++ b/solution.py
@@ -67,6 +67,10 @@
     return jnp.dot(left_side, right_side, preferred_element_type=jnp.float32)
 
 
+def matmul_exact(left_side, right_side):
+    return jnp.dot(left_side, right_side, precision=HIGHEST)
+
+
 def to_low(tensor):
     return tensor.astype(jnp.bfloat16)
 
@@ -161,101 +165,6 @@
     return buffer
 
 
-def both_sections(own, section):
-    other = xor_permute(own, "section", 1)
-    is_dec = section == 1
-    return jnp.where(is_dec, other, own), jnp.where(is_dec, own, other)
-
-
-def norm_backward(residual, gain_row, grad_normed):
-    _, norm_pull = jax.vjp(rms_norm, residual, gain_row)
-    return norm_pull(grad_normed)
-
-
-def self_forward(residual, gain_row, weight, bias_full, allowed):
-    normed = to_low(rms_norm(residual, gain_row))
-    projected = to_low(matmul(normed, weight[:, : 3 * HD]))
-    context, weights, low_weights = attend_forward(
-        projected[:, :HD], projected[:, HD : 2 * HD], projected[:, 2 * HD :], bias_full, allowed
-    )
-    return (
-        residual + matmul(context, weight[:, 3 * HD : 4 * HD].T),
-        (residual, normed, projected, context, weights, low_weights),
-    )
-
-
-def self_backward(kept, gain_row, weight, hot, grad_out):
-    residual, normed, projected, context, weights, low_weights = kept
-    grad_low = to_low(grad_out)
-    grad_wout = matmul(grad_low.T, context)
-    grad_context = to_low(matmul(grad_low, weight[:, 3 * HD : 4 * HD]))
-    grad_queries, grad_keys, grad_values, low_scores = attend_backward(
-        projected[:, :HD],
-        projected[:, HD : 2 * HD],
-        projected[:, 2 * HD :],
-        weights,
-        low_weights,
-        grad_context,
-    )
-    grad_projected = to_low(jnp.concatenate([grad_queries, grad_keys, grad_values], axis=1))
-    grad_win = matmul(normed.T, grad_projected)
-    grad_residual, grad_gain = norm_backward(
-        residual, gain_row, matmul(grad_projected, weight[:, : 3 * HD].T)
-    )
-    grad_bias = jnp.einsum(
-        "hqk,qkb->bh", low_scores, hot.astype(jnp.bfloat16), preferred_element_type=jnp.float32
-    )
-    return grad_out + grad_residual, grad_gain, grad_win, grad_wout, grad_bias
-
-
-def core_halves(grad, core, wide):
-    depth, columns = grad.shape
-    split = to_low(grad).reshape(wide, 2, depth // wide // 2, columns)
-    mine = lax.dynamic_index_in_dim(split, core, 1, keepdims=False)
-    sent = lax.dynamic_index_in_dim(split, 1 - core, 1, keepdims=False)
-    return mine.astype(jnp.float32) + xor_permute(sent, "section", 1).astype(jnp.float32)
-
-
-def to_owners(value, axis, wide):
-    place = lax.axis_index("wide")
-    size = value.shape[axis] // wide
-
-    def piece(owner):
-        return lax.dynamic_slice_in_dim(value, owner * size, size, axis)
-
-    got = [piece(place)] + [xor_permute(piece(place ^ v), "wide", v) for v in range(1, wide)]
-    return placed_rows([each[None] for each in got], place)
-
-
-def reduce_ffn(share_in, share_out, wide):
-    summed_in = lax.psum_scatter(share_in, "rows", scatter_dimension=0, tiled=True)[0]
-    summed_out = lax.psum_scatter(share_out, "rows", scatter_dimension=0, tiled=True)[0]
-    return to_owners(summed_in, 0, wide), to_owners(summed_out, 1, wide)
-
-
-def reduce_attn(grad, core, wide, rows):
-    depth, columns = grad.shape
-    halves = core_halves(grad, core, wide)
-    place = lax.axis_index("wide")
-    parts = [
-        lax.dynamic_index_in_dim(halves, place ^ v, 0, keepdims=False) for v in range(wide)
-    ]
-    mine = to_low(scatter_wide(parts))
-    pieces, start = [], 0
-    for width in (3 * HD, HD, HD, HD):
-        pieces.append(mine[:, start : start + width].reshape(mine.shape[0], rows, width // rows))
-        start += width
-    stacked = jnp.concatenate(pieces, axis=2).transpose(1, 0, 2)
-    return lax.psum_scatter(stacked, "rows", scatter_dimension=0, tiled=True)[0]
-
-
-def to_section(enc_half, dec_half, core):
-    is_dec = core == 1
-    own = jnp.where(is_dec, dec_half, enc_half)
-    got = xor_permute(jnp.where(is_dec, enc_half, dec_half), "section", 1)
-    return jnp.stack([jnp.where(is_dec, got, own), jnp.where(is_dec, own, got)])
-
-
 MESH = pl.DeviceIdType.MESH
 HBM = pl.BlockSpec(memory_space=pl.ANY)
 VM = pl.BlockSpec(memory_space=pltpu.VMEM)
@@ -296,7 +205,8 @@
 
 class GatherPlane:
     def __init__(self, blocks, sems, base, peers, rows):
-        half = rows // 2
+        half = split_at(rows)
+        rest = rows - half
         first, second = peers[0], peers[1]
         self.direct = [
             remote(blocks.at[0], blocks.at[1], sems, base, first),
@@ -307,8 +217,8 @@
                 blocks.at[1, pl.ds(0, half)], blocks.at[3, pl.ds(0, half)], sems, base + 2, second
             ),
             remote(
-                blocks.at[2, pl.ds(half, half)],
-                blocks.at[3, pl.ds(half, half)],
+                blocks.at[2, pl.ds(half, rest)],
+                blocks.at[3, pl.ds(half, rest)],
                 sems,
                 base + 3,
                 first,
@@ -334,10 +244,10 @@
 
 class ScatterPlane:
     def __init__(self, parts, landing, sems, base, peers, rows):
-        half = rows // 2
+        half = split_at(rows)
         first, second = peers[0], peers[1]
-        low, high = pl.ds(0, half), pl.ds(half, half)
-        self.parts, self.landing, self.half = parts, landing, half
+        low, high = pl.ds(0, half), pl.ds(half, rows - half)
+        self.parts, self.landing, self.low, self.high = parts, landing, low, high
         self.far = [
             remote(parts.at[3, low], landing.at[0, low], sems, base, first),
             remote(parts.at[3, high], landing.at[0, high], sems, base + 1, second),
@@ -359,7 +269,7 @@
             copy.start()
 
     def pass_on(self):
-        low, high = pl.ds(0, self.half), pl.ds(self.half, self.half)
+        low, high = self.low, self.high
         self.far[0].wait_recv()
         self.parts[2, low] = (
             self.parts[2, low].astype(jnp.float32) + self.landing[0, low].astype(jnp.float32)
@@ -393,86 +303,82 @@
     return grad_residual, jnp.sum(grad_normed * unit, axis=0, keepdims=True)
 
 
-def prepare_weights_kernel(wide, rows, in_ref, out_ref, *refs):
-    enc, dec = refs[:wide], refs[wide : 2 * wide]
-    blocks, send_sem, recv_sem, local_sem = refs[2 * wide :]
-    core, place = lax.axis_index("section"), lax.axis_index("wide")
-    sibling = {"section": 1 - core}
-    greet([sibling])
-    units = FF // (wide * rows * 2)
-    per_row = FF // rows
-    row_ids = lax.broadcasted_iota(jnp.int32, (2 * TILE, TILE), 0)
-    lane_ids = lax.broadcasted_iota(jnp.int32, (2 * TILE, TILE), 1)
-    straight = (
-        lax.broadcasted_iota(jnp.int32, (units, TILE), 0)
-        == lax.broadcasted_iota(jnp.int32, (units, TILE), 1)
-    ).astype(jnp.bfloat16)
-    for index in range(2 * wide):
-        target, half = index // 2, index % 2
-        offset = index * units
-        start, shift = offset // TILE * TILE, offset % TILE
-        picks = ((row_ids == lane_ids + shift) & (lane_ids < units)).astype(jnp.bfloat16)
-        window = min(2 * TILE, per_row - start)
-        picks = picks[:window]
-        for part in range(3):
-            for row in range(rows):
-                column = (part * rows + row) * TILE
-                if part < 2:
-                    source = in_ref[0, :, pl.ds(part * FF + row * per_row + start, window)]
-                    tile = matmul(source, picks)
-                else:
-                    source = out_ref[0, pl.ds(row * per_row + offset, units), :]
-                    tile = tn(source, straight)
-                blocks[half, target ^ place, :, pl.ds(column, TILE)] = tile.astype(jnp.bfloat16)
-    def move(outs):
-        copies = []
-        for v in range(wide):
-            keep = pltpu.make_async_copy(blocks.at[core, v], outs[v], local_sem.at[v])
-            give = remote(blocks.at[1 - core, v], outs[v], (send_sem, recv_sem), v, sibling)
-            keep.start()
-            give.start()
-            copies += [keep]
-            copies += [give]
-        for keep in copies[::2]:
-            keep.wait()
-        for give in copies[1::2]:
-            give.wait_send()
-
-    def receive(outs):
-        for v in range(wide):
-            remote(blocks.at[0, v], outs[v], (send_sem, recv_sem), v, sibling).wait_recv()
-
-    @pl.when(core == 0)
-    def _():
-        move(enc)
-        receive(dec)
-
-    @pl.when(core == 1)
-    def _():
-        move(dec)
-        receive(enc)
-
-
-def prepare_weights(wide, rows, ffn_in, ffn_out):
-    depth = ffn_in.shape[1]
-    block = jax.ShapeDtypeStruct((depth, 3 * rows * TILE), jnp.bfloat16)
-    outs = pl.pallas_call(
-        lambda *refs: prepare_weights_kernel(wide, rows, *refs),
-        out_shape=[block] * (2 * wide),
-        in_specs=[VM, VM],
-        out_specs=[HBM] * (2 * wide),
-        scratch_shapes=[
-            pltpu.VMEM((2, wide) + block.shape, jnp.bfloat16),
-            pltpu.SemaphoreType.DMA((wide,)),
-            pltpu.SemaphoreType.DMA((wide,)),
-            pltpu.SemaphoreType.DMA((wide,)),
-        ],
-        compiler_params=pltpu.CompilerParams(
-            collective_id=1, has_side_effects=True, vmem_limit_bytes=VMEM_LIMIT
-        ),
-        name="prepare_weights",
-    )(ffn_in, ffn_out)
-    return outs[:wide], outs[wide:]
+def token_groups(wide, rows):
+    if rows >= 2 * TILE:
+        return [[v] for v in range(wide)]
+    return [list(range(wide))]
+
+
+class ReduceRows:
+    def __init__(self, source_in, source_out, in_buf, in_land, out_buf, out_land, sems, base, local_sem, local_base):
+        row = lax.axis_index("rows")
+        near, far = {"rows": row ^ 1}, {"rows": row ^ 2}
+        self.bufs, self.lands, self.first, self.second = [], [], [], []
+        lanes = [pl.ds(0, TILE), pl.ds(TILE, TILE)]
+        views = [
+            (lambda ref, i, part=part: ref.at[i, :, part], source_in, in_buf, in_land)
+            for part in lanes
+        ] + [(lambda ref, i: ref.at[i], source_out, out_buf, out_land)]
+        for index, (view, source, buf, land) in enumerate(views):
+            at = base + 3 * index
+            self.first.append(
+                [
+                    remote(view(source, row ^ 1), view(land, 0), sems, at, near),
+                    remote(view(source, row ^ 3), view(land, 1), sems, at + 1, near),
+                ]
+            )
+            self.second.append(remote(view(buf, 1), view(land, 2), sems, at + 2, far))
+            self.bufs.append([view(buf, 0), view(buf, 1)])
+            self.lands.append([view(land, i) for i in range(3)])
+        self.loads = [
+            pltpu.make_async_copy(source.at[place], buf.at[i], local_sem.at[local_base + 2 * j + i])
+            for j, (source, buf) in enumerate(((source_in, in_buf), (source_out, out_buf)))
+            for i, place in enumerate((row, row ^ 2))
+        ]
+
+    def start(self):
+        for pair in self.first:
+            for copy in pair:
+                copy.start()
+        for load in self.loads:
+            load.start()
+
+    def loaded(self):
+        for load in self.loads:
+            load.wait()
+
+    def add(self, index, which, land):
+        ref = self.bufs[index][which]
+        ref[...] = (
+            ref[...].astype(jnp.float32) + self.lands[index][land][...].astype(jnp.float32)
+        ).astype(jnp.bfloat16)
+
+    def turn(self, index):
+        for copy in self.first[index]:
+            copy.wait_recv()
+        self.add(index, 1, 1)
+        self.second[index].start()
+        self.add(index, 0, 0)
+
+    def close(self, index):
+        self.second[index].wait_recv()
+        self.add(index, 0, 2)
+
+    def finish(self):
+        for pair, copy in zip(self.first, self.second):
+            for each in pair:
+                each.wait_send()
+            copy.wait_send()
+
+
+def reduce_rows_scratch(units):
+    low = jnp.bfloat16
+    return [
+        pltpu.VMEM((2, D, 2 * TILE), low),
+        pltpu.VMEM((3, D, 2 * TILE), low),
+        pltpu.VMEM((2, units, D), low),
+        pltpu.VMEM((3, units, D), low),
+    ]
 
 
 def ffn_forward_kernel(wide, x_ref, gain_ref, *refs):
@@ -502,19 +408,21 @@
         loads.append(load)
         swaps.append(swap)
     scatter = ScatterPlane(parts, landing, sems, 4, peers, rows)
-    for v in range(wide):
-        if v == 0:
+    for group in token_groups(wide, rows):
+        for v in group:
+            if v > 0:
+                gather.arrive(v - 1)
+        if group[0] == 0:
             for load in loads:
                 load.wait()
-        else:
-            gather.arrive(v - 1)
-        block = blocks[v]
+        count = len(group) * rows
+        block = blocks[group[0] : group[-1] + 1].reshape(count, D)
+        token_rows = pl.ds(group[0] * rows, count)
         for step in range(2):
-            if v == 0 and step == 1:
+            if group[0] == 0 and step == 1:
                 for swap in swaps:
                     swap.wait_recv()
             half = core if step == 0 else 1 - core
-            token_rows = pl.ds(v * rows, rows)
             gate = matmul(block, weight[half, :, pl.ds(0, span)])
             up = matmul(block, weight[half, :, pl.ds(span, span)])
             pre[half, token_rows, pl.ds(0, span)] = gate.astype(jnp.bfloat16)
@@ -524,14 +432,18 @@
             out = nt(low, weight[half, :, pl.ds(2 * span, span)])
             if step == 0:
                 acc[...] = out
-            elif v == 0:
-                y_ref[...] = residual + acc[...] + out
-            else:
-                parts[v] = (acc[...] + out).astype(jnp.bfloat16)
-        if v in (1, 2):
-            scatter.send_early(v - 1)
-        if v == 3:
-            scatter.send_far()
+                continue
+            for i, v in enumerate(group):
+                own = slice(i * rows, (i + 1) * rows)
+                if v == 0:
+                    y_ref[...] = residual + acc[own] + out[own]
+                else:
+                    parts[v] = (acc[own] + out[own]).astype(jnp.bfloat16)
+        for v in group:
+            if v in (1, 2):
+                scatter.send_early(v - 1)
+            if v == 3:
+                scatter.send_far()
     copies = [
         pltpu.make_async_copy(pre, pre_out, local_sem.at[4]),
         pltpu.make_async_copy(weight, weight_out, local_sem.at[5]),
@@ -579,7 +491,7 @@
             pltpu.VMEM((2, D, columns), low),
             pltpu.VMEM((wide, rows, D), low),
             pltpu.VMEM((3, rows, D), low),
-            pltpu.VMEM((rows, D), jnp.float32),
+            pltpu.VMEM((len(token_groups(wide, rows)[0]) * rows, D), jnp.float32),
             pltpu.SemaphoreType.DMA((14,)),
             pltpu.SemaphoreType.DMA((14,)),
             pltpu.SemaphoreType.DMA((7,)),
@@ -591,8 +503,18 @@
     )(residual, gain_row, *pieces)
 
 
-def ffn_backward_kernel(wide, rows_axis, g_ref, x_ref, gain_ref, at_in, pre_in, hidden_in, weight_in, *refs):
+def ffn_backward_kernel(
+    wide, rows_axis, g_ref, x_ref, gain_ref, at_in, pre_in, hidden_in, weight_in, *refs
+):
+    carried = len(refs) > 21
+    if carried:
+        ready_in, ready_out = refs[:2]
+        refs = refs[2:]
     gx_ref, gain_out, grad_in, grad_out = refs[:4]
+    refs = refs[4:]
+    if carried:
+        sum_in, sum_out = refs[:2]
+        refs = refs[2:]
     (
         blocks,
         at,
@@ -609,45 +531,53 @@
         send_sem,
         recv_sem,
         local_sem,
-    ) = refs[4:]
+    ) = refs[:15]
     rows = x_ref.shape[0]
     span = weight.shape[2] // 3
     units = FF // (wide * rows_axis * 2)
-    core = lax.axis_index("section")
+    core, row = lax.axis_index("section"), lax.axis_index("rows")
     peers = peers_of(wide)
     sems = (send_sem, recv_sem)
-    greet(peers)
+    greet(peers + ([{"rows": row ^ 1}, {"rows": row ^ 2}] if carried else []))
     loads = [
         pltpu.make_async_copy(weight_in, weight, local_sem.at[0]),
         pltpu.make_async_copy(pre_in, pre, local_sem.at[1]),
         pltpu.make_async_copy(hidden_in, hidden, local_sem.at[2]),
         pltpu.make_async_copy(at_in, at, local_sem.at[3]),
     ]
-    for load in loads:
-        load.start()
     blocks[0] = g_ref[...].astype(jnp.bfloat16)
     gather = GatherPlane(blocks, sems, 0, peers, rows)
     gather.start()
+    for load in loads:
+        load.start()
+    if carried:
+        line = ReduceRows(ready_in, ready_out, *refs[15:19], sems, 12, local_sem, 6)
+        line.start()
     scatter = ScatterPlane(parts, landing, sems, 4, peers, rows)
     loads[0].wait()
     loads[1].wait()
-    for v in range(wide):
-        if v > 0:
-            gather.arrive(v - 1)
-        block = blocks[v]
-        token_rows = pl.ds(v * rows, rows)
+    for group in token_groups(wide, rows):
+        for v in group:
+            if v > 0:
+                if carried and v == 3:
+                    line.loaded()
+                    line.turn(0)
+                gather.arrive(v - 1)
+        count = len(group) * rows
+        block = blocks[group[0] : group[-1] + 1].reshape(count, D)
+        token_rows = pl.ds(group[0] * rows, count)
         for half in range(2):
             grad_hidden = matmul(block, weight[half, :, pl.ds(2 * span, span)])
             gate = pre[half, token_rows, pl.ds(0, span)].astype(jnp.float32)
             up = pre[half, token_rows, pl.ds(span, span)].astype(jnp.float32)
-            inner = GELU_A * (gate + GELU_B * gate * gate * gate)
-            tanh = jnp.tanh(inner)
-            slope = 0.5 * (1.0 + tanh) + 0.5 * gate * (1.0 - tanh * tanh) * GELU_A * (
-                1.0 + 3.0 * GELU_B * gate * gate
+            square = gate * gate
+            tanh = jnp.tanh(GELU_A * gate * (1.0 + GELU_B * square))
+            upper = 0.5 * (1.0 + tanh)
+            slope = upper + 0.5 * gate * (1.0 - tanh * tanh) * (
+                GELU_A + 3.0 * GELU_A * GELU_B * square
             )
-            value = 0.5 * gate * (1.0 + tanh)
             low_gate = (grad_hidden * up * slope).astype(jnp.bfloat16)
-            low_up = (grad_hidden * value).astype(jnp.bfloat16)
+            low_up = (grad_hidden * (gate * upper)).astype(jnp.bfloat16)
             pre[half, token_rows, pl.ds(0, span)] = low_gate
             pre[half, token_rows, pl.ds(span, span)] = low_up
             out = nt(low_gate, weight[half, :, pl.ds(0, span)]) + nt(
@@ -655,16 +585,18 @@
             )
             if half == 0:
                 acc[...] = out
-            elif v == 0:
-                acc[...] += out
-                gx_ref[...] = acc[...]
-            else:
-                parts[v] = (acc[...] + out).astype(jnp.bfloat16)
-        if v in (1, 2):
-            scatter.send_early(v - 1)
-        if v == 3:
-            scatter.send_far()
-    scatter.pass_on()
+                continue
+            for i, v in enumerate(group):
+                own = slice(i * rows, (i + 1) * rows)
+                if v == 0:
+                    gx_ref[...] = acc[own] + out[own]
+                else:
+                    parts[v] = (acc[own] + out[own]).astype(jnp.bfloat16)
+        for v in group:
+            if v in (1, 2):
+                scatter.send_early(v - 1)
+            if v == 3:
+                scatter.send_far()
     loads[2].wait()
     loads[3].wait()
     chunk = 2 * TILE
@@ -676,22 +608,31 @@
     def output_rows(half):
         return matmul(hidden[half], blocks[...].reshape(wide * rows, D))
 
+    if carried:
+        line.turn(1)
+    out_rows = output_rows(1 - core)
+    for index in range(rows_axis):
+        give_out[index] = out_rows[index * TILE : index * TILE + units].astype(jnp.bfloat16)
+    swap_out = remote(give_out, got_out, sems, 11, peers[-1])
+    swap_out.start()
+    scatter.pass_on()
+
     @pl.loop(0, rows_axis)
     def _(index):
         give_in[index] = input_chunk(1 - core, index).astype(jnp.bfloat16)
 
     swap_in = remote(give_in, got_in, sems, 10, peers[-1])
     swap_in.start()
-    out_rows = output_rows(1 - core)
-    for row in range(rows_axis):
-        give_out[row] = out_rows[row * TILE : row * TILE + units].astype(jnp.bfloat16)
-    swap_out = remote(give_out, got_out, sems, 11, peers[-1])
-    swap_out.start()
-    total = gx_ref[...] + scatter.total()
-    grad_residual, grad_gain = norm_pull(x_ref[...], gain_ref[...], total)
-    gx_ref[...] = g_ref[...] + grad_residual
-    gain_out[...] = grad_gain
+    if carried:
+        line.turn(2)
     out_rows = output_rows(core)
+    swap_out.wait_recv()
+    for index in range(rows_axis):
+        got_out[index] = (
+            out_rows[index * TILE : index * TILE + units] + got_out[index].astype(jnp.float32)
+        ).astype(jnp.bfloat16)
+    store_out = pltpu.make_async_copy(got_out, grad_out, local_sem.at[5])
+    store_out.start()
     swap_in.wait_recv()
 
     @pl.loop(0, rows_axis)
@@ -702,13 +643,23 @@
 
     store_in = pltpu.make_async_copy(got_in, grad_in, local_sem.at[4])
     store_in.start()
-    swap_out.wait_recv()
-    for row in range(rows_axis):
-        got_out[row] = (
-            out_rows[row * TILE : row * TILE + units] + got_out[row].astype(jnp.float32)
-        ).astype(jnp.bfloat16)
-    store_out = pltpu.make_async_copy(got_out, grad_out, local_sem.at[5])
-    store_out.start()
+    total = gx_ref[...] + scatter.total()
+    grad_residual, grad_gain = norm_pull(x_ref[...], gain_ref[...], total)
+    gx_ref[...] = g_ref[...] + grad_residual
+    gain_out[...] = grad_gain
+    if carried:
+        for index in range(3):
+            line.close(index)
+        in_buf, out_buf = refs[15], refs[17]
+        stores = [
+            pltpu.make_async_copy(in_buf.at[0], sum_in, local_sem.at[6]),
+            pltpu.make_async_copy(out_buf.at[0], sum_out, local_sem.at[7]),
+        ]
+        for store in stores:
+            store.start()
+        for store in stores:
+            store.wait()
+        line.finish()
     store_in.wait()
     store_out.wait()
     swap_in.wait_send()
@@ -721,13 +672,14 @@
 GELU_B = 0.044715
 
 
-def ffn_backward_call(wide, rows_axis, grad, residual, gain_row, kept, call_id):
+def ffn_backward_call(wide, rows_axis, grad, residual, gain_row, kept, call_id, carried=()):
     at, pre, hidden, weight = kept
     rows = residual.shape[0]
     low = jnp.bfloat16
     units = FF // (wide * rows_axis * 2)
     share_in = (rows_axis, D, 2 * TILE)
     share_out = (rows_axis, units, D)
+    sums = [jax.ShapeDtypeStruct(each.shape[1:], low) for each in carried]
     return pl.pallas_call(
         lambda *refs: ffn_backward_kernel(wide, rows_axis, *refs),
         out_shape=[
@@ -735,9 +687,10 @@
             jax.ShapeDtypeStruct((1, D), jnp.float32),
             jax.ShapeDtypeStruct(share_in, low),
             jax.ShapeDtypeStruct(share_out, low),
-        ],
-        in_specs=[VM, VM, VM, HBM, HBM, HBM, HBM],
-        out_specs=[VM, VM, HBM, HBM],
+        ]
+        + sums,
+        in_specs=[VM, VM, VM, HBM, HBM, HBM, HBM] + [HBM] * len(sums),
+        out_specs=[VM, VM, HBM, HBM] + [HBM] * len(sums),
         scratch_shapes=[
             pltpu.VMEM((wide, rows, D), low),
             pltpu.VMEM(at.shape, low),
@@ -746,20 +699,1000 @@
             pltpu.VMEM(weight.shape, low),
             pltpu.VMEM((wide, rows, D), low),
             pltpu.VMEM((3, rows, D), low),
-            pltpu.VMEM((rows, D), jnp.float32),
+            pltpu.VMEM((len(token_groups(wide, rows)[0]) * rows, D), jnp.float32),
             pltpu.VMEM(share_in, low),
             pltpu.VMEM(share_out, low),
             pltpu.VMEM(share_in, low),
             pltpu.VMEM(share_out, low),
-            pltpu.SemaphoreType.DMA((12,)),
-            pltpu.SemaphoreType.DMA((12,)),
-            pltpu.SemaphoreType.DMA((6,)),
-        ],
+            pltpu.SemaphoreType.DMA((21,)),
+            pltpu.SemaphoreType.DMA((21,)),
+            pltpu.SemaphoreType.DMA((10,)),
+        ]
+        + (reduce_rows_scratch(units) if carried else []),
         compiler_params=pltpu.CompilerParams(
             collective_id=call_id, has_side_effects=True, vmem_limit_bytes=VMEM_LIMIT
         ),
         name="ffn_backward_%d" % rows,
-    )(grad, residual, gain_row, at, pre, hidden, weight)
+    )(grad, residual, gain_row, at, pre, hidden, weight, *carried)
+
+
+def start_weights_kernel(
+    wide, rows, win_in, wout_in, cin_in, cout_in, ffn_in, ffn_out, attn_ref, dec_half, *refs
+):
+    enc, dec = refs[:wide], refs[wide : 2 * wide]
+    held, blocks, spare, in_ref, out_ref, ffn, send_sem, recv_sem, local_sem = refs[2 * wide :]
+    core, place = lax.axis_index("section"), lax.axis_index("wide")
+    peers = peers_of(wide)
+    sibling = peers[-1]
+    sems = (send_sem, recv_sem)
+    depth = blocks.shape[1]
+    big = [
+        pltpu.make_async_copy(ffn_in.at[0], in_ref, local_sem.at[4]),
+        pltpu.make_async_copy(ffn_out.at[0], out_ref, local_sem.at[5]),
+    ]
+    packs = [
+        pltpu.make_async_copy(each, held.at[:, pl.ds(i * HD, HD)], local_sem.at[1 + i])
+        for i, each in enumerate((wout_in, cin_in.at[0], cout_in.at[0]))
+    ]
+    for pack in packs:
+        pack.start()
+    greet(peers)
+    for pack in packs:
+        pack.wait()
+
+    @pl.when(core == 0)
+    def _():
+        keep = pltpu.make_async_copy(win_in.at[0], blocks.at[0], local_sem.at[0])
+        keep.start()
+        give = remote(held, blocks.at[0], sems, 0, sibling)
+        give.start()
+        remote(win_in.at[0], spare, sems, 1, sibling).wait_recv()
+        keep.wait()
+
+    @pl.when(core == 1)
+    def _():
+        keep = pltpu.make_async_copy(held, spare, local_sem.at[0])
+        keep.start()
+        give = remote(win_in.at[0], spare, sems, 1, sibling)
+        give.start()
+        remote(held, blocks.at[0], sems, 0, sibling).wait_recv()
+        keep.wait()
+
+    gather = GatherPlane(blocks, sems, 2, peers, depth)
+    gather.start()
+    for load in big:
+        load.start()
+    dec_copy = pltpu.make_async_copy(spare, dec_half, local_sem.at[0])
+    dec_copy.start()
+    stores, gives = [], []
+    for v in range(wide):
+        rows_of = pl.ds(pl.multiple_of((place ^ v) * depth, 16), depth)
+        stores.append(
+            pltpu.make_async_copy(blocks.at[v], attn_ref.at[core, rows_of], local_sem.at[6 + v])
+        )
+        gives.append(remote(blocks.at[v], attn_ref.at[core, rows_of], sems, 6 + v, sibling))
+    stores[0].start()
+    gives[0].start()
+    for load in big:
+        load.wait()
+    units = FF // (wide * rows * 2)
+    per_row = FF // rows
+    row_ids = lax.broadcasted_iota(jnp.int32, (2 * TILE, TILE), 0)
+    lane_ids = lax.broadcasted_iota(jnp.int32, (2 * TILE, TILE), 1)
+    straight = (
+        lax.broadcasted_iota(jnp.int32, (units, TILE), 0)
+        == lax.broadcasted_iota(jnp.int32, (units, TILE), 1)
+    ).astype(jnp.bfloat16)
+
+    def prepare(index):
+        target, half = index // 2, index % 2
+        offset = index * units
+        start, shift = offset // TILE * TILE, offset % TILE
+        picks = ((row_ids == lane_ids + shift) & (lane_ids < units)).astype(jnp.bfloat16)
+        window = min(2 * TILE, per_row - start)
+        picks = picks[:window]
+        for part in range(3):
+            for row in range(rows):
+                column = (part * rows + row) * TILE
+                if part < 2:
+                    source = in_ref[:, pl.ds(part * FF + row * per_row + start, window)]
+                    tile = matmul(source, picks)
+                else:
+                    source = out_ref[pl.ds(row * per_row + offset, units), :]
+                    tile = tn(source, straight)
+                ffn[half, target ^ place, :, pl.ds(column, TILE)] = tile.astype(jnp.bfloat16)
+
+    for index in range(2 * wide):
+        prepare(index)
+
+    def move(outs, base):
+        for v in range(wide):
+            pltpu.make_async_copy(ffn.at[core, v], outs[v], local_sem.at[10 + v]).start()
+            remote(ffn.at[1 - core, v], outs[v], sems, base + v, sibling).start()
+
+    def settle(outs, base):
+        for v in range(wide):
+            pltpu.make_async_copy(ffn.at[core, v], outs[v], local_sem.at[10 + v]).wait()
+            remote(ffn.at[1 - core, v], outs[v], sems, base + v, sibling).wait_send()
+
+    def receive(outs, base):
+        for v in range(wide):
+            remote(ffn.at[0, v], outs[v], sems, base + v, sibling).wait_recv()
+
+    @pl.when(core == 0)
+    def _():
+        move(enc, 10)
+
+    @pl.when(core == 1)
+    def _():
+        move(dec, 10 + wide)
+
+    for v in range(1, wide):
+        gather.arrive(v - 1)
+        stores[v].start()
+        gives[v].start()
+    for v in range(wide):
+        gives[v].wait_recv()
+        stores[v].wait()
+    dec_copy.wait()
+
+    @pl.when(core == 0)
+    def _():
+        settle(enc, 10)
+        receive(dec, 10 + wide)
+        remote(held, blocks.at[0], sems, 0, sibling).wait_send()
+
+    @pl.when(core == 1)
+    def _():
+        settle(dec, 10 + wide)
+        receive(enc, 10)
+        remote(win_in.at[0], spare, sems, 1, sibling).wait_send()
+
+    gather.finish()
+    for give in gives:
+        give.wait_send()
+
+
+def start_weights(wide, rows, attn_in, attn_out, cross_in, cross_out, ffn_in, ffn_out):
+    depth = ffn_in.shape[1]
+    low = jnp.bfloat16
+    block = jax.ShapeDtypeStruct((depth, 3 * rows * TILE), low)
+    part = (depth, 3 * HD)
+    attn, dec_half, *outs = pl.pallas_call(
+        lambda *refs: start_weights_kernel(wide, rows, *refs),
+        out_shape=[
+            jax.ShapeDtypeStruct((2, wide * depth, 3 * HD), low),
+            jax.ShapeDtypeStruct(part, low),
+        ]
+        + [block] * (2 * wide),
+        in_specs=[HBM] * 6,
+        out_specs=[HBM] * (2 + 2 * wide),
+        scratch_shapes=[
+            pltpu.VMEM(part, low),
+            pltpu.VMEM((wide,) + part, low),
+            pltpu.VMEM(part, low),
+            pltpu.VMEM(ffn_in.shape[1:], low),
+            pltpu.VMEM(ffn_out.shape[1:], low),
+            pltpu.VMEM((2, wide) + block.shape, low),
+            pltpu.SemaphoreType.DMA((10 + 2 * wide,)),
+            pltpu.SemaphoreType.DMA((10 + 2 * wide,)),
+            pltpu.SemaphoreType.DMA((10 + wide,)),
+        ],
+        compiler_params=pltpu.CompilerParams(
+            collective_id=1, has_side_effects=True, vmem_limit_bytes=VMEM_LIMIT
+        ),
+        name="start_weights",
+    )(attn_in, attn_out[0].T, cross_in, cross_out, ffn_in, ffn_out)
+    return attn, dec_half, outs[:wide], outs[wide:]
+
+
+def place_weights_kernel(wide, *refs):
+    pieces = refs[: wide + 1]
+    attn_ref, send_sem, recv_sem, local_sem = refs[wide + 1 :]
+    core, place = lax.axis_index("section"), lax.axis_index("wide")
+    sibling = {"section": 1 - core}
+    depth = pieces[0].shape[0]
+    greet([sibling])
+    stores, gives = [], []
+    for index, piece in enumerate(pieces):
+        start = (place ^ min(index, wide - 1)) * depth
+        if index == wide:
+            start = start + pieces[wide - 1].shape[0]
+        target = attn_ref.at[core, pl.ds(pl.multiple_of(start, 16), piece.shape[0])]
+        stores.append(pltpu.make_async_copy(piece, target, local_sem.at[index]))
+        gives.append(remote(piece, target, (send_sem, recv_sem), index, sibling))
+        stores[-1].start()
+        gives[-1].start()
+    for store, give in zip(stores, gives):
+        store.wait()
+        give.wait()
+
+
+def place_weights(wide, pieces):
+    depth, columns = pieces[0].shape
+    return pl.pallas_call(
+        lambda *refs: place_weights_kernel(wide, *refs),
+        out_shape=jax.ShapeDtypeStruct((2, wide * depth, columns), jnp.bfloat16),
+        in_specs=[VM] * len(pieces),
+        out_specs=HBM,
+        scratch_shapes=[pltpu.SemaphoreType.DMA((len(pieces),))] * 3,
+        compiler_params=pltpu.CompilerParams(collective_id=6, has_side_effects=True),
+        name="place_weights",
+    )(*pieces)
+
+
+def split_at(rows):
+    return (rows // 2 + 15) // 16 * 16
+
+
+def reduce_kernel(wide, rows, *refs):
+    cross_ref, dec_ref, enc_ref, dec_in, dec_out, enc_in, enc_out, small_ref = refs[:8]
+    out_ref, ffn_ref, small_out = refs[8:11]
+    refs = refs[11:]
+    batches = (cross_ref, dec_ref, enc_ref)
+    count = len(batches)
+    owns, lands, planes, sends, zlands = [refs[i * count : (i + 1) * count] for i in range(5)]
+    refs = refs[5 * count :]
+    keep, give, ready, landing, small, small_land, small_plane, small_rows = refs[:8]
+    line_bufs, (send_sem, recv_sem, local_sem) = refs[8:12], refs[12:]
+    core, place, row = lax.axis_index("section"), lax.axis_index("wide"), lax.axis_index("rows")
+    peers = peers_of(wide)
+    sibling = peers[-1]
+    crossed = [{"section": 1 - core, "wide": place ^ v} for v in range(1, wide)]
+    others = [{"rows": row ^ k} for k in range(1, rows)]
+    sems = (send_sem, recv_sem)
+    depth = cross_ref.shape[0] // wide
+    size = owns[0].shape[1]
+    units = dec_out.shape[0]
+    low = jnp.bfloat16
+    greet(peers + crossed + others)
+
+    def rows_at(v, half):
+        start = (place ^ v) * depth + half * (depth - size)
+        return pl.ds(pl.multiple_of(start, 16), size)
+
+    loads, swaps, scatters, spreads = [], [], [], []
+    base, local_base = 0, 0
+    for index, batch in enumerate(batches):
+        loads.append(
+            [
+                pltpu.make_async_copy(
+                    batch.at[rows_at(v, core)], owns[index].at[v], local_sem.at[local_base + v]
+                )
+                for v in range(wide)
+            ]
+        )
+        local_base += wide
+        swaps.append(
+            [
+                remote(batch.at[rows_at(v, 1 - core)], lands[index].at[v], sems, base + v, sibling)
+                for v in range(wide)
+            ]
+        )
+        base += wide
+        scatters.append(ScatterPlane(owns[index], planes[index], sems, base, peers, size))
+        base += 6
+        chunk = batch.shape[1] // rows
+        spreads.append(
+            [
+                remote(
+                    sends[index].at[:, pl.ds(pl.multiple_of((row ^ k) * chunk, TILE), chunk)],
+                    zlands[index].at[k - 1],
+                    sems,
+                    base + k - 1,
+                    others[k - 1],
+                )
+                for k in range(1, rows)
+            ]
+        )
+        base += rows - 1
+    line = ReduceRows(enc_in, enc_out, *line_bufs, sems, base, local_sem, local_base)
+    base += 9
+    local_base += 4
+    line.start()
+    for v in (3, 1, 2, 0):
+        for index in range(count):
+            loads[index][v].start()
+            swaps[index][v].start()
+    first = remote(small_ref.at[1 - core], small_land, sems, base, sibling)
+    first.start()
+    plane = [
+        remote(small, small_plane.at[v - 1], sems, base + v, peers[v - 1]) for v in range(1, wide)
+    ]
+    base += wide
+    spread_small = [
+        remote(small, small_rows.at[k - 1], sems, base + k - 1, others[k - 1])
+        for k in range(1, rows)
+    ]
+    base += rows - 1
+    straight = (
+        lax.broadcasted_iota(jnp.int32, (units, TILE), 0)
+        == lax.broadcasted_iota(jnp.int32, (units, TILE), 1)
+    ).astype(low)
+
+    def hand(section, source, v):
+        return pltpu.make_async_remote_copy(
+            src_ref=ready.at[section, v],
+            dst_ref=landing.at[source, v],
+            send_sem=send_sem.at[base + section * wide + v],
+            recv_sem=recv_sem.at[base + source * wide + v],
+            device_id={"section": section, "wide": place ^ v},
+            device_id_type=MESH,
+        )
+
+    def hand_out(section, part_in, part_out):
+        turned = tn(part_out, straight).astype(low)
+        for owner in range(wide):
+            own = slice(owner * depth, (owner + 1) * depth)
+            ready[section, owner ^ place, :, pl.ds(0, 2 * TILE)] = part_in[own]
+            ready[section, owner ^ place, :, pl.ds(2 * TILE, TILE)] = turned[own]
+        for v in range(wide):
+            target = landing.at[core, v]
+            move = hand(section, core, v)
+            if v > 0:
+                move.start()
+                continue
+
+            @pl.when(core == section)
+            def _():
+                pltpu.make_async_copy(ready.at[section, 0], target, local_sem.at[local_base]).start()
+
+            @pl.when(core != section)
+            def _():
+                move.start()
+
+    def sent(section):
+        for v in range(wide):
+            wait = hand(section, core, v)
+            if v > 0:
+                wait.wait_send()
+                continue
+
+            @pl.when(core == section)
+            def _():
+                pltpu.make_async_copy(
+                    ready.at[section, 0], landing.at[core, 0], local_sem.at[local_base]
+                ).wait()
+
+            @pl.when(core != section)
+            def _():
+                wait.wait_send()
+
+    def came(source):
+        for v in range(wide):
+            wait = hand(0, source, v)
+            if v > 0:
+                wait.wait_recv()
+                continue
+
+            @pl.when(core != source)
+            def _():
+                wait.wait_recv()
+
+    def join(index, v):
+        loads[index][v].wait()
+        swaps[index][v].wait_recv()
+        owns[index][v] = (
+            owns[index][v].astype(jnp.float32) + lands[index][v].astype(jnp.float32)
+        ).astype(low)
+
+    for index in range(count):
+        join(index, 3)
+        scatters[index].send_far()
+    for index in range(count):
+        join(index, 1)
+        scatters[index].send_early(0)
+        join(index, 2)
+        scatters[index].send_early(1)
+        join(index, 0)
+    first.wait_recv()
+    small[...] = small_ref[core] + small_land[...]
+    for copy in plane:
+        copy.start()
+    hand_out(1, dec_in[...], dec_out[...])
+    line.loaded()
+    line.turn(0)
+    scatters[0].pass_on()
+    scatters[1].pass_on()
+    line.turn(1)
+    scatters[2].pass_on()
+    for copy in plane:
+        copy.wait()
+    small[...] = small[...] + jnp.sum(small_plane[...], axis=0)
+    for copy in spread_small:
+        copy.start()
+    line.turn(2)
+    for index in range(count):
+        sends[index][...] = (
+            owns[index][0].astype(jnp.float32) + scatters[index].total()
+        ).astype(low)
+        for spread in spreads[index]:
+            spread.start()
+    for index in range(3):
+        line.close(index)
+    hand_out(0, line_bufs[0][0], line_bufs[2][0])
+
+    def total(index, start, width):
+        chunk = batches[index].shape[1] // rows
+        lanes = pl.ds(pl.multiple_of(row * chunk + start, TILE), width)
+        out = sends[index][:, lanes].astype(jnp.float32)
+        for k in range(rows - 1):
+            out = out + zlands[index][k, :, pl.ds(start, width)].astype(jnp.float32)
+        return out
+
+    for index in range(count):
+        for spread in spreads[index]:
+            spread.wait_recv()
+    span = dec_ref.shape[1] // rows
+    extra = cross_ref.shape[1] // rows // 2
+    for own in range(2):
+
+        @pl.when(core == own)
+        def _():
+            keep[:, pl.ds(0, span)] = total(2 if own == 0 else 1, 0, span)
+            keep[:, pl.ds(span, extra)] = total(0, own * extra, extra)
+            give[:, pl.ds(0, span)] = total(1 if own == 0 else 2, 0, span)
+            give[:, pl.ds(span, extra)] = total(0, (1 - own) * extra, extra)
+
+    store = pltpu.make_async_copy(keep, out_ref.at[core], local_sem.at[local_base + 1])
+    last = remote(give, out_ref.at[core], sems, base + 2 * wide, sibling)
+    store.start()
+    last.start()
+    for copy in spread_small:
+        copy.wait_recv()
+    small_out[...] = small[...] + jnp.sum(small_rows[...], axis=0)
+    sent(0)
+    sent(1)
+    came(0)
+    came(1)
+    store_ffn = pltpu.make_async_copy(landing, ffn_ref, local_sem.at[local_base + 2])
+    store_ffn.start()
+    store.wait()
+    last.wait()
+    store_ffn.wait()
+    first.wait_send()
+    for copy in spread_small:
+        copy.wait_send()
+    for index in range(count):
+        for swap in swaps[index]:
+            swap.wait_send()
+        for spread in spreads[index]:
+            spread.wait_send()
+        scatters[index].finish()
+    line.finish()
+
+
+def reduce_weights(wide, rows, cross, dec, enc, dec_sums, enc_shares, small):
+    low = jnp.bfloat16
+    depth = D // wide
+    size = split_at(depth)
+    units = dec_sums[1].shape[0]
+    batches = (cross, dec, enc)
+    widths = [each.shape[1] for each in batches]
+    columns = (dec.shape[1] + cross.shape[1] // 2) // rows
+    copies = len(batches) * (wide + 6 + rows - 1) + 9 + wide + rows - 1 + 2 * wide + 1
+    small_one = pltpu.VMEM(small.shape[1:], jnp.float32)
+    return pl.pallas_call(
+        lambda *refs: reduce_kernel(wide, rows, *refs),
+        out_shape=[
+            jax.ShapeDtypeStruct((2, size, columns), jnp.float32),
+            jax.ShapeDtypeStruct((2, wide, depth, 3 * TILE), low),
+            jax.ShapeDtypeStruct(small.shape[1:], jnp.float32),
+        ],
+        in_specs=[HBM] * 3 + [VM] * 2 + [HBM] * 2 + [VM],
+        out_specs=[HBM, HBM, VM],
+        scratch_shapes=[pltpu.VMEM((wide, size, w), low) for w in widths]
+        + [pltpu.VMEM((wide, size, w), low) for w in widths]
+        + [pltpu.VMEM((3, size, w), low) for w in widths]
+        + [pltpu.VMEM((size, w), low) for w in widths]
+        + [pltpu.VMEM((rows - 1, size, w // rows), low) for w in widths]
+        + [
+            pltpu.VMEM((size, columns), jnp.float32),
+            pltpu.VMEM((size, columns), jnp.float32),
+            pltpu.VMEM((2, wide, depth, 3 * TILE), low),
+            pltpu.VMEM((2, wide, depth, 3 * TILE), low),
+            small_one,
+            small_one,
+            pltpu.VMEM((wide - 1,) + small.shape[1:], jnp.float32),
+            pltpu.VMEM((rows - 1,) + small.shape[1:], jnp.float32),
+        ]
+        + reduce_rows_scratch(units)
+        + [
+            pltpu.SemaphoreType.DMA((copies,)),
+            pltpu.SemaphoreType.DMA((copies,)),
+            pltpu.SemaphoreType.DMA((len(batches) * wide + 7,)),
+        ],
+        compiler_params=pltpu.CompilerParams(
+            collective_id=7, has_side_effects=True, vmem_limit_bytes=VMEM_LIMIT
+        ),
+        name="reduce_weights",
+    )(*batches, *dec_sums, *enc_shares, small)
+
+
+def assemble_kernel(units, parts_ref, in_ref, out_ref):
+    low = jnp.bfloat16
+    wide = parts_ref.shape[1]
+    place = lax.axis_index("wide")
+    pairs = 2 * wide
+    row_ids = lax.broadcasted_iota(jnp.int32, (TILE, TILE), 0)
+    lane_ids = lax.broadcasted_iota(jnp.int32, (TILE, TILE), 1)
+    for tile in range(in_ref.shape[2] // TILE):
+        total = None
+        for group in range(tile * TILE // units, ((tile + 1) * TILE - 1) // units + 1):
+            half, chip, block = group % 2, group % pairs // 2, group // pairs
+            shift = group * units - tile * TILE
+            picks = ((row_ids + shift == lane_ids) & (row_ids < units)).astype(low)
+            part = matmul(parts_ref[half, chip ^ place, :, pl.ds(block * TILE, TILE)], picks)
+            total = part if total is None else total + part
+        in_ref[0, :, pl.ds(tile * TILE, TILE)] = total
+    straight = (
+        lax.broadcasted_iota(jnp.int32, (units, TILE), 0)
+        == lax.broadcasted_iota(jnp.int32, (units, TILE), 1)
+    ).astype(low)
+    for chip in range(wide):
+        for half in range(2):
+            start = (chip * 2 + half) * units
+            out_ref[0, pl.ds(start, units), :] = nt(
+                straight, parts_ref[half, chip ^ place, :, pl.ds(2 * TILE, TILE)]
+            )
+
+
+def assemble(rows, parts):
+    wide, depth = parts.shape[1:3]
+    return pl.pallas_call(
+        lambda *refs: assemble_kernel(FF // (wide * rows * 2), *refs),
+        out_shape=[
+            jax.ShapeDtypeStruct((1, depth, 2 * FF // rows), jnp.float32),
+            jax.ShapeDtypeStruct((1, FF // rows, depth), jnp.float32),
+        ],
+        in_specs=[VM],
+        out_specs=[VM, VM],
+        compiler_params=pltpu.CompilerParams(vmem_limit_bytes=VMEM_LIMIT),
+        name="assemble",
+    )(parts)
+
+
+def bias_rows_kernel(enc_ref, dec_ref, enc_out, dec_out):
+    for source, target in ((enc_ref, enc_out), (dec_ref, dec_out)):
+        length, span = target.shape[1], source.shape[1]
+        for head in range(H):
+            row = jnp.broadcast_to(source[pl.ds(head, 1), :], (length, span))
+            target[head] = pltpu.roll(row, 0, 1, stride=1, stride_axis=0)[:, :length]
+
+
+def bias_rows(enc_row, dec_row):
+    return pl.pallas_call(
+        bias_rows_kernel,
+        out_shape=[
+            jax.ShapeDtypeStruct((H, LE, LE), jnp.float32),
+            jax.ShapeDtypeStruct((H, LD, LD), jnp.float32),
+        ],
+        in_specs=[VM, VM],
+        out_specs=[VM, VM],
+        name="bias_rows",
+    )(enc_row, dec_row)
+
+
+def bias_sums_kernel(enc_ref, dec_ref, enc_out, dec_out):
+    for source, target in ((enc_ref, enc_out), (dec_ref, dec_out)):
+        length, span = source.shape[1], target.shape[1]
+        flip = (
+            lax.broadcasted_iota(jnp.int32, (length, length), 0)
+            + lax.broadcasted_iota(jnp.int32, (length, length), 1)
+            == length - 1
+        ).astype(jnp.bfloat16)
+        target[...] = jnp.zeros_like(target)
+        for head in range(H):
+            flipped = matmul(flip, source[head])
+            wide = jnp.concatenate(
+                [flipped, jnp.zeros((length, span - length), jnp.float32)], axis=1
+            )
+            rolled = pltpu.roll(wide, 0, 1, stride=1, stride_axis=0)
+            target[pl.ds(head, 1), :] = jnp.sum(rolled, axis=0, keepdims=True)
+
+
+def bias_sums(enc_scores, dec_scores):
+    return pl.pallas_call(
+        bias_sums_kernel,
+        out_shape=[
+            jax.ShapeDtypeStruct((8, 2 * LE), jnp.float32),
+            jax.ShapeDtypeStruct((8, 2 * LD), jnp.float32),
+        ],
+        in_specs=[VM, VM],
+        out_specs=[VM, VM],
+        name="bias_sums",
+    )(enc_scores, dec_scores)
+
+
+def distance_hot(length, both_ways, first):
+    table = bucket_table(length, both_ways)
+    span = 2 * length
+    hot = np.zeros((NB, span), np.float32)
+    for entry in range(span):
+        distance = entry + first
+        if first == 0 and distance >= length:
+            distance -= span
+        if -length < distance < length:
+            query = max(0, -distance)
+            hot[table[query, query + distance], entry] = 1.0
+    return jnp.asarray(hot)
+
+
+def head_lanes(value, side):
+    lanes = lax.broadcasted_iota(jnp.int32, value.shape, 1)
+    return jnp.where((lanes < DH) == (side == 0), value, jnp.zeros_like(value))
+
+
+def attend_heads(query_of, key_of, value_of, bias_of, allowed, context_ref, weights_ref):
+    for pair in range(H // 2):
+        query, key, value = query_of(pair), key_of(pair), value_of(pair)
+        total = None
+        for side in range(2):
+            head = 2 * pair + side
+            scores = nt(head_lanes(query, side), key)
+            if bias_of is not None:
+                scores = scores + bias_of(head)
+            scores = jnp.where(allowed, scores, NEGATIVE)
+            shifted = jnp.exp(scores - jnp.max(scores, axis=-1, keepdims=True))
+            weights = shifted / jnp.sum(shifted, axis=-1, keepdims=True)
+            weights_ref[head] = weights
+            part = matmul(weights.astype(jnp.bfloat16), head_lanes(value, side))
+            total = part if total is None else total + part
+        context_ref[:, pl.ds(pair * TILE, TILE)] = total.astype(jnp.bfloat16)
+
+
+def attend_heads_backward(query_of, key_of, value_of, weights_ref, grad_of, put, scores_ref=None):
+    for pair in range(H // 2):
+        query, key, value, grad = query_of(pair), key_of(pair), value_of(pair), grad_of(pair)
+        sums = [None, None, None]
+        for side in range(2):
+            head = 2 * pair + side
+            weights = weights_ref[head]
+            own_grad = head_lanes(grad, side)
+            grad_weights = nt(own_grad, value)
+            inner = jnp.sum(grad_weights * weights, axis=-1, keepdims=True)
+            low = (weights * (grad_weights - inner)).astype(jnp.bfloat16)
+            if scores_ref is not None:
+                scores_ref[head] = low
+            parts = [
+                matmul(low, head_lanes(key, side)),
+                tn(low, head_lanes(query, side)),
+                tn(weights.astype(jnp.bfloat16), own_grad),
+            ]
+            sums = [b if a is None else a + b for a, b in zip(sums, parts)]
+        put(pair, *sums)
+
+
+def weight_spec(half, width, index):
+    return pl.BlockSpec((None, D, width), lambda step: (half, 0, index), memory_space=pltpu.VMEM)
+
+
+W_IN = weight_spec(0, 3 * HD, 0)
+W_OUT, C_IN, C_OUT = [weight_spec(1, HD, i) for i in range(3)]
+
+
+def tile_of(ref, base):
+    return lambda pair: ref[:, pl.ds(base + pair * TILE, TILE)]
+
+
+def self_forward_kernel(
+    causal, x_ref, gain_ref, win_ref, wout_ref, bias_ref, col_ref, row_ref, y_ref, normed_ref, projected_ref, context_ref, weights_ref
+):
+    residual = x_ref[...].astype(jnp.float32)
+    normed_ref[...] = (residual * rms_rows(residual) * gain_ref[...]).astype(jnp.bfloat16)
+    projected_ref[...] = matmul(normed_ref[...], win_ref[...]).astype(jnp.bfloat16)
+    allowed = col_ref[...] == row_ref[...]
+    if causal:
+        length = x_ref.shape[0]
+        allowed = allowed & (
+            lax.broadcasted_iota(jnp.int32, (length, length), 0)
+            >= lax.broadcasted_iota(jnp.int32, (length, length), 1)
+        )
+    attend_heads(
+        tile_of(projected_ref, 0),
+        tile_of(projected_ref, HD),
+        tile_of(projected_ref, 2 * HD),
+        lambda head: bias_ref[head],
+        allowed,
+        context_ref,
+        weights_ref,
+    )
+    y_ref[...] = residual + nt(context_ref[...], wout_ref[...])
+
+
+def self_forward(causal, residual, gain_row, weight, bias, items):
+    rows = residual.shape[0]
+    low = jnp.bfloat16
+    y, *kept = pl.pallas_call(
+        lambda *refs: self_forward_kernel(causal, *refs),
+        out_shape=[
+            jax.ShapeDtypeStruct((rows, D), jnp.float32),
+            jax.ShapeDtypeStruct((rows, D), low),
+            jax.ShapeDtypeStruct((rows, 3 * HD), low),
+            jax.ShapeDtypeStruct((rows, HD), low),
+            jax.ShapeDtypeStruct((H, rows, rows), jnp.float32),
+        ],
+        in_specs=[VM, VM, W_IN, W_OUT, VM, VM, VM],
+        out_specs=[VM] * 5,
+        grid=(1,),
+        compiler_params=pltpu.CompilerParams(vmem_limit_bytes=VMEM_LIMIT),
+        name="self_forward_%d" % rows,
+    )(residual, gain_row, weight, weight, bias, items[:, None], items[None, :])
+    return y, kept
+
+
+def self_backward_kernel(
+    g_ref,
+    x_ref,
+    gain_ref,
+    win_ref,
+    wout_ref,
+    normed_ref,
+    projected_ref,
+    context_ref,
+    weights_ref,
+    gx_ref,
+    gain_out,
+    scores_ref,
+    grad_ref,
+    context_grad,
+    projected_grad,
+):
+    low = jnp.bfloat16
+    grad_low = g_ref[...].astype(low)
+    context_grad[...] = matmul(grad_low, wout_ref[...]).astype(low)
+
+    def put(pair, query, key, value):
+        for index, part in enumerate((query, key, value)):
+            projected_grad[:, pl.ds(index * HD + pair * TILE, TILE)] = part.astype(low)
+
+    attend_heads_backward(
+        tile_of(projected_ref, 0),
+        tile_of(projected_ref, HD),
+        tile_of(projected_ref, 2 * HD),
+        weights_ref,
+        tile_of(context_grad, 0),
+        put,
+        scores_ref,
+    )
+    grad_normed = nt(projected_grad[...], win_ref[...])
+    residual = x_ref[...].astype(jnp.float32)
+    grad_residual, gain_out[...] = norm_pull(residual, gain_ref[...], grad_normed)
+    gx_ref[...] = g_ref[...] + grad_residual
+    both = jnp.concatenate([normed_ref[...], grad_low], axis=0)
+    chunks = grad_ref.shape[1] // HD
+    part_in, part_out = 3 * HD // chunks, HD // chunks
+
+    def picked(source, start, window, first, width):
+        base = start // TILE * TILE
+        window = min(window, source.shape[1] - base)
+        lanes = lax.broadcasted_iota(jnp.int32, (window, HD), 1) - first
+        rows_of = lax.broadcasted_iota(jnp.int32, (window, HD), 0) + (base - start)
+        pick = ((rows_of == lanes) & (lanes >= 0) & (lanes < width)).astype(low)
+        return matmul(source[:, pl.ds(base, window)], pick).astype(low)
+
+    for chunk in range(chunks):
+        right = jnp.concatenate(
+            [
+                picked(projected_grad, chunk * part_in, HD, 0, part_in),
+                picked(context_ref, chunk * part_out, 2 * TILE, part_in, part_out),
+            ],
+            axis=0,
+        )
+        grad_ref[:, pl.ds(chunk * HD, HD)] = tn(both, right).astype(low)
+
+
+def self_backward(grad, residual, gain_row, weight, kept):
+    rows = residual.shape[0]
+    low = jnp.bfloat16
+    return pl.pallas_call(
+        self_backward_kernel,
+        out_shape=[
+            jax.ShapeDtypeStruct((rows, D), jnp.float32),
+            jax.ShapeDtypeStruct((1, D), jnp.float32),
+            jax.ShapeDtypeStruct((H, rows, rows), low),
+            jax.ShapeDtypeStruct((D, 4 * HD), low),
+        ],
+        in_specs=[VM, VM, VM, W_IN, W_OUT] + [VM] * 4,
+        out_specs=[VM] * 4,
+        scratch_shapes=[pltpu.VMEM((rows, HD), low), pltpu.VMEM((rows, 3 * HD), low)],
+        grid=(1,),
+        compiler_params=pltpu.CompilerParams(vmem_limit_bytes=VMEM_LIMIT),
+        name="self_backward_%d" % rows,
+    )(grad, residual, gain_row, weight, weight, *kept)
+
+
+def cross_forward_kernel(
+    x_ref, final_ref, wkey_ref, wvalue_ref, y_ref, gain_ref, wquery_ref, wout_ref, col_ref, row_ref,
+    out_ref, memory_ref, kv_ref, normed_ref, query_ref, context_ref, weights_ref,
+):
+    low = jnp.bfloat16
+    residual = x_ref[...]
+    memory_ref[...] = (residual * rms_rows(residual) * final_ref[...]).astype(low)
+    kv_ref[:, pl.ds(0, HD)] = matmul(memory_ref[...], wkey_ref[...]).astype(low)
+    kv_ref[:, pl.ds(HD, HD)] = matmul(memory_ref[...], wvalue_ref[...]).astype(low)
+    target = y_ref[...]
+    normed_ref[...] = (target * rms_rows(target) * gain_ref[...]).astype(low)
+    query_ref[...] = matmul(normed_ref[...], wquery_ref[...]).astype(low)
+    attend_heads(
+        tile_of(query_ref, 0),
+        tile_of(kv_ref, 0),
+        tile_of(kv_ref, HD),
+        None,
+        col_ref[...] == row_ref[...],
+        context_ref,
+        weights_ref,
+    )
+    out_ref[...] = target + nt(context_ref[...], wout_ref[...])
+
+
+def cross_forward(x2, final_gain, enc_weight, y1, gain_row, dec_weight, dec_items, enc_items):
+    low = jnp.bfloat16
+    y2, *kept = pl.pallas_call(
+        cross_forward_kernel,
+        out_shape=[
+            jax.ShapeDtypeStruct((LD, D), jnp.float32),
+            jax.ShapeDtypeStruct((LE, D), low),
+            jax.ShapeDtypeStruct((LE, 2 * HD), low),
+            jax.ShapeDtypeStruct((LD, D), low),
+            jax.ShapeDtypeStruct((LD, HD), low),
+            jax.ShapeDtypeStruct((LD, HD), low),
+            jax.ShapeDtypeStruct((H, LD, LE), jnp.float32),
+        ],
+        in_specs=[VM, VM, C_IN, C_OUT, VM, VM, C_IN, C_OUT, VM, VM],
+        out_specs=[VM] * 7,
+        grid=(1,),
+        compiler_params=pltpu.CompilerParams(vmem_limit_bytes=VMEM_LIMIT),
+        name="cross_forward",
+    )(
+        x2,
+        final_gain,
+        enc_weight,
+        enc_weight,
+        y1,
+        gain_row,
+        dec_weight,
+        dec_weight,
+        dec_items[:, None],
+        enc_items[None, :],
+    )
+    return y2, kept
+
+
+def cross_backward_kernel(
+    g_ref, x_ref, final_ref, wkey_ref, wvalue_ref, y_ref, gain_ref, wquery_ref, wout_ref, kv_ref, query_ref, weights_ref,
+    gx_ref, gy_ref, final_out, gain_out, kv_grad, query_grad, context_grad,
+):
+    low = jnp.bfloat16
+    grad_low = g_ref[...].astype(low)
+    context_grad[...] = matmul(grad_low, wout_ref[...]).astype(low)
+
+    def put(pair, query, key, value):
+        query_grad[:, pl.ds(pair * TILE, TILE)] = query.astype(low)
+        kv_grad[:, pl.ds(pair * TILE, TILE)] = key.astype(low)
+        kv_grad[:, pl.ds(HD + pair * TILE, TILE)] = value.astype(low)
+
+    attend_heads_backward(
+        tile_of(query_ref, 0),
+        tile_of(kv_ref, 0),
+        tile_of(kv_ref, HD),
+        weights_ref,
+        tile_of(context_grad, 0),
+        put,
+    )
+    grad_memory = nt(kv_grad[:, pl.ds(0, HD)], wkey_ref[...]) + nt(
+        kv_grad[:, pl.ds(HD, HD)], wvalue_ref[...]
+    )
+    gx_ref[...], final_out[...] = norm_pull(x_ref[...], final_ref[...], grad_memory)
+    grad_residual, gain_out[...] = norm_pull(
+        y_ref[...], gain_ref[...], nt(query_grad[...], wquery_ref[...])
+    )
+    gy_ref[...] = g_ref[...] + grad_residual
+
+
+def cross_backward(g2, x2, final_gain, enc_weight, y1, gain_row, dec_weight, kv, query, weights):
+    low = jnp.bfloat16
+    return pl.pallas_call(
+        cross_backward_kernel,
+        out_shape=[
+            jax.ShapeDtypeStruct((LE, D), jnp.float32),
+            jax.ShapeDtypeStruct((LD, D), jnp.float32),
+            jax.ShapeDtypeStruct((1, D), jnp.float32),
+            jax.ShapeDtypeStruct((1, D), jnp.float32),
+            jax.ShapeDtypeStruct((LE, 2 * HD), low),
+            jax.ShapeDtypeStruct((LD, HD), low),
+        ],
+        in_specs=[VM, VM, VM, C_IN, C_OUT, VM, VM, C_IN, C_OUT, VM, VM, VM],
+        out_specs=[VM] * 6,
+        scratch_shapes=[pltpu.VMEM((LD, HD), low)],
+        grid=(1,),
+        compiler_params=pltpu.CompilerParams(vmem_limit_bytes=VMEM_LIMIT),
+        name="cross_backward",
+    )(g2, x2, final_gain, enc_weight, enc_weight, y1, gain_row, dec_weight, dec_weight, kv, query, weights)
+
+
+def column_picks(widths, rows, chunk):
+    picks, base = [], 0
+    for width in widths:
+        part = width // rows
+        pick = np.zeros((width, rows * chunk), np.float32)
+        for row in range(rows):
+            for lane in range(part):
+                pick[row * part + lane, row * chunk + base + lane] = 1.0
+        picks.append(jnp.asarray(pick, jnp.bfloat16))
+        base += part
+    return picks
+
+
+def plain_self_forward(residual, gain_row, weight, bias_full, allowed):
+    normed = to_low(rms_norm(residual, gain_row))
+    projected = to_low(matmul(normed, weight[:, : 3 * HD]))
+    context, weights, low_weights = attend_forward(
+        projected[:, :HD], projected[:, HD : 2 * HD], projected[:, 2 * HD :], bias_full, allowed
+    )
+    return (
+        residual + matmul(context, weight[:, 3 * HD : 4 * HD].T),
+        (residual, normed, projected, context, weights, low_weights),
+    )
+
+
+def plain_self_backward(kept, gain_row, weight, hot, grad_out):
+    residual, normed, projected, context, weights, low_weights = kept
+    grad_low = to_low(grad_out)
+    grad_wout = matmul(grad_low.T, context)
+    grad_context = to_low(matmul(grad_low, weight[:, 3 * HD : 4 * HD]))
+    grad_queries, grad_keys, grad_values, low_scores = attend_backward(
+        projected[:, :HD],
+        projected[:, HD : 2 * HD],
+        projected[:, 2 * HD :],
+        weights,
+        low_weights,
+        grad_context,
+    )
+    grad_projected = to_low(jnp.concatenate([grad_queries, grad_keys, grad_values], axis=1))
+    grad_win = matmul(normed.T, grad_projected)
+    grad_residual, grad_gain = plain_norm_backward(
+        residual, gain_row, matmul(grad_projected, weight[:, : 3 * HD].T)
+    )
+    grad_bias = jnp.einsum(
+        "hqk,qkb->bh", low_scores, hot.astype(jnp.bfloat16), preferred_element_type=jnp.float32
+    )
+    return grad_out + grad_residual, grad_gain, grad_win, grad_wout, grad_bias
+
+
+def plain_reduce_attn(grad, core, wide, rows):
+    depth, columns = grad.shape
+    halves = plain_core_halves(grad, core, wide)
+    place = lax.axis_index("wide")
+    parts = [
+        lax.dynamic_index_in_dim(halves, place ^ v, 0, keepdims=False) for v in range(wide)
+    ]
+    mine = to_low(scatter_wide(parts))
+    pieces, start = [], 0
+    for width in (3 * HD, HD, HD, HD):
+        pieces.append(mine[:, start : start + width].reshape(mine.shape[0], rows, width // rows))
+        start += width
+    stacked = jnp.concatenate(pieces, axis=2).transpose(1, 0, 2)
+    return lax.psum_scatter(stacked, "rows", scatter_dimension=0, tiled=True)[0]
+
+
+def plain_core_halves(grad, core, wide):
+    depth, columns = grad.shape
+    split = to_low(grad).reshape(wide, 2, depth // wide // 2, columns)
+    mine = lax.dynamic_index_in_dim(split, core, 1, keepdims=False)
+    sent = lax.dynamic_index_in_dim(split, 1 - core, 1, keepdims=False)
+    return mine.astype(jnp.float32) + xor_permute(sent, "section", 1).astype(jnp.float32)
+
+
+def plain_both_sections(own, section):
+    other = xor_permute(own, "section", 1)
+    is_dec = section == 1
+    return jnp.where(is_dec, other, own), jnp.where(is_dec, own, other)
+
+
+def plain_norm_backward(residual, gain_row, grad_normed):
+    _, norm_pull = jax.vjp(rms_norm, residual, gain_row)
+    return norm_pull(grad_normed)
 
 
 def plain_hidden_columns(weight):
@@ -793,7 +1726,7 @@
         low = to_low(jnp.concatenate([grad_gate, grad_up], axis=1))
         grad_both.append(low)
         parts.append(matmul(low, w_in.T))
-    grad_residual, grad_gain = norm_backward(residual, gain_row, scatter_wide(parts))
+    grad_residual, grad_gain = plain_norm_backward(residual, gain_row, scatter_wide(parts))
     joined = jnp.concatenate(grad_both, axis=0)
     grad_in = matmul(jnp.concatenate(blocks, axis=0).T, joined)
     grad_wout = matmul(jnp.concatenate(grad_blocks, axis=0).T, jnp.concatenate(hidden, axis=0))
@@ -807,7 +1740,7 @@
         [grad_in.reshape(depth, rows, -1), grad_wout.reshape(depth, rows, -1)], axis=2
     )
     columns = both.shape[2]
-    halves = core_halves(both.reshape(depth, rows * columns), core, wide)
+    halves = plain_core_halves(both.reshape(depth, rows * columns), core, wide)
     halves = to_low(halves).reshape(wide * (depth // wide // 2), rows, columns).transpose(1, 0, 2)
     summed = lax.psum_scatter(halves, "rows", scatter_dimension=0, tiled=True)[0]
     blocks = summed.reshape(wide, depth // wide // 2, columns)
@@ -849,7 +1782,7 @@
     unit = FF // (wide * rows)
 
     small = jnp.concatenate([norm_gains[0].reshape(-1), rel_bias[0].reshape(-1)])
-    enc_small, dec_small = both_sections(small, core)
+    enc_small, dec_small = plain_both_sections(small, core)
     gains = [each[: 3 * D].reshape(3, D) for each in (enc_small, dec_small)]
     biases = [each[3 * D :].reshape(NB, H) for each in (enc_small, dec_small)]
 
@@ -867,8 +1800,8 @@
         block = lax.dynamic_index_in_dim(ffn_blocks, place ^ v, 0, keepdims=False)
         ffn_got.append(xor_permute(block, "wide", v))
     ffn_own = placed_rows(ffn_got, place)
-    attn_enc, attn_dec = both_sections(attn_own, core)
-    ffn_enc, ffn_dec = both_sections(ffn_own, core)
+    attn_enc, attn_dec = plain_both_sections(attn_own, core)
+    ffn_enc, ffn_dec = plain_both_sections(ffn_own, core)
     memory_weight = attn_enc[:, 4 * HD :]
     cross_w_in, cross_w_out = attn_dec[:, 4 * HD : 5 * HD], attn_dec[:, 5 * HD :]
 
@@ -886,10 +1819,10 @@
     causal = jnp.arange(LD)[:, None] >= jnp.arange(LD)[None, :]
 
     cot_blocks = gather_wide(cot_row)
-    x1, enc_self = self_forward(
+    x1, enc_self = plain_self_forward(
         enc_row, gains[0][0], attn_enc, enc_bias, enc_items[:, None] == enc_items[None, :]
     )
-    y1, dec_self = self_forward(
+    y1, dec_self = plain_self_forward(
         dec_row,
         gains[1][0],
         attn_dec,
@@ -923,7 +1856,7 @@
     )
     grad_query_low = to_low(grad_queries)
     grad_kv = to_low(jnp.concatenate([grad_keys, grad_values], axis=1))
-    grad_x2, enc_final_gain = norm_backward(x2, gains[0][2], matmul(grad_kv, memory_weight.T))
+    grad_x2, enc_final_gain = plain_norm_backward(x2, gains[0][2], matmul(grad_kv, memory_weight.T))
     grad_x1, enc_ffn_gain, enc_ffn_grads = plain_ffn_backward(
         enc_ffn, gains[0][1], ffn_enc, grad_x2, gather_wide(to_low(grad_x2))
     )
@@ -931,22 +1864,22 @@
 
     grad_cross_in = matmul(cross_normed.T, grad_query_low)
     grad_memory = matmul(memory.T, grad_kv)
-    from_cross, dec_cross_gain = norm_backward(
+    from_cross, dec_cross_gain = plain_norm_backward(
         y1, gains[1][1], matmul(grad_query_low, cross_w_in.T)
     )
-    grad_y, dec_self_gain, dec_win, dec_wout, dec_bias_grad = self_backward(
+    grad_y, dec_self_gain, dec_win, dec_wout, dec_bias_grad = plain_self_backward(
         dec_self, gains[1][0], attn_dec, dec_hot, g2 + from_cross
     )
-    dec_attn_share = reduce_attn(
+    dec_attn_share = plain_reduce_attn(
         jnp.concatenate([dec_win, dec_wout, grad_cross_in, grad_cross_out], axis=1),
         core,
         wide,
         rows,
     )
-    grad_x, enc_self_gain, enc_win, enc_wout, enc_bias_grad = self_backward(
+    grad_x, enc_self_gain, enc_win, enc_wout, enc_bias_grad = plain_self_backward(
         enc_self, gains[0][0], attn_enc, enc_hot, grad_x1
     )
-    enc_attn_share = reduce_attn(
+    enc_attn_share = plain_reduce_attn(
         jnp.concatenate([enc_win, enc_wout, grad_memory], axis=1), core, wide, rows
     )
 
@@ -1018,128 +1951,108 @@
     cross_out,
 ):
     core = lax.axis_index("section")
-    place = lax.axis_index("wide")
     wide, rows = lax.axis_size("wide"), lax.axis_size("rows")
     depth = attn_in.shape[1]
-    unit = FF // (wide * rows)
-
-    small = jnp.concatenate([norm_gains[0].reshape(-1), rel_bias[0].reshape(-1)])
-    enc_small, dec_small = both_sections(small, core)
-    gains = [each[: 3 * D].reshape(3, D) for each in (enc_small, dec_small)]
-    biases = [each[3 * D :].reshape(NB, H) for each in (enc_small, dec_small)]
-
-    attn_shard = jnp.concatenate([attn_in[0], attn_out[0].T, cross_in[0], cross_out[0]], axis=1)
-    attn_own = placed_rows(gather_wide(attn_shard), place)
-    enc_blocks, dec_blocks = prepare_weights(wide, rows, ffn_in, ffn_out)
-    enc_pieces = [enc_blocks[0]] + [xor_permute(enc_blocks[v], "wide", v) for v in range(1, wide)]
-    dec_pieces = [dec_blocks[0]] + [xor_permute(dec_blocks[v], "wide", v) for v in range(1, wide)]
-    attn_enc, attn_dec = both_sections(attn_own, core)
-    memory_weight = attn_enc[:, 4 * HD :]
-    cross_w_in, cross_w_out = attn_dec[:, 4 * HD : 5 * HD], attn_dec[:, 5 * HD :]
+    is_dec = core == 1
 
     def own_row(array):
         return lax.dynamic_index_in_dim(array[:, 0], core, 0, keepdims=False)
 
-    enc_row = own_row(enc_embed).astype(jnp.float32)
-    dec_row = own_row(dec_embed).astype(jnp.float32)
-    cot_row = own_row(out_cot)
+    enc_attn, dec_half, enc_blocks, dec_blocks = start_weights(
+        wide, rows, attn_in, attn_out, cross_in, cross_out, ffn_in, ffn_out
+    )
+    enc_pieces = [enc_blocks[0]] + [xor_permute(enc_blocks[v], "wide", v) for v in range(1, wide)]
+
+    small = jnp.concatenate([norm_gains[0].reshape(-1), rel_bias[0].reshape(-1)])
+    other = xor_permute(small, "section", 1)
+    smalls = (jnp.where(is_dec, other, small), jnp.where(is_dec, small, other))
+    gains = [each[: 3 * D].reshape(3, D) for each in smalls]
+    biases = [each[3 * D :].reshape(NB, H) for each in smalls]
+    bias_lines = [
+        jnp.pad(
+            lax.dot_general(
+                bias, distance_hot(length, both, 0), (((0,), (0,)), ((), ())), precision=HIGHEST
+            ),
+            ((0, 2), (0, 0)),
+        )
+        for bias, length, both in ((biases[0], LE, True), (biases[1], LD, False))
+    ]
+    enc_bias, dec_bias = bias_rows(*bias_lines)
+    enc_row, dec_row, cot_row = own_row(enc_embed), own_row(dec_embed), own_row(out_cot)
     enc_items = item_ids(own_row(enc_lengths), LE)
     dec_items = item_ids(own_row(dec_lengths), LD)
-    enc_hot, dec_hot = one_hot(LE, True), one_hot(LD, False)
-    enc_bias = jnp.einsum("qkb,bh->hqk", enc_hot, biases[0], precision=HIGHEST)
-    dec_bias = jnp.einsum("qkb,bh->hqk", dec_hot, biases[1], precision=HIGHEST)
-    causal = jnp.arange(LD)[:, None] >= jnp.arange(LD)[None, :]
-
-    x1, enc_self = self_forward(
-        enc_row, gains[0][0], attn_enc, enc_bias, enc_items[:, None] == enc_items[None, :]
-    )
-    y1, dec_self = self_forward(
-        dec_row,
-        gains[1][0],
-        attn_dec,
-        dec_bias,
-        (dec_items[:, None] == dec_items[None, :]) & causal,
-    )
+
+    x1, enc_self = self_forward(False, enc_row, gains[0][0:1], enc_attn, enc_bias, enc_items)
+    dec_half, dec_blocks, _ = lax.optimization_barrier((dec_half, dec_blocks, enc_pieces))
     x2, *enc_ffn = ffn_forward_call(wide, x1, gains[0][1:2], enc_pieces, 2)
-    memory = to_low(rms_norm(x2, gains[0][2]))
-    memory_kv = to_low(matmul(memory, memory_weight))
-    cross_normed = to_low(rms_norm(y1, gains[1][1]))
-    queries = to_low(matmul(cross_normed, cross_w_in))
-    context, weights, low_weights = attend_forward(
-        queries,
-        memory_kv[:, :HD],
-        memory_kv[:, HD:],
-        0.0,
-        dec_items[:, None] == enc_items[None, :],
-    )
-    y2 = y1 + matmul(context, cross_w_out.T)
+    cut = split_at(depth)
+    first, second = xor_permute(dec_half, "wide", 1), xor_permute(dec_half, "wide", 2)
+    far = [xor_permute(first[:cut], "wide", 2), xor_permute(second[cut:], "wide", 1)]
+    dec_attn = place_weights(wide, [dec_half, first, second] + far)
+    dec_pieces = [dec_blocks[0]] + [xor_permute(dec_blocks[v], "wide", v) for v in range(1, wide)]
+    y1, dec_self = self_forward(True, dec_row, gains[1][0:1], dec_attn, dec_bias, dec_items)
+    y2, (memory, kv, normed, query, context, weights) = cross_forward(
+        x2, gains[0][2:3], enc_attn, y1, gains[1][1:2], dec_attn, dec_items, enc_items
+    )
     y3, *dec_ffn = ffn_forward_call(wide, y2, gains[1][2:3], dec_pieces, 3)
 
     g2, dec_ffn_gain, *dec_ffn_grads = ffn_backward_call(
         wide, rows, cot_row.astype(jnp.float32), y2, gains[1][2:3], dec_ffn, 4
     )
-    dec_ffn_share = reduce_ffn(*dec_ffn_grads, wide)
-    g2_low = to_low(g2)
-    grad_cross_out = matmul(g2_low.T, context)
-    grad_context = to_low(matmul(g2_low, cross_w_out))
-    grad_queries, grad_keys, grad_values, _ = attend_backward(
-        queries, memory_kv[:, :HD], memory_kv[:, HD:], weights, low_weights, grad_context
-    )
-    grad_query_low = to_low(grad_queries)
-    grad_kv = to_low(jnp.concatenate([grad_keys, grad_values], axis=1))
-    grad_x2, enc_final_gain = norm_backward(x2, gains[0][2], matmul(grad_kv, memory_weight.T))
-    grad_x1, enc_ffn_gain, *enc_ffn_grads = ffn_backward_call(
-        wide, rows, grad_x2, x1, gains[0][1:2], enc_ffn, 5
-    )
-    enc_ffn_share = reduce_ffn(*enc_ffn_grads, wide)
-    grad_cross_in = matmul(cross_normed.T, grad_query_low)
-    grad_memory = matmul(memory.T, grad_kv)
-    from_cross, dec_cross_gain = norm_backward(
-        y1, gains[1][1], matmul(grad_query_low, cross_w_in.T)
-    )
-    grad_y, dec_self_gain, dec_win, dec_wout, dec_bias_grad = self_backward(
-        dec_self, gains[1][0], attn_dec, dec_hot, g2 + from_cross
-    )
-    dec_attn_share = reduce_attn(
-        jnp.concatenate([dec_win, dec_wout, grad_cross_in, grad_cross_out], axis=1),
-        core,
-        wide,
-        rows,
-    )
-    grad_x, enc_self_gain, enc_win, enc_wout, enc_bias_grad = self_backward(
-        enc_self, gains[0][0], attn_enc, enc_hot, grad_x1
-    )
-    enc_attn_share = reduce_attn(
-        jnp.concatenate([enc_win, enc_wout, grad_memory], axis=1), core, wide, rows
-    )
-
+    grad_x2, g1, enc_final_gain, dec_cross_gain, kv_grad, query_grad = cross_backward(
+        g2, x2, gains[0][2:3], enc_attn, y1, gains[1][1:2], dec_attn, kv, query, weights
+    )
+    grad_x1, enc_ffn_gain, enc_in, enc_out, *dec_sums = ffn_backward_call(
+        wide, rows, grad_x2, x1, gains[0][1:2], enc_ffn, 5, dec_ffn_grads
+    )
+    grad_y, dec_self_gain, dec_scores, dec_grads = self_backward(
+        g1, dec_row, gains[1][0:1], dec_attn, dec_self
+    )
+    grad_x, enc_self_gain, enc_scores, enc_grads = self_backward(
+        grad_x1, enc_row, gains[0][0:1], enc_attn, enc_self
+    )
+    pair_picks = jnp.concatenate(column_picks((HD, HD), rows, 4 * TILE), axis=0)
+    shifted_picks = jnp.roll(pair_picks, 2 * TILE, axis=1)
+    cross_grads = to_low(
+        matmul(
+            jnp.concatenate([memory, normed, to_low(g2)], axis=0).T,
+            to_low(
+                jnp.concatenate(
+                    [
+                        matmul(kv_grad, pair_picks),
+                        matmul(query_grad, shifted_picks[:HD]),
+                        matmul(context, shifted_picks[HD:]),
+                    ],
+                    axis=0,
+                )
+            ),
+        )
+    )
+    enc_line, dec_line = bias_sums(enc_scores, dec_scores)
+    line_sums = [
+        matmul_exact(distance_hot(length, both, 1 - length), line[:H].T).reshape(1, -1)
+        for line, length, both in ((enc_line, LE, True), (dec_line, LD, False))
+    ]
+    lanes = (D + TILE - 1) // TILE * TILE
     small_grads = jnp.stack(
         [
             jnp.concatenate(
-                [enc_self_gain, enc_ffn_gain[0], enc_final_gain, enc_bias_grad.reshape(-1)]
-            ),
-            jnp.concatenate(
-                [dec_self_gain, dec_cross_gain, dec_ffn_gain[0], dec_bias_grad.reshape(-1)]
-            ),
+                [jnp.pad(each, ((0, 0), (0, lanes - each.shape[1]))) for each in group]
+                + [jnp.zeros((4, lanes), jnp.float32)],
+                axis=0,
+            )
+            for group in (
+                (enc_self_gain, enc_ffn_gain, enc_final_gain, line_sums[0]),
+                (dec_self_gain, dec_cross_gain, dec_ffn_gain, line_sums[1]),
+            )
         ]
     )
-    small_total = lax.psum(small_grads, ("section", "wide", "rows"))
-    small_own = jnp.where(core == 1, small_total[1], small_total[0])
-
-    attn_share = to_section(enc_attn_share, dec_attn_share, core).astype(jnp.float32)
-    attn_share = attn_share.reshape(depth, attn_share.shape[2])
-    in_share = to_section(enc_ffn_share[0], dec_ffn_share[0], core)
-    out_share = to_section(enc_ffn_share[1], dec_ffn_share[1], core)
-    units = unit // 2
-    ffn_in_grad = (
-        in_share.reshape(2, wide, depth, 2, TILE)[..., :units]
-        .transpose(2, 3, 1, 0, 4)
-        .reshape(depth, 2 * FF // rows)
-        .astype(jnp.float32)
-    )
-    ffn_out_grad = out_share.transpose(1, 0, 2, 3).reshape(FF // rows, depth).astype(jnp.float32)
-    widths = [3 * HD // rows, HD // rows, HD // rows]
-    edges = np.cumsum([0] + widths + [HD // rows])
+    attn_parts, ffn_parts, small_own = reduce_weights(
+        wide, rows, cross_grads, dec_grads, enc_grads, dec_sums, (enc_in, enc_out), small_grads
+    )
+    ffn_in_grad, ffn_out_grad = assemble(rows, ffn_parts)
+    attn_share = jnp.concatenate([attn_parts[0], attn_parts[1, 2 * cut - depth :]], axis=0)
+    edges = np.cumsum([0, 3 * HD // rows] + [HD // rows] * 3)
     win, wout, cin, cout = [attn_share[:, a:b] for a, b in zip(edges[:-1], edges[1:])]
 
     half = D // 2
@@ -1149,19 +2062,18 @@
         keep = lax.dynamic_index_in_dim(halves, core, 0, keepdims=False)
         send = lax.dynamic_index_in_dim(halves, 1 - core, 0, keepdims=False)
         got = xor_permute(send, "section", 1)
-        is_dec = core == 1
         return jnp.stack([jnp.where(is_dec, got, keep), jnp.where(is_dec, keep, got)])[:, None]
 
     return (
         by_half(to_low(y3)),
         by_half(grad_x),
         by_half(grad_y),
-        small_own[: 3 * D].reshape(1, 3, D),
-        small_own[3 * D :].reshape(1, NB, H),
+        small_own[None, :3, :D],
+        small_own[3, : NB * H].reshape(1, NB, H),
         win[None],
         wout.T[None],
-        ffn_in_grad[None],
-        ffn_out_grad[None],
+        ffn_in_grad,
+        ffn_out_grad,
         cin[None],
         cout[None],
     )

time: 723 us -> 624 us (0.86)
  the two profiles are of different devices: /device:TPU:0 before, /device:TPU:11 now
where the time goes in v3:
time: 624 us; the launch traced here: 614 us
  Pallas kernels  490 us (79%)
  waiting for transfers between devices  58.5 us (9%)
  local copies, waits for them, and re-layouts  32.1 us (5%)
  matrix products  12.7 us (2%)
  other arithmetic  9.71 us (2%)
  starting transfers between devices  9.06 us (1%)
    pallas_call x1, Pallas kernels, reduce_weights(): pl.pallas_call(lambda *refs: reduce_kernel(wide, rows, *refs), out_shape=...  139 us
    pallas_call x2, Pallas kernels, ffn_backward_call(): pl.pallas_call(lambda *refs: ffn_backward_kernel(wide, rows_axis, *refs),...  122 us
    pallas_call x2, Pallas kernels, ffn_forward_call(): pl.pallas_call(lambda *refs: ffn_forward_kernel(wide, *refs), out_shape=[...  119 us
    ppermute x14, waiting for transfers between devices, xor_permute(): return lax.ppermute(value, axis, [(i, i ^ distance) for i in range(count)])  58.5 us
    pallas_call x1, Pallas kernels, start_weights(): pl.pallas_call(lambda *refs: start_weights_kernel(wide, rows, *refs), out...  38.5 us
    pallas_call x2, Pallas kernels, self_backward(): pl.pallas_call(self_backward_kernel, out_shape=[jax.ShapeDtypeStruct((row...  22.7 us
    unnamed x77, local copies, waits for them, and re-layouts  15.4 us
    pallas_call x2, Pallas kernels, self_forward(): pl.pallas_call(lambda *refs: self_forward_kernel(causal, *refs), out_shap...  12.7 us
  transfers between devices with their start and end apart: 14, of which 5 were waited for; matrix products, arithmetic and copies ran while one was open for 4% of the time, Pallas kernels for 22%

profile of v3, /device:TPU:11, one launch (start us, length us, event | category | flops | bytes accessed | tf_op | source)
XLA Modules:
  0.0 613.8 jit_solution(17621189099299892695)
XLA Ops:
  0.7 4.6 copy.63.refs_5_
  5.3 38.5 %start_weights.1 = (bf16[2,1472,1152]{2,1,0:T(8,128)(2,1)}, bf16[368,1152]{1,0:T(8,128)(2,1)}, bf16[368,1536]{1,0:T(8,128)(2,1)}, bf16[368,1536]{1,0:T(8,128)(2,...) custom-call(bf16[1,368,1152]{2,1,0:T(8,128)(2,1)} %refs_0_.1, ...), custom_call_target="tpu_custom_call" | custom-call | tf_op jit(solution)/shard_map/start_weights/pallas_call | solution.py:861
  43.8 0.8 collective-permute-start.1
  45.4 1.2 collective-permute-start.3
  47.0 0.9 collective-permute-start
  48.3 0.8 bitcast_convert_fusion.refs_0_
  49.1 21.5 %collective-permute-done.1.refs_3_ = bf16[368,1536]{1,0:T(8,128)(2,1)S(1)} collective-permute-done((bf16[368,1536]{1,0:T(8,128)(2,1)}, bf16[368,1536]{1,0:T(8,128)(2,1)S(1)}, u32[]{:S(2)}, u32[]{:S(2)}) %collective-permute-start.1) | collective-permute-done | bytes 1130528 | tf_op jit(solution)/shard_map/ppermute | solution.py:127
  71.1 24.7 %collective-permute-done.3.refs_5_ = bf16[368,1536]{1,0:T(8,128)(2,1)} collective-permute-done((bf16[368,1536]{1,0:T(8,128)(2,1)}, bf16[368,1536]{1,0:T(8,128)(2,1)}, u32[]{:S(2)}, u32[]{:S(2)}) %collective-permute-start.3) | collective-permute-done | bytes 1130528 | tf_op jit(solution)/shard_map/ppermute | solution.py:127
  97.0 1.2 copy.61
  98.2 0.8 copy.64.refs_5_
  100.4 1.2 collective-permute-start.9
  104.2 11.4 %collective-permute-done.4.refs_1_ = bf16[368,1152]{1,0:T(8,128)(2,1)S(1)} collective-permute-done((bf16[368,1152]{1,0:T(8,128)(2,1)}, bf16[368,1152]{1,0:T(8,128)(2,1)S(1)}, u32[]{:S(2)}, u32[]{:S(2)}) %collective-permute-start.4) | collective-permute-done | bytes 847904 | tf_op jit(solution)/shard_map/ppermute | solution.py:127
  115.7 0.9 slice.199
  116.6 0.9 collective-permute-start.7
  122.1 2.4 bias_rows.1
  124.5 7.4 %self_forward_256.1 = (f32[256,1472]{1,0:T(8,128)}, bf16[256,1472]{1,0:T(8,128)(2,1)}, bf16[256,1152]{1,0:T(8,128)(2,1)}, bf16[256,384]{1,0:T(8,128)(2,1)}, f32[6,256,256]{2,1,0:T(8,128)}) custom-call(bf16[256,1472]{1,0:T(8,128)(2,1)} %bitcast.107, f32[1,1472]{1,0:T(1,128)} %slice.153.refs_1_.gain_ref, ...), custom_call_target="tpu_custom_call" | custom-call | tf_op jit(solution)/shard_map/self_forward_256/pallas_call | solution.py:1406
  132.0 97.2 %ffn_forward_256.1 = (f32[256,1472]{1,0:T(8,128)}, bf16[1472,1024]{1,0:T(8,128)(2,1)}, bf16[2,1024,1024]{2,1,0:T(8,128)(2,1)}, bf16[2,512,1024]{2,1,0:T(8,128)(2,1)}, bf16[2,1472,1536]{2,1,0:T(8,128)(2,1)}) custom-call(f32[256,1472]{1,0:T(8,128)} %get-tuple-element.88.refs_0_.refs_1_, f32[1,1472]{1,0:T(1,128)} %slice.160.refs_1_.refs_2_, ...), custom_call_target="tpu_custom_call" | custom-call | tf_op jit(solution)/shard_map/ffn_forward_256/pallas_call | solution.py:475
  230.7 12.2 %place_weights.1.refs_2_.refs_3_.wquery_ref.wout_ref.win_ref = bf16[2,1472,1152]{2,1,0:T(8,128)(2,1)} custom-call(bf16[368,1152]{1,0:T(8,128)(2,1)} %get-tuple-element.99.refs_0_, bf16[368,1152]{1,0:T(8,128)(2,1)} %copy-done.2, bf16[368,1152]{1,0:T(8,128)(2,1)} %copy-done.3, bf16[192,1152]{1,0:T(8,128)(2,1)} %copy-done.9, bf16[176,1152]{1,0:T(8,128)(2,1)} %copy-done.10), custom_call_target="tpu_custom_call" | custom-call | tf_op jit(solution)/shard_map/place_weights/pallas_call | solution.py:913
  242.9 5.3 self_forward_64.1
  248.2 6.5 %cross_forward.1 = (f32[64,1472]{1,0:T(8,128)}, bf16[256,1472]{1,0:T(8,128)(2,1)}, bf16[256,768]{1,0:T(8,128)(2,1)}, bf16[64,1472]{1,0:T(8,128)(2,1)}, bf16[64,3...) custom-call(f32[256,1472]{1,0:T(8,128)} %get-tuple-element.93.x_ref, f32[1,1472]{1,0:T(1,128)} %slice.162.final_ref, ...), custom_call_target="tpu_custom_call" | custom-call | tf_op jit(solution)/shard_map/cross_forward/pallas_call | solution.py:1531
  255.1 22.1 %ffn_forward_64.1 = (f32[64,1472]{1,0:T(8,128)}, bf16[1472,256]{1,0:T(8,128)(2,1)}, bf16[2,256,1024]{2,1,0:T(8,128)(2,1)}, bf16[2,512,256]{2,1,0:T(8,128)(2,1)}, bf16[2,1472,1536]{2,1,0:T(8,128)(2,1)}) custom-call(f32[64,1472]{1,0:T(8,128)} %get-tuple-element.102.refs_0_.refs_1_, f32[1,1472]{1,0:T(1,128)} %slice.171.refs_1_.refs_2_, ...), custom_call_target="tpu_custom_call" | custom-call | tf_op jit(solution)/shard_map/ffn_forward_64/pallas_call | solution.py:475
  277.2 35.5 %ffn_backward_64.1 = (f32[64,1472]{1,0:T(8,128)}, f32[1,1472]{1,0:T(1,128)}, bf16[4,1472,256]{2,1,0:T(8,128)(2,1)}, bf16[4,112,1472]{2,1,0:T(8,128)(2,1)}) custom-call(f32[64,1472]{1,0:T(8,128)} %bitcast_convert_fusion.refs_0_, f32[64,1472]{1,0:T(8,128)} %get-tuple-element.102.refs_0_.refs_1_, f32[1,1472]{1,0:T(1,128)} %slice.171.refs_1_.refs_2_, ...), custom_call_target="tpu_custom_call" | custom-call | tf_op jit(solution)/shard_map/ffn_backward_64/pallas_call | solution.py:683
  312.8 1.0 convert_element_type.40
  313.8 7.6 %cross_backward.1 = (f32[256,1472]{1,0:T(8,128)}, f32[64,1472]{1,0:T(8,128)}, f32[1,1472]{1,0:T(1,128)}, f32[1,1472]{1,0:T(1,128)}, bf16[256,768]{1,0:T(8,128)(2,1)}, /*index=5*/bf16[64,384]{1,0:T(8,128)(2,1)}) custom-call(f32[64,1472]{1,0:T(8,128)} %get-tuple-element.112.g_ref, f32[256,1472]{1,0:T(8,128)} %get-tuple-element.93.x_ref, ...), custom_call_target="tpu_custom_call" | custom-call | tf_op jit(solution)/shard_map/cross_backward/pallas_call | solution.py:1595
  321.4 8.9 %self_backward_64.1 = (f32[64,1472]{1,0:T(8,128)}, f32[1,1472]{1,0:T(1,128)}, bf16[6,64,64]{2,1,0:T(8,128)(2,1)}, bf16[1472,1536]{1,0:T(8,128)(2,1)}) custom-call(f32[64,1472]{1,0:T(8,128)} %get-tuple-element.129.g_ref, bf16[64,1472]{1,0:T(8,128)(2,1)} %dynamic-slice_bitcast_fusion.refs_0_.x_ref, f32[1,1472]{1,0:T(1,128)} %slice.164.refs_1_.gain_ref, ...), custom_call_target="tpu_custom_call" | custom-call | tf_op jit(solution)/shard_map/self_backward_64/pallas_call | solution.py:1488
  331.1 86.3 %ffn_backward_256.1 = (f32[256,1472]{1,0:T(8,128)}, f32[1,1472]{1,0:T(1,128)}, bf16[4,1472,256]{2,1,0:T(8,128)(2,1)}, bf16[4,112,1472]{2,1,0:T(8,128)(2,1)}, bf1...) custom-call(f32[256,1472]{1,0:T(8,128)} %get-tuple-element.116.refs_0_, f32[256,1472]{1,0:T(8,128)} %get-tuple-element.88.refs_0_.refs_1_, ...), custom_call_target="tpu_custom_call" | custom-call | tf_op jit(solution)/shard_map/ffn_backward_256/pallas_call | solution.py:683
  417.5 13.8 %self_backward_256.1 = (f32[256,1472]{1,0:T(8,128)}, f32[1,1472]{1,0:T(1,128)}, bf16[6,256,256]{2,1,0:T(8,128)(2,1)}, bf16[1472,1536]{1,0:T(8,128)(2,1)}) custom-call(f32[256,1472]{1,0:T(8,128)} %get-tuple-element.123.g_ref, bf16[256,1472]{1,0:T(8,128)(2,1)} %bitcast.108, f32[1,1472]{1,0:T(1,128)} %slice.153.refs_1_.gain_ref, ...), custom_call_target="tpu_custom_call" | custom-call | tf_op jit(solution)/shard_map/self_backward_256/pallas_call | solution.py:1488
  431.3 2.6 bias_sums.1
  433.9 0.8 fusion.31
  435.6 0.9 fusion.29
  436.6 1.9 convolution_convert_fusion.2
  438.9 3.0 convolution_convert_fusion.1
  442.7 5.4 convolution_convert_fusion.refs_0_
  448.1 138.8 %reduce_weights.1 = (f32[2,192,640]{2,1,0:T(8,128)}, bf16[2,4,368,384]{3,2,1,0:T(8,128)(2,1)}, f32[8,1536]{1,0:T(8,128)}) custom-call(bf16[1472,2048]{1,0:T(8,128)(2,1)} %convolution_convert_fusion.refs_0_, bf16[1472,1536]{1,0:T(8,128)(2,1)} %get-tuple-element.140.refs_1_, bf16[1472,1536]{1,0:T(8,128)(2,1)} %get-tuple-element.141.refs_2_, ...), custom_call_target="tpu_custom_call" | custom-call | tf_op jit(solution)/shard_map/reduce_weights/pallas_call | solution.py:1175
  587.0 1.1 slice_bitcast_fusion.2
  588.0 1.0 slice_bitcast_fusion.3
  589.1 0.9 fusion.24
  591.7 1.1 copy.67
  593.2 1.1 slice_bitcast_fusion.4
  596.9 1.0 copy.74
  597.9 1.7 copy.75
  599.6 5.1 assemble.1
  604.7 2.9 copy.76
  607.6 0.8 copy.77
  608.4 0.8 copy.78
  609.2 0.9 select_bitcast_fusion.3
  610.9 0.8 maximum_bitcast_fusion.1
  611.8 1.2 maximum_bitcast_fusion
  (151 shorter events, 22.8 us)
Async XLA Ops:
  0.6 48.4 %copy-start = (bf16[2,1,256,1472]{2,3,1,0:T(8,128)(2,1)S(1)}, bf16[2,1,256,1472]{2,3,1,0:T(8,128)(2,1)}, u32[]{:S(2)}) copy-start(bf16[2,1,256,1472]{2,3,1,0:T(8,128)(2,1)} %param.19) | copy-start | bytes 4521988
  5.3 41.3 %copy-start.27 = (f32[1,32,6]{1,0,2:T(1,128)S(1)}, f32[1,32,6]{1,0,2:T(1,128)}, u32[]{:S(2)}) copy-start(f32[1,32,6]{1,0,2:T(1,128)} %param.25) | copy-start | bytes 2308
  5.3 41.5 %copy-start.18 = (f32[1,3,1472]{2,0,1:T(1,128)S(1)}, f32[1,3,1472]{2,0,1:T(1,128)}, u32[]{:S(2)}) copy-start(f32[1,3,1472]{2,0,1:T(1,128)} %param.24) | copy-start | bytes 52996
  5.3 42.6 %copy-start.29 = (s32[2,1,8]{2,1,0:T(1,128)S(1)}, s32[2,1,8]{2,1,0:T(1,128)}, u32[]{:S(2)}) copy-start(s32[2,1,8]{2,1,0:T(1,128)} %param.22) | copy-start | bytes 196
  5.3 42.6 %copy-start.30 = (s32[2,1,8]{2,1,0:T(1,128)S(1)}, s32[2,1,8]{2,1,0:T(1,128)}, u32[]{:S(2)}) copy-start(s32[2,1,8]{2,1,0:T(1,128)} %param.23) | copy-start | bytes 196
  5.3 43.0 %copy-start.13 = (bf16[2,1,64,1472]{3,2,1,0:T(8,128)(2,1)S(1)}, bf16[2,1,64,1472]{3,2,1,0:T(8,128)(2,1)}, u32[]{:S(2)}) copy-start(bf16[2,1,64,1472]{3,2,1,0:T(8,128)(2,1)} %param.21) | copy-start | bytes 1130500
  43.8 26.9 %collective-permute-start.1 = (bf16[368,1536]{1,0:T(8,128)(2,1)}, bf16[368,1536]{1,0:T(8,128)(2,1)S(1)}, u32[]{:S(2)}, u32[]{:S(2)}) collective-permute-start(bf16[368,1536]{1,0:T(8,128)(2,1)} %get-tuple-element.90), channel_id=1, source_target_pairs={{0,4},{4,0},{8,12},{12,8},{1,5},{5,1},{9,13},{13,9},{2,6},{6,2},{1... | collective-permute-start | bytes 3391496 | tf_op jit(solution)/shard_map/ppermute | solution.py:127
  44.6 26.5 %collective-permute-start.2 = (bf16[368,1536]{1,0:T(8,128)(2,1)}, bf16[368,1536]{1,0:T(8,128)(2,1)}, u32[]{:S(2)}, u32[]{:S(2)}) collective-permute-start(bf16[368,1536]{1,0:T(8,128)(2,1)} %get-tuple-element.91), channel_id=1, source_target_pairs={{0,8},{4,12},{8,0},{12,4},{1,9},{5,13},{9,1},{13,5},{2,10},{6,14},... | collective-permute-start | bytes 3391496 | tf_op jit(solution)/shard_map/ppermute | solution.py:127
  45.4 50.4 %collective-permute-start.3 = (bf16[368,1536]{1,0:T(8,128)(2,1)}, bf16[368,1536]{1,0:T(8,128)(2,1)}, u32[]{:S(2)}, u32[]{:S(2)}) collective-permute-start(bf16[368,1536]{1,0:T(8,128)(2,1)} %get-tuple-element.92), channel_id=1, source_target_pairs={{0,12},{4,8},{8,4},{12,0},{1,13},{5,9},{9,5},{13,1},{2,14},{6,10},... | collective-permute-start | bytes 3391496 | tf_op jit(solution)/shard_map/ppermute | solution.py:127
  47.0 54.6 %collective-permute-start = (f32[4608]{0:T(1024)S(1)}, f32[4608]{0:T(1024)S(1)}, u32[]{:S(2)}, u32[]{:S(2)}) collective-permute-start(f32[4608]{0:T(1024)S(1)} %pad_maximum_fusion.2), channel_id=1, source_target_pairs={{0,16},{16,0},{1,17},{17,1},{2,18},{18,2},{3,19},{19,3},{4,20},{20... | collective-permute-start | bytes 55304 | tf_op jit(solution)/shard_map/ppermute | solution.py:127
  49.1 53.2 %copy-start.12 = (bf16[2,1,64,1472]{3,2,1,0:T(8,128)(2,1)S(1)}, bf16[2,1,64,1472]{3,2,1,0:T(8,128)(2,1)}, u32[]{:S(2)}) copy-start(bf16[2,1,64,1472]{3,2,1,0:T(8,128)(2,1)} %param.20) | copy-start | bytes 1130500
  70.7 25.1 %copy-start.6 = (bf16[368,1536]{1,0:T(8,128)(2,1)}, bf16[368,1536]{1,0:T(8,128)(2,1)S(1)}, u32[]{:S(2)}) copy-start(bf16[368,1536]{1,0:T(8,128)(2,1)S(1)} %collective-permute-done.1.refs_3_) | copy-start | bytes 3391492
  95.8 19.7 %collective-permute-start.4 = (bf16[368,1152]{1,0:T(8,128)(2,1)}, bf16[368,1152]{1,0:T(8,128)(2,1)S(1)}, u32[]{:S(2)}, u32[]{:S(2)}) collective-permute-start(bf16[368,1152]{1,0:T(8,128)(2,1)} %get-tuple-element.99.refs_0_), channel_id=1, source_target_pairs={{0,4},{4,0},{8,12},{12,8},{1,5},{5,1},{9,13},{13,9},{2,6},{6,2},{1... | collective-permute-start | bytes 2543624 | tf_op jit(solution)/shard_map/ppermute | solution.py:127
  96.1 19.6 %collective-permute-start.5 = (bf16[368,1152]{1,0:T(8,128)(2,1)}, bf16[368,1152]{1,0:T(8,128)(2,1)S(1)}, u32[]{:S(2)}, u32[]{:S(2)}) collective-permute-start(bf16[368,1152]{1,0:T(8,128)(2,1)} %get-tuple-element.99.refs_0_), channel_id=1, source_target_pairs={{0,8},{4,12},{8,0},{12,4},{1,9},{5,13},{9,1},{13,5},{2,10},{6,14},... | collective-permute-start | bytes 2543624 | tf_op jit(solution)/shard_map/ppermute | solution.py:127
  96.9 18.6 %copy-start.22 = (s32[256]{0:T(256)}, s32[256]{0:T(256)S(1)}, u32[]{:S(2)}) copy-start(s32[256]{0:T(256)S(1)} %convert_reduce_fusion) | copy-start | bytes 3076
  97.0 18.6 %copy-start.28 = (s32[64]{0:T(128)}, s32[64]{0:T(128)S(1)}, u32[]{:S(2)}) copy-start(s32[64]{0:T(128)S(1)} %convert_reduce_fusion.1) | copy-start | bytes 772
  98.2 19.3 %copy-start.15 = (f32[32,512]{1,0:T(8,128)S(1)}, f32[32,512]{1,0:T(8,128)}, u32[]{:S(2)}) copy-start(f32[32,512]{1,0:T(8,128)} %constant.71.clone) | copy-start | bytes 196612
  98.2 20.2 %copy-start.20 = (f32[32,128]{1,0:T(8,128)S(1)}, f32[32,128]{1,0:T(8,128)}, u32[]{:S(2)}) copy-start(f32[32,128]{1,0:T(8,128)} %constant.72.clone) | copy-start | bytes 49156
  99.7 155.0 %collective-permute-start.8 = (bf16[368,1536]{1,0:T(8,128)(2,1)}, bf16[368,1536]{1,0:T(8,128)(2,1)}, u32[]{:S(2)}, u32[]{:S(2)}) collective-permute-start(bf16[368,1536]{1,0:T(8,128)(2,1)} %get-tuple-element.104), channel_id=1, source_target_pairs={{0,4},{4,0},{8,12},{12,8},{1,5},{5,1},{9,13},{13,9},{2,6},{6,2},{1... | collective-permute-start | bytes 3391496 | tf_op jit(solution)/shard_map/ppermute | solution.py:127
  100.4 154.3 %collective-permute-start.9 = (bf16[368,1536]{1,0:T(8,128)(2,1)}, bf16[368,1536]{1,0:T(8,128)(2,1)}, u32[]{:S(2)}, u32[]{:S(2)}) collective-permute-start(bf16[368,1536]{1,0:T(8,128)(2,1)} %get-tuple-element.105), channel_id=1, source_target_pairs={{0,8},{4,12},{8,0},{12,4},{1,9},{5,13},{9,1},{13,5},{2,10},{6,14},... | collective-permute-start | bytes 3391496 | tf_op jit(solution)/shard_map/ppermute | solution.py:127
  101.6 153.5 %collective-permute-start.10 = (bf16[368,1536]{1,0:T(8,128)(2,1)}, bf16[368,1536]{1,0:T(8,128)(2,1)}, u32[]{:S(2)}, u32[]{:S(2)}) collective-permute-start(bf16[368,1536]{1,0:T(8,128)(2,1)} %get-tuple-element.106), channel_id=1, source_target_pairs={{0,12},{4,8},{8,4},{12,0},{1,13},{5,9},{9,5},{13,1},{2,14},{6,10},... | collective-permute-start | bytes 3391496 | tf_op jit(solution)/shard_map/ppermute | solution.py:127
  115.5 16.4 %copy-start.2 = (bf16[368,1152]{1,0:T(8,128)(2,1)}, bf16[368,1152]{1,0:T(8,128)(2,1)S(1)}, u32[]{:S(2)}) copy-start(bf16[368,1152]{1,0:T(8,128)(2,1)S(1)} %collective-permute-done.4.refs_1_) | copy-start | bytes 2543620
  115.6 113.6 %collective-permute-start.6 = (bf16[192,1152]{1,0:T(8,128)(2,1)S(1)}, bf16[192,1152]{1,0:T(8,128)(2,1)S(1)}, u32[]{:S(2)}, u32[]{:S(2)}) collective-permute-start(bf16[192,1152]{1,0:T(8,128)(2,1)S(1)} %slice.198), channel_id=1, source_target_pairs={{0,8},{4,12},{8,0},{12,4},{1,9},{5,13},{9,1},{13,5},{2,10},{6,14},... | collective-permute-start | bytes 1327112 | tf_op jit(solution)/shard_map/ppermute | solution.py:127
  115.7 16.3 %copy-start.3 = (bf16[368,1152]{1,0:T(8,128)(2,1)}, bf16[368,1152]{1,0:T(8,128)(2,1)S(1)}, u32[]{:S(2)}) copy-start(bf16[368,1152]{1,0:T(8,128)(2,1)S(1)} %collective-permute-done.5.refs_2_) | copy-start | bytes 2543620
  116.6 112.6 %collective-permute-start.7 = (bf16[176,1152]{1,0:T(8,128)(2,1)}, bf16[176,1152]{1,0:T(8,128)(2,1)S(1)}, u32[]{:S(2)}, u32[]{:S(2)}) collective-permute-start(bf16[176,1152]{1,0:T(8,128)(2,1)} %slice.199), channel_id=1, source_target_pairs={{0,4},{4,0},{8,12},{12,8},{1,5},{5,1},{9,13},{13,9},{2,6},{6,2},{1... | collective-permute-start | bytes 1216520 | tf_op jit(solution)/shard_map/ppermute | solution.py:127
  229.2 0.8 copy-start.10
  230.0 0.8 copy-start.9
  321.4 9.7 %copy-start.26 = (f32[1,1472]{1,0:T(1,128)S(1)}, f32[1,1472]{1,0:T(1,128)}, u32[]{:S(2)}) copy-start(f32[1,1472]{1,0:T(1,128)} %get-tuple-element.153) | copy-start | bytes 17668
  321.4 9.7 %copy-start.24 = (f32[1,1472]{1,0:T(1,128)S(1)}, f32[1,1472]{1,0:T(1,128)}, u32[]{:S(2)}) copy-start(f32[1,1472]{1,0:T(1,128)} %get-tuple-element.154) | copy-start | bytes 17668
  417.5 16.4 %copy-start.19 = (f32[32,128]{1,0:T(8,128)S(1)}, f32[32,128]{1,0:T(8,128)}, u32[]{:S(2)}) copy-start(f32[32,128]{1,0:T(8,128)} %constant.76.clone) | copy-start | bytes 49156
  417.5 18.0 %copy-start.25 = (f32[1,1472]{1,0:T(1,128)S(1)}, f32[1,1472]{1,0:T(1,128)}, u32[]{:S(2)}) copy-start(f32[1,1472]{1,0:T(1,128)} %get-tuple-element.147) | copy-start | bytes 17668
  417.5 18.1 %copy-start.23 = (f32[1,1472]{1,0:T(1,128)S(1)}, f32[1,1472]{1,0:T(1,128)}, u32[]{:S(2)}) copy-start(f32[1,1472]{1,0:T(1,128)} %get-tuple-element.148) | copy-start | bytes 17668
  417.5 18.1 %copy-start.14 = (f32[32,512]{1,0:T(8,128)S(1)}, f32[32,512]{1,0:T(8,128)}, u32[]{:S(2)}) copy-start(f32[32,512]{1,0:T(8,128)} %constant.75.clone) | copy-start | bytes 196612
  417.5 19.1 %copy-start.16 = (bf16[64,384]{1,0:T(8,128)(2,1)S(1)}, bf16[64,384]{1,0:T(8,128)(2,1)}, u32[]{:S(2)}) copy-start(bf16[64,384]{1,0:T(8,128)(2,1)} %get-tuple-element.139) | copy-start | bytes 147460
  431.3 7.2 %copy-start.4 = (bf16[384,2048]{1,0:T(8,128)(2,1)S(1)}, bf16[384,2048]{1,0:T(8,128)(2,1)}, u32[]{:S(2)}) copy-start(bf16[384,2048]{1,0:T(8,128)(2,1)} %constant.114) | copy-start | bytes 4718596
  431.3 7.2 %copy-start.17 = (bf16[64,384]{1,0:T(8,128)(2,1)S(1)}, bf16[64,384]{1,0:T(8,128)(2,1)}, u32[]{:S(2)}) copy-start(bf16[64,384]{1,0:T(8,128)(2,1)} %get-tuple-element.138) | copy-start | bytes 147460
  436.6 2.3 copy-start.32
  438.9 3.8 copy-start.31
  438.9 3.8 copy-start.33
  589.1 1.0 copy-start.11
  589.1 1.9 copy-start.5
  590.9 18.3 %collective-permute-start.11 = (bf16[64,736]{1,0:T(8,128)(2,1)}, bf16[64,736]{1,0:T(8,128)(2,1)}, u32[]{:S(2)}, u32[]{:S(2)}) collective-permute-start(bf16[64,736]{1,0:T(8,128)(2,1)} %fusion.28), channel_id=1, source_target_pairs={{0,16},{16,0},{1,17},{17,1},{2,18},{18,2},{3,19},{19,3},{4,20},{20... | collective-permute-start | bytes 282632 | tf_op jit(solution)/shard_map/ppermute | solution.py:127
  591.7 2.7 copy-start.21
  592.8 18.9 %collective-permute-start.12 = (f32[256,736]{0,1:T(8,128)}, f32[256,736]{0,1:T(8,128)S(1)}, u32[]{:S(2)}, u32[]{:S(2)}) collective-permute-start(f32[256,736]{0,1:T(8,128)} %bitcast.109), channel_id=1, source_target_pairs={{0,16},{16,0},{1,17},{17,1},{2,18},{18,2},{3,19},{19,3},{4,20},{20... | collective-permute-start | bytes 2261000 | tf_op jit(solution)/shard_map/ppermute | solution.py:127
  595.4 15.5 %collective-permute-start.13 = (f32[64,736]{1,0:T(8,128)}, f32[64,736]{1,0:T(8,128)S(1)}, u32[]{:S(2)}, u32[]{:S(2)}) collective-permute-start(f32[64,736]{1,0:T(8,128)} %fusion.19), channel_id=1, source_target_pairs={{0,16},{16,0},{1,17},{17,1},{2,18},{18,2},{3,19},{19,3},{4,20},{20... | collective-permute-start | bytes 565256 | tf_op jit(solution)/shard_map/ppermute | solution.py:127
  604.7 2.9 copy-start.8
  604.7 3.7 copy-start.7
  611.7 1.9 copy-start.1

commit v4 on v3

--- a/solution.py
+++ b/solution.py
@@ -303,10 +303,92 @@
     return grad_residual, jnp.sum(grad_normed * unit, axis=0, keepdims=True)
 
 
-def token_groups(wide, rows):
-    if rows >= 2 * TILE:
-        return [[v] for v in range(wide)]
-    return [list(range(wide))]
+def token_rows_at_once(wide, rows):
+    return rows if rows >= 2 * TILE else wide * rows
+
+
+def block_at(blocks, group, count):
+    if count == blocks.shape[1]:
+        return blocks[group]
+    return blocks[...].reshape(count, blocks.shape[2])
+
+
+def before_group(gather, group, groups):
+    if groups == 1:
+        for index in range(3):
+            gather.arrive(index)
+        return
+    for index in range(3):
+
+        @pl.when(group == index + 1)
+        def _():
+            gather.arrive(index)
+
+
+def put_parts(acc, parts, own_ref, group, groups, rows):
+    if groups == 1:
+        own_ref[...] = acc[pl.ds(0, rows)]
+        for v in range(1, parts.shape[0]):
+            parts[v] = acc[pl.ds(v * rows, rows)].astype(parts.dtype)
+        return
+
+    @pl.when(group == 0)
+    def _():
+        own_ref[...] = acc[...]
+
+    @pl.when(group > 0)
+    def _():
+        parts[group] = acc[...].astype(parts.dtype)
+
+
+def after_group(scatter, group, groups):
+    if groups == 1:
+        scatter.send_far()
+        scatter.send_early(0)
+        scatter.send_early(1)
+        return
+
+    @pl.when(group == 1)
+    def _():
+        scatter.send_early(0)
+
+    @pl.when(group == 2)
+    def _():
+        scatter.send_early(1)
+
+    @pl.when(group == 3)
+    def _():
+        scatter.send_far()
+
+
+class Reshard:
+    def __init__(self, blocks, pieces, direct, sems, base, peers):
+        row = lax.axis_index("rows")
+        shared = (blocks[0].shape[0] - direct) // 2
+        mine = pl.ds(direct + row % 2 * shared, shared)
+        other = {"rows": row ^ 1}
+        self.shared, self.direct, self.passed = [], [], []
+        for v, (block, piece) in enumerate(zip(blocks, pieces)):
+            at, peer, first = base + 3 * v, peers[v], pl.ds(0, direct)
+            self.shared.append(remote(block.at[mine], piece.at[mine], sems, at, peer))
+            self.passed.append(remote(piece.at[mine], piece.at[mine], sems, at + 1, other))
+            self.direct.append(remote(block.at[first], piece.at[first], sems, at + 2, peer))
+
+    def start(self):
+        for copy in self.shared:
+            copy.start()
+
+    def pass_on(self):
+        for copy in self.shared:
+            copy.wait_recv()
+        for copy in self.direct + self.passed:
+            copy.start()
+
+    def finish(self):
+        for copy in self.direct + self.passed:
+            copy.wait()
+        for copy in self.shared:
+            copy.wait_send()
 
 
 class ReduceRows:
@@ -314,10 +396,9 @@
         row = lax.axis_index("rows")
         near, far = {"rows": row ^ 1}, {"rows": row ^ 2}
         self.bufs, self.lands, self.first, self.second = [], [], [], []
-        lanes = [pl.ds(0, TILE), pl.ds(TILE, TILE)]
         views = [
-            (lambda ref, i, part=part: ref.at[i, :, part], source_in, in_buf, in_land)
-            for part in lanes
+            (lambda ref, i, part=part: ref.at[i, part], source_in, in_buf, in_land)
+            for part in range(2)
         ] + [(lambda ref, i: ref.at[i], source_out, out_buf, out_land)]
         for index, (view, source, buf, land) in enumerate(views):
             at = base + 3 * index
@@ -337,9 +418,8 @@
         ]
 
     def start(self):
-        for pair in self.first:
-            for copy in pair:
-                copy.start()
+        for copy in self.first[0]:
+            copy.start()
         for load in self.loads:
             load.start()
 
@@ -356,6 +436,8 @@
     def turn(self, index):
         for copy in self.first[index]:
             copy.wait_recv()
+        for copy in self.first[index + 1] if index < 2 else ():
+            copy.start()
         self.add(index, 1, 1)
         self.second[index].start()
         self.add(index, 0, 0)
@@ -374,76 +456,121 @@
 def reduce_rows_scratch(units):
     low = jnp.bfloat16
     return [
-        pltpu.VMEM((2, D, 2 * TILE), low),
-        pltpu.VMEM((3, D, 2 * TILE), low),
+        pltpu.VMEM((2, 2, D, TILE), low),
+        pltpu.VMEM((3, 2, D, TILE), low),
         pltpu.VMEM((2, units, D), low),
         pltpu.VMEM((3, units, D), low),
     ]
 
 
-def ffn_forward_kernel(wide, x_ref, gain_ref, *refs):
-    pieces = refs[:wide]
-    y_ref, at_out, pre_out, hidden_out, weight_out = refs[wide : wide + 5]
-    blocks, at, pre, hidden, weight, parts, landing, acc, send_sem, recv_sem, local_sem = refs[
-        wide + 5 :
-    ]
+def weight_tiles(weight, half, part):
+    lanes = pl.ds(part * TILE, TILE)
+    return jnp.concatenate(
+        [weight[half, quarter, :, lanes] for quarter in range(weight.shape[1])], axis=1
+    )
+
+
+def ffn_forward_kernel(wide, carried, count, x_ref, gain_ref, *refs):
+    pieces, refs = refs[:count], refs[count:]
+    if carried:
+        dec_half, dec_blocks, refs = refs[0], refs[1:wide], refs[wide:]
+    y_ref, at_out, pre_out, hidden_out, weight_out = refs[:5]
+    refs = refs[5:]
+    if carried:
+        dec_attn, dec_pieces, refs = refs[0], refs[1:wide], refs[wide:]
+    blocks, at, pre, hidden, weight, parts, landing, acc, send_sem, recv_sem, local_sem = refs[:11]
     rows = x_ref.shape[0]
-    depth = pieces[0].shape[0]
-    span = weight.shape[2] // 3
+    depth = pieces[0].shape[1]
+    span = weight.shape[1] * TILE
     core, place = lax.axis_index("section"), lax.axis_index("wide")
     peers = peers_of(wide)
     sems = (send_sem, recv_sem)
-    greet(peers)
+    greet(peers + ([{"rows": lax.axis_index("rows") ^ 1}] if carried else []))
     residual = x_ref[...]
     blocks[0] = (residual * rms_rows(residual) * gain_ref[...]).astype(jnp.bfloat16)
     gather = GatherPlane(blocks, sems, 0, peers, rows)
     gather.start()
     loads, swaps = [], []
-    for v in range(wide):
+    for index, piece in enumerate(pieces):
+        v = index if index < wide else index - wide + 1
         place_rows = pl.ds(pl.multiple_of((place ^ v) * depth, 16), depth)
-        load = pltpu.make_async_copy(pieces[v], weight.at[core, place_rows], local_sem.at[v])
-        swap = remote(pieces[v], weight.at[core, place_rows], sems, 10 + v, peers[-1])
+        target = weight.at[core, :, place_rows]
+        quarters = piece.shape[0]
+        if quarters < weight.shape[1]:
+            part = lax.axis_index("rows") % 2
+            part = part if index < wide else 1 - part
+            target = weight.at[core, pl.ds(part * quarters, quarters), place_rows]
+        load = pltpu.make_async_copy(piece, target, local_sem.at[12 + index])
+        swap = remote(piece, target, sems, 10 + index, peers[-1])
         load.start()
         swap.start()
         loads.append(load)
         swaps.append(swap)
     scatter = ScatterPlane(parts, landing, sems, 4, peers, rows)
-    for group in token_groups(wide, rows):
-        for v in group:
-            if v > 0:
-                gather.arrive(v - 1)
-        if group[0] == 0:
+    if carried:
+        held = refs[11]
+        other = {"rows": lax.axis_index("rows") ^ 1}
+        passed = [
+            remote(block, piece, sems, 24 + v, other)
+            for v, (block, piece) in enumerate(zip(dec_blocks, dec_pieces))
+        ]
+        for copy in passed:
+            copy.start()
+        dec_gather = GatherPlane(held, sems, 27, peers, depth)
+        fetch = pltpu.make_async_copy(dec_half, held.at[0], local_sem.at[7])
+        fetch.start()
+        stores, gives = [], []
+        for v in range(wide):
+            target = dec_attn.at[core, pl.ds(pl.multiple_of((place ^ v) * depth, 16), depth)]
+            stores.append(pltpu.make_async_copy(held.at[v], target, local_sem.at[8 + v]))
+            gives.append(remote(held.at[v], target, sems, 31 + v, peers[-1]))
+    count = token_rows_at_once(wide, rows)
+    groups = wide * rows // count
+
+    @pl.loop(0, groups)
+    def _(group):
+        before_group(gather, group, groups)
+
+        @pl.when(group == 0)
+        def _():
             for load in loads:
                 load.wait()
-        count = len(group) * rows
-        block = blocks[group[0] : group[-1] + 1].reshape(count, D)
-        token_rows = pl.ds(group[0] * rows, count)
-        for step in range(2):
-            if group[0] == 0 and step == 1:
+
+        token_rows = pl.ds(pl.multiple_of(group * count, count), count)
+
+        @pl.loop(0, 2)
+        def _(step):
+            @pl.when((group == 0) & (step == 1))
+            def _():
                 for swap in swaps:
                     swap.wait_recv()
-            half = core if step == 0 else 1 - core
-            gate = matmul(block, weight[half, :, pl.ds(0, span)])
-            up = matmul(block, weight[half, :, pl.ds(span, span)])
+
+            half = lax.rem(core + step, 2)
+            block = block_at(blocks, group, count)
+            gate = matmul(block, weight_tiles(weight, half, 0))
+            up = matmul(block, weight_tiles(weight, half, 1))
             pre[half, token_rows, pl.ds(0, span)] = gate.astype(jnp.bfloat16)
             pre[half, token_rows, pl.ds(span, span)] = up.astype(jnp.bfloat16)
             low = gated(gate, up).astype(jnp.bfloat16)
             hidden[half, token_rows, :] = low
-            out = nt(low, weight[half, :, pl.ds(2 * span, span)])
-            if step == 0:
-                acc[...] = out
-                continue
-            for i, v in enumerate(group):
-                own = slice(i * rows, (i + 1) * rows)
-                if v == 0:
-                    y_ref[...] = residual + acc[own] + out[own]
-                else:
-                    parts[v] = (acc[own] + out[own]).astype(jnp.bfloat16)
-        for v in group:
-            if v in (1, 2):
-                scatter.send_early(v - 1)
-            if v == 3:
-                scatter.send_far()
+            out = nt(low, weight_tiles(weight, half, 2))
+            acc[...] = jnp.where(step == 0, 0.0, acc[...]) + out
+
+        put_parts(acc, parts, y_ref, group, groups, rows)
+        after_group(scatter, group, groups)
+        if carried:
+
+            @pl.when(group == 0)
+            def _():
+                fetch.wait()
+                stores[0].start()
+                gives[0].start()
+
+            @pl.when(group == 1)
+            def _():
+                dec_gather.start()
+
+    y_ref[...] += residual
     copies = [
         pltpu.make_async_copy(pre, pre_out, local_sem.at[4]),
         pltpu.make_async_copy(weight, weight_out, local_sem.at[5]),
@@ -451,6 +578,11 @@
     for copy in copies:
         copy.start()
     scatter.pass_on()
+    if carried:
+        for v in range(1, 3):
+            dec_gather.arrive(v - 1)
+            stores[v].start()
+            gives[v].start()
     at[...] = jnp.concatenate([blocks[v] for v in range(wide)], axis=0).T
     last = pltpu.make_async_copy(at, at_out, local_sem.at[6])
     last.start()
@@ -458,6 +590,16 @@
     for half in range(2):
         hidden_out[half] = hidden[half].T
     y_ref[...] += scatter.total()
+    if carried:
+        dec_gather.arrive(2)
+        stores[3].start()
+        gives[3].start()
+        for store, give in zip(stores, gives):
+            store.wait()
+            give.wait()
+        dec_gather.finish()
+        for copy in passed:
+            copy.wait()
     for copy in copies:
         copy.wait()
     gather.finish()
@@ -466,41 +608,50 @@
         swap.wait_send()
 
 
-def ffn_forward_call(wide, residual, gain_row, pieces, call_id):
+def ffn_forward_call(wide, residual, gain_row, pieces, call_id, carried=()):
     rows = residual.shape[0]
     total = rows * wide
-    columns = pieces[0].shape[1]
-    span = columns // 3
+    quarters, _, columns = pieces[0].shape
+    span = quarters * TILE
     low = jnp.bfloat16
+    extra_out, extra_scratch = [], []
+    if carried:
+        depth, attn_columns = carried[0].shape
+        extra_out = [jax.ShapeDtypeStruct((2, D, attn_columns), low)] + [
+            jax.ShapeDtypeStruct(each.shape, low) for each in carried[1:]
+        ]
+        extra_scratch = [pltpu.VMEM((wide, depth, attn_columns), low)]
     return pl.pallas_call(
-        lambda *refs: ffn_forward_kernel(wide, *refs),
+        lambda *refs: ffn_forward_kernel(wide, bool(carried), len(pieces), *refs),
         out_shape=[
             jax.ShapeDtypeStruct((rows, D), jnp.float32),
             jax.ShapeDtypeStruct((D, total), low),
             jax.ShapeDtypeStruct((2, total, 2 * span), low),
             jax.ShapeDtypeStruct((2, span, total), low),
-            jax.ShapeDtypeStruct((2, D, columns), low),
-        ],
-        in_specs=[VM, VM] + [HBM] * wide,
-        out_specs=[VM, HBM, HBM, VM, HBM],
+            jax.ShapeDtypeStruct((2, quarters, D, columns), low),
+        ]
+        + extra_out,
+        in_specs=[VM, VM] + [HBM] * (len(pieces) + len(carried)),
+        out_specs=[VM, HBM, HBM, VM, HBM] + [HBM] * len(extra_out),
         scratch_shapes=[
             pltpu.VMEM((wide, rows, D), low),
             pltpu.VMEM((D, total), low),
             pltpu.VMEM((2, total, 2 * span), low),
             pltpu.VMEM((2, total, span), low),
-            pltpu.VMEM((2, D, columns), low),
+            pltpu.VMEM((2, quarters, D, columns), low),
             pltpu.VMEM((wide, rows, D), low),
             pltpu.VMEM((3, rows, D), low),
-            pltpu.VMEM((len(token_groups(wide, rows)[0]) * rows, D), jnp.float32),
-            pltpu.SemaphoreType.DMA((14,)),
-            pltpu.SemaphoreType.DMA((14,)),
-            pltpu.SemaphoreType.DMA((7,)),
-        ],
+            pltpu.VMEM((token_rows_at_once(wide, rows), D), jnp.float32),
+            pltpu.SemaphoreType.DMA((35,)),
+            pltpu.SemaphoreType.DMA((35,)),
+            pltpu.SemaphoreType.DMA((19,)),
+        ]
+        + extra_scratch,
         compiler_params=pltpu.CompilerParams(
             collective_id=call_id, has_side_effects=True, vmem_limit_bytes=VMEM_LIMIT
         ),
         name="ffn_forward_%d" % rows,
-    )(residual, gain_row, *pieces)
+    )(residual, gain_row, *pieces, *carried)
 
 
 def ffn_backward_kernel(
@@ -533,7 +684,7 @@
         local_sem,
     ) = refs[:15]
     rows = x_ref.shape[0]
-    span = weight.shape[2] // 3
+    span = weight.shape[1] * TILE
     units = FF // (wide * rows_axis * 2)
     core, row = lax.axis_index("section"), lax.axis_index("rows")
     peers = peers_of(wide)
@@ -556,18 +707,18 @@
     scatter = ScatterPlane(parts, landing, sems, 4, peers, rows)
     loads[0].wait()
     loads[1].wait()
-    for group in token_groups(wide, rows):
-        for v in group:
-            if v > 0:
-                if carried and v == 3:
-                    line.loaded()
-                    line.turn(0)
-                gather.arrive(v - 1)
-        count = len(group) * rows
-        block = blocks[group[0] : group[-1] + 1].reshape(count, D)
-        token_rows = pl.ds(group[0] * rows, count)
-        for half in range(2):
-            grad_hidden = matmul(block, weight[half, :, pl.ds(2 * span, span)])
+    count = token_rows_at_once(wide, rows)
+    groups = wide * rows // count
+
+    @pl.loop(0, groups)
+    def _(group):
+        before_group(gather, group, groups)
+        token_rows = pl.ds(pl.multiple_of(group * count, count), count)
+
+        @pl.loop(0, 2)
+        def _(half):
+            block = block_at(blocks, group, count)
+            grad_hidden = matmul(block, weight_tiles(weight, half, 2))
             gate = pre[half, token_rows, pl.ds(0, span)].astype(jnp.float32)
             up = pre[half, token_rows, pl.ds(span, span)].astype(jnp.float32)
             square = gate * gate
@@ -580,68 +731,84 @@
             low_up = (grad_hidden * (gate * upper)).astype(jnp.bfloat16)
             pre[half, token_rows, pl.ds(0, span)] = low_gate
             pre[half, token_rows, pl.ds(span, span)] = low_up
-            out = nt(low_gate, weight[half, :, pl.ds(0, span)]) + nt(
-                low_up, weight[half, :, pl.ds(span, span)]
+            out = nt(low_gate, weight_tiles(weight, half, 0)) + nt(
+                low_up, weight_tiles(weight, half, 1)
             )
-            if half == 0:
-                acc[...] = out
-                continue
-            for i, v in enumerate(group):
-                own = slice(i * rows, (i + 1) * rows)
-                if v == 0:
-                    gx_ref[...] = acc[own] + out[own]
-                else:
-                    parts[v] = (acc[own] + out[own]).astype(jnp.bfloat16)
-        for v in group:
-            if v in (1, 2):
-                scatter.send_early(v - 1)
-            if v == 3:
-                scatter.send_far()
+            acc[...] = jnp.where(half == 0, 0.0, acc[...]) + out
+
+        put_parts(acc, parts, gx_ref, group, groups, rows)
+        after_group(scatter, group, groups)
+        if carried:
+
+            @pl.when(group == 1)
+            def _():
+                line.loaded()
+                line.turn(0)
+
     loads[2].wait()
     loads[3].wait()
     chunk = 2 * TILE
-
-    def input_chunk(half, index):
-        columns = pl.ds(pl.multiple_of(index * chunk, chunk), chunk)
-        return matmul(at[...], pre[half, :, columns])
-
-    def output_rows(half):
-        return matmul(hidden[half], blocks[...].reshape(wide * rows, D))
-
+    swap_out = remote(give_out, got_out, sems, 11, peers[-1])
+    swap_in = remote(give_in, got_in, sems, 10, peers[-1])
+    store_in = pltpu.make_async_copy(got_in, grad_in, local_sem.at[4])
+    store_out = pltpu.make_async_copy(got_out, grad_out, local_sem.at[5])
     if carried:
         line.turn(1)
-    out_rows = output_rows(1 - core)
-    for index in range(rows_axis):
-        give_out[index] = out_rows[index * TILE : index * TILE + units].astype(jnp.bfloat16)
-    swap_out = remote(give_out, got_out, sems, 11, peers[-1])
-    swap_out.start()
-    scatter.pass_on()
-
-    @pl.loop(0, rows_axis)
-    def _(index):
-        give_in[index] = input_chunk(1 - core, index).astype(jnp.bfloat16)
-
-    swap_in = remote(give_in, got_in, sems, 10, peers[-1])
-    swap_in.start()
-    if carried:
-        line.turn(2)
-    out_rows = output_rows(core)
-    swap_out.wait_recv()
-    for index in range(rows_axis):
-        got_out[index] = (
-            out_rows[index * TILE : index * TILE + units] + got_out[index].astype(jnp.float32)
-        ).astype(jnp.bfloat16)
-    store_out = pltpu.make_async_copy(got_out, grad_out, local_sem.at[5])
-    store_out.start()
-    swap_in.wait_recv()
-
-    @pl.loop(0, rows_axis)
-    def _(index):
-        got_in[index] = (
-            input_chunk(core, index) + got_in[index].astype(jnp.float32)
-        ).astype(jnp.bfloat16)
-
-    store_in = pltpu.make_async_copy(got_in, grad_in, local_sem.at[4])
+
+    @pl.loop(0, 2)
+    def _(step):
+        half = lax.rem(core + 1 + step, 2)
+        total = matmul(hidden[half], blocks[...].reshape(wide * rows, D))
+
+        @pl.when(step == 0)
+        def _():
+            for index in range(rows_axis):
+                give_out[index] = total[index * TILE : index * TILE + units].astype(jnp.bfloat16)
+            swap_out.start()
+            scatter.pass_on()
+
+        @pl.when(step == 1)
+        def _():
+            swap_out.wait_recv()
+            for index in range(rows_axis):
+                got_out[index] = (
+                    total[index * TILE : index * TILE + units]
+                    + got_out[index].astype(jnp.float32)
+                ).astype(jnp.bfloat16)
+            store_out.start()
+
+    @pl.loop(0, 2 * rows_axis)
+    def _(step):
+        half = jnp.where(step < rows_axis, 1 - core, core)
+        index = lax.rem(step, rows_axis)
+        columns = pl.ds(pl.multiple_of(index * chunk, chunk), chunk)
+        total = matmul(at[...], pre[half, :, columns])
+
+        @pl.when(step < rows_axis)
+        def _():
+            for part in range(2):
+                give_in[index, part] = total[:, part * TILE : (part + 1) * TILE].astype(
+                    jnp.bfloat16
+                )
+
+        @pl.when(step == rows_axis - 1)
+        def _():
+            swap_in.start()
+            if carried:
+                line.turn(2)
+
+        @pl.when(step == rows_axis)
+        def _():
+            swap_in.wait_recv()
+
+        @pl.when(step >= rows_axis)
+        def _():
+            for part in range(2):
+                got_in[index, part] = (
+                    total[:, part * TILE : (part + 1) * TILE]
+                    + got_in[index, part].astype(jnp.float32)
+                ).astype(jnp.bfloat16)
+
     store_in.start()
     total = gx_ref[...] + scatter.total()
     grad_residual, grad_gain = norm_pull(x_ref[...], gain_ref[...], total)
@@ -677,7 +844,7 @@
     rows = residual.shape[0]
     low = jnp.bfloat16
     units = FF // (wide * rows_axis * 2)
-    share_in = (rows_axis, D, 2 * TILE)
+    share_in = (rows_axis, 2, D, TILE)
     share_out = (rows_axis, units, D)
     sums = [jax.ShapeDtypeStruct(each.shape[1:], low) for each in carried]
     return pl.pallas_call(
@@ -699,7 +866,7 @@
             pltpu.VMEM(weight.shape, low),
             pltpu.VMEM((wide, rows, D), low),
             pltpu.VMEM((3, rows, D), low),
-            pltpu.VMEM((len(token_groups(wide, rows)[0]) * rows, D), jnp.float32),
+            pltpu.VMEM((token_rows_at_once(wide, rows), D), jnp.float32),
             pltpu.VMEM(share_in, low),
             pltpu.VMEM(share_out, low),
             pltpu.VMEM(share_in, low),
@@ -728,7 +895,7 @@
     depth = blocks.shape[1]
     big = [
         pltpu.make_async_copy(ffn_in.at[0], in_ref, local_sem.at[4]),
-        pltpu.make_async_copy(ffn_out.at[0], out_ref, local_sem.at[5]),
+        pltpu.make_async_copy(ffn_out, out_ref, local_sem.at[5]),
     ]
     packs = [
         pltpu.make_async_copy(each, held.at[:, pl.ds(i * HD, HD)], local_sem.at[1 + i])
@@ -779,11 +946,6 @@
     per_row = FF // rows
     row_ids = lax.broadcasted_iota(jnp.int32, (2 * TILE, TILE), 0)
     lane_ids = lax.broadcasted_iota(jnp.int32, (2 * TILE, TILE), 1)
-    straight = (
-        lax.broadcasted_iota(jnp.int32, (units, TILE), 0)
-        == lax.broadcasted_iota(jnp.int32, (units, TILE), 1)
-    ).astype(jnp.bfloat16)
-
     def prepare(index):
         target, half = index // 2, index % 2
         offset = index * units
@@ -793,14 +955,14 @@
         picks = picks[:window]
         for part in range(3):
             for row in range(rows):
-                column = (part * rows + row) * TILE
                 if part < 2:
                     source = in_ref[:, pl.ds(part * FF + row * per_row + start, window)]
-                    tile = matmul(source, picks)
                 else:
-                    source = out_ref[pl.ds(row * per_row + offset, units), :]
-                    tile = tn(source, straight)
-                ffn[half, target ^ place, :, pl.ds(column, TILE)] = tile.astype(jnp.bfloat16)
+                    source = out_ref[:, pl.ds(row * per_row + start, window)]
+                tile = matmul(source, picks)
+                ffn[half, target ^ place, row, :, pl.ds(part * TILE, TILE)] = tile.astype(
+                    jnp.bfloat16
+                )
 
     for index in range(2 * wide):
         prepare(index)
@@ -856,7 +1018,7 @@
 def start_weights(wide, rows, attn_in, attn_out, cross_in, cross_out, ffn_in, ffn_out):
     depth = ffn_in.shape[1]
     low = jnp.bfloat16
-    block = jax.ShapeDtypeStruct((depth, 3 * rows * TILE), low)
+    block = jax.ShapeDtypeStruct((rows, depth, 3 * TILE), low)
     part = (depth, 3 * HD)
     attn, dec_half, *outs = pl.pallas_call(
         lambda *refs: start_weights_kernel(wide, rows, *refs),
@@ -872,7 +1034,7 @@
             pltpu.VMEM((wide,) + part, low),
             pltpu.VMEM(part, low),
             pltpu.VMEM(ffn_in.shape[1:], low),
-            pltpu.VMEM(ffn_out.shape[1:], low),
+            pltpu.VMEM((depth, FF), low),
             pltpu.VMEM((2, wide) + block.shape, low),
             pltpu.SemaphoreType.DMA((10 + 2 * wide,)),
             pltpu.SemaphoreType.DMA((10 + 2 * wide,)),
@@ -882,59 +1044,127 @@
             collective_id=1, has_side_effects=True, vmem_limit_bytes=VMEM_LIMIT
         ),
         name="start_weights",
-    )(attn_in, attn_out[0].T, cross_in, cross_out, ffn_in, ffn_out)
+    )(attn_in, attn_out[0].T, cross_in, cross_out, ffn_in, ffn_out[0].T)
     return attn, dec_half, outs[:wide], outs[wide:]
-
-
-def place_weights_kernel(wide, *refs):
-    pieces = refs[: wide + 1]
-    attn_ref, send_sem, recv_sem, local_sem = refs[wide + 1 :]
-    core, place = lax.axis_index("section"), lax.axis_index("wide")
-    sibling = {"section": 1 - core}
-    depth = pieces[0].shape[0]
-    greet([sibling])
-    stores, gives = [], []
-    for index, piece in enumerate(pieces):
-        start = (place ^ min(index, wide - 1)) * depth
-        if index == wide:
-            start = start + pieces[wide - 1].shape[0]
-        target = attn_ref.at[core, pl.ds(pl.multiple_of(start, 16), piece.shape[0])]
-        stores.append(pltpu.make_async_copy(piece, target, local_sem.at[index]))
-        gives.append(remote(piece, target, (send_sem, recv_sem), index, sibling))
-        stores[-1].start()
-        gives[-1].start()
-    for store, give in zip(stores, gives):
-        store.wait()
-        give.wait()
-
-
-def place_weights(wide, pieces):
-    depth, columns = pieces[0].shape
-    return pl.pallas_call(
-        lambda *refs: place_weights_kernel(wide, *refs),
-        out_shape=jax.ShapeDtypeStruct((2, wide * depth, columns), jnp.bfloat16),
-        in_specs=[VM] * len(pieces),
-        out_specs=HBM,
-        scratch_shapes=[pltpu.SemaphoreType.DMA((len(pieces),))] * 3,
-        compiler_params=pltpu.CompilerParams(collective_id=6, has_side_effects=True),
-        name="place_weights",
-    )(*pieces)
 
 
 def split_at(rows):
     return (rows // 2 + 15) // 16 * 16
 
 
-def reduce_kernel(wide, rows, *refs):
-    cross_ref, dec_ref, enc_ref, dec_in, dec_out, enc_in, enc_out, small_ref = refs[:8]
-    out_ref, ffn_ref, small_out = refs[8:11]
-    refs = refs[11:]
-    batches = (cross_ref, dec_ref, enc_ref)
-    count = len(batches)
-    owns, lands, planes, sends, zlands = [refs[i * count : (i + 1) * count] for i in range(5)]
-    refs = refs[5 * count :]
-    keep, give, ready, landing, small, small_land, small_plane, small_rows = refs[:8]
-    line_bufs, (send_sem, recv_sem, local_sem) = refs[8:12], refs[12:]
+class ReduceWeights:
+    def __init__(self, batch, bufs, sems, base, local_sem, local_base, peers, others, held):
+        self.own, self.land, self.plane, self.send, self.zland = bufs
+        self.batch, self.held = batch, held
+        core, place, row = lax.axis_index("section"), lax.axis_index("wide"), lax.axis_index("rows")
+        wide, size = self.own.shape[:2]
+        depth = batch.shape[0] // wide
+
+        def rows_at(v, half):
+            start = (place ^ v) * depth + half * (depth - size)
+            return pl.ds(pl.multiple_of(start, 16), size)
+
+        self.mine = [rows_at(v, core) for v in range(wide)]
+        self.loads = [
+            pltpu.make_async_copy(batch.at[self.mine[v]], self.own.at[v], local_sem.at[local_base + v])
+            for v in range(0 if held else wide)
+        ]
+        self.swaps = [
+            remote(batch.at[rows_at(v, 1 - core)], self.land.at[v], sems, base + v, peers[-1])
+            for v in range(wide)
+        ]
+        base += wide
+        self.scatter = ScatterPlane(self.own, self.plane, sems, base, peers, size)
+        base += 6
+        chunk = batch.shape[1] // (len(others) + 1)
+        self.row, self.chunk = row, chunk
+        self.spreads = [
+            remote(
+                self.send.at[:, pl.ds(pl.multiple_of((row ^ k) * chunk, TILE), chunk)],
+                self.zland.at[k - 1],
+                sems,
+                base + k - 1,
+                others[k - 1],
+            )
+            for k in range(1, len(others) + 1)
+        ]
+
+    def start(self):
+        for v in (3, 1, 2, 0):
+            self.swaps[v].start()
+            if not self.held:
+                self.loads[v].start()
+
+    def join(self):
+        def add(v):
+            self.swaps[v].wait_recv()
+            if self.held:
+                own = self.batch[self.mine[v], :]
+            else:
+                self.loads[v].wait()
+                own = self.own[v]
+            self.own[v] = (own.astype(jnp.float32) + self.land[v].astype(jnp.float32)).astype(
+                jnp.bfloat16
+            )
+
+        add(3)
+        self.scatter.send_far()
+        add(1)
+        self.scatter.send_early(0)
+        add(2)
+        self.scatter.send_early(1)
+        add(0)
+
+    def given(self):
+        for swap in self.swaps:
+            swap.wait_send()
+
+    def pass_on(self):
+        self.scatter.pass_on()
+
+    def spread(self):
+        self.send[...] = (self.own[0].astype(jnp.float32) + self.scatter.total()).astype(
+            jnp.bfloat16
+        )
+        for copy in self.spreads:
+            copy.start()
+
+    def total(self):
+        for copy in self.spreads:
+            copy.wait_recv()
+        lanes = pl.ds(pl.multiple_of(self.row * self.chunk, TILE), self.chunk)
+        out = self.send[:, lanes].astype(jnp.float32)
+        for k in range(len(self.spreads)):
+            out = out + self.zland[k].astype(jnp.float32)
+        return out
+
+    def finish(self):
+        for copy in self.spreads:
+            copy.wait_send()
+        self.scatter.finish()
+
+
+def reduce_weights_scratch(wide, rows, size, columns):
+    low = jnp.bfloat16
+    return [
+        pltpu.VMEM((wide, size, columns), low),
+        pltpu.VMEM((wide, size, columns), low),
+        pltpu.VMEM((3, size, columns), low),
+        pltpu.VMEM((size, columns), low),
+        pltpu.VMEM((rows - 1, size, columns // rows), low),
+    ]
+
+
+def last_kernel(wide, rows, *refs):
+    cross_ref, dec_in, dec_out, enc_in, enc_out, y_ref, dec_attn, enc_attn = refs[:8]
+    dec_self, enc_self, gains = refs[8:15], refs[15:22], refs[22:26]
+    out_ref, ffn_ref, small_out, y_half, x_half, t_half = refs[26:32]
+    refs = refs[32:]
+    batch_bufs = [refs[i * 5 : i * 5 + 5] for i in range(3)]
+    line_bufs, refs = refs[15:19], refs[19:]
+    held, win, wout, gx, gt, context_e, projected_e, context_d, projected_d = refs[:9]
+    keep, give, ready, landing, small, small_land, small_plane, small_rows = refs[9:17]
+    halves, (send_sem, recv_sem, local_sem) = refs[17:23], refs[23:]
     core, place, row = lax.axis_index("section"), lax.axis_index("wide"), lax.axis_index("rows")
     peers = peers_of(wide)
     sibling = peers[-1]
@@ -942,314 +1172,343 @@
     others = [{"rows": row ^ k} for k in range(1, rows)]
     sems = (send_sem, recv_sem)
     depth = cross_ref.shape[0] // wide
-    size = owns[0].shape[1]
     units = dec_out.shape[0]
     low = jnp.bfloat16
-    greet(peers + crossed + others)
-
-    def rows_at(v, half):
-        start = (place ^ v) * depth + half * (depth - size)
-        return pl.ds(pl.multiple_of(start, 16), size)
-
-    loads, swaps, scatters, spreads = [], [], [], []
-    base, local_base = 0, 0
-    for index, batch in enumerate(batches):
-        loads.append(
-            [
-                pltpu.make_async_copy(
-                    batch.at[rows_at(v, core)], owns[index].at[v], local_sem.at[local_base + v]
-                )
-                for v in range(wide)
-            ]
-        )
-        local_base += wide
-        swaps.append(
-            [
-                remote(batch.at[rows_at(v, 1 - core)], lands[index].at[v], sems, base + v, sibling)
-                for v in range(wide)
-            ]
-        )
-        base += wide
-        scatters.append(ScatterPlane(owns[index], planes[index], sems, base, peers, size))
-        base += 6
-        chunk = batch.shape[1] // rows
-        spreads.append(
-            [
-                remote(
-                    sends[index].at[:, pl.ds(pl.multiple_of((row ^ k) * chunk, TILE), chunk)],
-                    zlands[index].at[k - 1],
-                    sems,
-                    base + k - 1,
-                    others[k - 1],
-                )
-                for k in range(1, rows)
-            ]
-        )
-        base += rows - 1
-    line = ReduceRows(enc_in, enc_out, *line_bufs, sems, base, local_sem, local_base)
-    base += 9
-    local_base += 4
-    line.start()
-    for v in (3, 1, 2, 0):
-        for index in range(count):
-            loads[index][v].start()
-            swaps[index][v].start()
-    first = remote(small_ref.at[1 - core], small_land, sems, base, sibling)
-    first.start()
-    plane = [
-        remote(small, small_plane.at[v - 1], sems, base + v, peers[v - 1]) for v in range(1, wide)
-    ]
-    base += wide
-    spread_small = [
-        remote(small, small_rows.at[k - 1], sems, base + k - 1, others[k - 1])
-        for k in range(1, rows)
-    ]
-    base += rows - 1
     straight = (
         lax.broadcasted_iota(jnp.int32, (units, TILE), 0)
         == lax.broadcasted_iota(jnp.int32, (units, TILE), 1)
     ).astype(low)
 
+    def attn_loads(source):
+        return [
+            pltpu.make_async_copy(source.at[0], win, local_sem.at[0]),
+            pltpu.make_async_copy(source.at[1, :, pl.ds(0, HD)], wout, local_sem.at[1]),
+        ]
+
+    for load in attn_loads(dec_attn):
+        load.start()
+    greet(peers + crossed + others)
+    per_batch = wide + 6 + rows - 1
+    batches = [
+        ReduceWeights(
+            batch, bufs, sems, i * per_batch, local_sem, 2, peers, others, i > 0
+        )
+        for i, (batch, bufs) in enumerate(zip((cross_ref, held, held), batch_bufs))
+    ]
+    base = 3 * per_batch
+    line = ReduceRows(enc_in, enc_out, *line_bufs, sems, base, local_sem, 2 + wide)
+    base += 9
+    local_base = 6 + wide
+    first = remote(small.at[1 - core], small_land, sems, base, sibling)
+    plane = [
+        remote(small.at[core], small_plane.at[v - 1], sems, base + v, peers[v - 1])
+        for v in range(1, wide)
+    ]
+    base += wide
+    spread_small = [
+        remote(small.at[core], small_rows.at[k - 1], sems, base + k - 1, others[k - 1])
+        for k in range(1, rows)
+    ]
+    base += rows - 1
+    hand_base = base
+    base += 2 * wide
+
     def hand(section, source, v):
         return pltpu.make_async_remote_copy(
             src_ref=ready.at[section, v],
             dst_ref=landing.at[source, v],
-            send_sem=send_sem.at[base + section * wide + v],
-            recv_sem=recv_sem.at[base + source * wide + v],
+            send_sem=send_sem.at[hand_base + section * wide + v],
+            recv_sem=recv_sem.at[hand_base + source * wide + v],
             device_id={"section": section, "wide": place ^ v},
             device_id_type=MESH,
         )
+
+    def hand_home(section):
+        return pltpu.make_async_copy(ready.at[section, 0], landing.at[core, 0], local_sem.at[local_base])
 
     def hand_out(section, part_in, part_out):
         turned = tn(part_out, straight).astype(low)
         for owner in range(wide):
             own = slice(owner * depth, (owner + 1) * depth)
-            ready[section, owner ^ place, :, pl.ds(0, 2 * TILE)] = part_in[own]
+            for part in range(2):
+                ready[section, owner ^ place, :, pl.ds(part * TILE, TILE)] = part_in[part][own]
             ready[section, owner ^ place, :, pl.ds(2 * TILE, TILE)] = turned[own]
-        for v in range(wide):
-            target = landing.at[core, v]
-            move = hand(section, core, v)
-            if v > 0:
-                move.start()
-                continue
-
-            @pl.when(core == section)
+        for v in range(1, wide):
+            hand(section, core, v).start()
+
+        @pl.when(core == section)
+        def _():
+            hand_home(section).start()
+
+        @pl.when(core != section)
+        def _():
+            hand(section, core, 0).start()
+
+    def handed(section):
+        for v in range(1, wide):
+            hand(section, core, v).wait_send()
+
+        @pl.when(core == section)
+        def _():
+            hand_home(section).wait()
+
+        @pl.when(core != section)
+        def _():
+            hand(section, core, 0).wait_send()
+
+    def came(source):
+        for v in range(1, wide):
+            hand(0, source, v).wait_recv()
+
+        @pl.when(core != source)
+        def _():
+            hand(0, source, 0).wait_recv()
+
+    half_copies = []
+
+    def by_half(index, value, target):
+        mine, its = halves[2 * index : 2 * index + 2]
+        middle = D // 2
+        for own in range(2):
+
+            @pl.when(core == own)
             def _():
-                pltpu.make_async_copy(ready.at[section, 0], target, local_sem.at[local_base]).start()
-
-            @pl.when(core != section)
-            def _():
-                move.start()
-
-    def sent(section):
-        for v in range(wide):
-            wait = hand(section, core, v)
-            if v > 0:
-                wait.wait_send()
-                continue
-
-            @pl.when(core == section)
-            def _():
-                pltpu.make_async_copy(
-                    ready.at[section, 0], landing.at[core, 0], local_sem.at[local_base]
-                ).wait()
-
-            @pl.when(core != section)
-            def _():
-                wait.wait_send()
-
-    def came(source):
-        for v in range(wide):
-            wait = hand(0, source, v)
-            if v > 0:
-                wait.wait_recv()
-                continue
-
-            @pl.when(core != source)
-            def _():
-                wait.wait_recv()
-
-    def join(index, v):
-        loads[index][v].wait()
-        swaps[index][v].wait_recv()
-        owns[index][v] = (
-            owns[index][v].astype(jnp.float32) + lands[index][v].astype(jnp.float32)
-        ).astype(low)
-
-    for index in range(count):
-        join(index, 3)
-        scatters[index].send_far()
-    for index in range(count):
-        join(index, 1)
-        scatters[index].send_early(0)
-        join(index, 2)
-        scatters[index].send_early(1)
-        join(index, 0)
-    first.wait_recv()
-    small[...] = small_ref[core] + small_land[...]
+                parts = value[:, :middle], value[:, middle:]
+                mine[...] = parts[own].astype(mine.dtype)
+                its[...] = parts[1 - own].astype(its.dtype)
+
+        copies = (
+            pltpu.make_async_copy(mine, target.at[core], local_sem.at[local_base + 1 + index]),
+            remote(its, target.at[core], sems, base + index, sibling),
+        )
+        for copy in copies:
+            copy.start()
+            half_copies.append(copy)
+
+    line.start()
+    batches[0].start()
+    by_half(0, y_ref[...], y_half)
+    small[...] = jnp.zeros_like(small)
+    for i, gain in enumerate(gains):
+        small[i // 2, pl.ds(1 + i % 2, 1), pl.ds(0, D)] = gain[...]
+    hand_out(1, [dec_in[0], dec_in[1]], dec_out[...])
+    g_ref, x_ref, gain_ref, normed_ref, projected_ref, context_ref, weights_ref = dec_self
+    for load in attn_loads(dec_attn):
+        load.wait()
+    self_backward_rows(
+        g_ref, x_ref, gain_ref, win, wout, projected_ref, weights_ref, gt, small.at[1], context_d, projected_d
+    )
+    for load in attn_loads(enc_attn):
+        load.start()
+    batches[0].join()
+    self_backward_weights(g_ref, normed_ref, context_ref, projected_d, held)
+    batches[1].start()
+    by_half(2, gt[...], t_half)
+    line.loaded()
+    line.turn(0)
+    g_ref, x_ref, gain_ref, normed_ref, projected_ref, context_ref, weights_ref = enc_self
+    for load in attn_loads(enc_attn):
+        load.wait()
+    self_backward_rows(
+        g_ref, x_ref, gain_ref, win, wout, projected_ref, weights_ref, gx, small.at[0], context_e, projected_e
+    )
+    first.start()
+    batches[1].join()
+    batches[0].pass_on()
+    batches[1].given()
+    self_backward_weights(g_ref, normed_ref, context_ref, projected_e, held)
+    batches[2].start()
+    by_half(1, gx[...], x_half)
+    line.turn(1)
+    batches[2].join()
+    batches[0].spread()
+    first.wait()
+    small[core] = small[core] + small_land[...]
     for copy in plane:
         copy.start()
-    hand_out(1, dec_in[...], dec_out[...])
-    line.loaded()
-    line.turn(0)
-    scatters[0].pass_on()
-    scatters[1].pass_on()
-    line.turn(1)
-    scatters[2].pass_on()
+    batches[1].pass_on()
+    line.turn(2)
+    batches[1].spread()
+    batches[2].pass_on()
     for copy in plane:
         copy.wait()
-    small[...] = small[...] + jnp.sum(small_plane[...], axis=0)
+    small[core] = small[core] + jnp.sum(small_plane[...], axis=0)
     for copy in spread_small:
         copy.start()
-    line.turn(2)
-    for index in range(count):
-        sends[index][...] = (
-            owns[index][0].astype(jnp.float32) + scatters[index].total()
-        ).astype(low)
-        for spread in spreads[index]:
-            spread.start()
+    batches[2].spread()
     for index in range(3):
         line.close(index)
-    hand_out(0, line_bufs[0][0], line_bufs[2][0])
-
-    def total(index, start, width):
-        chunk = batches[index].shape[1] // rows
-        lanes = pl.ds(pl.multiple_of(row * chunk + start, TILE), width)
-        out = sends[index][:, lanes].astype(jnp.float32)
-        for k in range(rows - 1):
-            out = out + zlands[index][k, :, pl.ds(start, width)].astype(jnp.float32)
-        return out
-
-    for index in range(count):
-        for spread in spreads[index]:
-            spread.wait_recv()
-    span = dec_ref.shape[1] // rows
-    extra = cross_ref.shape[1] // rows // 2
+    hand_out(0, [line_bufs[0][0, 0], line_bufs[0][0, 1]], line_bufs[2][0])
+    span, part = keep.shape[1] - cross_ref.shape[1] // rows // 2, cross_ref.shape[1] // rows // 2
+    crosses = batches[0].total()
+    selfs = [batches[2].total(), batches[1].total()]
     for own in range(2):
 
         @pl.when(core == own)
         def _():
-            keep[:, pl.ds(0, span)] = total(2 if own == 0 else 1, 0, span)
-            keep[:, pl.ds(span, extra)] = total(0, own * extra, extra)
-            give[:, pl.ds(0, span)] = total(1 if own == 0 else 2, 0, span)
-            give[:, pl.ds(span, extra)] = total(0, (1 - own) * extra, extra)
-
-    store = pltpu.make_async_copy(keep, out_ref.at[core], local_sem.at[local_base + 1])
-    last = remote(give, out_ref.at[core], sems, base + 2 * wide, sibling)
+            keep[:, pl.ds(0, span)] = selfs[own]
+            keep[:, pl.ds(span, part)] = crosses[:, own * part : (own + 1) * part]
+            give[:, pl.ds(0, span)] = selfs[1 - own]
+            give[:, pl.ds(span, part)] = crosses[:, (1 - own) * part : (2 - own) * part]
+
+    store = pltpu.make_async_copy(keep, out_ref.at[core], local_sem.at[local_base + 4])
+    last = remote(give, out_ref.at[core], sems, base + 3, sibling)
     store.start()
     last.start()
     for copy in spread_small:
-        copy.wait_recv()
-    small_out[...] = small[...] + jnp.sum(small_rows[...], axis=0)
-    sent(0)
-    sent(1)
+        copy.wait()
+    small_out[...] = small[core] + jnp.sum(small_rows[...], axis=0)
+    handed(0)
+    handed(1)
     came(0)
     came(1)
-    store_ffn = pltpu.make_async_copy(landing, ffn_ref, local_sem.at[local_base + 2])
+    store_ffn = pltpu.make_async_copy(landing, ffn_ref, local_sem.at[local_base + 5])
     store_ffn.start()
     store.wait()
     last.wait()
     store_ffn.wait()
-    first.wait_send()
-    for copy in spread_small:
-        copy.wait_send()
-    for index in range(count):
-        for swap in swaps[index]:
-            swap.wait_send()
-        for spread in spreads[index]:
-            spread.wait_send()
-        scatters[index].finish()
+    for copy in half_copies:
+        copy.wait()
+    batches[0].given()
+    batches[2].given()
+    for batch in batches:
+        batch.finish()
     line.finish()
 
 
-def reduce_weights(wide, rows, cross, dec, enc, dec_sums, enc_shares, small):
+def last_step(wide, rows, cross, dec_sums, enc_shares, y3, dec_attn, enc_attn, dec_self, enc_self, gains):
     low = jnp.bfloat16
     depth = D // wide
     size = split_at(depth)
     units = dec_sums[1].shape[0]
-    batches = (cross, dec, enc)
-    widths = [each.shape[1] for each in batches]
-    columns = (dec.shape[1] + cross.shape[1] // 2) // rows
-    copies = len(batches) * (wide + 6 + rows - 1) + 9 + wide + rows - 1 + 2 * wide + 1
-    small_one = pltpu.VMEM(small.shape[1:], jnp.float32)
+    columns = cross.shape[1]
+    enc_rows, dec_rows = enc_self[0].shape[0], dec_self[0].shape[0]
+    wanted = (columns + columns // 2) // rows
+    copies = 3 * (wide + 6 + rows - 1) + 9 + wide + rows - 1 + 2 * wide + 4
+    small = (16, (D + TILE - 1) // TILE * TILE)
+    middle = D // 2
+    half_shapes = [(dec_rows, low), (enc_rows, jnp.float32), (dec_rows, jnp.float32)]
+    batch_scratch = reduce_weights_scratch(wide, rows, size, columns)
     return pl.pallas_call(
-        lambda *refs: reduce_kernel(wide, rows, *refs),
+        lambda *refs: last_kernel(wide, rows, *refs),
         out_shape=[
-            jax.ShapeDtypeStruct((2, size, columns), jnp.float32),
+            jax.ShapeDtypeStruct((2, size, wanted), jnp.float32),
             jax.ShapeDtypeStruct((2, wide, depth, 3 * TILE), low),
-            jax.ShapeDtypeStruct(small.shape[1:], jnp.float32),
-        ],
-        in_specs=[HBM] * 3 + [VM] * 2 + [HBM] * 2 + [VM],
-        out_specs=[HBM, HBM, VM],
-        scratch_shapes=[pltpu.VMEM((wide, size, w), low) for w in widths]
-        + [pltpu.VMEM((wide, size, w), low) for w in widths]
-        + [pltpu.VMEM((3, size, w), low) for w in widths]
-        + [pltpu.VMEM((size, w), low) for w in widths]
-        + [pltpu.VMEM((rows - 1, size, w // rows), low) for w in widths]
+            jax.ShapeDtypeStruct(small, jnp.float32),
+        ]
+        + [jax.ShapeDtypeStruct((2, each, middle), kind) for each, kind in half_shapes],
+        in_specs=[HBM, VM, VM, HBM, HBM, VM, HBM, HBM] + [VM] * 18,
+        out_specs=[HBM, HBM, VM, HBM, HBM, HBM],
+        scratch_shapes=batch_scratch * 3
+        + reduce_rows_scratch(units)
         + [
-            pltpu.VMEM((size, columns), jnp.float32),
-            pltpu.VMEM((size, columns), jnp.float32),
+            pltpu.VMEM((D, columns), low),
+            pltpu.VMEM((D, 3 * HD), low),
+            pltpu.VMEM((D, HD), low),
+            pltpu.VMEM((enc_rows, D), jnp.float32),
+            pltpu.VMEM((dec_rows, D), jnp.float32),
+            pltpu.VMEM((enc_rows, HD), low),
+            pltpu.VMEM((enc_rows, 3 * HD), low),
+            pltpu.VMEM((dec_rows, HD), low),
+            pltpu.VMEM((dec_rows, 3 * HD), low),
+            pltpu.VMEM((size, wanted), jnp.float32),
+            pltpu.VMEM((size, wanted), jnp.float32),
             pltpu.VMEM((2, wide, depth, 3 * TILE), low),
             pltpu.VMEM((2, wide, depth, 3 * TILE), low),
-            small_one,
-            small_one,
-            pltpu.VMEM((wide - 1,) + small.shape[1:], jnp.float32),
-            pltpu.VMEM((rows - 1,) + small.shape[1:], jnp.float32),
+            pltpu.VMEM((2,) + small, jnp.float32),
+            pltpu.VMEM(small, jnp.float32),
+            pltpu.VMEM((wide - 1,) + small, jnp.float32),
+            pltpu.VMEM((rows - 1,) + small, jnp.float32),
         ]
-        + reduce_rows_scratch(units)
+        + [pltpu.VMEM((each, middle), kind) for each, kind in half_shapes for _ in range(2)]
         + [
             pltpu.SemaphoreType.DMA((copies,)),
             pltpu.SemaphoreType.DMA((copies,)),
-            pltpu.SemaphoreType.DMA((len(batches) * wide + 7,)),
+            pltpu.SemaphoreType.DMA((12 + wide,)),
         ],
         compiler_params=pltpu.CompilerParams(
             collective_id=7, has_side_effects=True, vmem_limit_bytes=VMEM_LIMIT
         ),
-        name="reduce_weights",
-    )(*batches, *dec_sums, *enc_shares, small)
-
-
-def assemble_kernel(units, parts_ref, in_ref, out_ref):
+        name="last_step",
+    )(cross, *dec_sums, *enc_shares, y3, dec_attn, enc_attn, *dec_self, *enc_self, *gains)
+
+
+def assemble_kernel(
+    units, parts_ref, attn_ref, small_ref, enc_hot, dec_hot,
+    in_ref, out_ref, gain_ref, bias_ref, win_ref, wout_ref, cin_ref, cout_ref,
+):
     low = jnp.bfloat16
     wide = parts_ref.shape[1]
-    place = lax.axis_index("wide")
+    place, core = lax.axis_index("wide"), lax.axis_index("section")
     pairs = 2 * wide
     row_ids = lax.broadcasted_iota(jnp.int32, (TILE, TILE), 0)
     lane_ids = lax.broadcasted_iota(jnp.int32, (TILE, TILE), 1)
-    for tile in range(in_ref.shape[2] // TILE):
+
+    def tile_at(tile, first, columns):
         total = None
-        for group in range(tile * TILE // units, ((tile + 1) * TILE - 1) // units + 1):
+        last = min((tile + 1) * TILE, columns) - 1
+        for group in range(tile * TILE // units, last // units + 1):
             half, chip, block = group % 2, group % pairs // 2, group // pairs
             shift = group * units - tile * TILE
             picks = ((row_ids + shift == lane_ids) & (row_ids < units)).astype(low)
-            part = matmul(parts_ref[half, chip ^ place, :, pl.ds(block * TILE, TILE)], picks)
+            part = matmul(
+                parts_ref[half, chip ^ place, :, pl.ds((first + block) * TILE, TILE)], picks
+            )
             total = part if total is None else total + part
-        in_ref[0, :, pl.ds(tile * TILE, TILE)] = total
-    straight = (
-        lax.broadcasted_iota(jnp.int32, (units, TILE), 0)
-        == lax.broadcasted_iota(jnp.int32, (units, TILE), 1)
-    ).astype(low)
-    for chip in range(wide):
-        for half in range(2):
-            start = (chip * 2 + half) * units
-            out_ref[0, pl.ds(start, units), :] = nt(
-                straight, parts_ref[half, chip ^ place, :, pl.ds(2 * TILE, TILE)]
+        return total
+
+    for tile in range(in_ref.shape[2] // TILE):
+        in_ref[0, :, pl.ds(tile * TILE, TILE)] = tile_at(tile, 0, in_ref.shape[2])
+    for tile in range(out_ref.shape[2] // TILE):
+        out_ref[0, :, pl.ds(tile * TILE, TILE)] = tile_at(tile, 2, out_ref.shape[2])
+    gain_ref[0] = small_ref[0:3, 0:D]
+    for section, hot in enumerate((enc_hot, dec_hot)):
+
+        @pl.when(core == section)
+        def _():
+            sums = small_ref[8:16, 0 : hot.shape[1]]
+            bias = lax.dot_general(
+                hot[...], sums, (((1,), (1,)), ((), ())), precision=HIGHEST, preferred_element_type=jnp.float32
             )
-
-
-def assemble(rows, parts):
+            bias_ref[0] = bias[:, :H]
+
+    size, depth = attn_ref.shape[1], in_ref.shape[1]
+    whole = jnp.concatenate([attn_ref[0], attn_ref[1, 2 * size - depth :]], axis=0)
+    width_in, width = win_ref.shape[2], cin_ref.shape[2]
+    win_ref[0] = whole[:, :width_in]
+    base = width_in // TILE * TILE
+    turned = whole[:, base : base + TILE].T
+    wout_ref[0] = turned[width_in - base : width_in - base + width]
+    cin_ref[0] = whole[:, width_in + width : width_in + 2 * width]
+    cout_ref[0] = whole[:, width_in + 2 * width : width_in + 3 * width]
+
+
+def assemble(rows, parts, attn_parts, small):
     wide, depth = parts.shape[1:3]
+    shapes = [
+        (depth, 2 * FF // rows),
+        (depth, FF // rows),
+        (3, D),
+        (NB, H),
+        (depth, 3 * HD // rows),
+        (HD // rows, depth),
+        (depth, HD // rows),
+        (depth, HD // rows),
+    ]
     return pl.pallas_call(
         lambda *refs: assemble_kernel(FF // (wide * rows * 2), *refs),
-        out_shape=[
-            jax.ShapeDtypeStruct((1, depth, 2 * FF // rows), jnp.float32),
-            jax.ShapeDtypeStruct((1, FF // rows, depth), jnp.float32),
-        ],
-        in_specs=[VM],
-        out_specs=[VM, VM],
+        out_shape=[jax.ShapeDtypeStruct((1, *shape), jnp.float32) for shape in shapes],
+        in_specs=[VM] * 5,
+        out_specs=[VM] * len(shapes),
         compiler_params=pltpu.CompilerParams(vmem_limit_bytes=VMEM_LIMIT),
         name="assemble",
-    )(parts)
+    )(
+        parts,
+        attn_parts,
+        small,
+        distance_hot(LE, True, 1 - LE),
+        distance_hot(LD, False, 1 - LD),
+    )
 
 
 def bias_rows_kernel(enc_ref, dec_ref, enc_out, dec_out):
@@ -1273,35 +1532,17 @@
     )(enc_row, dec_row)
 
 
-def bias_sums_kernel(enc_ref, dec_ref, enc_out, dec_out):
-    for source, target in ((enc_ref, enc_out), (dec_ref, dec_out)):
-        length, span = source.shape[1], target.shape[1]
-        flip = (
-            lax.broadcasted_iota(jnp.int32, (length, length), 0)
-            + lax.broadcasted_iota(jnp.int32, (length, length), 1)
-            == length - 1
-        ).astype(jnp.bfloat16)
-        target[...] = jnp.zeros_like(target)
-        for head in range(H):
-            flipped = matmul(flip, source[head])
-            wide = jnp.concatenate(
-                [flipped, jnp.zeros((length, span - length), jnp.float32)], axis=1
-            )
-            rolled = pltpu.roll(wide, 0, 1, stride=1, stride_axis=0)
-            target[pl.ds(head, 1), :] = jnp.sum(rolled, axis=0, keepdims=True)
-
-
-def bias_sums(enc_scores, dec_scores):
-    return pl.pallas_call(
-        bias_sums_kernel,
-        out_shape=[
-            jax.ShapeDtypeStruct((8, 2 * LE), jnp.float32),
-            jax.ShapeDtypeStruct((8, 2 * LD), jnp.float32),
-        ],
-        in_specs=[VM, VM],
-        out_specs=[VM, VM],
-        name="bias_sums",
-    )(enc_scores, dec_scores)
+def distance_sums(scores, span):
+    length = scores.shape[0]
+    flip = (
+        lax.broadcasted_iota(jnp.int32, (length, length), 0)
+        + lax.broadcasted_iota(jnp.int32, (length, length), 1)
+        == length - 1
+    ).astype(jnp.bfloat16)
+    flipped = matmul(flip, scores)
+    padded = jnp.concatenate([flipped, jnp.zeros((length, span - length), jnp.float32)], axis=1)
+    rolled = pltpu.roll(padded, 0, 1, stride=1, stride_axis=0)
+    return jnp.sum(rolled, axis=0, keepdims=True)
 
 
 def distance_hot(length, both_ways, first):
@@ -1341,7 +1582,7 @@
         context_ref[:, pl.ds(pair * TILE, TILE)] = total.astype(jnp.bfloat16)
 
 
-def attend_heads_backward(query_of, key_of, value_of, weights_ref, grad_of, put, scores_ref=None):
+def attend_heads_backward(query_of, key_of, value_of, weights_ref, grad_of, put, put_scores=None):
     for pair in range(H // 2):
         query, key, value, grad = query_of(pair), key_of(pair), value_of(pair), grad_of(pair)
         sums = [None, None, None]
@@ -1352,8 +1593,8 @@
             grad_weights = nt(own_grad, value)
             inner = jnp.sum(grad_weights * weights, axis=-1, keepdims=True)
             low = (weights * (grad_weights - inner)).astype(jnp.bfloat16)
-            if scores_ref is not None:
-                scores_ref[head] = low
+            if put_scores is not None:
+                put_scores(head, low)
             parts = [
                 matmul(low, head_lanes(key, side)),
                 tn(low, head_lanes(query, side)),
@@ -1375,9 +1616,22 @@
     return lambda pair: ref[:, pl.ds(base + pair * TILE, TILE)]
 
 
-def self_forward_kernel(
-    causal, x_ref, gain_ref, win_ref, wout_ref, bias_ref, col_ref, row_ref, y_ref, normed_ref, projected_ref, context_ref, weights_ref
-):
+def self_forward_kernel(wide, causal, x_ref, gain_ref, win_ref, wout_ref, bias_ref, col_ref, row_ref, *refs):
+    if wide:
+        blocks, dec_blocks, refs = refs[: wide - 1], refs[wide - 1 : 2 * wide - 2], refs[2 * wide - 2 :]
+    y_ref, normed_ref, projected_ref, context_ref, weights_ref = refs[:5]
+    if wide:
+        pieces, dec_pieces, sems = refs[5 : 4 + wide], refs[4 + wide : 3 + 2 * wide], refs[3 + 2 * wide :]
+        peers = peers_of(wide)
+        greet(peers + [{"rows": lax.axis_index("rows") ^ 1}])
+        reshard = Reshard(blocks, pieces, blocks[0].shape[0] // 2, sems, 0, peers)
+        reshard.start()
+        half = dec_pieces[0].shape[0]
+        mine = pl.ds(lax.axis_index("rows") % 2 * half, half)
+        later = [
+            remote(block.at[mine], piece, sems, 9 + v, peers[v])
+            for v, (block, piece) in enumerate(zip(dec_blocks, dec_pieces))
+        ]
     residual = x_ref[...].astype(jnp.float32)
     normed_ref[...] = (residual * rms_rows(residual) * gain_ref[...]).astype(jnp.bfloat16)
     projected_ref[...] = matmul(normed_ref[...], win_ref[...]).astype(jnp.bfloat16)
@@ -1398,53 +1652,75 @@
         weights_ref,
     )
     y_ref[...] = residual + nt(context_ref[...], wout_ref[...])
-
-
-def self_forward(causal, residual, gain_row, weight, bias, items):
+    if wide:
+        reshard.pass_on()
+        for copy in later:
+            copy.start()
+        reshard.finish()
+        for copy in later:
+            copy.wait()
+
+
+def self_forward(causal, residual, gain_row, weight, bias, items, blocks=(), dec_blocks=()):
     rows = residual.shape[0]
     low = jnp.bfloat16
+    wide = len(blocks) + 1 if blocks else 0
+    params = dict(vmem_limit_bytes=VMEM_LIMIT)
+    if blocks:
+        params.update(collective_id=6, has_side_effects=True)
     y, *kept = pl.pallas_call(
-        lambda *refs: self_forward_kernel(causal, *refs),
+        lambda *refs: self_forward_kernel(wide, causal, *refs),
         out_shape=[
             jax.ShapeDtypeStruct((rows, D), jnp.float32),
             jax.ShapeDtypeStruct((rows, D), low),
             jax.ShapeDtypeStruct((rows, 3 * HD), low),
             jax.ShapeDtypeStruct((rows, HD), low),
             jax.ShapeDtypeStruct((H, rows, rows), jnp.float32),
-        ],
-        in_specs=[VM, VM, W_IN, W_OUT, VM, VM, VM],
-        out_specs=[VM] * 5,
+        ]
+        + [jax.ShapeDtypeStruct(each.shape, low) for each in blocks]
+        + [jax.ShapeDtypeStruct((each.shape[0] // 2, *each.shape[1:]), low) for each in dec_blocks],
+        in_specs=[VM, VM, W_IN, W_OUT, VM, VM, VM] + [HBM] * (2 * len(blocks)),
+        out_specs=[VM] * 5 + [HBM] * (2 * len(blocks)),
+        scratch_shapes=[pltpu.SemaphoreType.DMA((12,))] * 2 if blocks else [],
         grid=(1,),
-        compiler_params=pltpu.CompilerParams(vmem_limit_bytes=VMEM_LIMIT),
+        compiler_params=pltpu.CompilerParams(**params),
         name="self_forward_%d" % rows,
-    )(residual, gain_row, weight, weight, bias, items[:, None], items[None, :])
-    return y, kept
-
-
-def self_backward_kernel(
+    )(residual, gain_row, weight, weight, bias, items[:, None], items[None, :], *blocks, *dec_blocks)
+    return y, kept[:4], kept[4:]
+
+
+def picked(source, start, window, first, width):
+    base = start // TILE * TILE
+    window = min(window, source.shape[1] - base)
+    lanes = lax.broadcasted_iota(jnp.int32, (window, HD), 1) - first
+    rows_of = lax.broadcasted_iota(jnp.int32, (window, HD), 0) + (base - start)
+    pick = ((rows_of == lanes) & (lanes >= 0) & (lanes < width)).astype(jnp.bfloat16)
+    return matmul(source[:, pl.ds(base, window)], pick)
+
+
+def self_backward_rows(
     g_ref,
     x_ref,
     gain_ref,
     win_ref,
     wout_ref,
-    normed_ref,
     projected_ref,
-    context_ref,
     weights_ref,
     gx_ref,
-    gain_out,
-    scores_ref,
-    grad_ref,
+    small_ref,
     context_grad,
     projected_grad,
 ):
     low = jnp.bfloat16
-    grad_low = g_ref[...].astype(low)
-    context_grad[...] = matmul(grad_low, wout_ref[...]).astype(low)
+    length = x_ref.shape[0]
+    context_grad[...] = matmul(g_ref[...].astype(low), wout_ref[...]).astype(low)
 
     def put(pair, query, key, value):
         for index, part in enumerate((query, key, value)):
             projected_grad[:, pl.ds(index * HD + pair * TILE, TILE)] = part.astype(low)
+
+    def put_scores(head, scores):
+        small_ref[pl.ds(8 + head, 1), pl.ds(0, 2 * length)] = distance_sums(scores, 2 * length)
 
     attend_heads_backward(
         tile_of(projected_ref, 0),
@@ -1453,24 +1729,20 @@
         weights_ref,
         tile_of(context_grad, 0),
         put,
-        scores_ref,
+        put_scores,
     )
     grad_normed = nt(projected_grad[...], win_ref[...])
     residual = x_ref[...].astype(jnp.float32)
-    grad_residual, gain_out[...] = norm_pull(residual, gain_ref[...], grad_normed)
+    grad_residual, grad_gain = norm_pull(residual, gain_ref[...], grad_normed)
+    small_ref[pl.ds(0, 1), pl.ds(0, D)] = grad_gain
     gx_ref[...] = g_ref[...] + grad_residual
-    both = jnp.concatenate([normed_ref[...], grad_low], axis=0)
+
+
+def self_backward_weights(g_ref, normed_ref, context_ref, projected_grad, grad_ref):
+    low = jnp.bfloat16
+    both = jnp.concatenate([normed_ref[...], g_ref[...].astype(low)], axis=0)
     chunks = grad_ref.shape[1] // HD
     part_in, part_out = 3 * HD // chunks, HD // chunks
-
-    def picked(source, start, window, first, width):
-        base = start // TILE * TILE
-        window = min(window, source.shape[1] - base)
-        lanes = lax.broadcasted_iota(jnp.int32, (window, HD), 1) - first
-        rows_of = lax.broadcasted_iota(jnp.int32, (window, HD), 0) + (base - start)
-        pick = ((rows_of == lanes) & (lanes >= 0) & (lanes < width)).astype(low)
-        return matmul(source[:, pl.ds(base, window)], pick).astype(low)
-
     for chunk in range(chunks):
         right = jnp.concatenate(
             [
@@ -1478,28 +1750,8 @@
                 picked(context_ref, chunk * part_out, 2 * TILE, part_in, part_out),
             ],
             axis=0,
-        )
+        ).astype(low)
         grad_ref[:, pl.ds(chunk * HD, HD)] = tn(both, right).astype(low)
-
-
-def self_backward(grad, residual, gain_row, weight, kept):
-    rows = residual.shape[0]
-    low = jnp.bfloat16
-    return pl.pallas_call(
-        self_backward_kernel,
-        out_shape=[
-            jax.ShapeDtypeStruct((rows, D), jnp.float32),
-            jax.ShapeDtypeStruct((1, D), jnp.float32),
-            jax.ShapeDtypeStruct((H, rows, rows), low),
-            jax.ShapeDtypeStruct((D, 4 * HD), low),
-        ],
-        in_specs=[VM, VM, VM, W_IN, W_OUT] + [VM] * 4,
-        out_specs=[VM] * 4,
-        scratch_shapes=[pltpu.VMEM((rows, HD), low), pltpu.VMEM((rows, 3 * HD), low)],
-        grid=(1,),
-        compiler_params=pltpu.CompilerParams(vmem_limit_bytes=VMEM_LIMIT),
-        name="self_backward_%d" % rows,
-    )(grad, residual, gain_row, weight, weight, *kept)
 
 
 def cross_forward_kernel(
@@ -1561,7 +1813,7 @@
 
 def cross_backward_kernel(
     g_ref, x_ref, final_ref, wkey_ref, wvalue_ref, y_ref, gain_ref, wquery_ref, wout_ref, kv_ref, query_ref, weights_ref,
-    gx_ref, gy_ref, final_out, gain_out, kv_grad, query_grad, context_grad,
+    memory_ref, normed_ref, context_ref, gx_ref, gy_ref, final_out, gain_out, grad_ref, kv_grad, query_grad, context_grad,
 ):
     low = jnp.bfloat16
     grad_low = g_ref[...].astype(low)
@@ -1588,9 +1840,25 @@
         y_ref[...], gain_ref[...], nt(query_grad[...], wquery_ref[...])
     )
     gy_ref[...] = g_ref[...] + grad_residual
-
-
-def cross_backward(g2, x2, final_gain, enc_weight, y1, gain_row, dec_weight, kv, query, weights):
+    lefts = jnp.concatenate([memory_ref[...], normed_ref[...], grad_low], axis=0)
+    chunks = grad_ref.shape[1] // HD
+    part = HD // chunks
+    for chunk in range(chunks):
+        start = chunk * part
+        right = jnp.concatenate(
+            [
+                picked(kv_grad, start, 2 * TILE, 0, part)
+                + picked(kv_grad, HD + start, 2 * TILE, part, part),
+                picked(query_grad, start, 2 * TILE, 2 * part, part),
+                picked(context_ref, start, 2 * TILE, 3 * part, part),
+            ],
+            axis=0,
+        ).astype(low)
+        grad_ref[:, pl.ds(chunk * HD, HD)] = tn(lefts, right).astype(low)
+
+
+def cross_backward(g2, x2, final_gain, enc_weight, y1, gain_row, dec_weight, kept):
+    memory, kv, normed, query, context, weights = kept
     low = jnp.bfloat16
     return pl.pallas_call(
         cross_backward_kernel,
@@ -1599,29 +1867,35 @@
             jax.ShapeDtypeStruct((LD, D), jnp.float32),
             jax.ShapeDtypeStruct((1, D), jnp.float32),
             jax.ShapeDtypeStruct((1, D), jnp.float32),
-            jax.ShapeDtypeStruct((LE, 2 * HD), low),
-            jax.ShapeDtypeStruct((LD, HD), low),
+            jax.ShapeDtypeStruct((D, 4 * HD), low),
         ],
-        in_specs=[VM, VM, VM, C_IN, C_OUT, VM, VM, C_IN, C_OUT, VM, VM, VM],
-        out_specs=[VM] * 6,
-        scratch_shapes=[pltpu.VMEM((LD, HD), low)],
+        in_specs=[VM, VM, VM, C_IN, C_OUT, VM, VM, C_IN, C_OUT] + [VM] * 6,
+        out_specs=[VM] * 5,
+        scratch_shapes=[
+            pltpu.VMEM((LE, 2 * HD), low),
+            pltpu.VMEM((LD, HD), low),
+            pltpu.VMEM((LD, HD), low),
+        ],
         grid=(1,),
         compiler_params=pltpu.CompilerParams(vmem_limit_bytes=VMEM_LIMIT),
         name="cross_backward",
-    )(g2, x2, final_gain, enc_weight, enc_weight, y1, gain_row, dec_weight, dec_weight, kv, query, weights)
-
-
-def column_picks(widths, rows, chunk):
-    picks, base = [], 0
-    for width in widths:
-        part = width // rows
-        pick = np.zeros((width, rows * chunk), np.float32)
-        for row in range(rows):
-            for lane in range(part):
-                pick[row * part + lane, row * chunk + base + lane] = 1.0
-        picks.append(jnp.asarray(pick, jnp.bfloat16))
-        base += part
-    return picks
+    )(
+        g2,
+        x2,
+        final_gain,
+        enc_weight,
+        enc_weight,
+        y1,
+        gain_row,
+        dec_weight,
+        dec_weight,
+        kv,
+        query,
+        weights,
+        memory,
+        normed,
+        context,
+    )
 
 
 def plain_self_forward(residual, gain_row, weight, bias_full, allowed):
@@ -1961,8 +2235,6 @@
     enc_attn, dec_half, enc_blocks, dec_blocks = start_weights(
         wide, rows, attn_in, attn_out, cross_in, cross_out, ffn_in, ffn_out
     )
-    enc_pieces = [enc_blocks[0]] + [xor_permute(enc_blocks[v], "wide", v) for v in range(1, wide)]
-
     small = jnp.concatenate([norm_gains[0].reshape(-1), rel_bias[0].reshape(-1)])
     other = xor_permute(small, "section", 1)
     smalls = (jnp.where(is_dec, other, small), jnp.where(is_dec, small, other))
@@ -1982,16 +2254,23 @@
     enc_items = item_ids(own_row(enc_lengths), LE)
     dec_items = item_ids(own_row(dec_lengths), LD)
 
-    x1, enc_self = self_forward(False, enc_row, gains[0][0:1], enc_attn, enc_bias, enc_items)
-    dec_half, dec_blocks, _ = lax.optimization_barrier((dec_half, dec_blocks, enc_pieces))
-    x2, *enc_ffn = ffn_forward_call(wide, x1, gains[0][1:2], enc_pieces, 2)
-    cut = split_at(depth)
-    first, second = xor_permute(dec_half, "wide", 1), xor_permute(dec_half, "wide", 2)
-    far = [xor_permute(first[:cut], "wide", 2), xor_permute(second[cut:], "wide", 1)]
-    dec_attn = place_weights(wide, [dec_half, first, second] + far)
-    dec_pieces = [dec_blocks[0]] + [xor_permute(dec_blocks[v], "wide", v) for v in range(1, wide)]
-    y1, dec_self = self_forward(True, dec_row, gains[1][0:1], dec_attn, dec_bias, dec_items)
-    y2, (memory, kv, normed, query, context, weights) = cross_forward(
+    x1, enc_self, moved = self_forward(
+        False,
+        enc_row,
+        gains[0][0:1],
+        enc_attn,
+        enc_bias,
+        enc_items,
+        tuple(enc_blocks[1:]),
+        tuple(dec_blocks[1:]),
+    )
+    enc_pieces, dec_pieces = moved[: wide - 1], moved[wide - 1 :]
+    x2, *enc_ffn = ffn_forward_call(
+        wide, x1, gains[0][1:2], [enc_blocks[0], *enc_pieces], 2, (dec_half, *dec_pieces)
+    )
+    enc_ffn, dec_attn, dec_pieces = enc_ffn[:4], enc_ffn[4], [dec_blocks[0], *dec_pieces, *enc_ffn[5:]]
+    y1, dec_self, _ = self_forward(True, dec_row, gains[1][0:1], dec_attn, dec_bias, dec_items)
+    y2, cross_kept = cross_forward(
         x2, gains[0][2:3], enc_attn, y1, gains[1][1:2], dec_attn, dec_items, enc_items
     )
     y3, *dec_ffn = ffn_forward_call(wide, y2, gains[1][2:3], dec_pieces, 3)
@@ -1999,83 +2278,41 @@
     g2, dec_ffn_gain, *dec_ffn_grads = ffn_backward_call(
         wide, rows, cot_row.astype(jnp.float32), y2, gains[1][2:3], dec_ffn, 4
     )
-    grad_x2, g1, enc_final_gain, dec_cross_gain, kv_grad, query_grad = cross_backward(
-        g2, x2, gains[0][2:3], enc_attn, y1, gains[1][1:2], dec_attn, kv, query, weights
+    grad_x2, g1, enc_final_gain, dec_cross_gain, cross_grads = cross_backward(
+        g2, x2, gains[0][2:3], enc_attn, y1, gains[1][1:2], dec_attn, cross_kept
     )
     grad_x1, enc_ffn_gain, enc_in, enc_out, *dec_sums = ffn_backward_call(
         wide, rows, grad_x2, x1, gains[0][1:2], enc_ffn, 5, dec_ffn_grads
     )
-    grad_y, dec_self_gain, dec_scores, dec_grads = self_backward(
-        g1, dec_row, gains[1][0:1], dec_attn, dec_self
-    )
-    grad_x, enc_self_gain, enc_scores, enc_grads = self_backward(
-        grad_x1, enc_row, gains[0][0:1], enc_attn, enc_self
-    )
-    pair_picks = jnp.concatenate(column_picks((HD, HD), rows, 4 * TILE), axis=0)
-    shifted_picks = jnp.roll(pair_picks, 2 * TILE, axis=1)
-    cross_grads = to_low(
-        matmul(
-            jnp.concatenate([memory, normed, to_low(g2)], axis=0).T,
-            to_low(
-                jnp.concatenate(
-                    [
-                        matmul(kv_grad, pair_picks),
-                        matmul(query_grad, shifted_picks[:HD]),
-                        matmul(context, shifted_picks[HD:]),
-                    ],
-                    axis=0,
-                )
-            ),
-        )
-    )
-    enc_line, dec_line = bias_sums(enc_scores, dec_scores)
-    line_sums = [
-        matmul_exact(distance_hot(length, both, 1 - length), line[:H].T).reshape(1, -1)
-        for line, length, both in ((enc_line, LE, True), (dec_line, LD, False))
-    ]
-    lanes = (D + TILE - 1) // TILE * TILE
-    small_grads = jnp.stack(
-        [
-            jnp.concatenate(
-                [jnp.pad(each, ((0, 0), (0, lanes - each.shape[1]))) for each in group]
-                + [jnp.zeros((4, lanes), jnp.float32)],
-                axis=0,
-            )
-            for group in (
-                (enc_self_gain, enc_ffn_gain, enc_final_gain, line_sums[0]),
-                (dec_self_gain, dec_cross_gain, dec_ffn_gain, line_sums[1]),
-            )
-        ]
-    )
-    attn_parts, ffn_parts, small_own = reduce_weights(
-        wide, rows, cross_grads, dec_grads, enc_grads, dec_sums, (enc_in, enc_out), small_grads
-    )
-    ffn_in_grad, ffn_out_grad = assemble(rows, ffn_parts)
-    attn_share = jnp.concatenate([attn_parts[0], attn_parts[1, 2 * cut - depth :]], axis=0)
-    edges = np.cumsum([0, 3 * HD // rows] + [HD // rows] * 3)
-    win, wout, cin, cout = [attn_share[:, a:b] for a, b in zip(edges[:-1], edges[1:])]
-
-    half = D // 2
-
-    def by_half(own):
-        halves = jnp.stack([own[:, :half], own[:, half:]])
-        keep = lax.dynamic_index_in_dim(halves, core, 0, keepdims=False)
-        send = lax.dynamic_index_in_dim(halves, 1 - core, 0, keepdims=False)
-        got = xor_permute(send, "section", 1)
-        return jnp.stack([jnp.where(is_dec, got, keep), jnp.where(is_dec, keep, got)])[:, None]
-
+    attn_parts, ffn_parts, small_own, dec_out, enc_grad, dec_grad = last_step(
+        wide,
+        rows,
+        cross_grads,
+        dec_sums,
+        (enc_in, enc_out),
+        y3,
+        dec_attn,
+        enc_attn,
+        (g1, dec_row, gains[1][0:1], *dec_self),
+        (grad_x1, enc_row, gains[0][0:1], *enc_self),
+        (enc_ffn_gain, enc_final_gain, dec_cross_gain, dec_ffn_gain),
+    )
+    ffn_in_grad, ffn_out_grad, gain_grad, bias_grad, *attn_grads = assemble(
+        rows, ffn_parts, attn_parts, small_own
+    )
+    win, wout, cin, cout = attn_grads
     return (
-        by_half(to_low(y3)),
-        by_half(grad_x),
-        by_half(grad_y),
-        small_own[None, :3, :D],
-        small_own[3, : NB * H].reshape(1, NB, H),
-        win[None],
-        wout.T[None],
+        dec_out[:, None],
+        enc_grad[:, None],
+        dec_grad[:, None],
+        gain_grad,
+        bias_grad,
+        win,
+        wout,
         ffn_in_grad,
-        ffn_out_grad,
-        cin[None],
-        cout[None],
+        jnp.swapaxes(ffn_out_grad, 1, 2),
+        cin,
+        cout,
     )
 
 

time: 624 us -> 588 us (0.942)
  the two profiles are of different devices: /device:TPU:11 before, /device:TPU:19 now
where the time goes in v4:
time: 588 us; the launch traced here: 581 us
  Pallas kernels  553 us (94%)
  local copies, waits for them, and re-layouts  22.4 us (4%)
    pallas_call x1, Pallas kernels, last_step(): pl.pallas_call(lambda *refs: last_kernel(wide, rows, *refs), out_shape=[j...  148 us
    pallas_call x2, Pallas kernels, ffn_backward_call(): pl.pallas_call(lambda *refs: ffn_backward_kernel(wide, rows_axis, *refs),...  147 us
    pallas_call x2, Pallas kernels, ffn_forward_call(): pl.pallas_call(lambda *refs: ffn_forward_kernel(wide, bool(carried), len(...  117 us
    pallas_call x2, Pallas kernels, self_forward(): pl.pallas_call(lambda *refs: self_forward_kernel(wide, causal, *refs), ou...  76.6 us
    pallas_call x1, Pallas kernels, start_weights(): pl.pallas_call(lambda *refs: start_weights_kernel(wide, rows, *refs), out...  37.2 us
    unnamed x29, local copies, waits for them, and re-layouts  13.6 us
    pallas_call x1, Pallas kernels, cross_backward(): pl.pallas_call(cross_backward_kernel, out_shape=[jax.ShapeDtypeStruct((LE...  12.5 us
  transfers between devices with their start and end apart: 1, of which 0 were waited for; matrix products, arithmetic and copies ran while one was open for 1% of the time, Pallas kernels for 6%

profile of v4, /device:TPU:19, one launch (start us, length us, event | category | flops | bytes accessed | tf_op | source)
XLA Modules:
  0.0 580.5 jit_solution(2179776898095089833)
XLA Ops:
  0.7 0.9 copy.53
  1.6 0.1 reshape_squeeze.7
  1.7 0.8 reduce
  2.5 0.1 reshape_squeeze.6
  2.6 0.1 pad_maximum_fusion
  2.6 0.7 collective-permute-start
  3.3 0.7 fusion
  4.0 0.2 reduce-window.6
  4.2 0.2 reduce-window.9
  4.4 0.1 convert_reduce_fusion.1
  4.6 0.9 bitcast_convert_fusion
  5.5 0.1 convert_reduce_fusion
  5.5 0.7 copy.55.refs_5_.col_ref
  6.2 0.8 copy.54.refs_5_
  7.0 1.2 copy.52
  8.2 37.2 %start_weights.1 = (bf16[2,1472,1152]{2,1,0:T(8,128)(2,1)}, bf16[368,1152]{1,0:T(8,128)(2,1)}, bf16[4,368,384]{2,1,0:T(8,128)(2,1)}, bf16[4,368,384]{2,1,0:T(8,1...) custom-call(bf16[1,368,1152]{2,1,0:T(8,128)(2,1)} %refs_0_.1, ...), custom_call_target="tpu_custom_call" | custom-call | tf_op jit(solution)/shard_map/start_weights/pallas_call | solution.py:1023
  45.4 0.1 broadcast_select_fusion
  45.7 0.6 slice.101.refs_1_.refs_2_
  46.3 0.6 slice.99.gain_ref
  46.9 0.6 slice.96.refs_1_.refs_10_
  47.5 0.6 slice.85.refs_1_.refs_17_
  48.1 0.6 slice.92.refs_1_.refs_2_
  48.7 0.6 slice.94.final_ref
  49.3 0.1 slice.87
  49.4 0.1 slice.89
  49.5 0.2 fusion.4
  49.7 0.6 pad.8.enc_ref
  50.4 0.2 fusion.5
  50.5 0.6 pad.9.dec_ref
  51.2 2.4 bias_rows.1
  53.6 71.3 %self_forward_256.1 = (f32[256,1472]{1,0:T(8,128)}, bf16[256,1472]{1,0:T(8,128)(2,1)}, bf16[256,1152]{1,0:T(8,128)(2,1)}, bf16[256,384]{1,0:T(8,128)(2,1)}, f32[...) custom-call(bf16[256,1472]{1,0:T(8,128)(2,1)} %bitcast.36, ...), custom_call_target="tpu_custom_call" | custom-call | tf_op jit(solution)/shard_map/self_forward_256/pallas_call | solution.py:1671
  124.9 95.3 %ffn_forward_256.1 = (f32[256,1472]{1,0:T(8,128)}, bf16[1472,1024]{1,0:T(8,128)(2,1)}, bf16[2,1024,1024]{2,1,0:T(8,128)(2,1)}, bf16[2,512,1024]{2,1,0:T(8,128)(2...) custom-call(f32[256,1472]{1,0:T(8,128)} %get-tuple-element.97.refs_0, ...), custom_call_target="tpu_custom_call" | custom-call | tf_op jit(solution)/shard_map/ffn_forward_256/pallas_call | solution.py:624
  220.2 5.3 self_forward_64.1
  225.5 6.5 %cross_forward.1 = (f32[64,1472]{1,0:T(8,128)}, bf16[256,1472]{1,0:T(8,128)(2,1)}, bf16[256,768]{1,0:T(8,128)(2,1)}, bf16[64,1472]{1,0:T(8,128)(2,1)}, bf16[64,3...) custom-call(f32[256,1472]{1,0:T(8,128)} %get-tuple-element.106.x_ref, f32[1,1472]{1,0:T(1,128)} %slice.94.final_ref, ...), custom_call_target="tpu_custom_call" | custom-call | tf_op jit(solution)/shard_map/cross_forward/pallas_call | solution.py:1783
  232.0 22.1 %ffn_forward_64.1 = (f32[64,1472]{1,0:T(8,128)}, bf16[1472,256]{1,0:T(8,128)(2,1)}, bf16[2,256,1024]{2,1,0:T(8,128)(2,1)}, bf16[2,512,256]{2,1,0:T(8,128)(2,1)}, bf16[2,4,1472,384]{3,2,1,0:T(8,128)(2,1)}) custom-call(f32[64,1472]{1,0:T(8,128)} %get-tuple-element.110.refs_0_.refs_1_, f32[1,1472]{1,0:T(1,128)} %slice.101.refs_1_.refs_2_, ...), custom_call_target="tpu_custom_call" | custom-call | tf_op jit(solution)/shard_map/ffn_forward_64/pallas_call | solution.py:624
  254.1 45.2 %ffn_backward_64.1 = (f32[64,1472]{1,0:T(8,128)}, f32[1,1472]{1,0:T(1,128)}, bf16[4,2,1472,128]{3,2,1,0:T(8,128)(2,1)}, bf16[4,112,1472]{2,1,0:T(8,128)(2,1)}) custom-call(f32[64,1472]{1,0:T(8,128)} %get-tuple-element.208.refs_0_, f32[64,1472]{1,0:T(8,128)} %get-tuple-element.110.refs_0_.refs_1_, f32[1,1472]{1,0:T(1,128)} %slice.101.refs_1_.refs_2_, ...), custom_call_target="tpu_custom_call" | custom-call | tf_op jit(solution)/shard_map/ffn_backward_64/pallas_call | solution.py:850
  299.3 12.5 %cross_backward.1 = (f32[256,1472]{1,0:T(8,128)}, f32[64,1472]{1,0:T(8,128)}, f32[1,1472]{1,0:T(1,128)}, f32[1,1472]{1,0:T(1,128)}, bf16[1472,1536]{1,0:T(8,128)(2,1)}) custom-call(f32[64,1472]{1,0:T(8,128)} %get-tuple-element.119.g_ref, f32[256,1472]{1,0:T(8,128)} %get-tuple-element.106.x_ref, f32[1,1472]{1,0:T(1,128)} %slice.94.final_ref, ...), custom_call_target="tpu_custom_call" | custom-call | tf_op jit(solution)/shard_map/cross_backward/pallas_call | solution.py:1863
  311.8 101.3 %ffn_backward_256.1 = (f32[256,1472]{1,0:T(8,128)}, f32[1,1472]{1,0:T(1,128)}, bf16[4,2,1472,128]{3,2,1,0:T(8,128)(2,1)}, bf16[4,112,1472]{2,1,0:T(8,128)(2,1)},...) custom-call(f32[256,1472]{1,0:T(8,128)} %get-tuple-element.127.refs_0_, ...), custom_call_target="tpu_custom_call" | custom-call | tf_op jit(solution)/shard_map/ffn_backward_256/pallas_call | solution.py:850
  413.1 147.6 %last_step.1 = (f32[2,192,576]{2,1,0:T(8,128)}, bf16[2,4,368,384]{3,2,1,0:T(8,128)(2,1)}, f32[16,1536]{1,0:T(8,128)}, bf16[2,64,736]{2,1,0:T(8,128)(2,1)}, f32[2...) custom-call(bf16[1472,1536]{1,0:T(8,128)(2,1)} %get-tuple-element.126.refs_0_, ...), custom_call_target="tpu_custom_call" | custom-call | tf_op jit(solution)/shard_map/last_step/pallas_call | solution.py:1392
  560.7 3.0 copy.58
  563.7 6.7 %assemble.1 = (f32[1,368,1792]{2,1,0:T(8,128)}, f32[1,368,896]{2,1,0:T(8,128)}, f32[1,3,1472]{2,1,0:T(4,128)}, f32[1,32,6]{2,1,0:T(8,128)}, f32[1,368,288]{2,1,0...) custom-call(bf16[2,4,368,384]{3,2,1,0:T(8,128)(2,1)} %get-tuple-element.156.refs_0_, ...), custom_call_target="tpu_custom_call" | custom-call | tf_op jit(solution)/shard_map/assemble/pallas_call | solution.py:1498
  570.4 1.4 copy.60
  571.8 1.4 copy.61
  573.2 1.7 copy.63
  574.9 1.7 copy.64
  576.6 2.0 copy.62
  578.6 0.7 copy.67
  579.3 0.7 copy.68
  (27 shorter events, 0.3 us)
Async XLA Ops:
  0.6 3.8 copy-start
  0.7 3.9 copy-start.4
  0.7 3.9 copy-start.5
  2.6 42.8 %collective-permute-start = (f32[4608]{0:T(1024)S(1)}, f32[4608]{0:T(1024)S(1)}, u32[]{:S(2)}, u32[]{:S(2)}) collective-permute-start(f32[4608]{0:T(1024)S(1)} %pad_maximum_fusion), channel_id=1, source_target_pairs={{0,16},{16,0},{1,17},{17,1},{2,18},{18,2},{3,19},{19,3},{4,20},{20... | collective-permute-start | bytes 55304 | tf_op jit(solution)/shard_map/ppermute | solution.py:127
  4.5 3.7 copy-start.9
  5.5 39.9 %copy-start.8 = (s32[256]{0:T(256)}, s32[256]{0:T(256)S(1)}, u32[]{:S(2)}) copy-start(s32[256]{0:T(256)S(1)} %convert_reduce_fusion) | copy-start | bytes 3076
  8.2 41.3 %copy-start.6 = (f32[32,512]{1,0:T(8,128)S(1)}, f32[32,512]{1,0:T(8,128)}, u32[]{:S(2)}) copy-start(f32[32,512]{1,0:T(8,128)} %constant.46.clone) | copy-start | bytes 196612
  8.2 42.2 %copy-start.7 = (f32[32,128]{1,0:T(8,128)S(1)}, f32[32,128]{1,0:T(8,128)}, u32[]{:S(2)}) copy-start(f32[32,128]{1,0:T(8,128)} %constant.47.clone) | copy-start | bytes 49156
  563.7 16.4 %copy-start.1 = (bf16[2,1,256,1472]{2,3,1,0:T(8,128)(2,1)S(1)}, bf16[2,1,256,1472]{2,3,1,0:T(8,128)(2,1)}, u32[]{:S(2)}) copy-start(bf16[2,1,256,1472]{2,3,1,0:T(8,128)(2,1)} %param.17) | copy-start | bytes 4521988
  570.4 8.2 %copy-start.3 = (bf16[2,64,736]{2,1,0:T(8,128)(2,1)S(1)}, bf16[2,64,736]{2,1,0:T(8,128)(2,1)}, u32[]{:S(2)}) copy-start(bf16[2,64,736]{2,1,0:T(8,128)(2,1)} %get-tuple-element.153) | copy-start | bytes 565252
  570.4 8.9 %copy-start.2 = (f32[2,64,736]{2,1,0:T(8,128)S(1)}, f32[2,64,736]{2,1,0:T(8,128)}, u32[]{:S(2)}) copy-start(f32[2,64,736]{2,1,0:T(8,128)} %get-tuple-element.155) | copy-start | bytes 1130500

commit v5 on v4

--- a/solution.py
+++ b/solution.py
@@ -168,6 +168,7 @@
 MESH = pl.DeviceIdType.MESH
 HBM = pl.BlockSpec(memory_space=pl.ANY)
 VM = pl.BlockSpec(memory_space=pltpu.VMEM)
+SM = pl.BlockSpec(memory_space=pltpu.SMEM)
 TILE = 128
 VMEM_LIMIT = 60 * 1024 * 1024
 
@@ -372,17 +373,19 @@
             at, peer, first = base + 3 * v, peers[v], pl.ds(0, direct)
             self.shared.append(remote(block.at[mine], piece.at[mine], sems, at, peer))
             self.passed.append(remote(piece.at[mine], piece.at[mine], sems, at + 1, other))
-            self.direct.append(remote(block.at[first], piece.at[first], sems, at + 2, peer))
+            if direct:
+                self.direct.append(remote(block.at[first], piece.at[first], sems, at + 2, peer))
 
     def start(self):
         for copy in self.shared:
             copy.start()
 
     def pass_on(self):
-        for copy in self.shared:
+        for copy in self.direct:
+            copy.start()
+        for copy, after in zip(self.shared, self.passed):
             copy.wait_recv()
-        for copy in self.direct + self.passed:
-            copy.start()
+            after.start()
 
     def finish(self):
         for copy in self.direct + self.passed:
@@ -470,7 +473,34 @@
     )
 
 
-def ffn_forward_kernel(wide, carried, count, x_ref, gain_ref, *refs):
+def weight_copies(pieces, weight, sems, base, local_sem, local_base, sibling):
+    core, place = lax.axis_index("section"), lax.axis_index("wide")
+    wide, depth = lax.axis_size("wide"), pieces[0].shape[1]
+    loads, swaps = [], []
+    for index, piece in enumerate(pieces):
+        v = index if index < wide else index - wide + 1
+        place_rows = pl.ds(pl.multiple_of((place ^ v) * depth, 16), depth)
+        target = weight.at[core, :, place_rows]
+        quarters = piece.shape[0]
+        if quarters < weight.shape[1]:
+            part = lax.axis_index("rows") % 2
+            part = part if index < wide else 1 - part
+            target = weight.at[core, pl.ds(part * quarters, quarters), place_rows]
+        loads.append(pltpu.make_async_copy(piece, target, local_sem.at[local_base + index]))
+        swaps.append(remote(piece, target, sems, base + index, sibling))
+    return loads, swaps
+
+
+def gate_slopes(gate, up):
+    square = gate * gate
+    tanh = jnp.tanh(GELU_A * gate * (1.0 + GELU_B * square))
+    upper = 0.5 * (1.0 + tanh)
+    slope = upper + 0.5 * gate * (1.0 - tanh * tanh) * (GELU_A + 3.0 * GELU_A * GELU_B * square)
+    return gate * upper, slope
+
+
+def ffn_forward_kernel(wide, carried, count, gain_at, x_ref, gain_ref, *refs):
+    gain_ref = gain_ref.at[pl.ds(gain_at, 1)]
     pieces, refs = refs[:count], refs[count:]
     if carried:
         dec_half, dec_blocks, refs = refs[0], refs[1:wide], refs[wide:]
@@ -490,25 +520,13 @@
     blocks[0] = (residual * rms_rows(residual) * gain_ref[...]).astype(jnp.bfloat16)
     gather = GatherPlane(blocks, sems, 0, peers, rows)
     gather.start()
-    loads, swaps = [], []
-    for index, piece in enumerate(pieces):
-        v = index if index < wide else index - wide + 1
-        place_rows = pl.ds(pl.multiple_of((place ^ v) * depth, 16), depth)
-        target = weight.at[core, :, place_rows]
-        quarters = piece.shape[0]
-        if quarters < weight.shape[1]:
-            part = lax.axis_index("rows") % 2
-            part = part if index < wide else 1 - part
-            target = weight.at[core, pl.ds(part * quarters, quarters), place_rows]
-        load = pltpu.make_async_copy(piece, target, local_sem.at[12 + index])
-        swap = remote(piece, target, sems, 10 + index, peers[-1])
+    loads, swaps = weight_copies(pieces, weight, sems, 10, local_sem, 12, peers[-1])
+    for load, swap in zip(loads, swaps):
         load.start()
         swap.start()
-        loads.append(load)
-        swaps.append(swap)
     scatter = ScatterPlane(parts, landing, sems, 4, peers, rows)
     if carried:
-        held = refs[11]
+        held, far_held, whole = refs[11:14]
         other = {"rows": lax.axis_index("rows") ^ 1}
         passed = [
             remote(block, piece, sems, 24 + v, other)
@@ -516,14 +534,31 @@
         ]
         for copy in passed:
             copy.start()
-        dec_gather = GatherPlane(held, sems, 27, peers, depth)
-        fetch = pltpu.make_async_copy(dec_half, held.at[0], local_sem.at[7])
+        size = held.shape[1]
+        rest = depth - size
+        part = lax.axis_index("rows") % 2
+        dec_gather = GatherPlane(held, sems, 27, peers, size)
+        mine = pl.ds(pl.multiple_of(part * rest, 16), size)
+        fetch = pltpu.make_async_copy(dec_half.at[mine], held.at[0], local_sem.at[7])
         fetch.start()
-        stores, gives = [], []
-        for v in range(wide):
-            target = dec_attn.at[core, pl.ds(pl.multiple_of((place ^ v) * depth, 16), depth)]
-            stores.append(pltpu.make_async_copy(held.at[v], target, local_sem.at[8 + v]))
-            gives.append(remote(held.at[v], target, sems, 31 + v, peers[-1]))
+        stores, gives, crossings = [], [], []
+
+        def place_block(source, v, start, index):
+            target = dec_attn.at[
+                core, pl.ds(pl.multiple_of((place ^ v) * depth + start, 16), source.shape[0])
+            ]
+            stores.append(pltpu.make_async_copy(source, target, local_sem.at[19 + index]))
+            gives.append(remote(source, target, sems, 35 + index, peers[-1]))
+
+        place_block(whole, 0, 0, 0)
+        for v in range(1, wide):
+            place_block(held.at[v], v, part * rest, v)
+        for v in range(1, wide):
+            sent = pl.ds(pl.multiple_of(part * (size - rest), 16), rest)
+            crossings.append(remote(held.at[v, sent], far_held.at[v - 1], sems, 41 + v, other))
+            place_block(far_held.at[v - 1], v, (1 - part) * size, wide + v - 1)
+        whole_fetch = pltpu.make_async_copy(dec_half, whole, local_sem.at[8])
+        whole_fetch.start()
     count = token_rows_at_once(wide, rows)
     groups = wide * rows // count
 
@@ -562,12 +597,13 @@
 
             @pl.when(group == 0)
             def _():
-                fetch.wait()
+                whole_fetch.wait()
                 stores[0].start()
                 gives[0].start()
 
             @pl.when(group == 1)
             def _():
+                fetch.wait()
                 dec_gather.start()
 
     y_ref[...] += residual
@@ -581,19 +617,35 @@
     if carried:
         for v in range(1, 3):
             dec_gather.arrive(v - 1)
+            crossings[v - 1].start()
             stores[v].start()
             gives[v].start()
-    at[...] = jnp.concatenate([blocks[v] for v in range(wide)], axis=0).T
+
+    @pl.loop(0, groups)
+    def _(group):
+        lanes = pl.ds(pl.multiple_of(group * count, count), count)
+        at[:, lanes] = block_at(blocks, group, count).T
+
     last = pltpu.make_async_copy(at, at_out, local_sem.at[6])
     last.start()
     copies.append(last)
-    for half in range(2):
-        hidden_out[half] = hidden[half].T
+
+    @pl.loop(0, 2 * groups)
+    def _(step):
+        half, group = lax.rem(step, 2), step // 2
+        lanes = pl.ds(pl.multiple_of(group * count, count), count)
+        hidden_out[half, :, lanes] = hidden[half, lanes, :].T
+
     y_ref[...] += scatter.total()
     if carried:
         dec_gather.arrive(2)
+        crossings[2].start()
         stores[3].start()
         gives[3].start()
+        for v in range(1, wide):
+            crossings[v - 1].wait()
+            stores[wide + v - 1].start()
+            gives[wide + v - 1].start()
         for store, give in zip(stores, gives):
             store.wait()
             give.wait()
@@ -609,6 +661,7 @@
 
 
 def ffn_forward_call(wide, residual, gain_row, pieces, call_id, carried=()):
+    gain_row, gain_at = gain_row
     rows = residual.shape[0]
     total = rows * wide
     quarters, _, columns = pieces[0].shape
@@ -620,9 +673,14 @@
         extra_out = [jax.ShapeDtypeStruct((2, D, attn_columns), low)] + [
             jax.ShapeDtypeStruct(each.shape, low) for each in carried[1:]
         ]
-        extra_scratch = [pltpu.VMEM((wide, depth, attn_columns), low)]
+        size = split_at(depth)
+        extra_scratch = [
+            pltpu.VMEM((wide, size, attn_columns), low),
+            pltpu.VMEM((wide - 1, depth - size, attn_columns), low),
+            pltpu.VMEM((depth, attn_columns), low),
+        ]
     return pl.pallas_call(
-        lambda *refs: ffn_forward_kernel(wide, bool(carried), len(pieces), *refs),
+        lambda *refs: ffn_forward_kernel(wide, bool(carried), len(pieces), gain_at, *refs),
         out_shape=[
             jax.ShapeDtypeStruct((rows, D), jnp.float32),
             jax.ShapeDtypeStruct((D, total), low),
@@ -642,9 +700,9 @@
             pltpu.VMEM((wide, rows, D), low),
             pltpu.VMEM((3, rows, D), low),
             pltpu.VMEM((token_rows_at_once(wide, rows), D), jnp.float32),
-            pltpu.SemaphoreType.DMA((35,)),
-            pltpu.SemaphoreType.DMA((35,)),
-            pltpu.SemaphoreType.DMA((19,)),
+            pltpu.SemaphoreType.DMA((45,)),
+            pltpu.SemaphoreType.DMA((45,)),
+            pltpu.SemaphoreType.DMA((26,)),
         ]
         + extra_scratch,
         compiler_params=pltpu.CompilerParams(
@@ -655,8 +713,9 @@
 
 
 def ffn_backward_kernel(
-    wide, rows_axis, g_ref, x_ref, gain_ref, at_in, pre_in, hidden_in, weight_in, *refs
+    wide, rows_axis, gain_at, g_ref, x_ref, gain_ref, at_in, pre_in, hidden_in, weight_in, *refs
 ):
+    gain_ref = gain_ref.at[pl.ds(gain_at, 1)]
     carried = len(refs) > 21
     if carried:
         ready_in, ready_out = refs[:2]
@@ -721,14 +780,9 @@
             grad_hidden = matmul(block, weight_tiles(weight, half, 2))
             gate = pre[half, token_rows, pl.ds(0, span)].astype(jnp.float32)
             up = pre[half, token_rows, pl.ds(span, span)].astype(jnp.float32)
-            square = gate * gate
-            tanh = jnp.tanh(GELU_A * gate * (1.0 + GELU_B * square))
-            upper = 0.5 * (1.0 + tanh)
-            slope = upper + 0.5 * gate * (1.0 - tanh * tanh) * (
-                GELU_A + 3.0 * GELU_A * GELU_B * square
-            )
+            value, slope = gate_slopes(gate, up)
             low_gate = (grad_hidden * up * slope).astype(jnp.bfloat16)
-            low_up = (grad_hidden * (gate * upper)).astype(jnp.bfloat16)
+            low_up = (grad_hidden * value).astype(jnp.bfloat16)
             pre[half, token_rows, pl.ds(0, span)] = low_gate
             pre[half, token_rows, pl.ds(span, span)] = low_up
             out = nt(low_gate, weight_tiles(weight, half, 0)) + nt(
@@ -752,8 +806,41 @@
     swap_in = remote(give_in, got_in, sems, 10, peers[-1])
     store_in = pltpu.make_async_copy(got_in, grad_in, local_sem.at[4])
     store_out = pltpu.make_async_copy(got_out, grad_out, local_sem.at[5])
-    if carried:
-        line.turn(1)
+
+    @pl.loop(0, 2 * rows_axis)
+    def _(step):
+        half = jnp.where(step < rows_axis, 1 - core, core)
+        index = lax.rem(step, rows_axis)
+        columns = pl.ds(pl.multiple_of(index * chunk, chunk), chunk)
+        total = matmul(at[...], pre[half, :, columns])
+
+        @pl.when(step < rows_axis)
+        def _():
+            for part in range(2):
+                give_in[index, part] = total[:, part * TILE : (part + 1) * TILE].astype(
+                    jnp.bfloat16
+                )
+
+        @pl.when(step == rows_axis - 1)
+        def _():
+            swap_in.start()
+            if carried:
+                line.turn(1)
+            scatter.pass_on()
+
+        @pl.when(step == rows_axis)
+        def _():
+            swap_in.wait_recv()
+
+        @pl.when(step >= rows_axis)
+        def _():
+            for part in range(2):
+                got_in[index, part] = (
+                    total[:, part * TILE : (part + 1) * TILE]
+                    + got_in[index, part].astype(jnp.float32)
+                ).astype(jnp.bfloat16)
+
+    store_in.start()
 
     @pl.loop(0, 2)
     def _(step):
@@ -765,7 +852,6 @@
             for index in range(rows_axis):
                 give_out[index] = total[index * TILE : index * TILE + units].astype(jnp.bfloat16)
             swap_out.start()
-            scatter.pass_on()
 
         @pl.when(step == 1)
         def _():
@@ -777,42 +863,11 @@
                 ).astype(jnp.bfloat16)
             store_out.start()
 
-    @pl.loop(0, 2 * rows_axis)
-    def _(step):
-        half = jnp.where(step < rows_axis, 1 - core, core)
-        index = lax.rem(step, rows_axis)
-        columns = pl.ds(pl.multiple_of(index * chunk, chunk), chunk)
-        total = matmul(at[...], pre[half, :, columns])
-
-        @pl.when(step < rows_axis)
-        def _():
-            for part in range(2):
-                give_in[index, part] = total[:, part * TILE : (part + 1) * TILE].astype(
-                    jnp.bfloat16
-                )
-
-        @pl.when(step == rows_axis - 1)
-        def _():
-            swap_in.start()
-            if carried:
-                line.turn(2)
-
-        @pl.when(step == rows_axis)
-        def _():
-            swap_in.wait_recv()
-
-        @pl.when(step >= rows_axis)
-        def _():
-            for part in range(2):
-                got_in[index, part] = (
-                    total[:, part * TILE : (part + 1) * TILE]
-                    + got_in[index, part].astype(jnp.float32)
-                ).astype(jnp.bfloat16)
-
-    store_in.start()
+    if carried:
+        line.turn(2)
     total = gx_ref[...] + scatter.total()
     grad_residual, grad_gain = norm_pull(x_ref[...], gain_ref[...], total)
-    gx_ref[...] = g_ref[...] + grad_residual
+    gx_ref[...] = g_ref[...].astype(jnp.float32) + grad_residual
     gain_out[...] = grad_gain
     if carried:
         for index in range(3):
@@ -835,11 +890,216 @@
     scatter.finish()
 
 
+def ffn_both_kernel(wide, rows_axis, gain_at, x_ref, cot_ref, gain_ref, *refs):
+    pieces, refs = refs[: 2 * wide - 1], refs[2 * wide - 1 :]
+    gain_ref = gain_ref.at[pl.ds(gain_at, 1)]
+    y_ref, gx_ref, gain_out, grad_in, grad_out = refs[:5]
+    (
+        blocks,
+        cots,
+        weight,
+        pre,
+        hidden,
+        acc,
+        grad_acc,
+        parts,
+        grad_parts,
+        landing,
+        grad_landing,
+        give_in,
+        give_out,
+        got_in,
+        got_out,
+        send_sem,
+        recv_sem,
+        local_sem,
+    ) = refs[5:]
+    rows = x_ref.shape[0]
+    total_rows = wide * rows
+    span = weight.shape[1] * TILE
+    units = FF // (wide * rows_axis * 2)
+    core = lax.axis_index("section")
+    peers = peers_of(wide)
+    sems = (send_sem, recv_sem)
+    low = jnp.bfloat16
+    loads, swaps = weight_copies(pieces, weight, sems, 20, local_sem, 2, peers[-1])
+    greet(peers)
+    residual = x_ref[...]
+    blocks[0] = (residual * rms_rows(residual) * gain_ref[...]).astype(low)
+    cots[0] = cot_ref[...]
+    gather = GatherPlane(blocks, sems, 0, peers, rows)
+    cot_gather = GatherPlane(cots, sems, 4, peers, rows)
+    gather.start()
+    cot_gather.start()
+    for load, swap in zip(loads, swaps):
+        load.start()
+        swap.start()
+    for index in range(3):
+        gather.arrive(index)
+        cot_gather.arrive(index)
+    for load in loads:
+        load.wait()
+
+    @pl.loop(0, 2)
+    def _(step):
+        @pl.when(step == 1)
+        def _():
+            for swap in swaps:
+                swap.wait_recv()
+
+        half = lax.rem(core + step, 2)
+        block = blocks[...].reshape(total_rows, D)
+        gate = matmul(block, weight_tiles(weight, half, 0))
+        up = matmul(block, weight_tiles(weight, half, 1))
+        value, slope = gate_slopes(gate, up)
+        low_hidden = (value * up).astype(low)
+        hidden[half] = low_hidden
+        grad_hidden = matmul(cots[...].reshape(total_rows, D), weight_tiles(weight, half, 2))
+        low_gate = (grad_hidden * up * slope).astype(low)
+        low_up = (grad_hidden * value).astype(low)
+        pre[half, :, pl.ds(0, span)] = low_gate
+        pre[half, :, pl.ds(span, span)] = low_up
+        grad = nt(low_gate, weight_tiles(weight, half, 0)) + nt(
+            low_up, weight_tiles(weight, half, 1)
+        )
+        grad_acc[...] = jnp.where(step == 0, 0.0, grad_acc[...]) + grad
+        out = nt(low_hidden, weight_tiles(weight, half, 2))
+        acc[...] = jnp.where(step == 0, 0.0, acc[...]) + out
+
+    grad_scatter = ScatterPlane(grad_parts, grad_landing, sems, 8, peers, rows)
+    scatter = ScatterPlane(parts, landing, sems, 14, peers, rows)
+    put_parts(grad_acc, grad_parts, gx_ref, 0, 1, rows)
+    after_group(grad_scatter, 0, 1)
+    put_parts(acc, parts, y_ref, 0, 1, rows)
+    after_group(scatter, 0, 1)
+    swap_in = remote(give_in, got_in, sems, 27, peers[-1])
+    swap_out = remote(give_out, got_out, sems, 28, peers[-1])
+    store_in = pltpu.make_async_copy(got_in, grad_in, local_sem.at[0])
+    store_out = pltpu.make_async_copy(got_out, grad_out, local_sem.at[1])
+    chunk = 2 * TILE
+
+    @pl.loop(0, 2 * rows_axis)
+    def _(step):
+        half = jnp.where(step < rows_axis, 1 - core, core)
+        index = lax.rem(step, rows_axis)
+        columns = pl.ds(pl.multiple_of(index * chunk, chunk), chunk)
+        total = tn(blocks[...].reshape(total_rows, D), pre[half, :, columns])
+
+        @pl.when(step < rows_axis)
+        def _():
+            for part in range(2):
+                give_in[index, part] = total[:, part * TILE : (part + 1) * TILE].astype(low)
+
+        @pl.when(step == rows_axis - 1)
+        def _():
+            swap_in.start()
+            grad_scatter.pass_on()
+            scatter.pass_on()
+
+        @pl.when(step == rows_axis)
+        def _():
+            swap_in.wait_recv()
+
+        @pl.when(step >= rows_axis)
+        def _():
+            for part in range(2):
+                got_in[index, part] = (
+                    total[:, part * TILE : (part + 1) * TILE]
+                    + got_in[index, part].astype(jnp.float32)
+                ).astype(low)
+
+    store_in.start()
+
+    @pl.loop(0, 2)
+    def _(step):
+        half = lax.rem(core + 1 + step, 2)
+        total = tn(hidden[half], cots[...].reshape(total_rows, D))
+
+        @pl.when(step == 0)
+        def _():
+            for index in range(rows_axis):
+                give_out[index] = total[index * TILE : index * TILE + units].astype(low)
+            swap_out.start()
+
+        @pl.when(step == 1)
+        def _():
+            swap_out.wait_recv()
+            for index in range(rows_axis):
+                got_out[index] = (
+                    total[index * TILE : index * TILE + units]
+                    + got_out[index].astype(jnp.float32)
+                ).astype(low)
+            store_out.start()
+
+    grad_residual, gain_out[...] = norm_pull(
+        x_ref[...], gain_ref[...], gx_ref[...] + grad_scatter.total()
+    )
+    gx_ref[...] = cot_ref[...].astype(jnp.float32) + grad_residual
+    y_ref[...] = y_ref[...] + residual + scatter.total()
+    store_in.wait()
+    store_out.wait()
+    swap_in.wait_send()
+    swap_out.wait_send()
+    for each in (gather, cot_gather, grad_scatter, scatter):
+        each.finish()
+    for swap in swaps:
+        swap.wait_send()
+
+
+def ffn_both_call(wide, rows_axis, residual, cot, gain_row, pieces, call_id):
+    gain_row, gain_at = gain_row
+    rows = residual.shape[0]
+    total = wide * rows
+    quarters, _, columns = pieces[0].shape
+    span = quarters * TILE
+    low = jnp.bfloat16
+    units = FF // (wide * rows_axis * 2)
+    share_in = (rows_axis, 2, D, TILE)
+    share_out = (rows_axis, units, D)
+    return pl.pallas_call(
+        lambda *refs: ffn_both_kernel(wide, rows_axis, gain_at, *refs),
+        out_shape=[
+            jax.ShapeDtypeStruct((rows, D), jnp.float32),
+            jax.ShapeDtypeStruct((rows, D), jnp.float32),
+            jax.ShapeDtypeStruct((1, D), jnp.float32),
+            jax.ShapeDtypeStruct(share_in, low),
+            jax.ShapeDtypeStruct(share_out, low),
+        ],
+        in_specs=[VM, VM, VM] + [HBM] * len(pieces),
+        out_specs=[VM, VM, VM, HBM, HBM],
+        scratch_shapes=[
+            pltpu.VMEM((wide, rows, D), low),
+            pltpu.VMEM((wide, rows, D), low),
+            pltpu.VMEM((2, quarters, D, columns), low),
+            pltpu.VMEM((2, total, 2 * span), low),
+            pltpu.VMEM((2, total, span), low),
+            pltpu.VMEM((total, D), jnp.float32),
+            pltpu.VMEM((total, D), jnp.float32),
+            pltpu.VMEM((wide, rows, D), low),
+            pltpu.VMEM((wide, rows, D), low),
+            pltpu.VMEM((3, rows, D), low),
+            pltpu.VMEM((3, rows, D), low),
+            pltpu.VMEM(share_in, low),
+            pltpu.VMEM(share_out, low),
+            pltpu.VMEM(share_in, low),
+            pltpu.VMEM(share_out, low),
+            pltpu.SemaphoreType.DMA((29,)),
+            pltpu.SemaphoreType.DMA((29,)),
+            pltpu.SemaphoreType.DMA((9,)),
+        ],
+        compiler_params=pltpu.CompilerParams(
+            collective_id=call_id, has_side_effects=True, vmem_limit_bytes=VMEM_LIMIT
+        ),
+        name="ffn_both_%d" % rows,
+    )(residual, cot, gain_row, *pieces)
+
+
 GELU_A = float(np.sqrt(2.0 / np.pi))
 GELU_B = 0.044715
 
 
 def ffn_backward_call(wide, rows_axis, grad, residual, gain_row, kept, call_id, carried=()):
+    gain_row, gain_at = gain_row
     at, pre, hidden, weight = kept
     rows = residual.shape[0]
     low = jnp.bfloat16
@@ -848,7 +1108,7 @@
     share_out = (rows_axis, units, D)
     sums = [jax.ShapeDtypeStruct(each.shape[1:], low) for each in carried]
     return pl.pallas_call(
-        lambda *refs: ffn_backward_kernel(wide, rows_axis, *refs),
+        lambda *refs: ffn_backward_kernel(wide, rows_axis, gain_at, *refs),
         out_shape=[
             jax.ShapeDtypeStruct((rows, D), jnp.float32),
             jax.ShapeDtypeStruct((1, D), jnp.float32),
@@ -884,10 +1144,11 @@
 
 
 def start_weights_kernel(
-    wide, rows, win_in, wout_in, cin_in, cout_in, ffn_in, ffn_out, attn_ref, dec_half, *refs
+    wide, rows, win_in, wout_in, cin_in, cout_in, ffn_in, ffn_out, gains, enc_line, dec_line,
+    attn_ref, dec_half, enc_gains, dec_gains, enc_bias, dec_bias, *refs
 ):
     enc, dec = refs[:wide], refs[wide : 2 * wide]
-    held, blocks, spare, in_ref, out_ref, ffn, send_sem, recv_sem, local_sem = refs[2 * wide :]
+    held, blocks, spare, in_ref, out_ref, ffn, enc_row, dec_row, send_sem, recv_sem, local_sem = refs[2 * wide :]
     core, place = lax.axis_index("section"), lax.axis_index("wide")
     peers = peers_of(wide)
     sibling = peers[-1]
@@ -964,8 +1225,36 @@
                     jnp.bfloat16
                 )
 
+    lines = 10 + 2 * wide
+    gain_moves = [remote(gains, target, sems, lines, sibling) for target in (enc_gains, dec_gains)]
+    line_moves = [
+        remote(enc_line, enc_row, sems, lines + 1, sibling),
+        remote(dec_line, dec_row, sems, lines + 1, sibling),
+    ]
+    for own, (gain_ref, row_ref, line_ref) in enumerate(
+        ((enc_gains, enc_row, enc_line), (dec_gains, dec_row, dec_line))
+    ):
+
+        @pl.when(core == own)
+        def _():
+            gain_ref[...] = gains[...]
+            row_ref[...] = line_ref[...]
+            gain_moves[own].start()
+            line_moves[own].start()
+
     for index in range(2 * wide):
         prepare(index)
+    for own in range(2):
+
+        @pl.when(core == own)
+        def _():
+            gain_moves[1 - own].wait_recv()
+            line_moves[1 - own].wait_recv()
+            gain_moves[own].wait_send()
+            line_moves[own].wait_send()
+
+    bias_rows(enc_row, enc_bias)
+    bias_rows(dec_row, dec_bias)
 
     def move(outs, base):
         for v in range(wide):
@@ -1015,7 +1304,7 @@
         give.wait_send()
 
 
-def start_weights(wide, rows, attn_in, attn_out, cross_in, cross_out, ffn_in, ffn_out):
+def start_weights(wide, rows, attn_in, attn_out, cross_in, cross_out, ffn_in, ffn_out, gains, lines):
     depth = ffn_in.shape[1]
     low = jnp.bfloat16
     block = jax.ShapeDtypeStruct((rows, depth, 3 * TILE), low)
@@ -1025,10 +1314,14 @@
         out_shape=[
             jax.ShapeDtypeStruct((2, wide * depth, 3 * HD), low),
             jax.ShapeDtypeStruct(part, low),
+            jax.ShapeDtypeStruct(gains.shape, jnp.float32),
+            jax.ShapeDtypeStruct(gains.shape, jnp.float32),
+            jax.ShapeDtypeStruct((H, LE, LE), jnp.float32),
+            jax.ShapeDtypeStruct((H, LD, LD), jnp.float32),
         ]
         + [block] * (2 * wide),
-        in_specs=[HBM] * 6,
-        out_specs=[HBM] * (2 + 2 * wide),
+        in_specs=[HBM] * 6 + [VM] * 3,
+        out_specs=[HBM] * 2 + [VM] * 4 + [HBM] * (2 * wide),
         scratch_shapes=[
             pltpu.VMEM(part, low),
             pltpu.VMEM((wide,) + part, low),
@@ -1036,16 +1329,18 @@
             pltpu.VMEM(ffn_in.shape[1:], low),
             pltpu.VMEM((depth, FF), low),
             pltpu.VMEM((2, wide) + block.shape, low),
-            pltpu.SemaphoreType.DMA((10 + 2 * wide,)),
-            pltpu.SemaphoreType.DMA((10 + 2 * wide,)),
+            pltpu.VMEM(lines[0].shape, jnp.float32),
+            pltpu.VMEM(lines[1].shape, jnp.float32),
+            pltpu.SemaphoreType.DMA((12 + 2 * wide,)),
+            pltpu.SemaphoreType.DMA((12 + 2 * wide,)),
             pltpu.SemaphoreType.DMA((10 + wide,)),
         ],
         compiler_params=pltpu.CompilerParams(
             collective_id=1, has_side_effects=True, vmem_limit_bytes=VMEM_LIMIT
         ),
         name="start_weights",
-    )(attn_in, attn_out[0].T, cross_in, cross_out, ffn_in, ffn_out[0].T)
-    return attn, dec_half, outs[:wide], outs[wide:]
+    )(attn_in, attn_out[0].T, cross_in, cross_out, ffn_in, ffn_out[0].T, gains, *lines)
+    return attn, dec_half, outs[:2], outs[2:4], outs[4 : 4 + wide], outs[4 + wide :]
 
 
 def split_at(rows):
@@ -1077,16 +1372,16 @@
         self.scatter = ScatterPlane(self.own, self.plane, sems, base, peers, size)
         base += 6
         chunk = batch.shape[1] // (len(others) + 1)
-        self.row, self.chunk = row, chunk
+
+        def lanes(k):
+            return pl.ds(pl.multiple_of((row ^ k) * chunk, TILE), chunk)
+
+        self.kept, self.relayed = lanes(0), lanes(2)
+        near, far = others[0], others[1]
         self.spreads = [
-            remote(
-                self.send.at[:, pl.ds(pl.multiple_of((row ^ k) * chunk, TILE), chunk)],
-                self.zland.at[k - 1],
-                sems,
-                base + k - 1,
-                others[k - 1],
-            )
-            for k in range(1, len(others) + 1)
+            remote(self.send.at[:, lanes(1)], self.zland.at[0], sems, base, near),
+            remote(self.send.at[:, lanes(3)], self.zland.at[1], sems, base + 1, near),
+            remote(self.send.at[:, lanes(2)], self.zland.at[2], sems, base + 2, far),
         ]
 
     def start(self):
@@ -1126,16 +1421,21 @@
         self.send[...] = (self.own[0].astype(jnp.float32) + self.scatter.total()).astype(
             jnp.bfloat16
         )
-        for copy in self.spreads:
-            copy.start()
+        self.spreads[0].start()
+        self.spreads[1].start()
+
+    def relay(self):
+        self.spreads[1].wait_recv()
+        self.send[:, self.relayed] = (
+            self.send[:, self.relayed].astype(jnp.float32) + self.zland[1].astype(jnp.float32)
+        ).astype(jnp.bfloat16)
+        self.spreads[2].start()
 
     def total(self):
-        for copy in self.spreads:
-            copy.wait_recv()
-        lanes = pl.ds(pl.multiple_of(self.row * self.chunk, TILE), self.chunk)
-        out = self.send[:, lanes].astype(jnp.float32)
-        for k in range(len(self.spreads)):
-            out = out + self.zland[k].astype(jnp.float32)
+        out = self.send[:, self.kept].astype(jnp.float32)
+        for index in (0, 2):
+            self.spreads[index].wait_recv()
+            out = out + self.zland[index].astype(jnp.float32)
         return out
 
     def finish(self):
@@ -1164,7 +1464,7 @@
     line_bufs, refs = refs[15:19], refs[19:]
     held, win, wout, gx, gt, context_e, projected_e, context_d, projected_d = refs[:9]
     keep, give, ready, landing, small, small_land, small_plane, small_rows = refs[9:17]
-    halves, (send_sem, recv_sem, local_sem) = refs[17:23], refs[23:]
+    halves, (sums_ref, send_sem, recv_sem, local_sem) = refs[17:23], refs[23:]
     core, place, row = lax.axis_index("section"), lax.axis_index("wide"), lax.axis_index("rows")
     peers = peers_of(wide)
     sibling = peers[-1]
@@ -1211,58 +1511,50 @@
     ]
     base += rows - 1
     hand_base = base
-    base += 2 * wide
-
-    def hand(section, source, v):
+    base += 6 * wide
+
+    def hand(section, source, v, piece):
+        index = piece * wide + v
         return pltpu.make_async_remote_copy(
-            src_ref=ready.at[section, v],
-            dst_ref=landing.at[source, v],
-            send_sem=send_sem.at[hand_base + section * wide + v],
-            recv_sem=recv_sem.at[hand_base + source * wide + v],
+            src_ref=ready.at[section, v, piece],
+            dst_ref=landing.at[source, v, piece],
+            send_sem=send_sem.at[hand_base + section * 3 * wide + index],
+            recv_sem=recv_sem.at[hand_base + source * 3 * wide + index],
             device_id={"section": section, "wide": place ^ v},
             device_id_type=MESH,
         )
 
-    def hand_home(section):
-        return pltpu.make_async_copy(ready.at[section, 0], landing.at[core, 0], local_sem.at[local_base])
-
-    def hand_out(section, part_in, part_out):
-        turned = tn(part_out, straight).astype(low)
+    def hand_out(section, piece, value):
         for owner in range(wide):
-            own = slice(owner * depth, (owner + 1) * depth)
-            for part in range(2):
-                ready[section, owner ^ place, :, pl.ds(part * TILE, TILE)] = part_in[part][own]
-            ready[section, owner ^ place, :, pl.ds(2 * TILE, TILE)] = turned[own]
+            ready[section, owner ^ place, piece] = value[owner * depth : (owner + 1) * depth]
         for v in range(1, wide):
-            hand(section, core, v).start()
+            hand(section, core, v, piece).start()
 
         @pl.when(core == section)
         def _():
-            hand_home(section).start()
+            landing[core, 0, piece] = ready[section, 0, piece]
 
         @pl.when(core != section)
         def _():
-            hand(section, core, 0).start()
+            hand(section, core, 0, piece).start()
 
     def handed(section):
-        for v in range(1, wide):
-            hand(section, core, v).wait_send()
-
-        @pl.when(core == section)
-        def _():
-            hand_home(section).wait()
-
-        @pl.when(core != section)
-        def _():
-            hand(section, core, 0).wait_send()
+        for piece in range(3):
+            for v in range(1, wide):
+                hand(section, core, v, piece).wait_send()
+
+            @pl.when(core != section)
+            def _():
+                hand(section, core, 0, piece).wait_send()
 
     def came(source):
-        for v in range(1, wide):
-            hand(0, source, v).wait_recv()
-
-        @pl.when(core != source)
-        def _():
-            hand(0, source, 0).wait_recv()
+        for piece in range(3):
+            for v in range(1, wide):
+                hand(0, source, v, piece).wait_recv()
+
+            @pl.when(core != source)
+            def _():
+                hand(0, source, 0, piece).wait_recv()
 
     half_copies = []
 
@@ -1273,7 +1565,7 @@
 
             @pl.when(core == own)
             def _():
-                parts = value[:, :middle], value[:, middle:]
+                parts = (value[:, :middle], value[:, middle:]) if index != 1 else (value[:middle], value[middle:])
                 mine[...] = parts[own].astype(mine.dtype)
                 its[...] = parts[1 - own].astype(its.dtype)
 
@@ -1291,54 +1583,62 @@
     small[...] = jnp.zeros_like(small)
     for i, gain in enumerate(gains):
         small[i // 2, pl.ds(1 + i % 2, 1), pl.ds(0, D)] = gain[...]
-    hand_out(1, [dec_in[0], dec_in[1]], dec_out[...])
+    batches[0].join()
+    for piece in range(2):
+        hand_out(1, piece, dec_in[piece])
+    hand_out(1, 2, tn(dec_out[...], straight).astype(low))
     g_ref, x_ref, gain_ref, normed_ref, projected_ref, context_ref, weights_ref = dec_self
     for load in attn_loads(dec_attn):
         load.wait()
     self_backward_rows(
-        g_ref, x_ref, gain_ref, win, wout, projected_ref, weights_ref, gt, small.at[1], context_d, projected_d
+        g_ref, x_ref, gain_ref, win, wout, projected_ref, weights_ref, gt, small.at[1], context_d, projected_d, sums_ref
     )
     for load in attn_loads(enc_attn):
         load.start()
-    batches[0].join()
     self_backward_weights(g_ref, normed_ref, context_ref, projected_d, held)
     batches[1].start()
-    by_half(2, gt[...], t_half)
     line.loaded()
     line.turn(0)
+    batches[0].pass_on()
+    by_half(2, gt[...], t_half)
     g_ref, x_ref, gain_ref, normed_ref, projected_ref, context_ref, weights_ref = enc_self
     for load in attn_loads(enc_attn):
         load.wait()
     self_backward_rows(
-        g_ref, x_ref, gain_ref, win, wout, projected_ref, weights_ref, gx, small.at[0], context_e, projected_e
+        g_ref, x_ref, gain_ref, win, wout, projected_ref, weights_ref, gx, small.at[0], context_e, projected_e, sums_ref
     )
     first.start()
     batches[1].join()
-    batches[0].pass_on()
     batches[1].given()
     self_backward_weights(g_ref, normed_ref, context_ref, projected_e, held)
     batches[2].start()
-    by_half(1, gx[...], x_half)
     line.turn(1)
-    batches[2].join()
     batches[0].spread()
     first.wait()
     small[core] = small[core] + small_land[...]
     for copy in plane:
         copy.start()
+    batches[2].join()
     batches[1].pass_on()
-    line.turn(2)
-    batches[1].spread()
-    batches[2].pass_on()
+    by_half(1, gx[...].T, x_half)
     for copy in plane:
         copy.wait()
     small[core] = small[core] + jnp.sum(small_plane[...], axis=0)
     for copy in spread_small:
         copy.start()
+    line.close(0)
+    hand_out(0, 0, line_bufs[0][0, 0])
+    batches[0].relay()
+    line.turn(2)
+    batches[1].spread()
+    batches[2].pass_on()
+    line.close(1)
+    hand_out(0, 1, line_bufs[0][0, 1])
+    batches[1].relay()
     batches[2].spread()
-    for index in range(3):
-        line.close(index)
-    hand_out(0, [line_bufs[0][0, 0], line_bufs[0][0, 1]], line_bufs[2][0])
+    line.close(2)
+    hand_out(0, 2, tn(line_bufs[2][0], straight).astype(low))
+    batches[2].relay()
     span, part = keep.shape[1] - cross_ref.shape[1] // rows // 2, cross_ref.shape[1] // rows // 2
     crosses = batches[0].total()
     selfs = [batches[2].total(), batches[1].total()]
@@ -1384,19 +1684,23 @@
     columns = cross.shape[1]
     enc_rows, dec_rows = enc_self[0].shape[0], dec_self[0].shape[0]
     wanted = (columns + columns // 2) // rows
-    copies = 3 * (wide + 6 + rows - 1) + 9 + wide + rows - 1 + 2 * wide + 4
+    copies = 3 * (wide + 6 + rows - 1) + 9 + wide + rows - 1 + 6 * wide + 4
     small = (16, (D + TILE - 1) // TILE * TILE)
     middle = D // 2
-    half_shapes = [(dec_rows, low), (enc_rows, jnp.float32), (dec_rows, jnp.float32)]
+    half_shapes = [
+        ((dec_rows, middle), low),
+        ((middle, enc_rows), jnp.float32),
+        ((dec_rows, middle), jnp.float32),
+    ]
     batch_scratch = reduce_weights_scratch(wide, rows, size, columns)
     return pl.pallas_call(
         lambda *refs: last_kernel(wide, rows, *refs),
         out_shape=[
             jax.ShapeDtypeStruct((2, size, wanted), jnp.float32),
-            jax.ShapeDtypeStruct((2, wide, depth, 3 * TILE), low),
+            jax.ShapeDtypeStruct((2, wide, 3, depth, TILE), low),
             jax.ShapeDtypeStruct(small, jnp.float32),
         ]
-        + [jax.ShapeDtypeStruct((2, each, middle), kind) for each, kind in half_shapes],
+        + [jax.ShapeDtypeStruct((2, *each), kind) for each, kind in half_shapes],
         in_specs=[HBM, VM, VM, HBM, HBM, VM, HBM, HBM] + [VM] * 18,
         out_specs=[HBM, HBM, VM, HBM, HBM, HBM],
         scratch_shapes=batch_scratch * 3
@@ -1413,15 +1717,16 @@
             pltpu.VMEM((dec_rows, 3 * HD), low),
             pltpu.VMEM((size, wanted), jnp.float32),
             pltpu.VMEM((size, wanted), jnp.float32),
-            pltpu.VMEM((2, wide, depth, 3 * TILE), low),
-            pltpu.VMEM((2, wide, depth, 3 * TILE), low),
+            pltpu.VMEM((2, wide, 3, depth, TILE), low),
+            pltpu.VMEM((2, wide, 3, depth, TILE), low),
             pltpu.VMEM((2,) + small, jnp.float32),
             pltpu.VMEM(small, jnp.float32),
             pltpu.VMEM((wide - 1,) + small, jnp.float32),
             pltpu.VMEM((rows - 1,) + small, jnp.float32),
         ]
-        + [pltpu.VMEM((each, middle), kind) for each, kind in half_shapes for _ in range(2)]
+        + [pltpu.VMEM(each, kind) for each, kind in half_shapes for _ in range(2)]
         + [
+            pltpu.VMEM((H, 1, 2 * enc_rows), jnp.float32),
             pltpu.SemaphoreType.DMA((copies,)),
             pltpu.SemaphoreType.DMA((copies,)),
             pltpu.SemaphoreType.DMA((12 + wide,)),
@@ -1452,7 +1757,7 @@
             shift = group * units - tile * TILE
             picks = ((row_ids + shift == lane_ids) & (row_ids < units)).astype(low)
             part = matmul(
-                parts_ref[half, chip ^ place, :, pl.ds((first + block) * TILE, TILE)], picks
+                parts_ref[half, chip ^ place, first + block], picks
             )
             total = part if total is None else total + part
         return total
@@ -1461,43 +1766,43 @@
         in_ref[0, :, pl.ds(tile * TILE, TILE)] = tile_at(tile, 0, in_ref.shape[2])
     for tile in range(out_ref.shape[2] // TILE):
         out_ref[0, :, pl.ds(tile * TILE, TILE)] = tile_at(tile, 2, out_ref.shape[2])
-    gain_ref[0] = small_ref[0:3, 0:D]
+    for row in range(3):
+        gain_ref[row] = small_ref[row : row + 1, 0:D]
     for section, hot in enumerate((enc_hot, dec_hot)):
 
         @pl.when(core == section)
         def _():
             sums = small_ref[8:16, 0 : hot.shape[1]]
             bias = lax.dot_general(
-                hot[...], sums, (((1,), (1,)), ((), ())), precision=HIGHEST, preferred_element_type=jnp.float32
+                sums, hot[...], (((1,), (1,)), ((), ())), precision=HIGHEST, preferred_element_type=jnp.float32
             )
-            bias_ref[0] = bias[:, :H]
+            for head in range(H):
+                bias_ref[head] = bias[head : head + 1]
 
     size, depth = attn_ref.shape[1], in_ref.shape[1]
     whole = jnp.concatenate([attn_ref[0], attn_ref[1, 2 * size - depth :]], axis=0)
-    width_in, width = win_ref.shape[2], cin_ref.shape[2]
-    win_ref[0] = whole[:, :width_in]
-    base = width_in // TILE * TILE
-    turned = whole[:, base : base + TILE].T
-    wout_ref[0] = turned[width_in - base : width_in - base + width]
-    cin_ref[0] = whole[:, width_in + width : width_in + 2 * width]
-    cout_ref[0] = whole[:, width_in + 2 * width : width_in + 3 * width]
+    turned = whole.T
+    start = 0
+    for ref in (win_ref, wout_ref, cin_ref, cout_ref):
+        ref[0] = turned[start : start + ref.shape[1]]
+        start += ref.shape[1]
 
 
 def assemble(rows, parts, attn_parts, small):
-    wide, depth = parts.shape[1:3]
+    wide, depth = parts.shape[1], parts.shape[3]
     shapes = [
-        (depth, 2 * FF // rows),
-        (depth, FF // rows),
-        (3, D),
-        (NB, H),
-        (depth, 3 * HD // rows),
-        (HD // rows, depth),
-        (depth, HD // rows),
-        (depth, HD // rows),
+        (1, depth, 2 * FF // rows),
+        (1, depth, FF // rows),
+        (3, 1, D),
+        (H, 1, NB),
+        (1, 3 * HD // rows, depth),
+        (1, HD // rows, depth),
+        (1, HD // rows, depth),
+        (1, HD // rows, depth),
     ]
     return pl.pallas_call(
         lambda *refs: assemble_kernel(FF // (wide * rows * 2), *refs),
-        out_shape=[jax.ShapeDtypeStruct((1, *shape), jnp.float32) for shape in shapes],
+        out_shape=[jax.ShapeDtypeStruct(shape, jnp.float32) for shape in shapes],
         in_specs=[VM] * 5,
         out_specs=[VM] * len(shapes),
         compiler_params=pltpu.CompilerParams(vmem_limit_bytes=VMEM_LIMIT),
@@ -1511,25 +1816,11 @@
     )
 
 
-def bias_rows_kernel(enc_ref, dec_ref, enc_out, dec_out):
-    for source, target in ((enc_ref, enc_out), (dec_ref, dec_out)):
-        length, span = target.shape[1], source.shape[1]
-        for head in range(H):
-            row = jnp.broadcast_to(source[pl.ds(head, 1), :], (length, span))
-            target[head] = pltpu.roll(row, 0, 1, stride=1, stride_axis=0)[:, :length]
-
-
-def bias_rows(enc_row, dec_row):
-    return pl.pallas_call(
-        bias_rows_kernel,
-        out_shape=[
-            jax.ShapeDtypeStruct((H, LE, LE), jnp.float32),
-            jax.ShapeDtypeStruct((H, LD, LD), jnp.float32),
-        ],
-        in_specs=[VM, VM],
-        out_specs=[VM, VM],
-        name="bias_rows",
-    )(enc_row, dec_row)
+def bias_rows(source, target):
+    length, span = target.shape[1], source.shape[1]
+    for head in range(H):
+        row = jnp.broadcast_to(source[pl.ds(head, 1), :], (length, span))
+        target[head] = pltpu.roll(row, 0, 1, stride=1, stride_axis=0)[:, :length]
 
 
 def distance_sums(scores, span):
@@ -1565,7 +1856,8 @@
 
 
 def attend_heads(query_of, key_of, value_of, bias_of, allowed, context_ref, weights_ref):
-    for pair in range(H // 2):
+    @pl.loop(0, H // 2)
+    def _(pair):
         query, key, value = query_of(pair), key_of(pair), value_of(pair)
         total = None
         for side in range(2):
@@ -1579,11 +1871,12 @@
             weights_ref[head] = weights
             part = matmul(weights.astype(jnp.bfloat16), head_lanes(value, side))
             total = part if total is None else total + part
-        context_ref[:, pl.ds(pair * TILE, TILE)] = total.astype(jnp.bfloat16)
+        context_ref[:, pair_tile(pair, 0)] = total.astype(jnp.bfloat16)
 
 
 def attend_heads_backward(query_of, key_of, value_of, weights_ref, grad_of, put, put_scores=None):
-    for pair in range(H // 2):
+    @pl.loop(0, H // 2)
+    def _(pair):
         query, key, value, grad = query_of(pair), key_of(pair), value_of(pair), grad_of(pair)
         sums = [None, None, None]
         for side in range(2):
@@ -1604,6 +1897,19 @@
         put(pair, *sums)
 
 
+def pair_tile(pair, base):
+    return pl.ds(pl.multiple_of(base + pair * TILE, TILE), TILE)
+
+
+def item_numbers(lengths_ref, core, shape, axis):
+    positions = lax.broadcasted_iota(jnp.int32, shape, axis)
+    number, end = jnp.zeros(shape, jnp.int32), 0
+    for item in range(lengths_ref.shape[1] - 1):
+        end = end + lengths_ref[core, item]
+        number = number + (positions >= end).astype(jnp.int32)
+    return number
+
+
 def weight_spec(half, width, index):
     return pl.BlockSpec((None, D, width), lambda step: (half, 0, index), memory_space=pltpu.VMEM)
 
@@ -1613,18 +1919,21 @@
 
 
 def tile_of(ref, base):
-    return lambda pair: ref[:, pl.ds(base + pair * TILE, TILE)]
-
-
-def self_forward_kernel(wide, causal, x_ref, gain_ref, win_ref, wout_ref, bias_ref, col_ref, row_ref, *refs):
+    return lambda pair: ref[:, pair_tile(pair, base)]
+
+
+def self_forward_kernel(
+    wide, causal, x_ref, gain_ref, win_ref, wout_ref, bias_ref, lengths_ref, *refs
+):
+    core = lax.axis_index("section")
     if wide:
         blocks, dec_blocks, refs = refs[: wide - 1], refs[wide - 1 : 2 * wide - 2], refs[2 * wide - 2 :]
-    y_ref, normed_ref, projected_ref, context_ref, weights_ref = refs[:5]
+    y_ref, low_ref, normed_ref, projected_ref, context_ref, weights_ref = refs[:6]
     if wide:
-        pieces, dec_pieces, sems = refs[5 : 4 + wide], refs[4 + wide : 3 + 2 * wide], refs[3 + 2 * wide :]
+        pieces, dec_pieces, sems = refs[6 : 5 + wide], refs[5 + wide : 4 + 2 * wide], refs[4 + 2 * wide :]
         peers = peers_of(wide)
         greet(peers + [{"rows": lax.axis_index("rows") ^ 1}])
-        reshard = Reshard(blocks, pieces, blocks[0].shape[0] // 2, sems, 0, peers)
+        reshard = Reshard(blocks, pieces, 0, sems, 0, peers)
         reshard.start()
         half = dec_pieces[0].shape[0]
         mine = pl.ds(lax.axis_index("rows") % 2 * half, half)
@@ -1632,12 +1941,15 @@
             remote(block.at[mine], piece, sems, 9 + v, peers[v])
             for v, (block, piece) in enumerate(zip(dec_blocks, dec_pieces))
         ]
-    residual = x_ref[...].astype(jnp.float32)
-    normed_ref[...] = (residual * rms_rows(residual) * gain_ref[...]).astype(jnp.bfloat16)
+    low_ref[...] = x_ref[core] if causal else x_ref[core].T
+    residual = low_ref[...].astype(jnp.float32)
+    normed_ref[...] = (residual * rms_rows(residual) * gain_ref[pl.ds(0, 1), :]).astype(jnp.bfloat16)
     projected_ref[...] = matmul(normed_ref[...], win_ref[...]).astype(jnp.bfloat16)
-    allowed = col_ref[...] == row_ref[...]
+    length = low_ref.shape[0]
+    allowed = item_numbers(lengths_ref, core, (length, length), 0) == item_numbers(
+        lengths_ref, core, (length, length), 1
+    )
     if causal:
-        length = x_ref.shape[0]
         allowed = allowed & (
             lax.broadcasted_iota(jnp.int32, (length, length), 0)
             >= lax.broadcasted_iota(jnp.int32, (length, length), 1)
@@ -1653,16 +1965,16 @@
     )
     y_ref[...] = residual + nt(context_ref[...], wout_ref[...])
     if wide:
-        reshard.pass_on()
         for copy in later:
             copy.start()
+        reshard.pass_on()
         reshard.finish()
         for copy in later:
             copy.wait()
 
 
-def self_forward(causal, residual, gain_row, weight, bias, items, blocks=(), dec_blocks=()):
-    rows = residual.shape[0]
+def self_forward(causal, embed, gains, weight, bias, lengths, blocks=(), dec_blocks=()):
+    rows = embed.shape[1 if causal else 2]
     low = jnp.bfloat16
     wide = len(blocks) + 1 if blocks else 0
     params = dict(vmem_limit_bytes=VMEM_LIMIT)
@@ -1673,20 +1985,21 @@
         out_shape=[
             jax.ShapeDtypeStruct((rows, D), jnp.float32),
             jax.ShapeDtypeStruct((rows, D), low),
+            jax.ShapeDtypeStruct((rows, D), low),
             jax.ShapeDtypeStruct((rows, 3 * HD), low),
             jax.ShapeDtypeStruct((rows, HD), low),
             jax.ShapeDtypeStruct((H, rows, rows), jnp.float32),
         ]
         + [jax.ShapeDtypeStruct(each.shape, low) for each in blocks]
         + [jax.ShapeDtypeStruct((each.shape[0] // 2, *each.shape[1:]), low) for each in dec_blocks],
-        in_specs=[VM, VM, W_IN, W_OUT, VM, VM, VM] + [HBM] * (2 * len(blocks)),
-        out_specs=[VM] * 5 + [HBM] * (2 * len(blocks)),
+        in_specs=[VM, VM, W_IN, W_OUT, VM, SM] + [HBM] * (2 * len(blocks)),
+        out_specs=[VM] * 6 + [HBM] * (2 * len(blocks)),
         scratch_shapes=[pltpu.SemaphoreType.DMA((12,))] * 2 if blocks else [],
         grid=(1,),
         compiler_params=pltpu.CompilerParams(**params),
         name="self_forward_%d" % rows,
-    )(residual, gain_row, weight, weight, bias, items[:, None], items[None, :], *blocks, *dec_blocks)
-    return y, kept[:4], kept[4:]
+    )(embed, gains, weight, weight, bias, lengths, *blocks, *dec_blocks)
+    return y, kept[:5], kept[5:]
 
 
 def picked(source, start, window, first, width):
@@ -1710,6 +2023,7 @@
     small_ref,
     context_grad,
     projected_grad,
+    sums_ref,
 ):
     low = jnp.bfloat16
     length = x_ref.shape[0]
@@ -1717,10 +2031,10 @@
 
     def put(pair, query, key, value):
         for index, part in enumerate((query, key, value)):
-            projected_grad[:, pl.ds(index * HD + pair * TILE, TILE)] = part.astype(low)
+            projected_grad[:, pair_tile(pair, index * HD)] = part.astype(low)
 
     def put_scores(head, scores):
-        small_ref[pl.ds(8 + head, 1), pl.ds(0, 2 * length)] = distance_sums(scores, 2 * length)
+        sums_ref[head, :, pl.ds(0, 2 * length)] = distance_sums(scores, 2 * length)
 
     attend_heads_backward(
         tile_of(projected_ref, 0),
@@ -1731,9 +2045,11 @@
         put,
         put_scores,
     )
+    for head in range(H):
+        small_ref[pl.ds(8 + head, 1), pl.ds(0, 2 * length)] = sums_ref[head, :, pl.ds(0, 2 * length)]
     grad_normed = nt(projected_grad[...], win_ref[...])
     residual = x_ref[...].astype(jnp.float32)
-    grad_residual, grad_gain = norm_pull(residual, gain_ref[...], grad_normed)
+    grad_residual, grad_gain = norm_pull(residual, gain_ref[pl.ds(0, 1), :], grad_normed)
     small_ref[pl.ds(0, 1), pl.ds(0, D)] = grad_gain
     gx_ref[...] = g_ref[...] + grad_residual
 
@@ -1755,30 +2071,31 @@
 
 
 def cross_forward_kernel(
-    x_ref, final_ref, wkey_ref, wvalue_ref, y_ref, gain_ref, wquery_ref, wout_ref, col_ref, row_ref,
+    x_ref, final_ref, wkey_ref, wvalue_ref, y_ref, gain_ref, wquery_ref, wout_ref, dec_lengths, enc_lengths,
     out_ref, memory_ref, kv_ref, normed_ref, query_ref, context_ref, weights_ref,
 ):
     low = jnp.bfloat16
+    core = lax.axis_index("section")
     residual = x_ref[...]
-    memory_ref[...] = (residual * rms_rows(residual) * final_ref[...]).astype(low)
+    memory_ref[...] = (residual * rms_rows(residual) * final_ref[pl.ds(2, 1), :]).astype(low)
     kv_ref[:, pl.ds(0, HD)] = matmul(memory_ref[...], wkey_ref[...]).astype(low)
     kv_ref[:, pl.ds(HD, HD)] = matmul(memory_ref[...], wvalue_ref[...]).astype(low)
     target = y_ref[...]
-    normed_ref[...] = (target * rms_rows(target) * gain_ref[...]).astype(low)
+    normed_ref[...] = (target * rms_rows(target) * gain_ref[pl.ds(1, 1), :]).astype(low)
     query_ref[...] = matmul(normed_ref[...], wquery_ref[...]).astype(low)
     attend_heads(
         tile_of(query_ref, 0),
         tile_of(kv_ref, 0),
         tile_of(kv_ref, HD),
         None,
-        col_ref[...] == row_ref[...],
+        item_numbers(dec_lengths, core, (LD, LE), 0) == item_numbers(enc_lengths, core, (LD, LE), 1),
         context_ref,
         weights_ref,
     )
     out_ref[...] = target + nt(context_ref[...], wout_ref[...])
 
 
-def cross_forward(x2, final_gain, enc_weight, y1, gain_row, dec_weight, dec_items, enc_items):
+def cross_forward(x2, enc_gains, enc_weight, y1, dec_gains, dec_weight, dec_lengths, enc_lengths):
     low = jnp.bfloat16
     y2, *kept = pl.pallas_call(
         cross_forward_kernel,
@@ -1791,22 +2108,22 @@
             jax.ShapeDtypeStruct((LD, HD), low),
             jax.ShapeDtypeStruct((H, LD, LE), jnp.float32),
         ],
-        in_specs=[VM, VM, C_IN, C_OUT, VM, VM, C_IN, C_OUT, VM, VM],
+        in_specs=[VM, VM, C_IN, C_OUT, VM, VM, C_IN, C_OUT, SM, SM],
         out_specs=[VM] * 7,
         grid=(1,),
         compiler_params=pltpu.CompilerParams(vmem_limit_bytes=VMEM_LIMIT),
         name="cross_forward",
     )(
         x2,
-        final_gain,
+        enc_gains,
         enc_weight,
         enc_weight,
         y1,
-        gain_row,
+        dec_gains,
         dec_weight,
         dec_weight,
-        dec_items[:, None],
-        enc_items[None, :],
+        dec_lengths,
+        enc_lengths,
     )
     return y2, kept
 
@@ -1820,9 +2137,9 @@
     context_grad[...] = matmul(grad_low, wout_ref[...]).astype(low)
 
     def put(pair, query, key, value):
-        query_grad[:, pl.ds(pair * TILE, TILE)] = query.astype(low)
-        kv_grad[:, pl.ds(pair * TILE, TILE)] = key.astype(low)
-        kv_grad[:, pl.ds(HD + pair * TILE, TILE)] = value.astype(low)
+        query_grad[:, pair_tile(pair, 0)] = query.astype(low)
+        kv_grad[:, pair_tile(pair, 0)] = key.astype(low)
+        kv_grad[:, pair_tile(pair, HD)] = value.astype(low)
 
     attend_heads_backward(
         tile_of(query_ref, 0),
@@ -1835,9 +2152,9 @@
     grad_memory = nt(kv_grad[:, pl.ds(0, HD)], wkey_ref[...]) + nt(
         kv_grad[:, pl.ds(HD, HD)], wvalue_ref[...]
     )
-    gx_ref[...], final_out[...] = norm_pull(x_ref[...], final_ref[...], grad_memory)
+    gx_ref[...], final_out[...] = norm_pull(x_ref[...], final_ref[pl.ds(2, 1), :], grad_memory)
     grad_residual, gain_out[...] = norm_pull(
-        y_ref[...], gain_ref[...], nt(query_grad[...], wquery_ref[...])
+        y_ref[...], gain_ref[pl.ds(1, 1), :], nt(query_grad[...], wquery_ref[...])
     )
     gy_ref[...] = g_ref[...] + grad_residual
     lefts = jnp.concatenate([memory_ref[...], normed_ref[...], grad_low], axis=0)
@@ -1857,7 +2174,7 @@
         grad_ref[:, pl.ds(chunk * HD, HD)] = tn(lefts, right).astype(low)
 
 
-def cross_backward(g2, x2, final_gain, enc_weight, y1, gain_row, dec_weight, kept):
+def cross_backward(g2, x2, enc_gains, enc_weight, y1, dec_gains, dec_weight, kept):
     memory, kv, normed, query, context, weights = kept
     low = jnp.bfloat16
     return pl.pallas_call(
@@ -1882,11 +2199,11 @@
     )(
         g2,
         x2,
-        final_gain,
+        enc_gains,
         enc_weight,
         enc_weight,
         y1,
-        gain_row,
+        dec_gains,
         dec_weight,
         dec_weight,
         kv,
@@ -2224,65 +2541,50 @@
     cross_in,
     cross_out,
 ):
-    core = lax.axis_index("section")
     wide, rows = lax.axis_size("wide"), lax.axis_size("rows")
-    depth = attn_in.shape[1]
-    is_dec = core == 1
-
-    def own_row(array):
-        return lax.dynamic_index_in_dim(array[:, 0], core, 0, keepdims=False)
-
-    enc_attn, dec_half, enc_blocks, dec_blocks = start_weights(
-        wide, rows, attn_in, attn_out, cross_in, cross_out, ffn_in, ffn_out
-    )
-    small = jnp.concatenate([norm_gains[0].reshape(-1), rel_bias[0].reshape(-1)])
-    other = xor_permute(small, "section", 1)
-    smalls = (jnp.where(is_dec, other, small), jnp.where(is_dec, small, other))
-    gains = [each[: 3 * D].reshape(3, D) for each in smalls]
-    biases = [each[3 * D :].reshape(NB, H) for each in smalls]
-    bias_lines = [
+    lines = [
         jnp.pad(
             lax.dot_general(
-                bias, distance_hot(length, both, 0), (((0,), (0,)), ((), ())), precision=HIGHEST
+                rel_bias[0], distance_hot(length, both, 0), (((0,), (0,)), ((), ())), precision=HIGHEST
             ),
             ((0, 2), (0, 0)),
         )
-        for bias, length, both in ((biases[0], LE, True), (biases[1], LD, False))
+        for length, both in ((LE, True), (LD, False))
     ]
-    enc_bias, dec_bias = bias_rows(*bias_lines)
-    enc_row, dec_row, cot_row = own_row(enc_embed), own_row(dec_embed), own_row(out_cot)
-    enc_items = item_ids(own_row(enc_lengths), LE)
-    dec_items = item_ids(own_row(dec_lengths), LD)
-
+    enc_attn, dec_half, gains, biases, enc_blocks, dec_blocks = start_weights(
+        wide, rows, attn_in, attn_out, cross_in, cross_out, ffn_in, ffn_out, norm_gains[0], lines
+    )
+    enc_lengths, dec_lengths = enc_lengths[:, 0], dec_lengths[:, 0]
     x1, enc_self, moved = self_forward(
         False,
-        enc_row,
-        gains[0][0:1],
+        jnp.swapaxes(enc_embed[:, 0], 1, 2),
+        gains[0],
         enc_attn,
-        enc_bias,
-        enc_items,
+        biases[0],
+        enc_lengths,
         tuple(enc_blocks[1:]),
         tuple(dec_blocks[1:]),
     )
     enc_pieces, dec_pieces = moved[: wide - 1], moved[wide - 1 :]
     x2, *enc_ffn = ffn_forward_call(
-        wide, x1, gains[0][1:2], [enc_blocks[0], *enc_pieces], 2, (dec_half, *dec_pieces)
+        wide, x1, (gains[0], 1), [enc_blocks[0], *enc_pieces], 2, (dec_half, *dec_pieces)
     )
     enc_ffn, dec_attn, dec_pieces = enc_ffn[:4], enc_ffn[4], [dec_blocks[0], *dec_pieces, *enc_ffn[5:]]
-    y1, dec_self, _ = self_forward(True, dec_row, gains[1][0:1], dec_attn, dec_bias, dec_items)
+    y1, dec_self, _ = self_forward(
+        True, dec_embed[:, 0], gains[1], dec_attn, biases[1], dec_lengths
+    )
     y2, cross_kept = cross_forward(
-        x2, gains[0][2:3], enc_attn, y1, gains[1][1:2], dec_attn, dec_items, enc_items
-    )
-    y3, *dec_ffn = ffn_forward_call(wide, y2, gains[1][2:3], dec_pieces, 3)
-
-    g2, dec_ffn_gain, *dec_ffn_grads = ffn_backward_call(
-        wide, rows, cot_row.astype(jnp.float32), y2, gains[1][2:3], dec_ffn, 4
+        x2, gains[0], enc_attn, y1, gains[1], dec_attn, dec_lengths, enc_lengths
+    )
+    cot_row = lax.dynamic_index_in_dim(out_cot[:, 0], lax.axis_index("section"), 0, keepdims=False)
+    y3, g2, dec_ffn_gain, *dec_ffn_grads = ffn_both_call(
+        wide, rows, y2, cot_row, (gains[1], 2), dec_pieces, 3
     )
     grad_x2, g1, enc_final_gain, dec_cross_gain, cross_grads = cross_backward(
-        g2, x2, gains[0][2:3], enc_attn, y1, gains[1][1:2], dec_attn, cross_kept
+        g2, x2, gains[0], enc_attn, y1, gains[1], dec_attn, cross_kept
     )
     grad_x1, enc_ffn_gain, enc_in, enc_out, *dec_sums = ffn_backward_call(
-        wide, rows, grad_x2, x1, gains[0][1:2], enc_ffn, 5, dec_ffn_grads
+        wide, rows, grad_x2, x1, (gains[0], 1), enc_ffn, 5, dec_ffn_grads
     )
     attn_parts, ffn_parts, small_own, dec_out, enc_grad, dec_grad = last_step(
         wide,
@@ -2293,26 +2595,25 @@
         y3,
         dec_attn,
         enc_attn,
-        (g1, dec_row, gains[1][0:1], *dec_self),
-        (grad_x1, enc_row, gains[0][0:1], *enc_self),
+        (g1, dec_self[0], gains[1], *dec_self[1:]),
+        (grad_x1, enc_self[0], gains[0], *enc_self[1:]),
         (enc_ffn_gain, enc_final_gain, dec_cross_gain, dec_ffn_gain),
     )
-    ffn_in_grad, ffn_out_grad, gain_grad, bias_grad, *attn_grads = assemble(
+    ffn_in_grad, ffn_out_grad, gain_grad, bias_grad, win, wout, cin, cout = assemble(
         rows, ffn_parts, attn_parts, small_own
     )
-    win, wout, cin, cout = attn_grads
     return (
         dec_out[:, None],
-        enc_grad[:, None],
+        jnp.swapaxes(enc_grad, 1, 2)[:, None],
         dec_grad[:, None],
-        gain_grad,
-        bias_grad,
-        win,
+        gain_grad.transpose(1, 0, 2),
+        bias_grad.transpose(1, 2, 0),
+        jnp.swapaxes(win, 1, 2),
         wout,
         ffn_in_grad,
         jnp.swapaxes(ffn_out_grad, 1, 2),
-        cin,
-        cout,
+        jnp.swapaxes(cin, 1, 2),
+        jnp.swapaxes(cout, 1, 2),
     )
 
 

time: 588 us -> 516 us (0.88)
  the two profiles are of different devices: /device:TPU:19 before, /device:TPU:0 now
where the time goes in v5:
time: 516 us; the launch traced here: 508 us
  Pallas kernels  500 us (97%)
  local copies, waits for them, and re-layouts  5.93 us (1%)
    pallas_call x1, Pallas kernels, last_step(): pl.pallas_call(lambda *refs: last_kernel(wide, rows, *refs), out_shape=[j...  134 us
    pallas_call x1, Pallas kernels, ffn_backward_call(): pl.pallas_call(lambda *refs: ffn_backward_kernel(wide, rows_axis, gain_at...  98.4 us
    pallas_call x1, Pallas kernels, ffn_forward_call(): pl.pallas_call(lambda *refs: ffn_forward_kernel(wide, bool(carried), len(...  92.4 us
    pallas_call x2, Pallas kernels, self_forward(): pl.pallas_call(lambda *refs: self_forward_kernel(wide, causal, *refs), ou...  66.4 us
    pallas_call x1, Pallas kernels, start_weights(): pl.pallas_call(lambda *refs: start_weights_kernel(wide, rows, *refs), out...  41.8 us
    pallas_call x1, Pallas kernels, ffn_both_call(): pl.pallas_call(lambda *refs: ffn_both_kernel(wide, rows_axis, gain_at, *r...  40.2 us
    pallas_call x1, Pallas kernels, cross_backward(): pl.pallas_call(cross_backward_kernel, out_shape=[jax.ShapeDtypeStruct((LE...  13.3 us

profile of v5, /device:TPU:0, one launch (start us, length us, event | category | flops | bytes accessed | tf_op | source)
XLA Modules:
  0.0 508.3 jit_solution(6659359215480910087)
XLA Ops:
  0.6 0.0 copy-start
  0.7 0.9 convolution_bitcast_fusion.1
  1.6 0.6 pad.9.refs_8_
  2.2 1.0 convolution_bitcast_fusion
  3.2 0.6 pad.8.refs_7_
  3.8 1.3 copy.42
  5.1 0.0 copy-done
  5.1 0.7 dynamic-slice_bitcast_fusion.refs_1_
  5.8 41.8 %start_weights.1 = (bf16[2,1472,1152]{2,1,0:T(8,128)(2,1)}, bf16[368,1152]{1,0:T(8,128)(2,1)}, f32[3,1472]{1,0:T(4,128)}, f32[3,1472]{1,0:T(4,128)}, f32[6,256,2...) custom-call(bf16[1,368,1152]{2,1,0:T(8,128)(2,1)} %refs_0_.1, ...), custom_call_target="tpu_custom_call" | custom-call | tf_op jit(solution)/shard_map/start_weights/pallas_call | solution.py:1312
  47.6 60.6 %self_forward_256.1 = (f32[256,1472]{1,0:T(8,128)}, bf16[256,1472]{1,0:T(8,128)(2,1)}, bf16[256,1472]{1,0:T(8,128)(2,1)}, bf16[256,1152]{1,0:T(8,128)(2,1)}, bf1...) custom-call(bf16[2,1472,256]{2,1,0:T(8,128)(2,1)} %bitcast.46, ...), custom_call_target="tpu_custom_call" | custom-call | tf_op jit(solution)/shard_map/self_forward_256/pallas_call | solution.py:1983
  108.3 92.4 %ffn_forward_256.1 = (f32[256,1472]{1,0:T(8,128)}, bf16[1472,1024]{1,0:T(8,128)(2,1)}, bf16[2,1024,1024]{2,1,0:T(8,128)(2,1)}, bf16[2,512,1024]{2,1,0:T(8,128)(2...) custom-call(f32[256,1472]{1,0:T(8,128)} %get-tuple-element.98.refs_0, ...), custom_call_target="tpu_custom_call" | custom-call | tf_op jit(solution)/shard_map/ffn_forward_256/pallas_call | solution.py:682
  200.7 5.8 %self_forward_64.1 = (f32[64,1472]{1,0:T(8,128)}, bf16[64,1472]{1,0:T(8,128)(2,1)}, bf16[64,1472]{1,0:T(8,128)(2,1)}, bf16[64,1152]{1,0:T(8,128)(2,1)}, bf16[64,384]{1,0:T(8,128)(2,1)}, /*index=5*/f32[6,64,64]{2,1,0:T(8,128)}) custom-call(bf16[2,64,1472]{2,1,0:T(8,128)(2,1)} %bitcast.49, f32[3,1472]{1,0:T(4,128)} %get-tuple-element.108.refs_1_.gain_ref.refs_2_.refs_10_, ...), custom_call_target="tpu_custom_call" | custom-call | tf_op jit(solution)/shard_map/self_forward_64/pallas_call | solution.py:1983
  206.5 6.8 %cross_forward.1 = (f32[64,1472]{1,0:T(8,128)}, bf16[256,1472]{1,0:T(8,128)(2,1)}, bf16[256,768]{1,0:T(8,128)(2,1)}, bf16[64,1472]{1,0:T(8,128)(2,1)}, bf16[64,3...) custom-call(f32[256,1472]{1,0:T(8,128)} %get-tuple-element.107.x_ref, ...), custom_call_target="tpu_custom_call" | custom-call | tf_op jit(solution)/shard_map/cross_forward/pallas_call | solution.py:2100
  213.3 40.2 %ffn_both_64.1 = (f32[64,1472]{1,0:T(8,128)}, f32[64,1472]{1,0:T(8,128)}, f32[1,1472]{1,0:T(1,128)}, bf16[4,2,1472,128]{3,2,1,0:T(8,128)(2,1)}, bf16[4,112,1472]{2,1,0:T(8,128)(2,1)}) custom-call(f32[64,1472]{1,0:T(8,128)} %get-tuple-element.112.refs_0_, bf16[64,1472]{1,0:T(8,128)(2,1)} %dynamic-slice_bitcast_fusion.refs_1_, ...), custom_call_target="tpu_custom_call" | custom-call | tf_op jit(solution)/shard_map/ffn_both_64/pallas_call | solution.py:1059
  253.5 13.3 %cross_backward.1 = (f32[256,1472]{1,0:T(8,128)}, f32[64,1472]{1,0:T(8,128)}, f32[1,1472]{1,0:T(1,128)}, f32[1,1472]{1,0:T(1,128)}, bf16[1472,1536]{1,0:T(8,128)(2,1)}) custom-call(f32[64,1472]{1,0:T(8,128)} %get-tuple-element.117.g_ref, f32[256,1472]{1,0:T(8,128)} %get-tuple-element.107.x_ref, ...), custom_call_target="tpu_custom_call" | custom-call | tf_op jit(solution)/shard_map/cross_backward/pallas_call | solution.py:2180
  266.8 98.4 %ffn_backward_256.1 = (f32[256,1472]{1,0:T(8,128)}, f32[1,1472]{1,0:T(1,128)}, bf16[4,2,1472,128]{3,2,1,0:T(8,128)(2,1)}, bf16[4,112,1472]{2,1,0:T(8,128)(2,1)},...) custom-call(f32[256,1472]{1,0:T(8,128)} %get-tuple-element.125.refs_0_, ...), custom_call_target="tpu_custom_call" | custom-call | tf_op jit(solution)/shard_map/ffn_backward_256/pallas_call | solution.py:1110
  365.2 133.5 %last_step.1 = (f32[2,192,576]{2,1,0:T(8,128)}, bf16[2,4,3,368,128]{4,3,2,1,0:T(8,128)(2,1)}, f32[16,1536]{1,0:T(8,128)}, bf16[2,64,736]{2,1,0:T(8,128)(2,1)}, f...) custom-call(bf16[1472,1536]{1,0:T(8,128)(2,1)} %get-tuple-element.124.refs_0_, ...), custom_call_target="tpu_custom_call" | custom-call | tf_op jit(solution)/shard_map/last_step/pallas_call | solution.py:1696
  498.8 0.0 copy-start.4
  498.8 0.0 copy-start.2
  498.8 6.7 %assemble.1 = (f32[1,368,1792]{2,1,0:T(8,128)}, f32[1,368,896]{2,1,0:T(8,128)}, f32[3,1,1472]{2,1,0:T(1,128)}, f32[6,1,32]{2,1,0:T(1,128)}, f32[1,288,368]{2,1,0...) custom-call(bf16[2,4,3,368,128]{4,3,2,1,0:T(8,128)(2,1)} %get-tuple-element.156.refs_0_, ...), custom_call_target="tpu_custom_call" | custom-call | tf_op jit(solution)/shard_map/assemble/pallas_call | solution.py:1803
  505.4 0.0 copy-done.4
  505.4 0.0 copy-start.1
  505.5 0.7 copy.46
  506.1 0.0 copy-done.2
  506.1 0.0 copy-start.3
  506.1 1.1 copy.47
  507.3 0.1 copy-done.3
  507.4 0.7 copy.48
  508.1 0.0 copy-done.1
Async XLA Ops:
  0.6 4.5 copy-start
  498.8 6.7 %copy-start.4 = (bf16[2,64,736]{2,1,0:T(8,128)(2,1)S(1)}, bf16[2,64,736]{2,1,0:T(8,128)(2,1)}, u32[]{:S(2)}) copy-start(bf16[2,64,736]{2,1,0:T(8,128)(2,1)} %get-tuple-element.153) | copy-start | bytes 565252
  498.8 7.4 %copy-start.2 = (f32[2,736,256]{2,1,0:T(8,128)S(1)}, f32[2,736,256]{2,1,0:T(8,128)}, u32[]{:S(2)}) copy-start(f32[2,736,256]{2,1,0:T(8,128)} %get-tuple-element.154) | copy-start | bytes 4521988
  505.4 2.7 copy-start.1
  506.1 1.2 copy-start.3

commit v6 on v5

--- a/solution.py
+++ b/solution.py
@@ -170,7 +170,7 @@
 VM = pl.BlockSpec(memory_space=pltpu.VMEM)
 SM = pl.BlockSpec(memory_space=pltpu.SMEM)
 TILE = 128
-VMEM_LIMIT = 60 * 1024 * 1024
+VMEM_LIMIT = 62 * 1024 * 1024
 
 
 def peers_of(count):
@@ -613,13 +613,13 @@
     ]
     for copy in copies:
         copy.start()
-    scatter.pass_on()
     if carried:
         for v in range(1, 3):
             dec_gather.arrive(v - 1)
             crossings[v - 1].start()
             stores[v].start()
             gives[v].start()
+    scatter.pass_on()
 
     @pl.loop(0, groups)
     def _(group):
@@ -629,6 +629,11 @@
     last = pltpu.make_async_copy(at, at_out, local_sem.at[6])
     last.start()
     copies.append(last)
+    if carried:
+        dec_gather.arrive(2)
+        crossings[2].start()
+        stores[3].start()
+        gives[3].start()
 
     @pl.loop(0, 2 * groups)
     def _(step):
@@ -638,10 +643,6 @@
 
     y_ref[...] += scatter.total()
     if carried:
-        dec_gather.arrive(2)
-        crossings[2].start()
-        stores[3].start()
-        gives[3].start()
         for v in range(1, wide):
             crossings[v - 1].wait()
             stores[wide + v - 1].start()
@@ -772,6 +773,13 @@
     @pl.loop(0, groups)
     def _(group):
         before_group(gather, group, groups)
+        if carried:
+
+            @pl.when(group == 1)
+            def _():
+                line.loaded()
+                line.turn(0)
+
         token_rows = pl.ds(pl.multiple_of(group * count, count), count)
 
         @pl.loop(0, 2)
@@ -792,13 +800,8 @@
 
         put_parts(acc, parts, gx_ref, group, groups, rows)
         after_group(scatter, group, groups)
-        if carried:
-
-            @pl.when(group == 1)
-            def _():
-                line.loaded()
-                line.turn(0)
-
+    if carried:
+        line.turn(1)
     loads[2].wait()
     loads[3].wait()
     chunk = 2 * TILE
@@ -824,8 +827,6 @@
         @pl.when(step == rows_axis - 1)
         def _():
             swap_in.start()
-            if carried:
-                line.turn(1)
             scatter.pass_on()
 
         @pl.when(step == rows_axis)
@@ -841,6 +842,8 @@
                 ).astype(jnp.bfloat16)
 
     store_in.start()
+    if carried:
+        line.turn(2)
 
     @pl.loop(0, 2)
     def _(step):
@@ -863,8 +866,6 @@
                 ).astype(jnp.bfloat16)
             store_out.start()
 
-    if carried:
-        line.turn(2)
     total = gx_ref[...] + scatter.total()
     grad_residual, grad_gain = norm_pull(x_ref[...], gain_ref[...], total)
     gx_ref[...] = g_ref[...].astype(jnp.float32) + grad_residual
@@ -926,7 +927,7 @@
     greet(peers)
     residual = x_ref[...]
     blocks[0] = (residual * rms_rows(residual) * gain_ref[...]).astype(low)
-    cots[0] = cot_ref[...]
+    cots[0] = cot_ref[core]
     gather = GatherPlane(blocks, sems, 0, peers, rows)
     cot_gather = GatherPlane(cots, sems, 4, peers, rows)
     gather.start()
@@ -1034,7 +1035,7 @@
     grad_residual, gain_out[...] = norm_pull(
         x_ref[...], gain_ref[...], gx_ref[...] + grad_scatter.total()
     )
-    gx_ref[...] = cot_ref[...].astype(jnp.float32) + grad_residual
+    gx_ref[...] = cot_ref[core].astype(jnp.float32) + grad_residual
     y_ref[...] = y_ref[...] + residual + scatter.total()
     store_in.wait()
     store_out.wait()
@@ -1144,7 +1145,7 @@
 
 
 def start_weights_kernel(
-    wide, rows, win_in, wout_in, cin_in, cout_in, ffn_in, ffn_out, gains, enc_line, dec_line,
+    wide, rows, win_in, wout_in, cin_in, cout_in, ffn_in, ffn_out, gains, biases, enc_hot, dec_hot,
     attn_ref, dec_half, enc_gains, dec_gains, enc_bias, dec_bias, *refs
 ):
     enc, dec = refs[:wide], refs[wide : 2 * wide]
@@ -1228,17 +1229,18 @@
     lines = 10 + 2 * wide
     gain_moves = [remote(gains, target, sems, lines, sibling) for target in (enc_gains, dec_gains)]
     line_moves = [
-        remote(enc_line, enc_row, sems, lines + 1, sibling),
-        remote(dec_line, dec_row, sems, lines + 1, sibling),
+        remote(row_ref, row_ref, sems, lines + 1, sibling) for row_ref in (enc_row, dec_row)
     ]
-    for own, (gain_ref, row_ref, line_ref) in enumerate(
-        ((enc_gains, enc_row, enc_line), (dec_gains, dec_row, dec_line))
+    for own, (gain_ref, row_ref, hot) in enumerate(
+        ((enc_gains, enc_row, enc_hot), (dec_gains, dec_row, dec_hot))
     ):
 
         @pl.when(core == own)
         def _():
             gain_ref[...] = gains[...]
-            row_ref[...] = line_ref[...]
+            row_ref[pl.ds(0, H), :] = jnp.dot(
+                biases[...], hot[...], precision=HIGHEST, preferred_element_type=jnp.float32
+            )
             gain_moves[own].start()
             line_moves[own].start()
 
@@ -1304,7 +1306,7 @@
         give.wait_send()
 
 
-def start_weights(wide, rows, attn_in, attn_out, cross_in, cross_out, ffn_in, ffn_out, gains, lines):
+def start_weights(wide, rows, attn_in, attn_out, cross_in, cross_out, ffn_in, ffn_out, gains, biases):
     depth = ffn_in.shape[1]
     low = jnp.bfloat16
     block = jax.ShapeDtypeStruct((rows, depth, 3 * TILE), low)
@@ -1320,7 +1322,7 @@
             jax.ShapeDtypeStruct((H, LD, LD), jnp.float32),
         ]
         + [block] * (2 * wide),
-        in_specs=[HBM] * 6 + [VM] * 3,
+        in_specs=[HBM] * 6 + [VM] * 4,
         out_specs=[HBM] * 2 + [VM] * 4 + [HBM] * (2 * wide),
         scratch_shapes=[
             pltpu.VMEM(part, low),
@@ -1329,8 +1331,8 @@
             pltpu.VMEM(ffn_in.shape[1:], low),
             pltpu.VMEM((depth, FF), low),
             pltpu.VMEM((2, wide) + block.shape, low),
-            pltpu.VMEM(lines[0].shape, jnp.float32),
-            pltpu.VMEM(lines[1].shape, jnp.float32),
+            pltpu.VMEM((8, 2 * LE), jnp.float32),
+            pltpu.VMEM((8, 2 * LD), jnp.float32),
             pltpu.SemaphoreType.DMA((12 + 2 * wide,)),
             pltpu.SemaphoreType.DMA((12 + 2 * wide,)),
             pltpu.SemaphoreType.DMA((10 + wide,)),
@@ -1339,7 +1341,7 @@
             collective_id=1, has_side_effects=True, vmem_limit_bytes=VMEM_LIMIT
         ),
         name="start_weights",
-    )(attn_in, attn_out[0].T, cross_in, cross_out, ffn_in, ffn_out[0].T, gains, *lines)
+    )(attn_in, attn_out[0].T, cross_in, cross_out, ffn_in, ffn_out[0].T, gains, biases, distance_hot(LE, True, 0), distance_hot(LD, False, 0))
     return attn, dec_half, outs[:2], outs[2:4], outs[4 : 4 + wide], outs[4 + wide :]
 
 
@@ -1348,9 +1350,9 @@
 
 
 class ReduceWeights:
-    def __init__(self, batch, bufs, sems, base, local_sem, local_base, peers, others, held):
+    def __init__(self, batch, bufs, sems, base, peers, others):
         self.own, self.land, self.plane, self.send, self.zland = bufs
-        self.batch, self.held = batch, held
+        self.batch = batch
         core, place, row = lax.axis_index("section"), lax.axis_index("wide"), lax.axis_index("rows")
         wide, size = self.own.shape[:2]
         depth = batch.shape[0] // wide
@@ -1360,10 +1362,6 @@
             return pl.ds(pl.multiple_of(start, 16), size)
 
         self.mine = [rows_at(v, core) for v in range(wide)]
-        self.loads = [
-            pltpu.make_async_copy(batch.at[self.mine[v]], self.own.at[v], local_sem.at[local_base + v])
-            for v in range(0 if held else wide)
-        ]
         self.swaps = [
             remote(batch.at[rows_at(v, 1 - core)], self.land.at[v], sems, base + v, peers[-1])
             for v in range(wide)
@@ -1387,17 +1385,11 @@
     def start(self):
         for v in (3, 1, 2, 0):
             self.swaps[v].start()
-            if not self.held:
-                self.loads[v].start()
 
     def join(self):
         def add(v):
             self.swaps[v].wait_recv()
-            if self.held:
-                own = self.batch[self.mine[v], :]
-            else:
-                self.loads[v].wait()
-                own = self.own[v]
+            own = self.batch[self.mine[v], :]
             self.own[v] = (own.astype(jnp.float32) + self.land[v].astype(jnp.float32)).astype(
                 jnp.bfloat16
             )
@@ -1456,10 +1448,11 @@
 
 
 def last_kernel(wide, rows, *refs):
-    cross_ref, dec_in, dec_out, enc_in, enc_out, y_ref, dec_attn, enc_attn = refs[:8]
-    dec_self, enc_self, gains = refs[8:15], refs[15:22], refs[22:26]
-    out_ref, ffn_ref, small_out, y_half, x_half, t_half = refs[26:32]
-    refs = refs[32:]
+    cross, refs = refs[:6], refs[6:]
+    dec_in, dec_out, enc_in, enc_out, y_ref, dec_attn, enc_attn = refs[:7]
+    dec_self, enc_self, gains = refs[7:14], refs[14:21], refs[21:25]
+    out_ref, ffn_ref, small_out, y_half, x_half, t_half = refs[25:31]
+    refs = refs[31:]
     batch_bufs = [refs[i * 5 : i * 5 + 5] for i in range(3)]
     line_bufs, refs = refs[15:19], refs[19:]
     held, win, wout, gx, gt, context_e, projected_e, context_d, projected_d = refs[:9]
@@ -1471,7 +1464,7 @@
     crossed = [{"section": 1 - core, "wide": place ^ v} for v in range(1, wide)]
     others = [{"rows": row ^ k} for k in range(1, rows)]
     sems = (send_sem, recv_sem)
-    depth = cross_ref.shape[0] // wide
+    depth = held.shape[0] // wide
     units = dec_out.shape[0]
     low = jnp.bfloat16
     straight = (
@@ -1490,10 +1483,8 @@
     greet(peers + crossed + others)
     per_batch = wide + 6 + rows - 1
     batches = [
-        ReduceWeights(
-            batch, bufs, sems, i * per_batch, local_sem, 2, peers, others, i > 0
-        )
-        for i, (batch, bufs) in enumerate(zip((cross_ref, held, held), batch_bufs))
+        ReduceWeights(held, bufs, sems, i * per_batch, peers, others)
+        for i, bufs in enumerate(batch_bufs)
     ]
     base = 3 * per_batch
     line = ReduceRows(enc_in, enc_out, *line_bufs, sems, base, local_sem, 2 + wide)
@@ -1578,15 +1569,13 @@
             half_copies.append(copy)
 
     line.start()
+    cross_weights(*cross, held)
     batches[0].start()
     by_half(0, y_ref[...], y_half)
     small[...] = jnp.zeros_like(small)
     for i, gain in enumerate(gains):
         small[i // 2, pl.ds(1 + i % 2, 1), pl.ds(0, D)] = gain[...]
     batches[0].join()
-    for piece in range(2):
-        hand_out(1, piece, dec_in[piece])
-    hand_out(1, 2, tn(dec_out[...], straight).astype(low))
     g_ref, x_ref, gain_ref, normed_ref, projected_ref, context_ref, weights_ref = dec_self
     for load in attn_loads(dec_attn):
         load.wait()
@@ -1595,11 +1584,15 @@
     )
     for load in attn_loads(enc_attn):
         load.start()
+    batches[0].given()
     self_backward_weights(g_ref, normed_ref, context_ref, projected_d, held)
     batches[1].start()
     line.loaded()
     line.turn(0)
     batches[0].pass_on()
+    for piece in range(2):
+        hand_out(1, piece, dec_in[piece])
+    hand_out(1, 2, tn(dec_out[...], straight).astype(low))
     by_half(2, gt[...], t_half)
     g_ref, x_ref, gain_ref, normed_ref, projected_ref, context_ref, weights_ref = enc_self
     for load in attn_loads(enc_attn):
@@ -1626,20 +1619,21 @@
     small[core] = small[core] + jnp.sum(small_plane[...], axis=0)
     for copy in spread_small:
         copy.start()
+    line.turn(2)
+    batches[0].relay()
+    batches[1].spread()
+    batches[2].pass_on()
+    batches[1].relay()
+    batches[2].spread()
     line.close(0)
     hand_out(0, 0, line_bufs[0][0, 0])
-    batches[0].relay()
-    line.turn(2)
-    batches[1].spread()
-    batches[2].pass_on()
     line.close(1)
     hand_out(0, 1, line_bufs[0][0, 1])
-    batches[1].relay()
-    batches[2].spread()
+    batches[2].relay()
     line.close(2)
     hand_out(0, 2, tn(line_bufs[2][0], straight).astype(low))
-    batches[2].relay()
-    span, part = keep.shape[1] - cross_ref.shape[1] // rows // 2, cross_ref.shape[1] // rows // 2
+    part = held.shape[1] // rows // 2
+    span = keep.shape[1] - part
     crosses = batches[0].total()
     selfs = [batches[2].total(), batches[1].total()]
     for own in range(2):
@@ -1669,7 +1663,6 @@
     store_ffn.wait()
     for copy in half_copies:
         copy.wait()
-    batches[0].given()
     batches[2].given()
     for batch in batches:
         batch.finish()
@@ -1681,7 +1674,7 @@
     depth = D // wide
     size = split_at(depth)
     units = dec_sums[1].shape[0]
-    columns = cross.shape[1]
+    columns = 4 * HD
     enc_rows, dec_rows = enc_self[0].shape[0], dec_self[0].shape[0]
     wanted = (columns + columns // 2) // rows
     copies = 3 * (wide + 6 + rows - 1) + 9 + wide + rows - 1 + 6 * wide + 4
@@ -1701,7 +1694,7 @@
             jax.ShapeDtypeStruct(small, jnp.float32),
         ]
         + [jax.ShapeDtypeStruct((2, *each), kind) for each, kind in half_shapes],
-        in_specs=[HBM, VM, VM, HBM, HBM, VM, HBM, HBM] + [VM] * 18,
+        in_specs=[VM] * 6 + [VM, VM, HBM, HBM, VM, HBM, HBM] + [VM] * 18,
         out_specs=[HBM, HBM, VM, HBM, HBM, HBM],
         scratch_shapes=batch_scratch * 3
         + reduce_rows_scratch(units)
@@ -1735,7 +1728,7 @@
             collective_id=7, has_side_effects=True, vmem_limit_bytes=VMEM_LIMIT
         ),
         name="last_step",
-    )(cross, *dec_sums, *enc_shares, y3, dec_attn, enc_attn, *dec_self, *enc_self, *gains)
+    )(*cross, *dec_sums, *enc_shares, y3, dec_attn, enc_attn, *dec_self, *enc_self, *gains)
 
 
 def assemble_kernel(
@@ -2130,7 +2123,7 @@
 
 def cross_backward_kernel(
     g_ref, x_ref, final_ref, wkey_ref, wvalue_ref, y_ref, gain_ref, wquery_ref, wout_ref, kv_ref, query_ref, weights_ref,
-    memory_ref, normed_ref, context_ref, gx_ref, gy_ref, final_out, gain_out, grad_ref, kv_grad, query_grad, context_grad,
+    gx_ref, gy_ref, final_out, gain_out, kv_grad, query_grad, context_grad,
 ):
     low = jnp.bfloat16
     grad_low = g_ref[...].astype(low)
@@ -2157,7 +2150,11 @@
         y_ref[...], gain_ref[pl.ds(1, 1), :], nt(query_grad[...], wquery_ref[...])
     )
     gy_ref[...] = g_ref[...] + grad_residual
-    lefts = jnp.concatenate([memory_ref[...], normed_ref[...], grad_low], axis=0)
+
+
+def cross_weights(g_ref, kv_grad, query_grad, memory_ref, normed_ref, context_ref, grad_ref):
+    low = jnp.bfloat16
+    lefts = jnp.concatenate([memory_ref[...], normed_ref[...], g_ref[...].astype(low)], axis=0)
     chunks = grad_ref.shape[1] // HD
     part = HD // chunks
     for chunk in range(chunks):
@@ -2175,7 +2172,7 @@
 
 
 def cross_backward(g2, x2, enc_gains, enc_weight, y1, dec_gains, dec_weight, kept):
-    memory, kv, normed, query, context, weights = kept
+    _, kv, _, query, _, weights = kept
     low = jnp.bfloat16
     return pl.pallas_call(
         cross_backward_kernel,
@@ -2184,15 +2181,12 @@
             jax.ShapeDtypeStruct((LD, D), jnp.float32),
             jax.ShapeDtypeStruct((1, D), jnp.float32),
             jax.ShapeDtypeStruct((1, D), jnp.float32),
-            jax.ShapeDtypeStruct((D, 4 * HD), low),
+            jax.ShapeDtypeStruct((LE, 2 * HD), low),
+            jax.ShapeDtypeStruct((LD, HD), low),
         ],
-        in_specs=[VM, VM, VM, C_IN, C_OUT, VM, VM, C_IN, C_OUT] + [VM] * 6,
-        out_specs=[VM] * 5,
-        scratch_shapes=[
-            pltpu.VMEM((LE, 2 * HD), low),
-            pltpu.VMEM((LD, HD), low),
-            pltpu.VMEM((LD, HD), low),
-        ],
+        in_specs=[VM, VM, VM, C_IN, C_OUT, VM, VM, C_IN, C_OUT] + [VM] * 3,
+        out_specs=[VM] * 6,
+        scratch_shapes=[pltpu.VMEM((LD, HD), low)],
         grid=(1,),
         compiler_params=pltpu.CompilerParams(vmem_limit_bytes=VMEM_LIMIT),
         name="cross_backward",
@@ -2209,9 +2203,6 @@
         kv,
         query,
         weights,
-        memory,
-        normed,
-        context,
     )
 
 
@@ -2542,17 +2533,8 @@
     cross_out,
 ):
     wide, rows = lax.axis_size("wide"), lax.axis_size("rows")
-    lines = [
-        jnp.pad(
-            lax.dot_general(
-                rel_bias[0], distance_hot(length, both, 0), (((0,), (0,)), ((), ())), precision=HIGHEST
-            ),
-            ((0, 2), (0, 0)),
-        )
-        for length, both in ((LE, True), (LD, False))
-    ]
     enc_attn, dec_half, gains, biases, enc_blocks, dec_blocks = start_weights(
-        wide, rows, attn_in, attn_out, cross_in, cross_out, ffn_in, ffn_out, norm_gains[0], lines
+        wide, rows, attn_in, attn_out, cross_in, cross_out, ffn_in, ffn_out, norm_gains[0], rel_bias[0].T
     )
     enc_lengths, dec_lengths = enc_lengths[:, 0], dec_lengths[:, 0]
     x1, enc_self, moved = self_forward(
@@ -2576,11 +2558,10 @@
     y2, cross_kept = cross_forward(
         x2, gains[0], enc_attn, y1, gains[1], dec_attn, dec_lengths, enc_lengths
     )
-    cot_row = lax.dynamic_index_in_dim(out_cot[:, 0], lax.axis_index("section"), 0, keepdims=False)
     y3, g2, dec_ffn_gain, *dec_ffn_grads = ffn_both_call(
-        wide, rows, y2, cot_row, (gains[1], 2), dec_pieces, 3
-    )
-    grad_x2, g1, enc_final_gain, dec_cross_gain, cross_grads = cross_backward(
+        wide, rows, y2, out_cot[:, 0], (gains[1], 2), dec_pieces, 3
+    )
+    grad_x2, g1, enc_final_gain, dec_cross_gain, kv_grad, query_grad = cross_backward(
         g2, x2, gains[0], enc_attn, y1, gains[1], dec_attn, cross_kept
     )
     grad_x1, enc_ffn_gain, enc_in, enc_out, *dec_sums = ffn_backward_call(
@@ -2589,7 +2570,7 @@
     attn_parts, ffn_parts, small_own, dec_out, enc_grad, dec_grad = last_step(
         wide,
         rows,
-        cross_grads,
+        (g2, kv_grad, query_grad, cross_kept[0], cross_kept[2], cross_kept[4]),
         dec_sums,
         (enc_in, enc_out),
         y3,

time: 516 us -> 495 us (0.959)
  Pallas kernels: 500 us -> 483 us
    pallas_call x1, Pallas kernels: 92.4 us -> 83.8 us  [ffn_forward_call(): pl.pallas_call(lambda *refs: ffn_forward_kernel(wide, bool(carried), len(...]
where the time goes in v6:
time: 495 us; the launch traced here: 489 us
  Pallas kernels  483 us (98%)
  local copies, waits for them, and re-layouts  5.28 us (1%)
    pallas_call x1, Pallas kernels, last_step(): pl.pallas_call(lambda *refs: last_kernel(wide, rows, *refs), out_shape=[j...  133 us
    pallas_call x1, Pallas kernels, ffn_backward_call(): pl.pallas_call(lambda *refs: ffn_backward_kernel(wide, rows_axis, gain_at...  94.3 us
    pallas_call x1, Pallas kernels, ffn_forward_call(): pl.pallas_call(lambda *refs: ffn_forward_kernel(wide, bool(carried), len(...  83.8 us
    pallas_call x2, Pallas kernels, self_forward(): pl.pallas_call(lambda *refs: self_forward_kernel(wide, causal, *refs), ou...  66.4 us
    pallas_call x1, Pallas kernels, start_weights(): pl.pallas_call(lambda *refs: start_weights_kernel(wide, rows, *refs), out...  41.9 us
    pallas_call x1, Pallas kernels, ffn_both_call(): pl.pallas_call(lambda *refs: ffn_both_kernel(wide, rows_axis, gain_at, *r...  41.3 us

profile of v6, /device:TPU:0, one launch (start us, length us, event | category | flops | bytes accessed | tf_op | source)
XLA Modules:
  0.0 489.0 jit_solution(10375545465262658369)
XLA Ops:
  0.6 1.3 copy.36
  1.9 1.3 copy.35
  3.3 41.9 %start_weights.1 = (bf16[2,1472,1152]{2,1,0:T(8,128)(2,1)}, bf16[368,1152]{1,0:T(8,128)(2,1)}, f32[3,1472]{1,0:T(4,128)}, f32[3,1472]{1,0:T(4,128)}, f32[6,256,2...) custom-call(bf16[1,368,1152]{2,1,0:T(8,128)(2,1)} %refs_0_.1, ...), custom_call_target="tpu_custom_call" | custom-call | tf_op jit(solution)/shard_map/start_weights/pallas_call | solution.py:1314
  45.1 60.6 %self_forward_256.1 = (f32[256,1472]{1,0:T(8,128)}, bf16[256,1472]{1,0:T(8,128)(2,1)}, bf16[256,1472]{1,0:T(8,128)(2,1)}, bf16[256,1152]{1,0:T(8,128)(2,1)}, bf1...) custom-call(bf16[2,1472,256]{2,1,0:T(8,128)(2,1)} %bitcast.39, ...), custom_call_target="tpu_custom_call" | custom-call | tf_op jit(solution)/shard_map/self_forward_256/pallas_call | solution.py:1976
  105.8 83.8 %ffn_forward_256.1 = (f32[256,1472]{1,0:T(8,128)}, bf16[1472,1024]{1,0:T(8,128)(2,1)}, bf16[2,1024,1024]{2,1,0:T(8,128)(2,1)}, bf16[2,512,1024]{2,1,0:T(8,128)(2...) custom-call(f32[256,1472]{1,0:T(8,128)} %get-tuple-element.99.refs_0, ...), custom_call_target="tpu_custom_call" | custom-call | tf_op jit(solution)/shard_map/ffn_forward_256/pallas_call | solution.py:683
  189.5 5.8 %self_forward_64.1 = (f32[64,1472]{1,0:T(8,128)}, bf16[64,1472]{1,0:T(8,128)(2,1)}, bf16[64,1472]{1,0:T(8,128)(2,1)}, bf16[64,1152]{1,0:T(8,128)(2,1)}, bf16[64,384]{1,0:T(8,128)(2,1)}, /*index=5*/f32[6,64,64]{2,1,0:T(8,128)}) custom-call(bf16[2,64,1472]{2,1,0:T(8,128)(2,1)} %bitcast.42, f32[3,1472]{1,0:T(4,128)} %get-tuple-element.109.refs_1_.gain_ref.refs_2_.refs_15_, ...), custom_call_target="tpu_custom_call" | custom-call | tf_op jit(solution)/shard_map/self_forward_64/pallas_call | solution.py:1976
  195.3 6.8 %cross_forward.1 = (f32[64,1472]{1,0:T(8,128)}, bf16[256,1472]{1,0:T(8,128)(2,1)}, bf16[256,768]{1,0:T(8,128)(2,1)}, bf16[64,1472]{1,0:T(8,128)(2,1)}, bf16[64,3...) custom-call(f32[256,1472]{1,0:T(8,128)} %get-tuple-element.108.x_ref, ...), custom_call_target="tpu_custom_call" | custom-call | tf_op jit(solution)/shard_map/cross_forward/pallas_call | solution.py:2093
  202.2 41.3 %ffn_both_64.1 = (f32[64,1472]{1,0:T(8,128)}, f32[64,1472]{1,0:T(8,128)}, f32[1,1472]{1,0:T(1,128)}, bf16[4,2,1472,128]{3,2,1,0:T(8,128)(2,1)}, bf16[4,112,1472]{2,1,0:T(8,128)(2,1)}) custom-call(f32[64,1472]{1,0:T(8,128)} %get-tuple-element.113.refs_0_, bf16[2,64,1472]{2,1,0:T(8,128)(2,1)} %bitcast.43, ...), custom_call_target="tpu_custom_call" | custom-call | tf_op jit(solution)/shard_map/ffn_both_64/pallas_call | solution.py:1060
  243.5 8.4 %cross_backward.1 = (f32[256,1472]{1,0:T(8,128)}, f32[64,1472]{1,0:T(8,128)}, f32[1,1472]{1,0:T(1,128)}, f32[1,1472]{1,0:T(1,128)}, bf16[256,768]{1,0:T(8,128)(2,1)}, /*index=5*/bf16[64,384]{1,0:T(8,128)(2,1)}) custom-call(f32[64,1472]{1,0:T(8,128)} %get-tuple-element.118.g_ref.refs_0_, f32[256,1472]{1,0:T(8,128)} %get-tuple-element.108.x_ref, ...), custom_call_target="tpu_custom_call" | custom-call | tf_op jit(solution)/shard_map/cross_backward/pallas_call | solution.py:2177
  251.9 94.3 %ffn_backward_256.1 = (f32[256,1472]{1,0:T(8,128)}, f32[1,1472]{1,0:T(1,128)}, bf16[4,2,1472,128]{3,2,1,0:T(8,128)(2,1)}, bf16[4,112,1472]{2,1,0:T(8,128)(2,1)},...) custom-call(f32[256,1472]{1,0:T(8,128)} %get-tuple-element.127.refs_0_, ...), custom_call_target="tpu_custom_call" | custom-call | tf_op jit(solution)/shard_map/ffn_backward_256/pallas_call | solution.py:1111
  346.2 133.2 %last_step.1 = (f32[2,192,576]{2,1,0:T(8,128)}, bf16[2,4,3,368,128]{4,3,2,1,0:T(8,128)(2,1)}, f32[16,1536]{1,0:T(8,128)}, bf16[2,64,736]{2,1,0:T(8,128)(2,1)}, f...) custom-call(f32[64,1472]{1,0:T(8,128)} %get-tuple-element.118.g_ref.refs_0_, bf16[256,768]{1,0:T(8,128)(2,1)} %get-tuple-element.122.refs_1_, ...), custom_call_target="tpu_custom_call" | custom-call | tf_op jit(solution)/shard_map/last_step/pallas_call | solution.py:1689
  479.4 0.0 copy-start.2
  479.4 0.0 copy-start
  479.4 6.7 %assemble.1 = (f32[1,368,1792]{2,1,0:T(8,128)}, f32[1,368,896]{2,1,0:T(8,128)}, f32[3,1,1472]{2,1,0:T(1,128)}, f32[6,1,32]{2,1,0:T(1,128)}, f32[1,288,368]{2,1,0...) custom-call(bf16[2,4,3,368,128]{4,3,2,1,0:T(8,128)(2,1)} %get-tuple-element.158.refs_0_, ...), custom_call_target="tpu_custom_call" | custom-call | tf_op jit(solution)/shard_map/assemble/pallas_call | solution.py:1796
  486.1 0.0 copy-done.2
  486.1 0.7 copy.40
  486.8 0.0 copy-done
  486.8 0.0 copy-start.1
  486.8 1.1 copy.41
  487.9 0.1 copy-done.1
  488.0 0.7 copy.42
Async XLA Ops:
  479.4 6.7 %copy-start.2 = (bf16[2,64,736]{2,1,0:T(8,128)(2,1)S(1)}, bf16[2,64,736]{2,1,0:T(8,128)(2,1)}, u32[]{:S(2)}) copy-start(bf16[2,64,736]{2,1,0:T(8,128)(2,1)} %get-tuple-element.155) | copy-start | bytes 565252
  479.4 7.4 %copy-start = (f32[2,736,256]{2,1,0:T(8,128)S(1)}, f32[2,736,256]{2,1,0:T(8,128)}, u32[]{:S(2)}) copy-start(f32[2,736,256]{2,1,0:T(8,128)} %get-tuple-element.156) | copy-start | bytes 4521988
  486.8 1.2 copy-start.1

commit v7 on v6

--- a/solution.py
+++ b/solution.py
@@ -714,18 +714,34 @@
 
 
 def ffn_backward_kernel(
-    wide, rows_axis, gain_at, g_ref, x_ref, gain_ref, at_in, pre_in, hidden_in, weight_in, *refs
+    wide, rows_axis, gain_at, x_ref, gains_ref, at_in, pre_in, hidden_in, weight_in, *refs
 ):
-    gain_ref = gain_ref.at[pl.ds(gain_at, 1)]
-    carried = len(refs) > 21
-    if carried:
-        ready_in, ready_out = refs[:2]
-        refs = refs[2:]
-    gx_ref, gain_out, grad_in, grad_out = refs[:4]
-    refs = refs[4:]
-    if carried:
-        sum_in, sum_out = refs[:2]
-        refs = refs[2:]
+    gain_ref = gains_ref.at[pl.ds(gain_at, 1)]
+    (
+        ready_in,
+        ready_out,
+        enc_attn,
+        dec_attn,
+        dec_gains,
+        g2_ref,
+        x2_ref,
+        y1_ref,
+        kv_ref,
+        query_ref,
+        weights_ref,
+        gx_ref,
+        gain_out,
+        grad_in,
+        grad_out,
+        sum_in,
+        sum_out,
+        gy_ref,
+        final_out,
+        cross_gain,
+        kv_grad,
+        query_grad,
+    ) = refs[:22]
+    refs = refs[22:]
     (
         blocks,
         at,
@@ -749,21 +765,60 @@
     core, row = lax.axis_index("section"), lax.axis_index("rows")
     peers = peers_of(wide)
     sems = (send_sem, recv_sem)
-    greet(peers + ([{"rows": row ^ 1}, {"rows": row ^ 2}] if carried else []))
+    greet(peers + [{"rows": row ^ 1}, {"rows": row ^ 2}])
     loads = [
         pltpu.make_async_copy(weight_in, weight, local_sem.at[0]),
         pltpu.make_async_copy(pre_in, pre, local_sem.at[1]),
         pltpu.make_async_copy(hidden_in, hidden, local_sem.at[2]),
         pltpu.make_async_copy(at_in, at, local_sem.at[3]),
     ]
+    line = ReduceRows(ready_in, ready_out, *refs[15:19], sems, 12, local_sem, 6)
+    line.start()
+    g_ref, context_grad = refs[19:21]
+    fetches = [
+        pltpu.make_async_copy(
+            dec_attn.at[1, :, pl.ds(HD, 2 * HD)], at.at[:, pl.ds(0, 2 * HD)], local_sem.at[10]
+        )
+    ]
+    for tile in range(2 * HD // TILE):
+        fetches.append(
+            pltpu.make_async_copy(
+                enc_attn.at[1, :, pl.ds(HD + tile * TILE, TILE)],
+                give_in.at[tile // 2, tile % 2],
+                local_sem.at[11 + tile],
+            )
+        )
+    for fetch in fetches:
+        fetch.start()
+    for load in loads[:3]:
+        load.start()
+    for fetch in fetches:
+        fetch.wait()
+    cross_backward_rows(
+        g2_ref,
+        x2_ref,
+        gains_ref,
+        Tiles(give_in, 0),
+        Tiles(give_in, HD // TILE),
+        y1_ref,
+        dec_gains,
+        at.at[:, pl.ds(0, HD)],
+        at.at[:, pl.ds(HD, HD)],
+        kv_ref,
+        query_ref,
+        weights_ref,
+        g_ref,
+        gy_ref,
+        final_out,
+        cross_gain,
+        kv_grad,
+        query_grad,
+        context_grad,
+    )
     blocks[0] = g_ref[...].astype(jnp.bfloat16)
     gather = GatherPlane(blocks, sems, 0, peers, rows)
     gather.start()
-    for load in loads:
-        load.start()
-    if carried:
-        line = ReduceRows(ready_in, ready_out, *refs[15:19], sems, 12, local_sem, 6)
-        line.start()
+    loads[3].start()
     scatter = ScatterPlane(parts, landing, sems, 4, peers, rows)
     loads[0].wait()
     loads[1].wait()
@@ -772,14 +827,16 @@
 
     @pl.loop(0, groups)
     def _(group):
+        @pl.when(group == 1)
+        def _():
+            line.loaded()
+            line.turn(0)
+
+        @pl.when(group == 3)
+        def _():
+            line.turn(1)
+
         before_group(gather, group, groups)
-        if carried:
-
-            @pl.when(group == 1)
-            def _():
-                line.loaded()
-                line.turn(0)
-
         token_rows = pl.ds(pl.multiple_of(group * count, count), count)
 
         @pl.loop(0, 2)
@@ -800,8 +857,6 @@
 
         put_parts(acc, parts, gx_ref, group, groups, rows)
         after_group(scatter, group, groups)
-    if carried:
-        line.turn(1)
     loads[2].wait()
     loads[3].wait()
     chunk = 2 * TILE
@@ -842,8 +897,7 @@
                 ).astype(jnp.bfloat16)
 
     store_in.start()
-    if carried:
-        line.turn(2)
+    line.turn(2)
 
     @pl.loop(0, 2)
     def _(step):
@@ -870,19 +924,17 @@
     grad_residual, grad_gain = norm_pull(x_ref[...], gain_ref[...], total)
     gx_ref[...] = g_ref[...].astype(jnp.float32) + grad_residual
     gain_out[...] = grad_gain
-    if carried:
-        for index in range(3):
-            line.close(index)
-        in_buf, out_buf = refs[15], refs[17]
-        stores = [
-            pltpu.make_async_copy(in_buf.at[0], sum_in, local_sem.at[6]),
-            pltpu.make_async_copy(out_buf.at[0], sum_out, local_sem.at[7]),
-        ]
-        for store in stores:
-            store.start()
-        for store in stores:
-            store.wait()
-        line.finish()
+    for index in range(3):
+        line.close(index)
+    stores = [
+        pltpu.make_async_copy(refs[15].at[0], sum_in, local_sem.at[6]),
+        pltpu.make_async_copy(refs[17].at[0], sum_out, local_sem.at[7]),
+    ]
+    for store in stores:
+        store.start()
+    for store in stores:
+        store.wait()
+    line.finish()
     store_in.wait()
     store_out.wait()
     swap_in.wait_send()
@@ -1099,26 +1151,43 @@
 GELU_B = 0.044715
 
 
-def ffn_backward_call(wide, rows_axis, grad, residual, gain_row, kept, call_id, carried=()):
+class Tiles:
+    def __init__(self, ref, first):
+        self.ref, self.first = ref, first
+
+    def __getitem__(self, _):
+        tiles = range(self.first, self.first + HD // TILE)
+        return jnp.concatenate([self.ref[tile // 2, tile % 2] for tile in tiles], axis=1)
+
+
+def ffn_backward_call(wide, rows_axis, residual, gain_row, kept, call_id, carried, crossed):
     gain_row, gain_at = gain_row
     at, pre, hidden, weight = kept
     rows = residual.shape[0]
+    target_rows = crossed[3].shape[0]
     low = jnp.bfloat16
     units = FF // (wide * rows_axis * 2)
     share_in = (rows_axis, 2, D, TILE)
     share_out = (rows_axis, units, D)
-    sums = [jax.ShapeDtypeStruct(each.shape[1:], low) for each in carried]
+    line_of = jax.ShapeDtypeStruct((1, D), jnp.float32)
     return pl.pallas_call(
         lambda *refs: ffn_backward_kernel(wide, rows_axis, gain_at, *refs),
         out_shape=[
             jax.ShapeDtypeStruct((rows, D), jnp.float32),
-            jax.ShapeDtypeStruct((1, D), jnp.float32),
+            line_of,
             jax.ShapeDtypeStruct(share_in, low),
             jax.ShapeDtypeStruct(share_out, low),
         ]
-        + sums,
-        in_specs=[VM, VM, VM, HBM, HBM, HBM, HBM] + [HBM] * len(sums),
-        out_specs=[VM, VM, HBM, HBM] + [HBM] * len(sums),
+        + [jax.ShapeDtypeStruct(each.shape[1:], low) for each in carried]
+        + [
+            jax.ShapeDtypeStruct((target_rows, D), jnp.float32),
+            line_of,
+            line_of,
+            jax.ShapeDtypeStruct((rows, 2 * HD), low),
+            jax.ShapeDtypeStruct((target_rows, HD), low),
+        ],
+        in_specs=[VM, VM] + [HBM] * 8 + [VM] * 7,
+        out_specs=[VM, VM, HBM, HBM, HBM, HBM] + [VM] * 5,
         scratch_shapes=[
             pltpu.VMEM((wide, rows, D), low),
             pltpu.VMEM(at.shape, low),
@@ -1134,14 +1203,15 @@
             pltpu.VMEM(share_out, low),
             pltpu.SemaphoreType.DMA((21,)),
             pltpu.SemaphoreType.DMA((21,)),
-            pltpu.SemaphoreType.DMA((10,)),
+            pltpu.SemaphoreType.DMA((17,)),
         ]
-        + (reduce_rows_scratch(units) if carried else []),
+        + reduce_rows_scratch(units)
+        + [pltpu.VMEM((rows, D), jnp.float32), pltpu.VMEM((target_rows, HD), low)],
         compiler_params=pltpu.CompilerParams(
             collective_id=call_id, has_side_effects=True, vmem_limit_bytes=VMEM_LIMIT
         ),
         name="ffn_backward_%d" % rows,
-    )(grad, residual, gain_row, at, pre, hidden, weight, *carried)
+    )(residual, gain_row, at, pre, hidden, weight, *carried, *crossed)
 
 
 def start_weights_kernel(
@@ -2121,7 +2191,7 @@
     return y2, kept
 
 
-def cross_backward_kernel(
+def cross_backward_rows(
     g_ref, x_ref, final_ref, wkey_ref, wvalue_ref, y_ref, gain_ref, wquery_ref, wout_ref, kv_ref, query_ref, weights_ref,
     gx_ref, gy_ref, final_out, gain_out, kv_grad, query_grad, context_grad,
 ):
@@ -2169,41 +2239,6 @@
             axis=0,
         ).astype(low)
         grad_ref[:, pl.ds(chunk * HD, HD)] = tn(lefts, right).astype(low)
-
-
-def cross_backward(g2, x2, enc_gains, enc_weight, y1, dec_gains, dec_weight, kept):
-    _, kv, _, query, _, weights = kept
-    low = jnp.bfloat16
-    return pl.pallas_call(
-        cross_backward_kernel,
-        out_shape=[
-            jax.ShapeDtypeStruct((LE, D), jnp.float32),
-            jax.ShapeDtypeStruct((LD, D), jnp.float32),
-            jax.ShapeDtypeStruct((1, D), jnp.float32),
-            jax.ShapeDtypeStruct((1, D), jnp.float32),
-            jax.ShapeDtypeStruct((LE, 2 * HD), low),
-            jax.ShapeDtypeStruct((LD, HD), low),
-        ],
-        in_specs=[VM, VM, VM, C_IN, C_OUT, VM, VM, C_IN, C_OUT] + [VM] * 3,
-        out_specs=[VM] * 6,
-        scratch_shapes=[pltpu.VMEM((LD, HD), low)],
-        grid=(1,),
-        compiler_params=pltpu.CompilerParams(vmem_limit_bytes=VMEM_LIMIT),
-        name="cross_backward",
-    )(
-        g2,
-        x2,
-        enc_gains,
-        enc_weight,
-        enc_weight,
-        y1,
-        dec_gains,
-        dec_weight,
-        dec_weight,
-        kv,
-        query,
-        weights,
-    )
 
 
 def plain_self_forward(residual, gain_row, weight, bias_full, allowed):
@@ -2561,11 +2596,26 @@
     y3, g2, dec_ffn_gain, *dec_ffn_grads = ffn_both_call(
         wide, rows, y2, out_cot[:, 0], (gains[1], 2), dec_pieces, 3
     )
-    grad_x2, g1, enc_final_gain, dec_cross_gain, kv_grad, query_grad = cross_backward(
-        g2, x2, gains[0], enc_attn, y1, gains[1], dec_attn, cross_kept
-    )
-    grad_x1, enc_ffn_gain, enc_in, enc_out, *dec_sums = ffn_backward_call(
-        wide, rows, grad_x2, x1, (gains[0], 1), enc_ffn, 5, dec_ffn_grads
+    (
+        grad_x1,
+        enc_ffn_gain,
+        enc_in,
+        enc_out,
+        *dec_sums,
+        g1,
+        enc_final_gain,
+        dec_cross_gain,
+        kv_grad,
+        query_grad,
+    ) = ffn_backward_call(
+        wide,
+        rows,
+        x1,
+        (gains[0], 1),
+        enc_ffn,
+        5,
+        dec_ffn_grads,
+        (enc_attn, dec_attn, gains[1], g2, x2, y1, cross_kept[1], cross_kept[3], cross_kept[5]),
     )
     attn_parts, ffn_parts, small_own, dec_out, enc_grad, dec_grad = last_step(
         wide,

time: 495 us -> 479 us (0.968)
  Pallas kernels: 483 us -> 467 us
    pallas_call x1 -> x0, Pallas kernels: 8.4 us -> none  [cross_backward(): pl.pallas_call(cross_backward_kernel, out_shape=[jax.ShapeDtypeStruct((LE...]
    pallas_call x1, Pallas kernels: 133 us -> 125 us  [last_step(): pl.pallas_call(lambda *refs: last_kernel(wide, rows, *refs), out_shape=[j...]
where the time goes in v7:
time: 479 us; the launch traced here: 473 us
  Pallas kernels  467 us (97%)
  local copies, waits for them, and re-layouts  5.28 us (1%)
    pallas_call x1, Pallas kernels, last_step(): pl.pallas_call(lambda *refs: last_kernel(wide, rows, *refs), out_shape=[j...  125 us
    pallas_call x1, Pallas kernels, ffn_backward_call(): pl.pallas_call(lambda *refs: ffn_backward_kernel(wide, rows_axis, gain_at...  94.3 us
    pallas_call x1, Pallas kernels, ffn_forward_call(): pl.pallas_call(lambda *refs: ffn_forward_kernel(wide, bool(carried), len(...  83.8 us
    pallas_call x2, Pallas kernels, self_forward(): pl.pallas_call(lambda *refs: self_forward_kernel(wide, causal, *refs), ou...  66.4 us
    pallas_call x1, Pallas kernels, start_weights(): pl.pallas_call(lambda *refs: start_weights_kernel(wide, rows, *refs), out...  41.9 us
    pallas_call x1, Pallas kernels, ffn_both_call(): pl.pallas_call(lambda *refs: ffn_both_kernel(wide, rows_axis, gain_at, *r...  41.3 us

profile of v7, /device:TPU:0, one launch (start us, length us, event | category | flops | bytes accessed | tf_op | source)
XLA Modules:
  0.0 472.8 jit_solution(15921804206236392479)
XLA Ops:
  0.6 1.3 copy.36
  1.9 1.3 copy.35
  3.3 41.9 %start_weights.1 = (bf16[2,1472,1152]{2,1,0:T(8,128)(2,1)}, bf16[368,1152]{1,0:T(8,128)(2,1)}, f32[3,1472]{1,0:T(4,128)}, f32[3,1472]{1,0:T(4,128)}, f32[6,256,2...) custom-call(bf16[1,368,1152]{2,1,0:T(8,128)(2,1)} %refs_0_.1, ...), custom_call_target="tpu_custom_call" | custom-call | tf_op jit(solution)/shard_map/start_weights/pallas_call | solution.py:1384
  45.1 60.6 %self_forward_256.1 = (f32[256,1472]{1,0:T(8,128)}, bf16[256,1472]{1,0:T(8,128)(2,1)}, bf16[256,1472]{1,0:T(8,128)(2,1)}, bf16[256,1152]{1,0:T(8,128)(2,1)}, bf1...) custom-call(bf16[2,1472,256]{2,1,0:T(8,128)(2,1)} %bitcast.39, ...), custom_call_target="tpu_custom_call" | custom-call | tf_op jit(solution)/shard_map/self_forward_256/pallas_call | solution.py:2046
  105.8 83.8 %ffn_forward_256.1 = (f32[256,1472]{1,0:T(8,128)}, bf16[1472,1024]{1,0:T(8,128)(2,1)}, bf16[2,1024,1024]{2,1,0:T(8,128)(2,1)}, bf16[2,512,1024]{2,1,0:T(8,128)(2...) custom-call(f32[256,1472]{1,0:T(8,128)} %get-tuple-element.98.refs_0, ...), custom_call_target="tpu_custom_call" | custom-call | tf_op jit(solution)/shard_map/ffn_forward_256/pallas_call | solution.py:683
  189.6 5.8 %self_forward_64.1 = (f32[64,1472]{1,0:T(8,128)}, bf16[64,1472]{1,0:T(8,128)(2,1)}, bf16[64,1472]{1,0:T(8,128)(2,1)}, bf16[64,1152]{1,0:T(8,128)(2,1)}, bf16[64,384]{1,0:T(8,128)(2,1)}, /*index=5*/f32[6,64,64]{2,1,0:T(8,128)}) custom-call(bf16[2,64,1472]{2,1,0:T(8,128)(2,1)} %bitcast.42, ...), custom_call_target="tpu_custom_call" | custom-call | tf_op jit(solution)/shard_map/self_forward_64/pallas_call | solution.py:2046
  195.4 6.8 %cross_forward.1 = (f32[64,1472]{1,0:T(8,128)}, bf16[256,1472]{1,0:T(8,128)(2,1)}, bf16[256,768]{1,0:T(8,128)(2,1)}, bf16[64,1472]{1,0:T(8,128)(2,1)}, bf16[64,3...) custom-call(f32[256,1472]{1,0:T(8,128)} %get-tuple-element.107.x_ref.refs_12_, ...), custom_call_target="tpu_custom_call" | custom-call | tf_op jit(solution)/shard_map/cross_forward/pallas_call | solution.py:2163
  202.2 41.3 %ffn_both_64.1 = (f32[64,1472]{1,0:T(8,128)}, f32[64,1472]{1,0:T(8,128)}, f32[1,1472]{1,0:T(1,128)}, bf16[4,2,1472,128]{3,2,1,0:T(8,128)(2,1)}, bf16[4,112,1472]{2,1,0:T(8,128)(2,1)}) custom-call(f32[64,1472]{1,0:T(8,128)} %get-tuple-element.112.refs_0_, bf16[2,64,1472]{2,1,0:T(8,128)(2,1)} %bitcast.43, ...), custom_call_target="tpu_custom_call" | custom-call | tf_op jit(solution)/shard_map/ffn_both_64/pallas_call | solution.py:1112
  243.6 94.3 %ffn_backward_256.1 = (f32[256,1472]{1,0:T(8,128)}, f32[1,1472]{1,0:T(1,128)}, bf16[4,2,1472,128]{3,2,1,0:T(8,128)(2,1)}, bf16[4,112,1472]{2,1,0:T(8,128)(2,1)},...) custom-call(f32[256,1472]{1,0:T(8,128)} %get-tuple-element.98.refs_0, ...), custom_call_target="tpu_custom_call" | custom-call | tf_op jit(solution)/shard_map/ffn_backward_256/pallas_call | solution.py:1173
  337.9 125.3 %last_step.1 = (f32[2,192,576]{2,1,0:T(8,128)}, bf16[2,4,3,368,128]{4,3,2,1,0:T(8,128)(2,1)}, f32[16,1536]{1,0:T(8,128)}, bf16[2,64,736]{2,1,0:T(8,128)(2,1)}, f...) custom-call(f32[64,1472]{1,0:T(8,128)} %get-tuple-element.117.refs_11_.refs_0_, ...), custom_call_target="tpu_custom_call" | custom-call | tf_op jit(solution)/shard_map/last_step/pallas_call | solution.py:1759
  463.3 0.0 copy-start.2
  463.3 0.0 copy-start
  463.3 6.7 %assemble.1 = (f32[1,368,1792]{2,1,0:T(8,128)}, f32[1,368,896]{2,1,0:T(8,128)}, f32[3,1,1472]{2,1,0:T(1,128)}, f32[6,1,32]{2,1,0:T(1,128)}, f32[1,288,368]{2,1,0...) custom-call(bf16[2,4,3,368,128]{4,3,2,1,0:T(8,128)(2,1)} %get-tuple-element.156.refs_0_, ...), custom_call_target="tpu_custom_call" | custom-call | tf_op jit(solution)/shard_map/assemble/pallas_call | solution.py:1866
  469.9 0.0 copy-done.2
  469.9 0.7 copy.40
  470.6 0.0 copy-done
  470.6 0.0 copy-start.1
  470.6 1.1 copy.41
  471.8 0.1 copy-done.1
  471.9 0.7 copy.42
Async XLA Ops:
  463.3 6.7 %copy-start.2 = (bf16[2,64,736]{2,1,0:T(8,128)(2,1)S(1)}, bf16[2,64,736]{2,1,0:T(8,128)(2,1)}, u32[]{:S(2)}) copy-start(bf16[2,64,736]{2,1,0:T(8,128)(2,1)} %get-tuple-element.153) | copy-start | bytes 565252
  463.3 7.4 %copy-start = (f32[2,736,256]{2,1,0:T(8,128)S(1)}, f32[2,736,256]{2,1,0:T(8,128)}, u32[]{:S(2)}) copy-start(f32[2,736,256]{2,1,0:T(8,128)} %get-tuple-element.154) | copy-start | bytes 4521988
  470.6 1.2 copy-start.1

commit v8 on v7

--- a/solution.py
+++ b/solution.py
@@ -943,10 +943,14 @@
     scatter.finish()
 
 
-def ffn_both_kernel(wide, rows_axis, gain_at, x_ref, cot_ref, gain_ref, *refs):
+def decoder_kernel(wide, rows_axis, gain_at, cot_ref, gains_ref, *refs):
     pieces, refs = refs[: 2 * wide - 1], refs[2 * wide - 1 :]
-    gain_ref = gain_ref.at[pl.ds(gain_at, 1)]
-    y_ref, gx_ref, gain_out, grad_in, grad_out = refs[:5]
+    gain_ref = gains_ref.at[pl.ds(gain_at, 1)]
+    x2_ref, enc_gains, embed_ref, bias_ref, dec_lengths, enc_lengths, enc_attn, dec_attn = refs[:8]
+    y_ref, gx_ref, gain_out, grad_in, grad_out, y1_ref = refs[8:14]
+    self_kept, cross_kept, refs = refs[14:19], refs[19:25], refs[25:]
+    dec_in, dec_rest, enc_rest, x_ref = refs[:4]
+    refs = refs[4:]
     (
         blocks,
         cots,
@@ -966,7 +970,7 @@
         send_sem,
         recv_sem,
         local_sem,
-    ) = refs[5:]
+    ) = refs
     rows = x_ref.shape[0]
     total_rows = wide * rows
     span = weight.shape[1] * TILE
@@ -976,20 +980,49 @@
     sems = (send_sem, recv_sem)
     low = jnp.bfloat16
     loads, swaps = weight_copies(pieces, weight, sems, 20, local_sem, 2, peers[-1])
+    fetches = [
+        pltpu.make_async_copy(dec_attn.at[0], dec_in, local_sem.at[9]),
+        pltpu.make_async_copy(dec_attn.at[1], dec_rest, local_sem.at[10]),
+        pltpu.make_async_copy(
+            enc_attn.at[1, :, pl.ds(HD, 2 * HD)], enc_rest, local_sem.at[11]
+        ),
+    ]
+    for fetch in fetches:
+        fetch.start()
     greet(peers)
-    residual = x_ref[...]
-    blocks[0] = (residual * rms_rows(residual) * gain_ref[...]).astype(low)
     cots[0] = cot_ref[core]
     gather = GatherPlane(blocks, sems, 0, peers, rows)
     cot_gather = GatherPlane(cots, sems, 4, peers, rows)
-    gather.start()
     cot_gather.start()
+    for fetch in fetches:
+        fetch.wait()
     for load, swap in zip(loads, swaps):
         load.start()
         swap.start()
+    thirds = [pl.ds(i * HD, HD) for i in range(3)]
+    self_forward_rows(
+        True, embed_ref, gains_ref, dec_in, dec_rest.at[:, thirds[0]], bias_ref, dec_lengths, y1_ref, *self_kept
+    )
+    cross_forward_rows(
+        x2_ref,
+        enc_gains,
+        enc_rest.at[:, thirds[0]],
+        enc_rest.at[:, thirds[1]],
+        y1_ref,
+        gains_ref,
+        dec_rest.at[:, thirds[1]],
+        dec_rest.at[:, thirds[2]],
+        dec_lengths,
+        enc_lengths,
+        x_ref,
+        *cross_kept,
+    )
+    residual = x_ref[...]
+    blocks[0] = (residual * rms_rows(residual) * gain_ref[...]).astype(low)
+    gather.start()
     for index in range(3):
+        cot_gather.arrive(index)
         gather.arrive(index)
-        cot_gather.arrive(index)
     for load in loads:
         load.wait()
 
@@ -1099,9 +1132,11 @@
         swap.wait_send()
 
 
-def ffn_both_call(wide, rows_axis, residual, cot, gain_row, pieces, call_id):
+def decoder_call(
+    wide, rows_axis, cot, gain_row, pieces, x2, enc_gains, embed, bias, dec_lengths, enc_lengths, enc_attn, dec_attn, call_id
+):
     gain_row, gain_at = gain_row
-    rows = residual.shape[0]
+    rows, enc_rows = embed.shape[1], x2.shape[0]
     total = wide * rows
     quarters, _, columns = pieces[0].shape
     span = quarters * TILE
@@ -1109,18 +1144,35 @@
     units = FF // (wide * rows_axis * 2)
     share_in = (rows_axis, 2, D, TILE)
     share_out = (rows_axis, units, D)
-    return pl.pallas_call(
-        lambda *refs: ffn_both_kernel(wide, rows_axis, gain_at, *refs),
-        out_shape=[
-            jax.ShapeDtypeStruct((rows, D), jnp.float32),
-            jax.ShapeDtypeStruct((rows, D), jnp.float32),
-            jax.ShapeDtypeStruct((1, D), jnp.float32),
-            jax.ShapeDtypeStruct(share_in, low),
-            jax.ShapeDtypeStruct(share_out, low),
-        ],
-        in_specs=[VM, VM, VM] + [HBM] * len(pieces),
-        out_specs=[VM, VM, VM, HBM, HBM],
+    outs = [
+        ((rows, D), jnp.float32),
+        ((rows, D), jnp.float32),
+        ((1, D), jnp.float32),
+        (share_in, low),
+        (share_out, low),
+        ((rows, D), jnp.float32),
+        ((rows, D), low),
+        ((rows, D), low),
+        ((rows, 3 * HD), low),
+        ((rows, HD), low),
+        ((H, rows, rows), jnp.float32),
+        ((enc_rows, D), low),
+        ((enc_rows, 2 * HD), low),
+        ((rows, D), low),
+        ((rows, HD), low),
+        ((rows, HD), low),
+        ((H, rows, enc_rows), jnp.float32),
+    ]
+    y3, g2, gain, grad_in, grad_out, y1, *kept = pl.pallas_call(
+        lambda *refs: decoder_kernel(wide, rows_axis, gain_at, *refs),
+        out_shape=[jax.ShapeDtypeStruct(shape, kind) for shape, kind in outs],
+        in_specs=[VM, VM] + [HBM] * len(pieces) + [VM] * 4 + [SM, SM, HBM, HBM],
+        out_specs=[VM, VM, VM, HBM, HBM] + [VM] * 12,
         scratch_shapes=[
+            pltpu.VMEM((D, 3 * HD), low),
+            pltpu.VMEM((D, 3 * HD), low),
+            pltpu.VMEM((D, 2 * HD), low),
+            pltpu.VMEM((rows, D), jnp.float32),
             pltpu.VMEM((wide, rows, D), low),
             pltpu.VMEM((wide, rows, D), low),
             pltpu.VMEM((2, quarters, D, columns), low),
@@ -1138,13 +1190,14 @@
             pltpu.VMEM(share_out, low),
             pltpu.SemaphoreType.DMA((29,)),
             pltpu.SemaphoreType.DMA((29,)),
-            pltpu.SemaphoreType.DMA((9,)),
+            pltpu.SemaphoreType.DMA((12,)),
         ],
         compiler_params=pltpu.CompilerParams(
             collective_id=call_id, has_side_effects=True, vmem_limit_bytes=VMEM_LIMIT
         ),
-        name="ffn_both_%d" % rows,
-    )(residual, cot, gain_row, *pieces)
+        name="decoder",
+    )(cot, gain_row, *pieces, x2, enc_gains, embed, bias, dec_lengths, enc_lengths, enc_attn, dec_attn)
+    return y3, g2, gain, (grad_in, grad_out), y1, kept[:5], kept[5:]
 
 
 GELU_A = float(np.sqrt(2.0 / np.pi))
@@ -1297,7 +1350,7 @@
                 )
 
     lines = 10 + 2 * wide
-    gain_moves = [remote(gains, target, sems, lines, sibling) for target in (enc_gains, dec_gains)]
+    gain_moves = [remote(target, target, sems, lines, sibling) for target in (enc_gains, dec_gains)]
     line_moves = [
         remote(row_ref, row_ref, sems, lines + 1, sibling) for row_ref in (enc_row, dec_row)
     ]
@@ -1307,9 +1360,10 @@
 
         @pl.when(core == own)
         def _():
-            gain_ref[...] = gains[...]
+            for index in range(gains.shape[0]):
+                gain_ref[pl.ds(index, 1), :] = gains[index]
             row_ref[pl.ds(0, H), :] = jnp.dot(
-                biases[...], hot[...], precision=HIGHEST, preferred_element_type=jnp.float32
+                biases[:, 0, :], hot[...], precision=HIGHEST, preferred_element_type=jnp.float32
             )
             gain_moves[own].start()
             line_moves[own].start()
@@ -1386,8 +1440,8 @@
         out_shape=[
             jax.ShapeDtypeStruct((2, wide * depth, 3 * HD), low),
             jax.ShapeDtypeStruct(part, low),
-            jax.ShapeDtypeStruct(gains.shape, jnp.float32),
-            jax.ShapeDtypeStruct(gains.shape, jnp.float32),
+            jax.ShapeDtypeStruct((gains.shape[0], D), jnp.float32),
+            jax.ShapeDtypeStruct((gains.shape[0], D), jnp.float32),
             jax.ShapeDtypeStruct((H, LE, LE), jnp.float32),
             jax.ShapeDtypeStruct((H, LD, LD), jnp.float32),
         ]
@@ -1985,10 +2039,38 @@
     return lambda pair: ref[:, pair_tile(pair, base)]
 
 
+def self_forward_rows(
+    causal, x_ref, gain_ref, win_ref, wout_ref, bias_ref, lengths_ref, y_ref, low_ref, normed_ref, projected_ref, context_ref, weights_ref
+):
+    core = lax.axis_index("section")
+    low_ref[...] = x_ref[core] if causal else x_ref[core].T
+    residual = low_ref[...].astype(jnp.float32)
+    normed_ref[...] = (residual * rms_rows(residual) * gain_ref[pl.ds(0, 1), :]).astype(jnp.bfloat16)
+    projected_ref[...] = matmul(normed_ref[...], win_ref[...]).astype(jnp.bfloat16)
+    length = low_ref.shape[0]
+    allowed = item_numbers(lengths_ref, core, (length, length), 0) == item_numbers(
+        lengths_ref, core, (length, length), 1
+    )
+    if causal:
+        allowed = allowed & (
+            lax.broadcasted_iota(jnp.int32, (length, length), 0)
+            >= lax.broadcasted_iota(jnp.int32, (length, length), 1)
+        )
+    attend_heads(
+        tile_of(projected_ref, 0),
+        tile_of(projected_ref, HD),
+        tile_of(projected_ref, 2 * HD),
+        lambda head: bias_ref[head],
+        allowed,
+        context_ref,
+        weights_ref,
+    )
+    y_ref[...] = residual + nt(context_ref[...], wout_ref[...])
+
+
 def self_forward_kernel(
     wide, causal, x_ref, gain_ref, win_ref, wout_ref, bias_ref, lengths_ref, *refs
 ):
-    core = lax.axis_index("section")
     if wide:
         blocks, dec_blocks, refs = refs[: wide - 1], refs[wide - 1 : 2 * wide - 2], refs[2 * wide - 2 :]
     y_ref, low_ref, normed_ref, projected_ref, context_ref, weights_ref = refs[:6]
@@ -2004,29 +2086,9 @@
             remote(block.at[mine], piece, sems, 9 + v, peers[v])
             for v, (block, piece) in enumerate(zip(dec_blocks, dec_pieces))
         ]
-    low_ref[...] = x_ref[core] if causal else x_ref[core].T
-    residual = low_ref[...].astype(jnp.float32)
-    normed_ref[...] = (residual * rms_rows(residual) * gain_ref[pl.ds(0, 1), :]).astype(jnp.bfloat16)
-    projected_ref[...] = matmul(normed_ref[...], win_ref[...]).astype(jnp.bfloat16)
-    length = low_ref.shape[0]
-    allowed = item_numbers(lengths_ref, core, (length, length), 0) == item_numbers(
-        lengths_ref, core, (length, length), 1
-    )
-    if causal:
-        allowed = allowed & (
-            lax.broadcasted_iota(jnp.int32, (length, length), 0)
-            >= lax.broadcasted_iota(jnp.int32, (length, length), 1)
-        )
-    attend_heads(
-        tile_of(projected_ref, 0),
-        tile_of(projected_ref, HD),
-        tile_of(projected_ref, 2 * HD),
-        lambda head: bias_ref[head],
-        allowed,
-        context_ref,
-        weights_ref,
-    )
-    y_ref[...] = residual + nt(context_ref[...], wout_ref[...])
+    self_forward_rows(
+        causal, x_ref, gain_ref, win_ref, wout_ref, bias_ref, lengths_ref, y_ref, low_ref, normed_ref, projected_ref, context_ref, weights_ref
+    )
     if wide:
         for copy in later:
             copy.start()
@@ -2133,7 +2195,7 @@
         grad_ref[:, pl.ds(chunk * HD, HD)] = tn(both, right).astype(low)
 
 
-def cross_forward_kernel(
+def cross_forward_rows(
     x_ref, final_ref, wkey_ref, wvalue_ref, y_ref, gain_ref, wquery_ref, wout_ref, dec_lengths, enc_lengths,
     out_ref, memory_ref, kv_ref, normed_ref, query_ref, context_ref, weights_ref,
 ):
@@ -2158,39 +2220,6 @@
     out_ref[...] = target + nt(context_ref[...], wout_ref[...])
 
 
-def cross_forward(x2, enc_gains, enc_weight, y1, dec_gains, dec_weight, dec_lengths, enc_lengths):
-    low = jnp.bfloat16
-    y2, *kept = pl.pallas_call(
-        cross_forward_kernel,
-        out_shape=[
-            jax.ShapeDtypeStruct((LD, D), jnp.float32),
-            jax.ShapeDtypeStruct((LE, D), low),
-            jax.ShapeDtypeStruct((LE, 2 * HD), low),
-            jax.ShapeDtypeStruct((LD, D), low),
-            jax.ShapeDtypeStruct((LD, HD), low),
-            jax.ShapeDtypeStruct((LD, HD), low),
-            jax.ShapeDtypeStruct((H, LD, LE), jnp.float32),
-        ],
-        in_specs=[VM, VM, C_IN, C_OUT, VM, VM, C_IN, C_OUT, SM, SM],
-        out_specs=[VM] * 7,
-        grid=(1,),
-        compiler_params=pltpu.CompilerParams(vmem_limit_bytes=VMEM_LIMIT),
-        name="cross_forward",
-    )(
-        x2,
-        enc_gains,
-        enc_weight,
-        enc_weight,
-        y1,
-        dec_gains,
-        dec_weight,
-        dec_weight,
-        dec_lengths,
-        enc_lengths,
-    )
-    return y2, kept
-
-
 def cross_backward_rows(
     g_ref, x_ref, final_ref, wkey_ref, wvalue_ref, y_ref, gain_ref, wquery_ref, wout_ref, kv_ref, query_ref, weights_ref,
     gx_ref, gy_ref, final_out, gain_out, kv_grad, query_grad, context_grad,
@@ -2569,7 +2598,7 @@
 ):
     wide, rows = lax.axis_size("wide"), lax.axis_size("rows")
     enc_attn, dec_half, gains, biases, enc_blocks, dec_blocks = start_weights(
-        wide, rows, attn_in, attn_out, cross_in, cross_out, ffn_in, ffn_out, norm_gains[0], rel_bias[0].T
+        wide, rows, attn_in, attn_out, cross_in, cross_out, ffn_in, ffn_out, jnp.swapaxes(norm_gains, 0, 1), rel_bias.transpose(2, 0, 1)
     )
     enc_lengths, dec_lengths = enc_lengths[:, 0], dec_lengths[:, 0]
     x1, enc_self, moved = self_forward(
@@ -2587,14 +2616,21 @@
         wide, x1, (gains[0], 1), [enc_blocks[0], *enc_pieces], 2, (dec_half, *dec_pieces)
     )
     enc_ffn, dec_attn, dec_pieces = enc_ffn[:4], enc_ffn[4], [dec_blocks[0], *dec_pieces, *enc_ffn[5:]]
-    y1, dec_self, _ = self_forward(
-        True, dec_embed[:, 0], gains[1], dec_attn, biases[1], dec_lengths
-    )
-    y2, cross_kept = cross_forward(
-        x2, gains[0], enc_attn, y1, gains[1], dec_attn, dec_lengths, enc_lengths
-    )
-    y3, g2, dec_ffn_gain, *dec_ffn_grads = ffn_both_call(
-        wide, rows, y2, out_cot[:, 0], (gains[1], 2), dec_pieces, 3
+    y3, g2, dec_ffn_gain, dec_ffn_grads, y1, dec_self, cross_kept = decoder_call(
+        wide,
+        rows,
+        out_cot[:, 0],
+        (gains[1], 2),
+        dec_pieces,
+        x2,
+        gains[0],
+        dec_embed[:, 0],
+        biases[1],
+        dec_lengths,
+        enc_lengths,
+        enc_attn,
+        dec_attn,
+        3,
     )
     (
         grad_x1,

time: 479 us -> 475 us (level)
    pallas_call x1, Pallas kernels: 125 us -> 132 us  [last_step(): pl.pallas_call(lambda *refs: last_kernel(wide, rows, *refs), out_shape=[j...]
    pallas_call x2 -> x1, Pallas kernels: 66.4 us -> 60.6 us  [self_forward(): pl.pallas_call(lambda *refs: self_forward_kernel(wide, causal, *refs), ou...]
    pallas_call x2 -> x1, Pallas kernels: 48.2 us -> 46.9 us  [decoder_call(): pl.pallas_call(lambda *refs: decoder_kernel(wide, rows_axis, gain_at, *re...]
where the time goes in v8:
time: 475 us; the launch traced here: 470 us
  Pallas kernels  466 us (98%)
    pallas_call x1, Pallas kernels, last_step(): pl.pallas_call(lambda *refs: last_kernel(wide, rows, *refs), out_shape=[j...  132 us
    pallas_call x1, Pallas kernels, ffn_backward_call(): pl.pallas_call(lambda *refs: ffn_backward_kernel(wide, rows_axis, gain_at...  94.3 us
    pallas_call x1, Pallas kernels, ffn_forward_call(): pl.pallas_call(lambda *refs: ffn_forward_kernel(wide, bool(carried), len(...  83.7 us
    pallas_call x1, Pallas kernels, self_forward(): pl.pallas_call(lambda *refs: self_forward_kernel(wide, causal, *refs), ou...  60.6 us
    pallas_call x1, Pallas kernels, decoder_call(): pl.pallas_call(lambda *refs: decoder_kernel(wide, rows_axis, gain_at, *re...  46.9 us
    pallas_call x1, Pallas kernels, start_weights(): pl.pallas_call(lambda *refs: start_weights_kernel(wide, rows, *refs), out...  42 us

profile of v8, /device:TPU:0, one launch (start us, length us, event | category | flops | bytes accessed | tf_op | source)
XLA Modules:
  0.0 469.8 jit_solution(12330348115402249829)
XLA Ops:
  0.6 42.0 %start_weights.1 = (bf16[2,1472,1152]{2,1,0:T(8,128)(2,1)}, bf16[368,1152]{1,0:T(8,128)(2,1)}, f32[3,1472]{1,0:T(4,128)}, f32[3,1472]{1,0:T(4,128)}, f32[6,256,2...) custom-call(bf16[1,368,1152]{2,1,0:T(8,128)(2,1)} %refs_0_.1, ...), custom_call_target="tpu_custom_call" | custom-call | tf_op jit(solution)/shard_map/start_weights/pallas_call | solution.py:1438
  42.6 60.6 %self_forward_256.1 = (f32[256,1472]{1,0:T(8,128)}, bf16[256,1472]{1,0:T(8,128)(2,1)}, bf16[256,1472]{1,0:T(8,128)(2,1)}, bf16[256,1152]{1,0:T(8,128)(2,1)}, bf1...) custom-call(bf16[2,1472,256]{2,1,0:T(8,128)(2,1)} %bitcast.33, ...), custom_call_target="tpu_custom_call" | custom-call | tf_op jit(solution)/shard_map/self_forward_256/pallas_call | solution.py:2108
  103.2 83.7 %ffn_forward_256.1 = (f32[256,1472]{1,0:T(8,128)}, bf16[1472,1024]{1,0:T(8,128)(2,1)}, bf16[2,1024,1024]{2,1,0:T(8,128)(2,1)}, bf16[2,512,1024]{2,1,0:T(8,128)(2...) custom-call(f32[256,1472]{1,0:T(8,128)} %get-tuple-element.102.refs_, ...), custom_call_target="tpu_custom_call" | custom-call | tf_op jit(solution)/shard_map/ffn_forward_256/pallas_call | solution.py:683
  186.9 46.9 %decoder.1 = (f32[64,1472]{1,0:T(8,128)}, f32[64,1472]{1,0:T(8,128)}, f32[1,1472]{1,0:T(1,128)}, bf16[4,2,1472,128]{3,2,1,0:T(8,128)(2,1)}, bf16[4,112,1472]{2,1...) custom-call(bf16[2,64,1472]{2,1,0:T(8,128)(2,1)} %bitcast.36, ...), custom_call_target="tpu_custom_call" | custom-call | tf_op jit(solution)/shard_map/decoder/pallas_call | solution.py:1166
  233.8 94.3 %ffn_backward_256.1 = (f32[256,1472]{1,0:T(8,128)}, f32[1,1472]{1,0:T(1,128)}, bf16[4,2,1472,128]{3,2,1,0:T(8,128)(2,1)}, bf16[4,112,1472]{2,1,0:T(8,128)(2,1)},...) custom-call(f32[256,1472]{1,0:T(8,128)} %get-tuple-element.102.refs_, ...), custom_call_target="tpu_custom_call" | custom-call | tf_op jit(solution)/shard_map/ffn_backward_256/pallas_call | solution.py:1226
  328.1 132.1 %last_step.1 = (f32[2,192,576]{2,1,0:T(8,128)}, bf16[2,4,3,368,128]{4,3,2,1,0:T(8,128)(2,1)}, f32[16,1536]{1,0:T(8,128)}, bf16[2,64,736]{2,1,0:T(8,128)(2,1)}, f...) custom-call(f32[64,1472]{1,0:T(8,128)} %get-tuple-element.114.refs_11_.refs_0_, ...), custom_call_target="tpu_custom_call" | custom-call | tf_op jit(solution)/shard_map/last_step/pallas_call | solution.py:1813
  460.3 0.0 copy-start.2
  460.3 0.0 copy-start
  460.3 6.7 %assemble.1 = (f32[1,368,1792]{2,1,0:T(8,128)}, f32[1,368,896]{2,1,0:T(8,128)}, f32[3,1,1472]{2,1,0:T(1,128)}, f32[6,1,32]{2,1,0:T(1,128)}, f32[1,288,368]{2,1,0...) custom-call(bf16[2,4,3,368,128]{4,3,2,1,0:T(8,128)(2,1)} %get-tuple-element.154.refs_0_, ...), custom_call_target="tpu_custom_call" | custom-call | tf_op jit(solution)/shard_map/assemble/pallas_call | solution.py:1920
  466.9 0.0 copy-done.2
  466.9 0.7 copy.34
  467.6 0.0 copy-done
  467.6 0.0 copy-start.1
  467.6 1.1 copy.35
  468.7 0.1 copy-done.1
  468.8 0.7 copy.36
Async XLA Ops:
  460.3 6.7 %copy-start.2 = (bf16[2,64,736]{2,1,0:T(8,128)(2,1)S(1)}, bf16[2,64,736]{2,1,0:T(8,128)(2,1)}, u32[]{:S(2)}) copy-start(bf16[2,64,736]{2,1,0:T(8,128)(2,1)} %get-tuple-element.151) | copy-start | bytes 565252
  460.3 7.4 %copy-start = (f32[2,736,256]{2,1,0:T(8,128)S(1)}, f32[2,736,256]{2,1,0:T(8,128)}, u32[]{:S(2)}) copy-start(f32[2,736,256]{2,1,0:T(8,128)} %get-tuple-element.152) | copy-start | bytes 4521988
  467.6 1.2 copy-start.1
